TPU v7x, 32 devices: a whole 2x2x4 slice. The times are simulated.
32 devices in a mesh: groups: 2 (over y), row: 4 (over x, core), col: 4 (over z).
Axes of the slice: x: 2, y: 2, z: 4, core: 2. Of those that a mesh axis runs over, the one named last changes fastest.
Arguments:
- density: float32 [8, 4, 1, 8, 4096], P(('groups', 'row'), 'col'), parts along dimension 0, may hold values from -0.84 to 0.84
- density_pattern: int32 [8, 4, 1, 8], P(('groups', 'row'), 'col'), parts along dimension 0, may hold values from -1 to 15, as said below
- response: float32 [8, 4, 1, 8, 4096], P(('groups', 'row'), 'col'), parts along dimension 0, may hold values from -0.84 to 0.84
- response_pattern: int32 [8, 4, 1, 8], P(('groups', 'row'), 'col'), parts along dimension 0, may hold values from -1 to 15, as said below
- density_next_pattern: int32 [8, 4, 1, 8], P(('groups', 'row'), 'col'), parts along dimension 0, may hold values from -1 to 15, as said below
- response_next_pattern: int32 [8, 4, 1, 8], P(('groups', 'row'), 'col'), parts along dimension 0, may hold values from -1 to 15, as said below
- density_out_pattern: int32 [8, 4, 1, 8], P(('groups', 'row'), 'col'), parts along dimension 0, may hold values from -1 to 15, as said below
- response_out_pattern: int32 [8, 4, 1, 8], P(('groups', 'row'), 'col'), parts along dimension 0, may hold values from -1 to 15, as said below
Outputs:
- density_final: float32 [8, 4, 1, 8, 4096], P(('groups', 'row'), 'col'), parts along dimension 0
- response_final: float32 [8, 4, 1, 8, 4096], P(('groups', 'row'), 'col'), parts along dimension 0
There are 2 independent parts, one for each index of `groups`. A program takes and returns all parts, laid end to end along the dimension named above; each array names one. Nothing has to cross between parts.
Inputs may be any that keep to these rules, and one draw needn't show every extreme that they name: `density_pattern`: in every block row the live entries (not -1) are distinct ids of atom groups held by the owning device or by one of its eight neighbours on the periodic 4 x 4 grid of device positions; at least 4 entries of a row are live, and some row has all 8 live. `response_pattern`: as for density_pattern. `density_next_pattern`: as for density_pattern. `response_next_pattern`: as for density_pattern. `density_out_pattern`: as for density_pattern. `response_out_pattern`: as for density_pattern.
All inputs are finite; a program needn't handle non-finite values.
Results may differ from a plain program's by a relative error of at most 0.0003.
Values sent between devices are 32-bit elements; how exact they have to be, the bound alone decides.
No kernel may reach another device: no remote copies, remote signals or barrier semaphores. Data moves between devices by JAX's collectives and lax.ppermute only.
A program may use at most 64 MiB of HBM per device.

v0:
```python
import jax
import jax.numpy as jnp
from jax import lax
from jax.sharding import PartitionSpec as P

BLOCK = 64


def with_halo(cells, sides, width):
    for axis, dim in sides:
        count = lax.axis_size(axis)
        head = lax.slice_in_dim(cells, 0, width, axis=dim)
        tail = lax.slice_in_dim(cells, cells.shape[dim] - width, cells.shape[dim], axis=dim)
        cells = jnp.concatenate(
            [
                lax.ppermute(tail, axis, [(i, (i + 1) % count) for i in range(count)]),
                cells,
                lax.ppermute(head, axis, [((i + 1) % count, i) for i in range(count)]),
            ],
            axis=dim,
        )
    return cells


def carry_over(block_data, pattern, target):
    slot_range = jnp.arange(pattern.shape[-1], dtype=jnp.int32)
    matches = (pattern[..., None, :] == target[..., :, None]) & (target[..., :, None] >= 0)
    located = jnp.any(matches, axis=-1)
    slot_hit = jnp.sum(jnp.where(matches, slot_range, 0), axis=-1)
    picked = jnp.take_along_axis(block_data, slot_hit[..., None], axis=-2)
    return jnp.where(located[..., None], picked, 0.0)


def neighbors(first_data, first_pattern, second_data, second_pattern):
    stacked_data = jnp.stack([first_data, second_data], axis=2)
    stacked_pattern = jnp.stack([first_pattern, second_pattern], axis=2)
    widened_data = with_halo(stacked_data, (("col", 1),), 1)
    widened_pattern = with_halo(stacked_pattern, (("col", 1),), 1)
    near_data = with_halo(widened_data, (("row", 0),), 1)
    near_pattern = with_halo(widened_pattern, (("row", 0),), 1)
    return (near_data[:, :, 0], near_pattern[:, :, 0], near_data[:, :, 1], near_pattern[:, :, 1])


def block_product(left_data, left_pattern, near_data, near_pattern, target_pattern, position):
    row_at, col_at, row_total, col_total = position
    groups = left_pattern.shape[2]
    slot_count = left_pattern.shape[3]
    slot_range = jnp.arange(slot_count, dtype=jnp.int32)
    left_cols = left_pattern.reshape(groups, slot_count)
    target = target_pattern.reshape(groups, slot_count)
    live_left = left_cols >= 0
    source = jnp.where(live_left, left_cols, 0)
    owner_row = source // (col_total * groups)
    owner_col = source // groups % col_total
    member = source % groups
    near_index = (
        (owner_row - row_at + 1) % row_total * 3 + (owner_col - col_at + 1) % col_total
    ) * groups + member
    flat_pattern = near_pattern.reshape(9 * groups, slot_count)
    flat_blocks = near_data.reshape(9 * groups * slot_count, BLOCK * BLOCK)
    left_blocks = left_data.reshape(groups, slot_count, BLOCK, BLOCK)
    target_live = target >= 0
    right_cols = flat_pattern[near_index]
    matches = (
        (right_cols[:, :, None, :] == target[:, None, :, None])
        & target_live[:, None, :, None]
        & live_left[:, :, None, None]
    )
    located = jnp.any(matches, axis=3)
    slot_hit = jnp.sum(jnp.where(matches, slot_range, 0), axis=3)
    picked = flat_blocks[near_index[:, :, None] * slot_count + slot_hit]
    picked = jnp.where(located[..., None], picked, 0.0).reshape(
        groups, slot_count, slot_count, BLOCK, BLOCK
    )
    result = jnp.einsum("gaxz,gaszy->gsxy", left_blocks, picked, precision=lax.Precision.HIGHEST)
    result = result.reshape(groups, slot_count, BLOCK * BLOCK)
    result = jnp.where(target_live[..., None], result, 0.0)
    return result.reshape(1, 1, groups, slot_count, BLOCK * BLOCK)


def shards(
    density,
    density_pattern,
    response,
    response_pattern,
    density_next_pattern,
    response_next_pattern,
    density_out_pattern,
    response_out_pattern,
):
    position = (
        lax.axis_index("row"),
        lax.axis_index("col"),
        lax.axis_size("row"),
        lax.axis_size("col"),
    )
    near_density, near_density_pattern, near_response, near_response_pattern = neighbors(
        density, density_pattern, response, response_pattern
    )
    density_next = block_product(
        density, density_pattern, near_density, near_density_pattern, density_next_pattern, position
    )
    response_next = block_product(
        density,
        density_pattern,
        near_response,
        near_response_pattern,
        response_next_pattern,
        position,
    ) + block_product(
        response,
        response_pattern,
        near_density,
        near_density_pattern,
        response_next_pattern,
        position,
    )
    near_dnext, near_dnext_pattern, near_rnext, near_rnext_pattern = neighbors(
        density_next, density_next_pattern, response_next, response_next_pattern
    )
    density_final = 2.0 * carry_over(
        density_next, density_next_pattern, density_out_pattern
    ) - block_product(
        density_next,
        density_next_pattern,
        near_dnext,
        near_dnext_pattern,
        density_out_pattern,
        position,
    )
    response_final = 2.0 * carry_over(
        response_next, response_next_pattern, response_out_pattern
    ) - (
        block_product(
            density_next,
            density_next_pattern,
            near_rnext,
            near_rnext_pattern,
            response_out_pattern,
            position,
        )
        + block_product(
            response_next,
            response_next_pattern,
            near_dnext,
            near_dnext_pattern,
            response_out_pattern,
            position,
        )
    )
    return (density_final, response_final)


def solution(mesh):
    in_specs = (
        P(("groups", "row"), "col", None, None, None),
        P(("groups", "row"), "col", None, None),
        P(("groups", "row"), "col", None, None, None),
        P(("groups", "row"), "col", None, None),
        P(("groups", "row"), "col", None, None),
        P(("groups", "row"), "col", None, None),
        P(("groups", "row"), "col", None, None),
        P(("groups", "row"), "col", None, None),
    )
    out_specs = (
        P(("groups", "row"), "col", None, None, None),
        P(("groups", "row"), "col", None, None, None),
    )
    return jax.shard_map(shards, mesh=mesh, in_specs=in_specs, out_specs=out_specs, check_vma=False)
```

profile of v0, /device:TPU:1, one launch (start us, length us, event | category | flops | bytes accessed | tf_op | source)
XLA Modules:
  0.0 161.9 jit_solution(3098607786463070022)
XLA Ops:
  0.7 0.8 pad_add_fusion.4
  1.5 4.2 %collective-permute-start.1 = (s32[1,1,2,1,8]{4,3,2,1,0:T(1,128)S(1)}, s32[1,1,2,1,8]{4,3,2,1,0:T(1,128)S(1)}, u32[]{:S(2)}, u32[]{:S(2)}) collective-permute-start(s32[1,1,2,1,8]{4,3,2,1,0:T(1,128)S(1)} %pad_add_fusion.4), channel_id=1, source_target_pairs={{1,0},{2,1},{3,2},{0,3},{5,4},{6,5},{7,6},{4,7},{9,8},{10,9},{11,1... | collective-permute-start | bytes 200 | tf_op jit(solution)/shard_map/ppermute | solution.py:18
  6.3 3.3 %collective-permute-start.9 = (s32[1,1,2,1,8]{4,3,2,1,0:T(1,128)S(1)}, s32[1,1,2,1,8]{4,3,2,1,0:T(1,128)S(1)}, u32[]{:S(2)}, u32[]{:S(2)}) collective-permute-start(s32[1,1,2,1,8]{4,3,2,1,0:T(1,128)S(1)} %pad_add_fusion.5), channel_id=1, source_target_pairs={{1,0},{2,1},{3,2},{0,3},{5,4},{6,5},{7,6},{4,7},{9,8},{10,9},{11,1... | collective-permute-start | bytes 200 | tf_op jit(solution)/shard_map/ppermute | solution.py:18
  9.6 1.0 pad_maximum_fusion.4
  10.6 3.3 %collective-permute-start.5 = (f32[1,1,2,1,8,4096]{5,4,3,2,1,0:T(8,128)S(1)}, f32[1,1,2,1,8,4096]{5,4,3,2,1,0:T(8,128)S(1)}, u32[]{:S(2)}, u32[]{:S(2)}) collective-permute-start(f32[1,1,2,1,8,4096]{5,4,3,2,1,0:T(8,128)S(1)} %pad_maximum_fusion.4), channel_id=1, source_target_pairs={{1,0},{2,1},{3,2},{0,3},{5,4},{6,5},{7,6},{4,7},{9,8},{10,9},{11,1... | collective-permute-start | bytes 786440 | tf_op jit(solution)/shard_map/ppermute | solution.py:18
  14.6 0.9 select_reduce_fusion.7
  16.0 0.9 select_reduce_fusion.6
  17.4 1.4 fusion.29
  18.8 1.4 fusion.30
  24.4 1.7 %reshape.2687 = f32[8,64,64,1]{2,1,0,3:T(8,128)} reshape(f32[1,1,1,8,4096]{4,3,2,1,0:T(8,128)} %param.10) | data formatting | bytes 262144 | tf_op jit(solution)/shard_map/reshape.13
  27.3 1.7 %reshape.2690 = f32[8,64,64,1]{2,1,0,3:T(8,128)} reshape(f32[1,1,1,8,4096]{4,3,2,1,0:T(8,128)} %param.12) | data formatting | bytes 262144 | tf_op jit(solution)/shard_map/reshape.76
  29.7 2.1 %collective-permute-start.11 = (s32[1,3,2,1,8]{4,3,2,1,0:T(1,128)S(1)}, s32[1,3,2,1,8]{4,3,2,1,0:T(1,128)S(1)}, u32[]{:S(2)}, u32[]{:S(2)}) collective-permute-start(s32[1,3,2,1,8]{4,3,2,1,0:T(1,128)S(1)} %pad_add_fusion.3), channel_id=1, source_target_pairs={{4,0},{8,4},{12,8},{0,12},{5,1},{9,5},{13,9},{1,13},{6,2},{10,6},{... | collective-permute-start | bytes 584 | tf_op jit(solution)/shard_map/ppermute | solution.py:18
  31.8 1.2 collective-permute-start.10
  33.6 0.8 collective-permute-done.11
  34.5 0.9 collective-permute-start.2
  40.3 1.7 %select_reduce_fusion.1 = (s32[8,8]{1,0:T(8,128)S(1)}, s32[8,8]{1,0:T(8,128)S(1)}, s32[8,8]{1,0:T(8,128)S(1)}, s32[8,8]{1,0:T(8,128)S(1)}, s32[8,8]{1,0:T(8,128)S(1)}, /*index=5*/s32[8,8]{1,0:T(8,128)S(1)}) fusion(s32[8,8]{1,0:T(8,128)S(1)} %gather_fusion.8, s32[8]{0:T(128)} %bitcast.291, pred[8]{0:T(512)(128)(4,1)S(1)} %get-tuple-element.43, ...), kind=kLoop, calls=%fused_computation.62 | loop fusion | flops 14976 | bytes 3248 | tf_op jit(solution)/shard_map/reduce_sum | solution.py:70
  42.8 1.0 pad_maximum_fusion.2
  43.8 1.7 %collective-permute-start.6 = (f32[1,3,2,1,8,4096]{5,4,3,2,1,0:T(8,128)S(1)}, f32[1,3,2,1,8,4096]{5,4,3,2,1,0:T(8,128)S(1)}, u32[]{:S(2)}, u32[]{:S(2)}) collective-permute-start(f32[1,3,2,1,8,4096]{5,4,3,2,1,0:T(8,128)S(1)} %pad_maximum_fusion.2), channel_id=1, source_target_pairs={{0,4},{4,8},{8,12},{12,0},{1,5},{5,9},{9,13},{13,1},{2,6},{6,10},{... | collective-permute-start | bytes 2359304 | tf_op jit(solution)/shard_map/ppermute | solution.py:16
  48.0 1.6 fusion.27
  49.6 14.3 %collective-permute-done.7 = f32[1,3,2,1,8,4096]{5,4,3,2,1,0:T(8,128)S(1)} collective-permute-done((f32[1,3,2,1,8,4096]{5,4,3,2,1,0:T(8,128)S(1)}, f32[1,3,2,1,8,4096]{5,4,3,2,1,0:T(8,128)S(1)}, u32[]{:S(2)}, u32[]{:S(2)}) %collective-permute-start.7) | collective-permute-done | bytes 786464 | tf_op jit(solution)/shard_map/ppermute | solution.py:18
  64.3 0.9 gather_fusion.1
  65.3 1.1 bitcast_select_fusion.5
  66.4 3.1 %select_n.997 = f32[8,8,64,64]{3,2,1,0:T(8,128)} reshape(f32[1,8,8,4096]{3,2,1,0:T(8,128)} %bitcast_select_fusion.5) | data formatting | bytes 2097152 | tf_op jit(solution)/shard_map/jit(_where)/select_n | solution.py:72
  69.6 5.0 %convolution_bitcast_fusion.5 = f32[1,8,64,64]{2,3,1,0:T(8,128)S(1)} fusion(f32[8,8,64,64]{3,2,1,0:T(8,128)} %select_n.997, f32[8,64,64,1]{2,1,0,3:T(8,128)S(1)} %copy-done.2), kind=kOutput, calls=%fused_computation.21 | convolution fusion | flops 201326592 | bytes 1310720 | tf_op jit(solution)/shard_map/gaxz,gaszy->gsxy/dot_general | solution.py:75
  74.7 0.8 reshape.2509
  75.5 0.8 reshape.2507
  76.3 0.9 gather_fusion.6
  77.2 1.1 bitcast_select_fusion.3
  78.3 2.2 %select_n.1027 = f32[8,8,64,64]{3,2,1,0:T(8,128)S(1)} reshape(f32[1,8,8,4096]{3,2,1,0:T(8,128)} %bitcast_select_fusion.3) | data formatting | bytes 2097152 | tf_op jit(solution)/shard_map/jit(_where)/select_n | solution.py:72
  80.5 4.4 %convolution_bitcast_fusion.3 = f32[1,8,64,64]{2,3,1,0:T(8,128)S(1)} fusion(f32[8,8,64,64]{3,2,1,0:T(8,128)S(1)} %select_n.1027, f32[8,64,64,1]{2,1,0,3:T(8,128)} %reshape.2690), kind=kOutput, calls=%fused_computation.19 | convolution fusion | flops 201326592 | bytes 1310720 | tf_op jit(solution)/shard_map/gaxz,gaszy->gsxy/dot_general | solution.py:75
  85.0 0.8 reshape.2515
  85.8 1.6 %broadcast_select_fusion = f32[1,1,1,1,8,4096]{5,4,3,2,1,0:T(8,128)} fusion(f32[1,1,1,1,8,4096]{5,4,3,2,1,0:T(8,128)} %reshape.2509, pred[8]{0:T(512)(128)(4,1)S(1)} %get-tuple-element.42), kind=kLoop, calls=%fused_computation.60 | loop fusion | flops 32768 | bytes 262152 | tf_op jit(solution)/shard_map/jit(_where)/select_n | solution.py:77
  87.4 1.0 gather_fusion.4
  88.5 0.7 bitcast_select_fusion.4
  89.2 0.8 select_n.1011
  90.2 3.4 %convolution_bitcast_fusion.4 = f32[1,8,64,64]{2,3,1,0:T(8,128)S(1)} fusion(f32[8,8,64,64]{3,2,1,0:T(8,128)S(1)} %select_n.1011, f32[8,64,64,1]{2,1,0,3:T(8,128)S(1)} %copy-done.3), kind=kOutput, calls=%fused_computation.20 | convolution fusion | flops 201326592 | bytes 1310720 | tf_op jit(solution)/shard_map/gaxz,gaszy->gsxy/dot_general | solution.py:75
  94.0 3.6 %collective-permute-start.13 = (f32[1,1,2,1,8,4096]{5,4,3,2,1,0:T(8,128)S(1)}, f32[1,1,2,1,8,4096]{5,4,3,2,1,0:T(8,128)S(1)}, u32[]{:S(2)}, u32[]{:S(2)}) collective-permute-start(f32[1,1,2,1,8,4096]{5,4,3,2,1,0:T(8,128)S(1)} %pad_maximum_fusion.5), channel_id=1, source_target_pairs={{1,0},{2,1},{3,2},{0,3},{5,4},{6,5},{7,6},{4,7},{9,8},{10,9},{11,1... | collective-permute-start | bytes 786440 | tf_op jit(solution)/shard_map/ppermute | solution.py:18
  97.7 0.8 reshape.2519
  98.5 0.8 reshape.2518
  99.2 1.5 gather_fusion.12
  100.7 2.2 %collective-permute-done.13 = f32[1,1,2,1,8,4096]{5,4,3,2,1,0:T(8,128)S(1)} collective-permute-done((f32[1,1,2,1,8,4096]{5,4,3,2,1,0:T(8,128)S(1)}, f32[1,1,2,1,8,4096]{5,4,3,2,1,0:T(8,128)S(1)}, u32[]{:S(2)}, u32[]{:S(2)}) %collective-permute-start.13) | collective-permute-done | bytes 262176 | tf_op jit(solution)/shard_map/ppermute | solution.py:18
  103.0 6.6 %collective-permute-done.12 = f32[1,1,2,1,8,4096]{5,4,3,2,1,0:T(8,128)S(1)} collective-permute-done((f32[1,1,2,1,8,4096]{5,4,3,2,1,0:T(8,128)S(1)}, f32[1,1,2,1,8,4096]{5,4,3,2,1,0:T(8,128)S(1)}, u32[]{:S(2)}, u32[]{:S(2)}) %collective-permute-start.12) | collective-permute-done | bytes 262176 | tf_op jit(solution)/shard_map/ppermute | solution.py:16
  109.7 1.0 collective-permute-start.15
  110.6 0.8 collective-permute-start.14
  111.5 1.4 gather_fusion.13
  112.9 16.6 %collective-permute-done.15 = f32[1,3,2,1,8,4096]{5,4,3,2,1,0:T(8,128)S(1)} collective-permute-done((f32[1,3,2,1,8,4096]{5,4,3,2,1,0:T(8,128)S(1)}, f32[1,3,2,1,8,4096]{5,4,3,2,1,0:T(8,128)S(1)}, u32[]{:S(2)}, u32[]{:S(2)}) %collective-permute-start.15) | collective-permute-done | bytes 786464 | tf_op jit(solution)/shard_map/ppermute | solution.py:18
  130.5 0.9 gather_fusion.11
  131.4 1.8 %gather_fusion.7 = f32[64,4096]{1,0:T(8,128)} fusion(f32[72,4096]{1,0:T(8,128)S(1)} %bitcast.260, s32[1024]{0:T(1024)S(1)} %copy-done.23), kind=kCustom, calls=%fused_computation.9 | custom fusion | bytes 2097408 | tf_op jit(solution)/shard_map/gather | solution.py:71
  133.3 1.2 bitcast_select_fusion
  134.4 2.0 %select_n.1063 = f32[8,8,64,64]{3,2,1,0:T(8,128)S(1)} reshape(f32[1,8,8,4096]{3,2,1,0:T(8,128)} %bitcast_select_fusion) | data formatting | bytes 2097152 | tf_op jit(solution)/shard_map/jit(_where)/select_n | solution.py:72
  136.5 5.1 %convolution_bitcast_fusion = f32[1,8,64,64]{2,3,1,0:T(8,128)} fusion(f32[8,8,64,64]{3,2,1,0:T(8,128)S(1)} %select_n.1063, f32[1,8,64,64]{2,3,1,0:T(8,128)S(1)} %copy-done.5, f32[1,8,64,64]{2,3,1,0:T(8,128)} %copy-done.6, pred[8]{0:T(512)(128)(4,1)S(1)} %get-tuple-element.41), kind=kOutput, calls=%fused_computation.16 | convolution fusion | flops 201424896 | bytes 1441800 | tf_op jit(solution)/shard_map/gaxz,gaszy->gsxy/dot_general | solution.py:75
  141.6 1.1 copy.48
  142.7 0.8 reshape.2523
  143.4 2.4 %bitcast_select_fusion.2 = f32[1,8,8,4096]{3,2,1,0:T(8,128)} fusion(f32[64,4096]{1,0:T(8,128)} %gather_fusion.7, pred[8,8]{1,0:T(8,128)(4,1)} %get-tuple-element.21), kind=kLoop, calls=%fused_computation.24 | loop fusion | flops 262144 | bytes 2097216 | tf_op jit(solution)/shard_map/jit(_where)/select_n | solution.py:72
  145.8 2.0 %select_n.1037 = f32[8,8,64,64]{3,2,1,0:T(8,128)S(1)} reshape(f32[1,8,8,4096]{3,2,1,0:T(8,128)} %bitcast_select_fusion.2) | data formatting | bytes 2097152 | tf_op jit(solution)/shard_map/jit(_where)/select_n | solution.py:72
  147.9 4.2 %convolution_bitcast_fusion.2 = f32[1,8,64,64]{2,3,1,0:T(8,128)} fusion(f32[8,8,64,64]{3,2,1,0:T(8,128)S(1)} %select_n.1037, f32[1,8,64,64]{2,3,1,0:T(8,128)S(1)} %copy-done.1, pred[8]{0:T(512)(128)(4,1)S(1)} %get-tuple-element.42), kind=kOutput, calls=%fused_computation.18 | convolution fusion | flops 201359360 | bytes 1310728 | tf_op jit(solution)/shard_map/gaxz,gaszy->gsxy/dot_general | solution.py:75
  152.0 1.1 copy.40
  153.1 0.8 reshape.2517
  153.9 0.9 gather_fusion.9
  154.8 0.8 bitcast_select_fusion.1
  155.7 0.8 select_n.1047
  156.6 3.5 %convolution_bitcast_fusion.1 = f32[1,8,64,64]{2,3,1,0:T(8,128)S(1)} fusion(f32[8,8,64,64]{3,2,1,0:T(8,128)S(1)} %select_n.1047, f32[1,8,64,64]{2,3,1,0:T(8,128)S(1)} %copy-done.1, pred[8]{0:T(512)(128)(4,1)S(1)} %get-tuple-element.42), kind=kOutput, calls=%fused_computation.17 | convolution fusion | flops 201359360 | bytes 1310728 | tf_op jit(solution)/shard_map/gaxz,gaszy->gsxy/dot_general | solution.py:75
  160.3 0.8 fusion.16
  161.1 0.8 fusion.13
  (146 shorter events, 19.9 us)
Async XLA Ops:
  0.6 47.3 %copy-start.21 = (s32[1,1,1,8]{3,2,1,0:T(1,128)S(1)}, s32[1,1,1,8]{3,2,1,0:T(1,128)}, u32[]{:S(2)}) copy-start(s32[1,1,1,8]{3,2,1,0:T(1,128)} %param.14) | copy-start | bytes 100
  0.6 47.3 %copy-start.20 = (s32[1,1,1,8]{3,2,1,0:T(1,128)S(1)}, s32[1,1,1,8]{3,2,1,0:T(1,128)}, u32[]{:S(2)}) copy-start(s32[1,1,1,8]{3,2,1,0:T(1,128)} %param.15) | copy-start | bytes 100
  0.7 63.2 %copy-start.9 = (f32[1,1,1,8,4096]{4,3,2,1,0:T(8,128)S(1)}, f32[1,1,1,8,4096]{4,3,2,1,0:T(8,128)}, u32[]{:S(2)}) copy-start(f32[1,1,1,8,4096]{4,3,2,1,0:T(8,128)} %param.12) | copy-start | bytes 393220
  0.7 63.2 %copy-start.10 = (f32[1,1,1,8,4096]{4,3,2,1,0:T(8,128)S(1)}, f32[1,1,1,8,4096]{4,3,2,1,0:T(8,128)}, u32[]{:S(2)}) copy-start(f32[1,1,1,8,4096]{4,3,2,1,0:T(8,128)} %param.10) | copy-start | bytes 393220
  0.7 47.3 %copy-start.25 = (s32[1,1,1,8]{3,2,1,0:T(1,128)S(1)}, s32[1,1,1,8]{3,2,1,0:T(1,128)}, u32[]{:S(2)}) copy-start(s32[1,1,1,8]{3,2,1,0:T(1,128)} %param.17) | copy-start | bytes 100
  0.7 47.3 %copy-start.26 = (s32[1,1,1,8]{3,2,1,0:T(1,128)S(1)}, s32[1,1,1,8]{3,2,1,0:T(1,128)}, u32[]{:S(2)}) copy-start(s32[1,1,1,8]{3,2,1,0:T(1,128)} %param.16) | copy-start | bytes 100
  1.5 30.3 %collective-permute-start.1 = (s32[1,1,2,1,8]{4,3,2,1,0:T(1,128)S(1)}, s32[1,1,2,1,8]{4,3,2,1,0:T(1,128)S(1)}, u32[]{:S(2)}, u32[]{:S(2)}) collective-permute-start(s32[1,1,2,1,8]{4,3,2,1,0:T(1,128)S(1)} %pad_add_fusion.4), channel_id=1, source_target_pairs={{1,0},{2,1},{3,2},{0,3},{5,4},{6,5},{7,6},{4,7},{9,8},{10,9},{11,1... | collective-permute-start | bytes 200 | tf_op jit(solution)/shard_map/ppermute | solution.py:18
  5.6 27.3 %collective-permute-start = (s32[1,1,2,1,8]{4,3,2,1,0:T(1,128)S(1)}, s32[1,1,2,1,8]{4,3,2,1,0:T(1,128)S(1)}, u32[]{:S(2)}, u32[]{:S(2)}) collective-permute-start(s32[1,1,2,1,8]{4,3,2,1,0:T(1,128)S(1)} %pad_add_fusion.4), channel_id=1, source_target_pairs={{0,1},{1,2},{2,3},{3,0},{4,5},{5,6},{6,7},{7,4},{8,9},{9,10},{10,1... | collective-permute-start | bytes 200 | tf_op jit(solution)/shard_map/ppermute | solution.py:16
  6.3 22.7 %collective-permute-start.9 = (s32[1,1,2,1,8]{4,3,2,1,0:T(1,128)S(1)}, s32[1,1,2,1,8]{4,3,2,1,0:T(1,128)S(1)}, u32[]{:S(2)}, u32[]{:S(2)}) collective-permute-start(s32[1,1,2,1,8]{4,3,2,1,0:T(1,128)S(1)} %pad_add_fusion.5), channel_id=1, source_target_pairs={{1,0},{2,1},{3,2},{0,3},{5,4},{6,5},{7,6},{4,7},{9,8},{10,9},{11,1... | collective-permute-start | bytes 200 | tf_op jit(solution)/shard_map/ppermute | solution.py:18
  9.6 19.5 %collective-permute-start.8 = (s32[1,1,2,1,8]{4,3,2,1,0:T(1,128)S(1)}, s32[1,1,2,1,8]{4,3,2,1,0:T(1,128)S(1)}, u32[]{:S(2)}, u32[]{:S(2)}) collective-permute-start(s32[1,1,2,1,8]{4,3,2,1,0:T(1,128)S(1)} %pad_add_fusion.5), channel_id=1, source_target_pairs={{0,1},{1,2},{2,3},{3,0},{4,5},{5,6},{6,7},{7,4},{8,9},{9,10},{10,1... | collective-permute-start | bytes 200 | tf_op jit(solution)/shard_map/ppermute | solution.py:16
  10.6 32.2 %collective-permute-start.5 = (f32[1,1,2,1,8,4096]{5,4,3,2,1,0:T(8,128)S(1)}, f32[1,1,2,1,8,4096]{5,4,3,2,1,0:T(8,128)S(1)}, u32[]{:S(2)}, u32[]{:S(2)}) collective-permute-start(f32[1,1,2,1,8,4096]{5,4,3,2,1,0:T(8,128)S(1)} %pad_maximum_fusion.4), channel_id=1, source_target_pairs={{1,0},{2,1},{3,2},{0,3},{5,4},{6,5},{7,6},{4,7},{9,8},{10,9},{11,1... | collective-permute-start | bytes 786440 | tf_op jit(solution)/shard_map/ppermute | solution.py:18
  29.0 13.7 %collective-permute-start.4 = (f32[1,1,2,1,8,4096]{5,4,3,2,1,0:T(8,128)S(1)}, f32[1,1,2,1,8,4096]{5,4,3,2,1,0:T(8,128)S(1)}, u32[]{:S(2)}, u32[]{:S(2)}) collective-permute-start(f32[1,1,2,1,8,4096]{5,4,3,2,1,0:T(8,128)S(1)} %pad_maximum_fusion.4), channel_id=1, source_target_pairs={{0,1},{1,2},{2,3},{3,0},{4,5},{5,6},{6,7},{7,4},{8,9},{9,10},{10,1... | collective-permute-start | bytes 786440 | tf_op jit(solution)/shard_map/ppermute | solution.py:16
  29.7 4.8 %collective-permute-start.11 = (s32[1,3,2,1,8]{4,3,2,1,0:T(1,128)S(1)}, s32[1,3,2,1,8]{4,3,2,1,0:T(1,128)S(1)}, u32[]{:S(2)}, u32[]{:S(2)}) collective-permute-start(s32[1,3,2,1,8]{4,3,2,1,0:T(1,128)S(1)} %pad_add_fusion.3), channel_id=1, source_target_pairs={{4,0},{8,4},{12,8},{0,12},{5,1},{9,5},{13,9},{1,13},{6,2},{10,6},{... | collective-permute-start | bytes 584 | tf_op jit(solution)/shard_map/ppermute | solution.py:18
  31.8 3.6 %collective-permute-start.10 = (s32[1,3,2,1,8]{4,3,2,1,0:T(1,128)S(1)}, s32[1,3,2,1,8]{4,3,2,1,0:T(1,128)S(1)}, u32[]{:S(2)}, u32[]{:S(2)}) collective-permute-start(s32[1,3,2,1,8]{4,3,2,1,0:T(1,128)S(1)} %pad_add_fusion.3), channel_id=1, source_target_pairs={{0,4},{4,8},{8,12},{12,0},{1,5},{5,9},{9,13},{13,1},{2,6},{6,10},{... | collective-permute-start | bytes 584 | tf_op jit(solution)/shard_map/ppermute | solution.py:16
  33.6 4.2 %collective-permute-start.3 = (s32[1,3,2,1,8]{4,3,2,1,0:T(1,128)S(1)}, s32[1,3,2,1,8]{4,3,2,1,0:T(1,128)S(1)}, u32[]{:S(2)}, u32[]{:S(2)}) collective-permute-start(s32[1,3,2,1,8]{4,3,2,1,0:T(1,128)S(1)} %pad_add_fusion.2), channel_id=1, source_target_pairs={{4,0},{8,4},{12,8},{0,12},{5,1},{9,5},{13,9},{1,13},{6,2},{10,6},{... | collective-permute-start | bytes 584 | tf_op jit(solution)/shard_map/ppermute | solution.py:18
  34.5 3.3 %collective-permute-start.2 = (s32[1,3,2,1,8]{4,3,2,1,0:T(1,128)S(1)}, s32[1,3,2,1,8]{4,3,2,1,0:T(1,128)S(1)}, u32[]{:S(2)}, u32[]{:S(2)}) collective-permute-start(s32[1,3,2,1,8]{4,3,2,1,0:T(1,128)S(1)} %pad_add_fusion.2), channel_id=1, source_target_pairs={{0,4},{4,8},{8,12},{12,0},{1,5},{5,9},{9,13},{13,1},{2,6},{6,10},{... | collective-permute-start | bytes 584 | tf_op jit(solution)/shard_map/ppermute | solution.py:16
  43.8 20.1 %collective-permute-start.7 = (f32[1,3,2,1,8,4096]{5,4,3,2,1,0:T(8,128)S(1)}, f32[1,3,2,1,8,4096]{5,4,3,2,1,0:T(8,128)S(1)}, u32[]{:S(2)}, u32[]{:S(2)}) collective-permute-start(f32[1,3,2,1,8,4096]{5,4,3,2,1,0:T(8,128)S(1)} %pad_maximum_fusion.2), channel_id=1, source_target_pairs={{4,0},{8,4},{12,8},{0,12},{5,1},{9,5},{13,9},{1,13},{6,2},{10,6},{... | collective-permute-start | bytes 2359304 | tf_op jit(solution)/shard_map/ppermute | solution.py:18
  43.8 20.0 %collective-permute-start.6 = (f32[1,3,2,1,8,4096]{5,4,3,2,1,0:T(8,128)S(1)}, f32[1,3,2,1,8,4096]{5,4,3,2,1,0:T(8,128)S(1)}, u32[]{:S(2)}, u32[]{:S(2)}) collective-permute-start(f32[1,3,2,1,8,4096]{5,4,3,2,1,0:T(8,128)S(1)} %pad_maximum_fusion.2), channel_id=1, source_target_pairs={{0,4},{4,8},{8,12},{12,0},{1,5},{5,9},{9,13},{13,1},{2,6},{6,10},{... | collective-permute-start | bytes 2359304 | tf_op jit(solution)/shard_map/ppermute | solution.py:16
  66.4 3.1 %copy-start.2 = (f32[8,64,64,1]{2,1,0,3:T(8,128)S(1)}, f32[8,64,64,1]{2,1,0,3:T(8,128)}, u32[]{:S(2)}) copy-start(f32[8,64,64,1]{2,1,0,3:T(8,128)} %reshape.2687) | copy-start | bytes 393220
  74.6 0.9 copy-start
  84.9 3.6 %copy-start.4 = (f32[1,8,64,64]{2,3,1,0:T(8,128)}, f32[1,8,64,64]{2,3,1,0:T(8,128)S(1)}, u32[]{:S(2)}) copy-start(f32[1,8,64,64]{2,3,1,0:T(8,128)S(1)} %convolution_bitcast_fusion.3) | copy-start | bytes 393220
  85.0 2.4 %copy-start.7 = (f32[1,8,64,64]{3,2,1,0:T(8,128)}, f32[1,8,64,64]{3,2,1,0:T(8,128)S(1)}, u32[]{:S(2)}) copy-start(f32[1,8,64,64]{3,2,1,0:T(8,128)S(1)} %copy.37) | copy-start | bytes 393220
  89.2 1.0 copy-start.3
  90.2 3.7 %copy-start.19 = (f32[1,1,1,1,8,4096]{5,4,3,2,1,0:T(8,128)S(1)}, f32[1,1,1,1,8,4096]{5,4,3,2,1,0:T(8,128)}, u32[]{:S(2)}) copy-start(f32[1,1,1,1,8,4096]{5,4,3,2,1,0:T(8,128)} %reshape.2515) | copy-start | bytes 393220
  90.2 3.8 %copy-start.11 = (f32[1,1,1,1,8,4096]{5,4,3,2,1,0:T(8,128)S(1)}, f32[1,1,1,1,8,4096]{5,4,3,2,1,0:T(8,128)}, u32[]{:S(2)}) copy-start(f32[1,1,1,1,8,4096]{5,4,3,2,1,0:T(8,128)} %broadcast_select_fusion) | copy-start | bytes 393220
  90.2 7.4 %copy-start.15 = (f32[1,1,1,8,4096]{4,3,2,1,0:T(8,128)S(1)}, f32[1,1,1,8,4096]{4,3,2,1,0:T(8,128)}, u32[]{:S(2)}) copy-start(f32[1,1,1,8,4096]{4,3,2,1,0:T(8,128)} %reshape.2507) | copy-start | bytes 393220
  90.2 7.5 %copy-start.8 = (f32[1,8,64,64]{3,2,1,0:T(8,128)S(1)}, f32[1,8,64,64]{3,2,1,0:T(8,128)}, u32[]{:S(2)}) copy-start(f32[1,8,64,64]{3,2,1,0:T(8,128)} %copy-done.7) | copy-start | bytes 393220
  93.6 16.0 %copy-start.6 = (f32[1,8,64,64]{2,3,1,0:T(8,128)}, f32[1,8,64,64]{2,3,1,0:T(8,128)S(1)}, u32[]{:S(2)}) copy-start(f32[1,8,64,64]{2,3,1,0:T(8,128)S(1)} %convolution_bitcast_fusion.4) | copy-start | bytes 393220
  94.0 8.9 %collective-permute-start.13 = (f32[1,1,2,1,8,4096]{5,4,3,2,1,0:T(8,128)S(1)}, f32[1,1,2,1,8,4096]{5,4,3,2,1,0:T(8,128)S(1)}, u32[]{:S(2)}, u32[]{:S(2)}) collective-permute-start(f32[1,1,2,1,8,4096]{5,4,3,2,1,0:T(8,128)S(1)} %pad_maximum_fusion.5), channel_id=1, source_target_pairs={{1,0},{2,1},{3,2},{0,3},{5,4},{6,5},{7,6},{4,7},{9,8},{10,9},{11,1... | collective-permute-start | bytes 786440 | tf_op jit(solution)/shard_map/ppermute | solution.py:18
  97.6 12.0 %collective-permute-start.12 = (f32[1,1,2,1,8,4096]{5,4,3,2,1,0:T(8,128)S(1)}, f32[1,1,2,1,8,4096]{5,4,3,2,1,0:T(8,128)S(1)}, u32[]{:S(2)}, u32[]{:S(2)}) collective-permute-start(f32[1,1,2,1,8,4096]{5,4,3,2,1,0:T(8,128)S(1)} %pad_maximum_fusion.5), channel_id=1, source_target_pairs={{0,1},{1,2},{2,3},{3,0},{4,5},{5,6},{6,7},{7,4},{8,9},{9,10},{10,1... | collective-permute-start | bytes 786440 | tf_op jit(solution)/shard_map/ppermute | solution.py:16
  99.2 12.2 %copy-start.17 = (f32[1,1,1,8,4096]{4,3,2,1,0:T(8,128)S(1)}, f32[1,1,1,8,4096]{4,3,2,1,0:T(8,128)}, u32[]{:S(2)}) copy-start(f32[1,1,1,8,4096]{4,3,2,1,0:T(8,128)} %reshape.2519) | copy-start | bytes 393220
  99.2 12.2 %copy-start.18 = (f32[1,1,1,8,4096]{4,3,2,1,0:T(8,128)S(1)}, f32[1,1,1,8,4096]{4,3,2,1,0:T(8,128)}, u32[]{:S(2)}) copy-start(f32[1,1,1,8,4096]{4,3,2,1,0:T(8,128)} %reshape.2518) | copy-start | bytes 393220
  109.7 19.9 %collective-permute-start.15 = (f32[1,3,2,1,8,4096]{5,4,3,2,1,0:T(8,128)S(1)}, f32[1,3,2,1,8,4096]{5,4,3,2,1,0:T(8,128)S(1)}, u32[]{:S(2)}, u32[]{:S(2)}) collective-permute-start(f32[1,3,2,1,8,4096]{5,4,3,2,1,0:T(8,128)S(1)} %pad_maximum_fusion.3), channel_id=1, source_target_pairs={{4,0},{8,4},{12,8},{0,12},{5,1},{9,5},{13,9},{1,13},{6,2},{10,6},{... | collective-permute-start | bytes 2359304 | tf_op jit(solution)/shard_map/ppermute | solution.py:18
  110.6 18.9 %collective-permute-start.14 = (f32[1,3,2,1,8,4096]{5,4,3,2,1,0:T(8,128)S(1)}, f32[1,3,2,1,8,4096]{5,4,3,2,1,0:T(8,128)S(1)}, u32[]{:S(2)}, u32[]{:S(2)}) collective-permute-start(f32[1,3,2,1,8,4096]{5,4,3,2,1,0:T(8,128)S(1)} %pad_maximum_fusion.3), channel_id=1, source_target_pairs={{0,4},{4,8},{8,12},{12,0},{1,5},{5,9},{9,13},{13,1},{2,6},{6,10},{... | collective-permute-start | bytes 2359304 | tf_op jit(solution)/shard_map/ppermute | solution.py:16
  129.8 0.7 copy-start.24
  130.5 0.9 copy-start.23
  131.4 1.9 %copy-start.27 = (pred[8,8]{1,0:T(8,128)(4,1)S(1)}, pred[8,8]{1,0:T(8,128)(4,1)}, u32[]{:S(2)}) copy-start(pred[8,8]{1,0:T(8,128)(4,1)} %get-tuple-element.8) | copy-start | bytes 196
  134.4 2.1 %copy-start.5 = (f32[1,8,64,64]{2,3,1,0:T(8,128)S(1)}, f32[1,8,64,64]{2,3,1,0:T(8,128)}, u32[]{:S(2)}) copy-start(f32[1,8,64,64]{2,3,1,0:T(8,128)} %copy-done.4) | copy-start | bytes 393220
  145.8 2.1 %copy-start.1 = (f32[1,8,64,64]{2,3,1,0:T(8,128)S(1)}, f32[1,8,64,64]{2,3,1,0:T(8,128)}, u32[]{:S(2)}) copy-start(f32[1,8,64,64]{2,3,1,0:T(8,128)} %copy-done) | copy-start | bytes 393220
  147.9 6.0 %copy-start.22 = (s32[1024]{0:T(1024)S(1)}, s32[1024]{0:T(1024)}, u32[]{:S(2)}) copy-start(s32[1024]{0:T(1024)} %pad_clamp_fusion.2) | copy-start | bytes 12292
  156.5 3.8 %copy-start.14 = (f32[8,4096]{1,0:T(8,128)S(1)}, f32[8,4096]{1,0:T(8,128)}, u32[]{:S(2)}) copy-start(f32[8,4096]{1,0:T(8,128)} %gather_fusion.12) | copy-start | bytes 393220
  156.5 3.8 %copy-start.16 = (f32[1,1,1,8,4096]{4,3,2,1,0:T(8,128)S(1)}, f32[1,1,1,8,4096]{4,3,2,1,0:T(8,128)}, u32[]{:S(2)}) copy-start(f32[1,1,1,8,4096]{4,3,2,1,0:T(8,128)} %reshape.2517) | copy-start | bytes 393220
  156.5 3.8 %copy-start.29 = (pred[8]{0:T(512)(128)(4,1)S(1)}, pred[8]{0:T(512)(128)(4,1)}, u32[]{:S(2)}) copy-start(pred[8]{0:T(512)(128)(4,1)} %fusion.30) | copy-start | bytes 28
  156.5 3.8 %copy-start.31 = (pred[8]{0:T(512)(128)(4,1)S(1)}, pred[8]{0:T(512)(128)(4,1)}, u32[]{:S(2)}) copy-start(pred[8]{0:T(512)(128)(4,1)} %and_bitcast_fusion.1) | copy-start | bytes 28
  156.5 4.6 %copy-start.12 = (f32[8,4096]{1,0:T(8,128)S(1)}, f32[8,4096]{1,0:T(8,128)}, u32[]{:S(2)}) copy-start(f32[8,4096]{1,0:T(8,128)} %gather_fusion.13) | copy-start | bytes 393220
  156.5 4.5 %copy-start.13 = (f32[1,1,1,8,4096]{4,3,2,1,0:T(8,128)S(1)}, f32[1,1,1,8,4096]{4,3,2,1,0:T(8,128)}, u32[]{:S(2)}) copy-start(f32[1,1,1,8,4096]{4,3,2,1,0:T(8,128)} %reshape.2523) | copy-start | bytes 393220
  156.6 4.5 %copy-start.28 = (pred[8]{0:T(512)(128)(4,1)S(1)}, pred[8]{0:T(512)(128)(4,1)}, u32[]{:S(2)}) copy-start(pred[8]{0:T(512)(128)(4,1)} %fusion.29) | copy-start | bytes 28
  156.6 4.5 %copy-start.30 = (pred[8]{0:T(512)(128)(4,1)S(1)}, pred[8]{0:T(512)(128)(4,1)}, u32[]{:S(2)}) copy-start(pred[8]{0:T(512)(128)(4,1)} %and_bitcast_fusion) | copy-start | bytes 28
where the time goes:
time: 163 us; the launch traced here: 162 us
  waiting for transfers between devices  40.7 us (25%)
  local copies, waits for them, and re-layouts  37.2 us (23%)
  other arithmetic  35.1 us (22%)
  matrix products  25.5 us (16%)
  starting transfers between devices  22.1 us (14%)
    ppermute x8, waiting for transfers between devices, with_halo(): lax.ppermute(head, axis, [((i + 1) % count, i) for i in range(count)])  34 us
    dot_general x6, matrix products, block_product(): jnp.einsum('gaxz,gaszy->gsxy', left_blocks, picked, precision=lax.Precisi...  25.5 us
    ppermute x8, starting transfers between devices, with_halo(): lax.ppermute(head, axis, [((i + 1) % count, i) for i in range(count)])  17.4 us
    select_n x6, local copies, waits for them, and re-layouts, block_product(): jnp.where(located[..., None], picked, 0.0)  11.1 us
    select_n x6, other arithmetic, block_product(): jnp.where(located[..., None], picked, 0.0)  7.38 us
    ppermute x8, waiting for transfers between devices, with_halo(): lax.ppermute(tail, axis, [(i, (i + 1) % count) for i in range(count)])  6.65 us
    gather x6, local copies, waits for them, and re-layouts, block_product(): picked = flat_blocks[near_index[:, :, None] * slot_count + slot_hit]  6.59 us
    reshape x9, local copies, waits for them, and re-layouts, block_product(): result = result.reshape(groups, slot_count, BLOCK * BLOCK)  5.6 us
  transfers between devices with their start and end apart: 16, of which 5 were waited for; matrix products, arithmetic and copies ran while one was open for 21% of the time, Pallas kernels for 0%

commit v1 on v0

v1 whole, which is shorter than its diff:
```python
import functools

import jax
import jax.numpy as jnp
from jax import lax
from jax.experimental import pallas as pl
from jax.experimental.pallas import tpu as pltpu
from jax.sharding import PartitionSpec as P

BLOCK = 64
WIDE = 2 * BLOCK
HALF = BLOCK // 2
F32 = jnp.float32
BF16 = jnp.bfloat16
VMEM_LIMIT = 16 * 1024 * 1024


def on_left(rows):
    return lax.broadcasted_iota(jnp.int32, (rows, WIDE), 1) < BLOCK


def swap(tile):
    return pltpu.roll(tile, BLOCK, 1)


def place_of(ident, grid):
    rows, cols = grid
    source = jnp.maximum(ident, 0)
    owner_row = lax.div(source, jnp.int32(cols))
    owner_col = lax.rem(source, jnp.int32(cols))
    down = lax.rem(owner_row - lax.axis_index("row") + 1 + rows, jnp.int32(rows))
    across = lax.rem(owner_col - lax.axis_index("col") + 1 + cols, jnp.int32(cols))
    return jnp.where(ident < 0, 9, down * 3 + across)


def note_slots(pattern, table, grid, slots):
    for place in range(10):
        table[place] = slots
    for slot in range(slots):
        table[place_of(pattern[slot], grid)] = slot


def note_live(pattern, table, grid, slots):
    for place in range(10):
        table[place] = 0
    for slot in range(slots):
        table[place_of(pattern[slot], grid)] = 1


def send_tiles(left, right, to_left, to_right, to_next, to_last, which):
    for e in range(3):
        to_left[e, which] = left[e]
        to_right[e, which] = right[e]
    first = on_left(BLOCK)
    for message, low in ((to_next, 1), (to_last, 0)):
        message[0, which] = left[low]
        message[1, which] = left[low + 1]
        message[2, which] = jnp.where(first, swap(right[low]), right[low + 1])


def spread_kernel(
    grid, slots, first_pattern, second_pattern, first, second, to_left, to_right, to_next, to_last, rows, table
):
    first_half = on_left(HALF)
    even, odd = pl.ds(0, HALF, stride=2), pl.ds(1, HALF, stride=2)
    for which, (pattern, data) in enumerate(((first_pattern, first), (second_pattern, second))):
        note_slots(pattern, table, grid, slots)
        for step in range(HALF):
            rows[which, pl.ds(step, slots, stride=HALF), :] = data[:, step * WIDE : (step + 1) * WIDE]
        rows[which, slots * HALF : (slots + 1) * HALF, :] = jnp.zeros((HALF, WIDE), F32)

        def block(place):
            at = pl.multiple_of(table[place] * HALF, HALF)
            own = rows[which, pl.ds(at, HALF), :]
            return own, swap(own)

        def tile(low, high):
            return (jnp.where(first_half, low[0], high[1]), jnp.where(first_half, low[1], high[0]))

        def put(ref, at, pair):
            ref[at, which, even, :] = pair[0]
            ref[at, which, odd, :] = pair[1]

        last = None
        for e in range(3):
            a, b, c = block(3 * e), block(3 * e + 1), block(3 * e + 2)
            left = tile(a, b)
            put(to_left, e, left)
            put(to_right, e, tile(b, c))
            if e >= 1:
                put(to_next, e - 1, left)
                pair = tile(last, c)
                put(to_next if e == 2 else to_last, 2, pair)
            if e <= 1:
                put(to_last, e, left)
            last = c


def split(tile):
    high = tile.astype(BF16)
    return high, (tile - high.astype(F32)).astype(BF16)


def fill_left_factor(own_left, own_right, factor):
    for side, ref in enumerate((own_left, own_right)):
        for e in range(3):
            at = pl.ds(e * WIDE, WIDE)
            for which, (high_at, low_at) in enumerate(((1, 2), (0, 3))):
                high, low = split(ref[e, which])
                factor[side, high_at * BLOCK : (high_at + 1) * BLOCK, at] = high
                factor[side, low_at * BLOCK : (low_at + 1) * BLOCK, at] = low


def fill_right_factor(
    which, own_left, own_right, from_left, from_right, from_last, from_next, corner_last, corner_next, factor
):
    first = on_left(BLOCK)
    zero = jnp.zeros((BLOCK, WIDE), BF16)

    def put(side, k, e, tile):
        for part, value in enumerate((zero, zero) if tile is None else split(tile)):
            factor[side, part, k * BLOCK : (k + 1) * BLOCK, e * WIDE : (e + 1) * WIDE] = value

    def only_right(tile):
        return jnp.where(first, 0.0, tile)

    for e in range(3):
        put(0, 2, e, from_left[e, which])
        put(0, 3, e, own_left[e, which])
        put(1, 2, e, only_right(own_right[e, which]))
        put(1, 3, e, from_right[e, which])
    for row, own, corner, low in ((0, from_last, corner_last, 0), (2, from_next, corner_next, 1)):
        pack = own[2, which]
        for at in range(2):
            e = low + at
            put(0, 2 * row, e, corner[at, which])
            put(0, 2 * row + 1, e, own[at, which])
            put(1, 2 * row, e, only_right(swap(pack) if at == 0 else pack))
            put(1, 2 * row + 1, e, corner[2 + at, which])
        for side in range(2):
            for k in (2 * row, 2 * row + 1):
                put(side, k, 2 - row, None)


def dot(a, b):
    return lax.dot_general(a, b, (((1,), (0,)), ((), ())), preferred_element_type=F32)


def products(left_factor, right_factor, by_first, by_second):
    sides = []
    for side in range(2):
        a = left_factor[side]
        high = dot(a, by_first[side, 0])
        low = dot(a[: 2 * BLOCK], by_first[side, 1])
        other = dot(a[BLOCK : 3 * BLOCK], by_second[side, 0])
        rest = dot(a[BLOCK : 2 * BLOCK], by_second[side, 1])
        one = high[BLOCK : 2 * BLOCK] + (high[2 * BLOCK : 3 * BLOCK] + low[BLOCK:])
        two = (high[:BLOCK] + (high[3 * BLOCK :] + low[:BLOCK])) + (other[:BLOCK] + (other[BLOCK:] + rest))
        sides.append((one, two))
    first = on_left(BLOCK)
    results = []
    for which in range(2):
        left, right = [], []
        for e in range(3):
            a = sides[0][which][:, e * WIDE : (e + 1) * WIDE]
            b = sides[1][which][:, e * WIDE : (e + 1) * WIDE]
            left.append(a + jnp.where(first, 0.0, swap(b)))
            right.append(b + jnp.where(first, swap(a), 0.0))
        results.append((left, right))
    return results


def multiply(operands, scratch):
    own_left, own_right = operands[:2]
    left_factor, by_first, by_second = scratch
    fill_left_factor(own_left, own_right, left_factor)
    fill_right_factor(0, *operands, by_first)
    fill_right_factor(1, *operands, by_second)
    return products(left_factor, None, by_first, by_second)


def next_kernel(grid, slots, first_pattern, second_pattern, *refs):
    operands, outputs, scratch, table = refs[:8], refs[8:12], refs[12:15], refs[15]
    first = on_left(BLOCK)
    for which, (left, right) in enumerate(multiply(operands, scratch)):
        note_live((first_pattern, second_pattern)[which], table, grid, slots)
        for e in range(3):
            keep_left = jnp.where(first, table[3 * e], table[3 * e + 1]) > 0
            keep_right = jnp.where(first, table[3 * e + 1], table[3 * e + 2]) > 0
            left[e] = jnp.where(keep_left, left[e], 0.0)
            right[e] = jnp.where(keep_right, right[e], 0.0)
        send_tiles(left, right, *outputs, which)


def final_kernel(grid, slots, first_pattern, second_pattern, *refs):
    operands, outputs, scratch, (dense, packed, chosen) = refs[:8], refs[8:10], refs[10:13], refs[13:]
    own_left, own_right = operands[:2]
    first_half = on_left(HALF)
    even, odd = pl.ds(0, HALF, stride=2), pl.ds(1, HALF, stride=2)
    for which, (left, right) in enumerate(multiply(operands, scratch)):
        pattern, out = (first_pattern, second_pattern)[which], outputs[which]
        for e in range(3):
            dense[which, e] = 2.0 * own_left[e, which] - left[e]
            dense[which, 3 + e] = 2.0 * own_right[e, which] - right[e]
        for e in range(3):
            a, b = dense[which, e, even, :], dense[which, e, odd, :]
            packed[which, 3 * e] = jnp.where(first_half, a, swap(b))
            packed[which, 3 * e + 1] = jnp.where(first_half, swap(a), b)
            a, b = dense[which, 3 + e, even, :], dense[which, 3 + e, odd, :]
            packed[which, 3 * e + 2] = jnp.where(first_half, swap(a), b)
        packed[which, 9] = jnp.zeros((HALF, WIDE), F32)
        for slot in range(slots):
            chosen[which, slot * HALF : (slot + 1) * HALF, :] = packed[which, place_of(pattern[slot], grid)]
        for step in range(HALF):
            out[:, step * WIDE : (step + 1) * WIDE] = chosen[which, pl.ds(step, slots, stride=HALF), :]


def shift(block, axis, by):
    count = lax.axis_size(axis)
    return lax.ppermute(block, axis, [(i, (i + by) % count) for i in range(count)])


def exchange(to_left, to_right, to_next, to_last):
    from_left = shift(to_right, "col", 1)
    from_right = shift(to_left, "col", -1)
    from_last = shift(to_next, "row", 1)
    from_next = shift(to_last, "row", -1)
    corner_last = shift(jnp.concatenate([from_left[1:], from_right[1:]]), "row", 1)
    corner_next = shift(jnp.concatenate([from_left[:2], from_right[:2]]), "row", -1)
    return to_left, to_right, from_left, from_right, from_last, from_next, corner_last, corner_next


def shards(
    density,
    density_pattern,
    response,
    response_pattern,
    density_next_pattern,
    response_next_pattern,
    density_out_pattern,
    response_out_pattern,
):
    slots = density.shape[3]
    grid = (lax.axis_size("row"), lax.axis_size("col"))
    smem = pl.BlockSpec(memory_space=pltpu.SMEM)
    vmem = pl.BlockSpec(memory_space=pltpu.VMEM)
    params = pltpu.CompilerParams(vmem_limit_bytes=VMEM_LIMIT)
    message = jax.ShapeDtypeStruct((3, 2, BLOCK, WIDE), F32)
    factors = [
        pltpu.VMEM((2, 4 * BLOCK, 3 * WIDE), BF16),
        pltpu.VMEM((2, 2, 3 * WIDE, 3 * WIDE), BF16),
        pltpu.VMEM((2, 2, 3 * WIDE, 3 * WIDE), BF16),
    ]
    table = pltpu.SMEM((16,), jnp.int32)

    def flat(pattern):
        return pattern.reshape(slots)

    sent = pl.pallas_call(
        functools.partial(spread_kernel, grid, slots),
        out_shape=[message] * 4,
        in_specs=[smem, smem, vmem, vmem],
        out_specs=[vmem] * 4,
        scratch_shapes=[pltpu.VMEM((2, (slots + 1) * HALF, WIDE), F32), table],
        compiler_params=params,
        name="spread",
    )(
        flat(density_pattern),
        flat(response_pattern),
        density.reshape(slots, BLOCK * BLOCK),
        response.reshape(slots, BLOCK * BLOCK),
    )
    sent = pl.pallas_call(
        functools.partial(next_kernel, grid, slots),
        out_shape=[message] * 4,
        in_specs=[smem, smem] + [vmem] * 8,
        out_specs=[vmem] * 4,
        scratch_shapes=factors + [table],
        compiler_params=params,
        name="next_step",
    )(flat(density_next_pattern), flat(response_next_pattern), *exchange(*sent))
    outputs = pl.pallas_call(
        functools.partial(final_kernel, grid, slots),
        out_shape=[jax.ShapeDtypeStruct((slots, BLOCK * BLOCK), F32)] * 2,
        in_specs=[smem, smem] + [vmem] * 8,
        out_specs=[vmem] * 2,
        scratch_shapes=factors
        + [
            pltpu.VMEM((2, 6, BLOCK, WIDE), F32),
            pltpu.VMEM((2, 10, HALF, WIDE), F32),
            pltpu.VMEM((2, slots * HALF, WIDE), F32),
        ],
        compiler_params=params,
        name="final_step",
    )(flat(density_out_pattern), flat(response_out_pattern), *exchange(*sent))
    return tuple(out.reshape(density.shape) for out in outputs)


def solution(mesh):
    data = P(("groups", "row"), "col", None, None, None)
    pattern = P(("groups", "row"), "col", None, None)
    return jax.shard_map(
        shards,
        mesh=mesh,
        in_specs=(data, pattern, data, pattern, pattern, pattern, pattern, pattern),
        out_specs=(data, data),
        check_vma=False,
    )
```

time: 163 us -> 60.1 us (0.37)
  other arithmetic: 35.1 us -> 0.07 us
  local copies, waits for them, and re-layouts: 37.2 us -> 3.86 us
  matrix products: 25.5 us -> 0 us
  starting transfers between devices: 22.1 us -> 15.3 us
  waiting for transfers between devices: 40.7 us -> 35.1 us
  Pallas kernels: 0 us -> 4.78 us
    dot_general x6 -> x0, matrix products: 25.5 us -> none  [block_product(): jnp.einsum('gaxz,gaszy->gsxy', left_blocks, picked, precision=lax.Precisi...]
    gather x14 -> x0, local copies, waits for them, and re-layouts: 12.8 us -> none  [the longest x6 6.59 us: block_product(): picked = flat_blocks[near_index[:, :, None] * slot_count + slot_hit]]
    select_n x12 -> x0, local copies, waits for them, and re-layouts: 11.5 us -> none  [the longest x6 11.1 us: block_product(): jnp.where(located[..., None], picked, 0.0)]
    select_n x13 -> x0, other arithmetic: 10.7 us -> none  [the longest x6 7.38 us: block_product(): jnp.where(located[..., None], picked, 0.0)]
    ppermute x16 -> x12, starting transfers between devices: 22.1 us -> 15.3 us  [shift(): lax.ppermute(block, axis, [(i, (i + by) % count) for i in range(count)])]
    ppermute x16 -> x12, waiting for transfers between devices: 40.7 us -> 35.1 us  [shift(): lax.ppermute(block, axis, [(i, (i + by) % count) for i in range(count)])]
    reshape x9 -> x0, local copies, waits for them, and re-layouts: 5.6 us -> none  [block_product(): result = result.reshape(groups, slot_count, BLOCK * BLOCK)]
    pallas_call x0 -> x3, Pallas kernels: none -> 4.78 us  [the longest x1 2.38 us: shards(): pl.pallas_call(functools.partial(final_kernel, grid, slots), out_shape=[j...]
  transfers between devices with their start and end apart: 16 -> 12, of which waited for: 5 -> 8; matrix products, arithmetic and copies ran while one was open for 21% -> 0% of each run, Pallas kernels for 0% -> 0%
where the time goes in v1:
time: 60.1 us; the launch traced here: 59.9 us
  waiting for transfers between devices  35.1 us (58%)
  starting transfers between devices  15.3 us (25%)
  Pallas kernels  4.78 us (8%)
  local copies, waits for them, and re-layouts  3.86 us (6%)
  between operations  0.76 us (1%)
    ppermute x12, waiting for transfers between devices, shift(): lax.ppermute(block, axis, [(i, (i + by) % count) for i in range(count)])  35.1 us
    ppermute x12, starting transfers between devices, shift(): lax.ppermute(block, axis, [(i, (i + by) % count) for i in range(count)])  15.3 us
    unnamed x16, local copies, waits for them, and re-layouts  3.79 us
    pallas_call x1, Pallas kernels, shards(): pl.pallas_call(functools.partial(final_kernel, grid, slots), out_shape=[j...  2.38 us
    pallas_call x1, Pallas kernels, shards(): pl.pallas_call(functools.partial(next_kernel, grid, slots), out_shape=[me...  1.51 us
  transfers between devices with their start and end apart: 12, of which 8 were waited for; matrix products, arithmetic and copies ran while one was open for 0% of the time, Pallas kernels for 0%

profile of v1, /device:TPU:1, one launch (start us, length us, event | category | flops | bytes accessed | tf_op | source)
XLA Modules:
  0.0 59.9 jit_solution(3409281620970005847)
XLA Ops:
  0.6 0.0 copy-start.2
  0.6 0.0 copy-start.3
  0.7 0.6 %copy-done.2 = s32[1,1,1,8]{3,2,1,0:T(1,128)S(1)} copy-done((s32[1,1,1,8]{3,2,1,0:T(1,128)S(1)}, s32[1,1,1,8]{3,2,1,0:T(1,128)}, u32[]{:S(2)}) %copy-start.2) | copy-done | bytes 56
  1.3 0.0 copy-done.3
  1.3 0.0 copy-start
  1.3 0.9 %copy-done = f32[1,1,1,8,4096]{4,3,2,1,0:T(8,128)S(1)} copy-done((f32[1,1,1,8,4096]{4,3,2,1,0:T(8,128)S(1)}, f32[1,1,1,8,4096]{4,3,2,1,0:T(8,128)}, u32[]{:S(2)}) %copy-start) | copy-done | bytes 131096
  2.2 0.0 copy-start.1
  2.2 0.9 %copy-done.1 = f32[1,1,1,8,4096]{4,3,2,1,0:T(8,128)S(1)} copy-done((f32[1,1,1,8,4096]{4,3,2,1,0:T(8,128)S(1)}, f32[1,1,1,8,4096]{4,3,2,1,0:T(8,128)}, u32[]{:S(2)}) %copy-start.1) | copy-done | bytes 131096
  3.1 0.9 %spread.1 = (f32[3,2,64,128]{3,2,1,0:T(8,128)S(1)}, f32[3,2,64,128]{3,2,1,0:T(8,128)S(1)}, f32[3,2,64,128]{3,2,1,0:T(8,128)S(1)}, f32[3,2,64,128]{3,2,1,0:T(8,128)S(1)}) custom-call(s32[8]{0:T(128)S(1)} %bitcast.12, s32[8]{0:T(128)S(1)} %bitcast.13, f32[8,4096]{1,0:T(8,128)S(1)} %bitcast.10, f32[8,4096]{1,0:T(8,128)S(1)} %bitcast.11), custom_call_target="tpu_custom_call" | custom-call | tf_op jit(solution)/shard_map/spread/pallas_call | solution.py:259
  4.0 2.2 %collective-permute-start = (f32[3,2,64,128]{3,2,1,0:T(8,128)S(1)}, f32[3,2,64,128]{3,2,1,0:T(8,128)S(1)}, u32[]{:S(2)}, u32[]{:S(2)}) collective-permute-start(f32[3,2,64,128]{3,2,1,0:T(8,128)S(1)} %get-tuple-element.13.refs_1_), channel_id=1, source_target_pairs={{0,1},{1,2},{2,3},{3,0},{4,5},{5,6},{6,7},{7,4},{8,9},{9,10},{10,1... | collective-permute-start | bytes 589832 | tf_op jit(solution)/shard_map/ppermute | solution.py:220
  6.2 2.1 %collective-permute-start.1 = (f32[3,2,64,128]{3,2,1,0:T(8,128)S(1)}, f32[3,2,64,128]{3,2,1,0:T(8,128)S(1)}, u32[]{:S(2)}, u32[]{:S(2)}) collective-permute-start(f32[3,2,64,128]{3,2,1,0:T(8,128)S(1)} %get-tuple-element.12.refs_0_), channel_id=1, source_target_pairs={{0,3},{1,0},{2,1},{3,2},{4,7},{5,4},{6,5},{7,6},{8,11},{9,8},{10,9... | collective-permute-start | bytes 589832 | tf_op jit(solution)/shard_map/ppermute | solution.py:220
  8.3 4.6 %collective-permute-done.refs_2_ = f32[3,2,64,128]{3,2,1,0:T(8,128)S(1)} collective-permute-done((f32[3,2,64,128]{3,2,1,0:T(8,128)S(1)}, f32[3,2,64,128]{3,2,1,0:T(8,128)S(1)}, u32[]{:S(2)}, u32[]{:S(2)}) %collective-permute-start) | collective-permute-done | bytes 196640 | tf_op jit(solution)/shard_map/ppermute | solution.py:220
  12.9 3.7 %collective-permute-done.1.refs_3_ = f32[3,2,64,128]{3,2,1,0:T(8,128)S(1)} collective-permute-done((f32[3,2,64,128]{3,2,1,0:T(8,128)S(1)}, f32[3,2,64,128]{3,2,1,0:T(8,128)S(1)}, u32[]{:S(2)}, u32[]{:S(2)}) %collective-permute-start.1) | collective-permute-done | bytes 196640 | tf_op jit(solution)/shard_map/ppermute | solution.py:220
  16.7 2.3 %collective-permute-start.4 = (f32[4,2,64,128]{3,2,1,0:T(8,128)S(1)}, f32[4,2,64,128]{3,2,1,0:T(8,128)S(1)}, u32[]{:S(2)}, u32[]{:S(2)}) collective-permute-start(f32[4,2,64,128]{3,2,1,0:T(8,128)S(1)} %pad_maximum_fusion), channel_id=1, source_target_pairs={{0,4},{4,8},{8,12},{12,0},{1,5},{5,9},{9,13},{13,1},{2,6},{6,10},{... | collective-permute-start | bytes 786440 | tf_op jit(solution)/shard_map/ppermute | solution.py:220
  18.9 0.1 collective-permute-start.5
  19.0 1.7 %collective-permute-start.2 = (f32[3,2,64,128]{3,2,1,0:T(8,128)S(1)}, f32[3,2,64,128]{3,2,1,0:T(8,128)S(1)}, u32[]{:S(2)}, u32[]{:S(2)}) collective-permute-start(f32[3,2,64,128]{3,2,1,0:T(8,128)S(1)} %get-tuple-element.14), channel_id=1, source_target_pairs={{0,4},{4,8},{8,12},{12,0},{1,5},{5,9},{9,13},{13,1},{2,6},{6,10},{... | collective-permute-start | bytes 589832 | tf_op jit(solution)/shard_map/ppermute | solution.py:220
  20.7 0.0 collective-permute-start.3
  20.7 7.6 %collective-permute-done.2.refs_4_ = f32[3,2,64,128]{3,2,1,0:T(8,128)S(1)} collective-permute-done((f32[3,2,64,128]{3,2,1,0:T(8,128)S(1)}, f32[3,2,64,128]{3,2,1,0:T(8,128)S(1)}, u32[]{:S(2)}, u32[]{:S(2)}) %collective-permute-start.2) | collective-permute-done | bytes 196640 | tf_op jit(solution)/shard_map/ppermute | solution.py:220
  28.4 1.6 %collective-permute-done.3.refs_5_ = f32[3,2,64,128]{3,2,1,0:T(8,128)S(1)} collective-permute-done((f32[3,2,64,128]{3,2,1,0:T(8,128)S(1)}, f32[3,2,64,128]{3,2,1,0:T(8,128)S(1)}, u32[]{:S(2)}, u32[]{:S(2)}) %collective-permute-start.3) | collective-permute-done | bytes 196640 | tf_op jit(solution)/shard_map/ppermute | solution.py:220
  30.0 0.0 collective-permute-done.4.refs_6_
  30.0 0.0 collective-permute-done.5.refs_7_
  30.0 0.0 copy-start.4
  30.0 0.0 copy-start.5
  30.0 0.6 %copy-done.4 = s32[1,1,1,8]{3,2,1,0:T(1,128)S(1)} copy-done((s32[1,1,1,8]{3,2,1,0:T(1,128)S(1)}, s32[1,1,1,8]{3,2,1,0:T(1,128)}, u32[]{:S(2)}) %copy-start.4) | copy-done | bytes 56
  30.6 0.0 copy-done.5
  30.6 1.5 %next_step.1 = (f32[3,2,64,128]{3,2,1,0:T(8,128)S(1)}, f32[3,2,64,128]{3,2,1,0:T(8,128)S(1)}, f32[3,2,64,128]{3,2,1,0:T(8,128)S(1)}, f32[3,2,64,128]{3,2,1,0:T(8,128)S(1)}) custom-call(s32[8]{0:T(128)S(1)} %bitcast.14, s32[8]{0:T(128)S(1)} %bitcast.15, f32[3,2,64,128]{3,2,1,0:T(8,128)S(1)} %get-tuple-element.12.refs_0_, ...), custom_call_target="tpu_custom_call" | custom-call | tf_op jit(solution)/shard_map/next_step/pallas_call | solution.py:273
  32.2 0.9 %collective-permute-start.6 = (f32[3,2,64,128]{3,2,1,0:T(8,128)S(1)}, f32[3,2,64,128]{3,2,1,0:T(8,128)S(1)}, u32[]{:S(2)}, u32[]{:S(2)}) collective-permute-start(f32[3,2,64,128]{3,2,1,0:T(8,128)S(1)} %get-tuple-element.17.refs_1_), channel_id=1, source_target_pairs={{0,1},{1,2},{2,3},{3,0},{4,5},{5,6},{6,7},{7,4},{8,9},{9,10},{10,1... | collective-permute-start | bytes 589832 | tf_op jit(solution)/shard_map/ppermute | solution.py:220
  33.1 2.4 %collective-permute-start.7 = (f32[3,2,64,128]{3,2,1,0:T(8,128)S(1)}, f32[3,2,64,128]{3,2,1,0:T(8,128)S(1)}, u32[]{:S(2)}, u32[]{:S(2)}) collective-permute-start(f32[3,2,64,128]{3,2,1,0:T(8,128)S(1)} %get-tuple-element.16.refs_0_), channel_id=1, source_target_pairs={{0,3},{1,0},{2,1},{3,2},{4,7},{5,4},{6,5},{7,6},{8,11},{9,8},{10,9... | collective-permute-start | bytes 589832 | tf_op jit(solution)/shard_map/ppermute | solution.py:220
  35.5 5.3 %collective-permute-done.6.refs_2_ = f32[3,2,64,128]{3,2,1,0:T(8,128)S(1)} collective-permute-done((f32[3,2,64,128]{3,2,1,0:T(8,128)S(1)}, f32[3,2,64,128]{3,2,1,0:T(8,128)S(1)}, u32[]{:S(2)}, u32[]{:S(2)}) %collective-permute-start.6) | collective-permute-done | bytes 196640 | tf_op jit(solution)/shard_map/ppermute | solution.py:220
  40.8 3.0 %collective-permute-done.7.refs_3_ = f32[3,2,64,128]{3,2,1,0:T(8,128)S(1)} collective-permute-done((f32[3,2,64,128]{3,2,1,0:T(8,128)S(1)}, f32[3,2,64,128]{3,2,1,0:T(8,128)S(1)}, u32[]{:S(2)}, u32[]{:S(2)}) %collective-permute-start.7) | collective-permute-done | bytes 196640 | tf_op jit(solution)/shard_map/ppermute | solution.py:220
  43.9 1.9 %collective-permute-start.10 = (f32[4,2,64,128]{3,2,1,0:T(8,128)S(1)}, f32[4,2,64,128]{3,2,1,0:T(8,128)S(1)}, u32[]{:S(2)}, u32[]{:S(2)}) collective-permute-start(f32[4,2,64,128]{3,2,1,0:T(8,128)S(1)} %pad_maximum_fusion.2), channel_id=1, source_target_pairs={{0,4},{4,8},{8,12},{12,0},{1,5},{5,9},{9,13},{13,1},{2,6},{6,10},{... | collective-permute-start | bytes 786440 | tf_op jit(solution)/shard_map/ppermute | solution.py:220
  45.8 0.1 collective-permute-start.11
  45.9 1.7 %collective-permute-start.8 = (f32[3,2,64,128]{3,2,1,0:T(8,128)S(1)}, f32[3,2,64,128]{3,2,1,0:T(8,128)S(1)}, u32[]{:S(2)}, u32[]{:S(2)}) collective-permute-start(f32[3,2,64,128]{3,2,1,0:T(8,128)S(1)} %get-tuple-element.18), channel_id=1, source_target_pairs={{0,4},{4,8},{8,12},{12,0},{1,5},{5,9},{9,13},{13,1},{2,6},{6,10},{... | collective-permute-start | bytes 589832 | tf_op jit(solution)/shard_map/ppermute | solution.py:220
  47.6 0.0 collective-permute-start.9
  47.6 7.6 %collective-permute-done.8.refs_4_ = f32[3,2,64,128]{3,2,1,0:T(8,128)S(1)} collective-permute-done((f32[3,2,64,128]{3,2,1,0:T(8,128)S(1)}, f32[3,2,64,128]{3,2,1,0:T(8,128)S(1)}, u32[]{:S(2)}, u32[]{:S(2)}) %collective-permute-start.8) | collective-permute-done | bytes 196640 | tf_op jit(solution)/shard_map/ppermute | solution.py:220
  55.3 1.6 %collective-permute-done.9.refs_5_ = f32[3,2,64,128]{3,2,1,0:T(8,128)S(1)} collective-permute-done((f32[3,2,64,128]{3,2,1,0:T(8,128)S(1)}, f32[3,2,64,128]{3,2,1,0:T(8,128)S(1)}, u32[]{:S(2)}, u32[]{:S(2)}) %collective-permute-start.9) | collective-permute-done | bytes 196640 | tf_op jit(solution)/shard_map/ppermute | solution.py:220
  56.8 0.0 collective-permute-done.10.refs_6_
  56.8 0.0 collective-permute-done.11.refs_7_
  56.8 0.0 copy-start.6
  56.8 0.0 copy-start.7
  56.8 0.6 %copy-done.6 = s32[1,1,1,8]{3,2,1,0:T(1,128)S(1)} copy-done((s32[1,1,1,8]{3,2,1,0:T(1,128)S(1)}, s32[1,1,1,8]{3,2,1,0:T(1,128)}, u32[]{:S(2)}) %copy-start.6) | copy-done | bytes 56
  57.5 0.0 copy-done.7
  57.5 2.4 %final_step.1 = (f32[8,4096]{1,0:T(8,128)}, f32[8,4096]{1,0:T(8,128)}) custom-call(s32[8]{0:T(128)S(1)} %bitcast.16, s32[8]{0:T(128)S(1)} %bitcast.17, f32[3,2,64,128]{3,2,1,0:T(8,128)S(1)} %get-tuple-element.16.refs_0_, f32[3,2,64,128]{3,2,1,0:T(8,128)S(1)} %get-tuple-element.17.refs_1_, f32[3,2,64,128]{3,2,1,0:T(8,128)S(1)} %collective-permute-done.6.refs_2_, ...), custom_call_target="tpu_custom_call" | custom-call | tf_op jit(solution)/shard_map/final_step/pallas_call | solution.py:282
  (8 shorter events, 0.1 us)
Async XLA Ops:
  0.6 0.7 %copy-start.2 = (s32[1,1,1,8]{3,2,1,0:T(1,128)S(1)}, s32[1,1,1,8]{3,2,1,0:T(1,128)}, u32[]{:S(2)}) copy-start(s32[1,1,1,8]{3,2,1,0:T(1,128)} %param.9) | copy-start | bytes 100
  0.6 0.7 %copy-start.3 = (s32[1,1,1,8]{3,2,1,0:T(1,128)S(1)}, s32[1,1,1,8]{3,2,1,0:T(1,128)}, u32[]{:S(2)}) copy-start(s32[1,1,1,8]{3,2,1,0:T(1,128)} %param.11) | copy-start | bytes 100
  1.3 0.9 %copy-start = (f32[1,1,1,8,4096]{4,3,2,1,0:T(8,128)S(1)}, f32[1,1,1,8,4096]{4,3,2,1,0:T(8,128)}, u32[]{:S(2)}) copy-start(f32[1,1,1,8,4096]{4,3,2,1,0:T(8,128)} %param.8) | copy-start | bytes 393220
  2.2 0.9 %copy-start.1 = (f32[1,1,1,8,4096]{4,3,2,1,0:T(8,128)S(1)}, f32[1,1,1,8,4096]{4,3,2,1,0:T(8,128)}, u32[]{:S(2)}) copy-start(f32[1,1,1,8,4096]{4,3,2,1,0:T(8,128)} %param.10) | copy-start | bytes 393220
  4.0 8.9 %collective-permute-start = (f32[3,2,64,128]{3,2,1,0:T(8,128)S(1)}, f32[3,2,64,128]{3,2,1,0:T(8,128)S(1)}, u32[]{:S(2)}, u32[]{:S(2)}) collective-permute-start(f32[3,2,64,128]{3,2,1,0:T(8,128)S(1)} %get-tuple-element.13.refs_1_), channel_id=1, source_target_pairs={{0,1},{1,2},{2,3},{3,0},{4,5},{5,6},{6,7},{7,4},{8,9},{9,10},{10,1... | collective-permute-start | bytes 589832 | tf_op jit(solution)/shard_map/ppermute | solution.py:220
  6.2 10.4 %collective-permute-start.1 = (f32[3,2,64,128]{3,2,1,0:T(8,128)S(1)}, f32[3,2,64,128]{3,2,1,0:T(8,128)S(1)}, u32[]{:S(2)}, u32[]{:S(2)}) collective-permute-start(f32[3,2,64,128]{3,2,1,0:T(8,128)S(1)} %get-tuple-element.12.refs_0_), channel_id=1, source_target_pairs={{0,3},{1,0},{2,1},{3,2},{4,7},{5,4},{6,5},{7,6},{8,11},{9,8},{10,9... | collective-permute-start | bytes 589832 | tf_op jit(solution)/shard_map/ppermute | solution.py:220
  16.7 13.3 %collective-permute-start.4 = (f32[4,2,64,128]{3,2,1,0:T(8,128)S(1)}, f32[4,2,64,128]{3,2,1,0:T(8,128)S(1)}, u32[]{:S(2)}, u32[]{:S(2)}) collective-permute-start(f32[4,2,64,128]{3,2,1,0:T(8,128)S(1)} %pad_maximum_fusion), channel_id=1, source_target_pairs={{0,4},{4,8},{8,12},{12,0},{1,5},{5,9},{9,13},{13,1},{2,6},{6,10},{... | collective-permute-start | bytes 786440 | tf_op jit(solution)/shard_map/ppermute | solution.py:220
  18.9 11.0 %collective-permute-start.5 = (f32[4,2,64,128]{3,2,1,0:T(8,128)S(1)}, f32[4,2,64,128]{3,2,1,0:T(8,128)S(1)}, u32[]{:S(2)}, u32[]{:S(2)}) collective-permute-start(f32[4,2,64,128]{3,2,1,0:T(8,128)S(1)} %pad_maximum_fusion.1), channel_id=1, source_target_pairs={{0,12},{4,0},{8,4},{12,8},{1,13},{5,1},{9,5},{13,9},{2,14},{6,2},{... | collective-permute-start | bytes 786440 | tf_op jit(solution)/shard_map/ppermute | solution.py:220
  19.0 9.4 %collective-permute-start.2 = (f32[3,2,64,128]{3,2,1,0:T(8,128)S(1)}, f32[3,2,64,128]{3,2,1,0:T(8,128)S(1)}, u32[]{:S(2)}, u32[]{:S(2)}) collective-permute-start(f32[3,2,64,128]{3,2,1,0:T(8,128)S(1)} %get-tuple-element.14), channel_id=1, source_target_pairs={{0,4},{4,8},{8,12},{12,0},{1,5},{5,9},{9,13},{13,1},{2,6},{6,10},{... | collective-permute-start | bytes 589832 | tf_op jit(solution)/shard_map/ppermute | solution.py:220
  20.7 9.2 %collective-permute-start.3 = (f32[3,2,64,128]{3,2,1,0:T(8,128)S(1)}, f32[3,2,64,128]{3,2,1,0:T(8,128)S(1)}, u32[]{:S(2)}, u32[]{:S(2)}) collective-permute-start(f32[3,2,64,128]{3,2,1,0:T(8,128)S(1)} %get-tuple-element.15), channel_id=1, source_target_pairs={{0,12},{4,0},{8,4},{12,8},{1,13},{5,1},{9,5},{13,9},{2,14},{6,2},{... | collective-permute-start | bytes 589832 | tf_op jit(solution)/shard_map/ppermute | solution.py:220
  30.0 0.7 %copy-start.4 = (s32[1,1,1,8]{3,2,1,0:T(1,128)S(1)}, s32[1,1,1,8]{3,2,1,0:T(1,128)}, u32[]{:S(2)}) copy-start(s32[1,1,1,8]{3,2,1,0:T(1,128)} %param.12) | copy-start | bytes 100
  30.0 0.7 %copy-start.5 = (s32[1,1,1,8]{3,2,1,0:T(1,128)S(1)}, s32[1,1,1,8]{3,2,1,0:T(1,128)}, u32[]{:S(2)}) copy-start(s32[1,1,1,8]{3,2,1,0:T(1,128)} %param.13) | copy-start | bytes 100
  32.2 8.7 %collective-permute-start.6 = (f32[3,2,64,128]{3,2,1,0:T(8,128)S(1)}, f32[3,2,64,128]{3,2,1,0:T(8,128)S(1)}, u32[]{:S(2)}, u32[]{:S(2)}) collective-permute-start(f32[3,2,64,128]{3,2,1,0:T(8,128)S(1)} %get-tuple-element.17.refs_1_), channel_id=1, source_target_pairs={{0,1},{1,2},{2,3},{3,0},{4,5},{5,6},{6,7},{7,4},{8,9},{9,10},{10,1... | collective-permute-start | bytes 589832 | tf_op jit(solution)/shard_map/ppermute | solution.py:220
  33.1 10.8 %collective-permute-start.7 = (f32[3,2,64,128]{3,2,1,0:T(8,128)S(1)}, f32[3,2,64,128]{3,2,1,0:T(8,128)S(1)}, u32[]{:S(2)}, u32[]{:S(2)}) collective-permute-start(f32[3,2,64,128]{3,2,1,0:T(8,128)S(1)} %get-tuple-element.16.refs_0_), channel_id=1, source_target_pairs={{0,3},{1,0},{2,1},{3,2},{4,7},{5,4},{6,5},{7,6},{8,11},{9,8},{10,9... | collective-permute-start | bytes 589832 | tf_op jit(solution)/shard_map/ppermute | solution.py:220
  43.9 12.9 %collective-permute-start.10 = (f32[4,2,64,128]{3,2,1,0:T(8,128)S(1)}, f32[4,2,64,128]{3,2,1,0:T(8,128)S(1)}, u32[]{:S(2)}, u32[]{:S(2)}) collective-permute-start(f32[4,2,64,128]{3,2,1,0:T(8,128)S(1)} %pad_maximum_fusion.2), channel_id=1, source_target_pairs={{0,4},{4,8},{8,12},{12,0},{1,5},{5,9},{9,13},{13,1},{2,6},{6,10},{... | collective-permute-start | bytes 786440 | tf_op jit(solution)/shard_map/ppermute | solution.py:220
  45.8 11.0 %collective-permute-start.11 = (f32[4,2,64,128]{3,2,1,0:T(8,128)S(1)}, f32[4,2,64,128]{3,2,1,0:T(8,128)S(1)}, u32[]{:S(2)}, u32[]{:S(2)}) collective-permute-start(f32[4,2,64,128]{3,2,1,0:T(8,128)S(1)} %pad_maximum_fusion.3), channel_id=1, source_target_pairs={{0,12},{4,0},{8,4},{12,8},{1,13},{5,1},{9,5},{13,9},{2,14},{6,2},{... | collective-permute-start | bytes 786440 | tf_op jit(solution)/shard_map/ppermute | solution.py:220
  45.9 9.4 %collective-permute-start.8 = (f32[3,2,64,128]{3,2,1,0:T(8,128)S(1)}, f32[3,2,64,128]{3,2,1,0:T(8,128)S(1)}, u32[]{:S(2)}, u32[]{:S(2)}) collective-permute-start(f32[3,2,64,128]{3,2,1,0:T(8,128)S(1)} %get-tuple-element.18), channel_id=1, source_target_pairs={{0,4},{4,8},{8,12},{12,0},{1,5},{5,9},{9,13},{13,1},{2,6},{6,10},{... | collective-permute-start | bytes 589832 | tf_op jit(solution)/shard_map/ppermute | solution.py:220
  47.6 9.2 %collective-permute-start.9 = (f32[3,2,64,128]{3,2,1,0:T(8,128)S(1)}, f32[3,2,64,128]{3,2,1,0:T(8,128)S(1)}, u32[]{:S(2)}, u32[]{:S(2)}) collective-permute-start(f32[3,2,64,128]{3,2,1,0:T(8,128)S(1)} %get-tuple-element.19), channel_id=1, source_target_pairs={{0,12},{4,0},{8,4},{12,8},{1,13},{5,1},{9,5},{13,9},{2,14},{6,2},{... | collective-permute-start | bytes 589832 | tf_op jit(solution)/shard_map/ppermute | solution.py:220
  56.8 0.7 %copy-start.6 = (s32[1,1,1,8]{3,2,1,0:T(1,128)S(1)}, s32[1,1,1,8]{3,2,1,0:T(1,128)}, u32[]{:S(2)}) copy-start(s32[1,1,1,8]{3,2,1,0:T(1,128)} %param.14) | copy-start | bytes 100
  56.8 0.7 %copy-start.7 = (s32[1,1,1,8]{3,2,1,0:T(1,128)S(1)}, s32[1,1,1,8]{3,2,1,0:T(1,128)}, u32[]{:S(2)}) copy-start(s32[1,1,1,8]{3,2,1,0:T(1,128)} %param.15) | copy-start | bytes 100

commit v2 on v1

v2 whole, which is shorter than its diff:
```python
import functools

import jax
import jax.numpy as jnp
from jax import lax
from jax.experimental import pallas as pl
from jax.experimental.pallas import tpu as pltpu
from jax.sharding import PartitionSpec as P

BLOCK = 64
WIDE = 2 * BLOCK
HALF = BLOCK // 2
DEPTH = 3 * BLOCK
F32 = jnp.float32
BF16 = jnp.bfloat16
VMEM_LIMIT = 16 * 1024 * 1024


def on_left(rows):
    return lax.broadcasted_iota(jnp.int32, (rows, WIDE), 1) < BLOCK


def swap(tile):
    return pltpu.roll(tile, BLOCK, 1)


def place_of(ident, grid):
    rows, cols = grid
    source = jnp.maximum(ident, 0)
    owner_row = lax.div(source, jnp.int32(cols))
    owner_col = lax.rem(source, jnp.int32(cols))
    down = lax.rem(owner_row - lax.axis_index("row") + 1 + rows, jnp.int32(rows))
    across = lax.rem(owner_col - lax.axis_index("col") + 1 + cols, jnp.int32(cols))
    return jnp.where(ident < 0, 9, down * 3 + across)


def note_slots(pattern, table, grid, slots):
    for place in range(10):
        table[place] = slots
    for slot in range(slots):
        table[place_of(pattern[0, slot], grid)] = slot


def note_live(pattern, table, grid, slots):
    for place in range(10):
        table[place] = 0
    for slot in range(slots):
        table[place_of(pattern[0, slot], grid)] = 1


def fetch(sources, targets, sems):
    copies = [pltpu.make_async_copy(s, t, sems.at[i]) for i, (s, t) in enumerate(zip(sources, targets))]
    for copy in copies:
        copy.start()
    return copies


def spread_kernel(grid, slots, *refs):
    sources, (to_left, to_right, ask_next, ask_last) = refs[:4], refs[4:8]
    first_pattern, second_pattern, first, second, rows, table, sems = refs[8:]
    copies = fetch(sources, (first_pattern, second_pattern, first, second), sems)
    first_half = on_left(HALF)
    even, odd = pl.ds(0, HALF, stride=2), pl.ds(1, HALF, stride=2)
    for which, (pattern, data) in enumerate(((first_pattern, first), (second_pattern, second))):
        copies[which].wait()
        note_slots(pattern, table, grid, slots)
        rows[which, slots * HALF : (slots + 1) * HALF, :] = jnp.zeros((HALF, WIDE), F32)
        copies[2 + which].wait()
        for step in range(HALF):
            rows[which, pl.ds(step, slots, stride=HALF), :] = data[:, step * WIDE : (step + 1) * WIDE]

        def block(place):
            at = pl.multiple_of(table[place] * HALF, HALF)
            own = rows[which, pl.ds(at, HALF), :]
            return own, swap(own)

        def tile(low, high):
            return (jnp.where(first_half, low[0], high[1]), jnp.where(first_half, low[1], high[0]))

        for e in range(3):
            a, b, c = block(3 * e), block(3 * e + 1), block(3 * e + 2)
            left, right = tile(a, b), tile(b, c)
            for part, stride in enumerate((even, odd)):
                to_left[which, e, stride, :] = left[part]
                to_right[which, e, stride, :] = right[part]
            if e != 1:
                ask = ask_next if e == 2 else ask_last
                for part, stride in enumerate((even, odd)):
                    ask[which, stride, :] = left[part]
                fold_into(ask, which, to_right[which, e])


def fold_into(ask, which, right):
    ask[which, BLOCK:, :] = jnp.where(on_left(HALF), swap(right[:HALF]), right[HALF:])


def split(tile):
    high = tile.astype(BF16)
    return high, (tile - high.astype(F32)).astype(BF16)


HIGH_AT, LOW_AT = (2, 1), (3, 0)


def fill_left_factor(which, left, folded, factor):
    for part, at in ((0, HIGH_AT[which]), (1, LOW_AT[which])):
        factor[at * BLOCK : (at + 1) * BLOCK, :WIDE] = split(left)[part]
        top = split(folded)[part]
        bottom = split(swap(folded))[part]
        factor[at * BLOCK : at * BLOCK + HALF, WIDE:] = top[:, :BLOCK]
        factor[at * BLOCK + HALF : (at + 1) * BLOCK, WIDE:] = bottom[:, :BLOCK]


def fill_right_factor(which, own_left, own_right, from_left, from_right, factor):
    first = on_left(BLOCK)
    zero = jnp.zeros((BLOCK, WIDE), BF16)
    for e in range(3):
        column = e * 2 * WIDE
        tiles = (
            (from_left[which, e], None),
            (own_left[which, e], jnp.where(first, 0.0, own_right[which, e])),
            (None, from_right[which, e]),
        )
        for k, pair in enumerate(tiles):
            for side, tile in enumerate(pair):
                values = (zero, zero) if tile is None else split(tile)
                at = pl.ds(column + side * WIDE, WIDE)
                for part in range(2):
                    factor[part, k * BLOCK : (k + 1) * BLOCK, at] = values[part]


def dot(a, b):
    return lax.dot_general(a, b, (((1,), (0,)), ((), ())), preferred_element_type=F32)


def products(factor, by_first, by_second, low, count):
    at = slice(low * 2 * WIDE, (low + count) * 2 * WIDE)
    high = dot(factor[...], by_first[0, :, at])
    fine = dot(factor[BLOCK : 3 * BLOCK, :], by_first[1, :, at])
    other = dot(factor[2 * BLOCK :, :], by_second[0, :, at])
    rest = dot(factor[2 * BLOCK : 3 * BLOCK, :], by_second[1, :, at])
    one = high[2 * BLOCK : 3 * BLOCK] + (high[3 * BLOCK :] + fine[BLOCK:])
    two = (high[BLOCK : 2 * BLOCK] + (high[:BLOCK] + fine[:BLOCK])) + (other[:BLOCK] + (other[BLOCK:] + rest))
    first = on_left(BLOCK)
    results = []
    for total in (one, two):
        left, right = [], []
        for e in range(count):
            a = total[:, 2 * e * WIDE : (2 * e + 1) * WIDE]
            b = total[:, (2 * e + 1) * WIDE : (2 * e + 2) * WIDE]
            left.append(a + jnp.where(first, 0.0, swap(b)))
            right.append(b)
        results.append((left, right))
    return results


def share_kernel(own_left, own_right, from_left, from_right, from_last, from_next, *refs):
    to_last, to_next, by_first, by_second, factor = refs
    first = on_left(BLOCK)
    for which, by in enumerate((by_first, by_second)):
        fill_right_factor(which, own_left, own_right, from_left, from_right, by)
    for asked, share, low in ((from_last, to_last, 0), (from_next, to_next, 1)):
        for which in range(2):
            fill_left_factor(which, asked[which, :BLOCK], asked[which, BLOCK:], factor)
        for which, (left, right) in enumerate(products(factor, by_first, by_second, low, 2)):
            share[which, 0] = left[0]
            share[which, 1] = left[1]
            share[which, 2] = jnp.where(first, swap(right[0]), right[1])


def own_kernel(own_left, own_right, by_first, by_second, sums, factor):
    for which in range(2):
        right = own_right[which, 1]
        folded = jnp.where(on_left(HALF), swap(right[:HALF]), right[HALF:])
        fill_left_factor(which, own_left[which, 1], folded, factor)
    for which, (left, right) in enumerate(products(factor, by_first, by_second, 0, 3)):
        for e in range(3):
            sums[which, e] = left[e]
            sums[which, 3 + e] = right[e]


def total(which, sums, from_last, from_next):
    left = [sums[which, e] for e in range(3)]
    right = [sums[which, 3 + e] for e in range(3)]
    for share, low in ((from_last, 0), (from_next, 1)):
        left[low] += share[which, 0]
        left[low + 1] += share[which, 1]
        right[low] += swap(share[which, 2])
        right[low + 1] += share[which, 2]
    return left, right


def next_kernel(grid, slots, *refs):
    patterns, (sums, from_last, from_next) = refs[:2], refs[2:5]
    to_left, to_right, ask_next, ask_last = refs[5:9]
    first_pattern, second_pattern, table, sems = refs[9:]
    copies = fetch(patterns, (first_pattern, second_pattern), sems)
    first = on_left(BLOCK)
    for which, pattern in enumerate((first_pattern, second_pattern)):
        left, right = total(which, sums, from_last, from_next)
        copies[which].wait()
        note_live(pattern, table, grid, slots)
        for e in range(3):
            keep = jnp.where(first, table[3 * e], table[3 * e + 1]) > 0
            left_tile = jnp.where(keep, left[e], 0.0)
            right_tile = jnp.where(first, swap(left_tile), jnp.where(table[3 * e + 2] > 0, right[e], 0.0))
            to_left[which, e] = left_tile
            to_right[which, e] = right_tile
            if e != 1:
                ask = ask_next if e == 2 else ask_last
                ask[which, :BLOCK, :] = left_tile
                fold_into(ask, which, right_tile)


def final_kernel(grid, slots, *refs):
    patterns, (own_left, own_right, sums, from_last, from_next), outputs = refs[:2], refs[2:7], refs[7:9]
    first_pattern, second_pattern, dense, packed, chosen, sems = refs[9:]
    copies = fetch(patterns, (first_pattern, second_pattern), sems)
    first_half = on_left(HALF)
    even, odd = pl.ds(0, HALF, stride=2), pl.ds(1, HALF, stride=2)
    for which, pattern in enumerate((first_pattern, second_pattern)):
        out = outputs[which]
        left, right = total(which, sums, from_last, from_next)
        for e in range(3):
            dense[which, e] = 2.0 * own_left[which, e] - left[e]
            dense[which, 3 + e] = 2.0 * own_right[which, e] - right[e]
        for e in range(3):
            a, b = dense[which, e, even, :], dense[which, e, odd, :]
            packed[which, 3 * e] = jnp.where(first_half, a, swap(b))
            packed[which, 3 * e + 1] = jnp.where(first_half, swap(a), b)
            a, b = dense[which, 3 + e, even, :], dense[which, 3 + e, odd, :]
            packed[which, 3 * e + 2] = jnp.where(first_half, swap(a), b)
        packed[which, 9] = jnp.zeros((HALF, WIDE), F32)
        copies[which].wait()
        for slot in range(slots):
            chosen[which, slot * HALF : (slot + 1) * HALF, :] = packed[which, place_of(pattern[0, slot], grid)]
        for step in range(HALF):
            out[:, step * WIDE : (step + 1) * WIDE] = chosen[which, pl.ds(step, slots, stride=HALF), :]


def shift(block, axis, by):
    count = lax.axis_size(axis)
    return lax.ppermute(block, axis, [(i, (i + by) % count) for i in range(count)])


VM = pl.BlockSpec(memory_space=pltpu.VMEM)
HB = pl.BlockSpec(memory_space=pltpu.HBM)
PARAMS = pltpu.CompilerParams(vmem_limit_bytes=VMEM_LIMIT)


def stay(operand):
    return pltpu.with_memory_space_constraint(operand, pltpu.HBM)


def shape(*sizes):
    return jax.ShapeDtypeStruct(sizes, F32)


def multiply(own_left, own_right, ask_next, ask_last):
    from_left = shift(own_right, "col", 1)
    from_right = shift(own_left, "col", -1)
    from_last = shift(ask_next, "row", 1)
    from_next = shift(ask_last, "row", -1)
    by = jax.ShapeDtypeStruct((2, DEPTH, 6 * WIDE), BF16)
    factor = pltpu.VMEM((4 * BLOCK, DEPTH), BF16)
    to_last, to_next, by_first, by_second = pl.pallas_call(
        share_kernel,
        out_shape=[shape(2, 3, BLOCK, WIDE)] * 2 + [by] * 2,
        in_specs=[VM] * 6,
        out_specs=[VM] * 4,
        scratch_shapes=[factor],
        compiler_params=PARAMS,
        name="share",
    )(own_left, own_right, from_left, from_right, from_last, from_next)
    sums = pl.pallas_call(
        own_kernel,
        out_shape=shape(2, 6, BLOCK, WIDE),
        in_specs=[VM] * 4,
        out_specs=VM,
        scratch_shapes=[factor],
        compiler_params=PARAMS,
        cost_estimate=pl.CostEstimate(flops=10**9, bytes_accessed=3 * 10**6, transcendentals=0),
        name="own",
    )(own_left, own_right, by_first, by_second)
    return sums, shift(to_next, "row", 1), shift(to_last, "row", -1)


def shards(
    density,
    density_pattern,
    response,
    response_pattern,
    density_next_pattern,
    response_next_pattern,
    density_out_pattern,
    response_out_pattern,
):
    slots = density.shape[3]
    grid = (lax.axis_size("row"), lax.axis_size("col"))
    pattern = pltpu.SMEM((1, slots), jnp.int32)
    table = pltpu.SMEM((16,), jnp.int32)
    messages = [shape(2, 3, BLOCK, WIDE)] * 2 + [shape(2, BLOCK + HALF, WIDE)] * 2

    def flat(pattern):
        return stay(pattern.reshape(1, slots))

    sent = pl.pallas_call(
        functools.partial(spread_kernel, grid, slots),
        out_shape=messages,
        in_specs=[HB] * 4,
        out_specs=[VM] * 4,
        scratch_shapes=[pattern] * 2
        + [pltpu.VMEM((slots, BLOCK * BLOCK), F32)] * 2
        + [pltpu.VMEM((2, (slots + 1) * HALF, WIDE), F32), table, pltpu.SemaphoreType.DMA((4,))],
        compiler_params=PARAMS,
        name="spread",
    )(
        flat(density_pattern),
        flat(response_pattern),
        stay(density.reshape(slots, BLOCK * BLOCK)),
        stay(response.reshape(slots, BLOCK * BLOCK)),
    )
    sent = pl.pallas_call(
        functools.partial(next_kernel, grid, slots),
        out_shape=messages,
        in_specs=[HB] * 2 + [VM] * 3,
        out_specs=[VM] * 4,
        scratch_shapes=[pattern] * 2 + [table, pltpu.SemaphoreType.DMA((2,))],
        compiler_params=PARAMS,
        name="next_step",
    )(flat(density_next_pattern), flat(response_next_pattern), *multiply(*sent))
    outputs = pl.pallas_call(
        functools.partial(final_kernel, grid, slots),
        out_shape=[shape(slots, BLOCK * BLOCK)] * 2,
        in_specs=[HB] * 2 + [VM] * 5,
        out_specs=[VM] * 2,
        scratch_shapes=[pattern] * 2
        + [
            pltpu.VMEM((2, 6, BLOCK, WIDE), F32),
            pltpu.VMEM((2, 10, HALF, WIDE), F32),
            pltpu.VMEM((2, slots * HALF, WIDE), F32),
            pltpu.SemaphoreType.DMA((2,)),
        ],
        compiler_params=PARAMS,
        name="final_step",
    )(flat(density_out_pattern), flat(response_out_pattern), *sent[:2], *multiply(*sent))
    return tuple(out.reshape(density.shape) for out in outputs)


def solution(mesh):
    data = P(("groups", "row"), "col", None, None, None)
    pattern = P(("groups", "row"), "col", None, None)
    return jax.shard_map(
        shards,
        mesh=mesh,
        in_specs=(data, pattern, data, pattern, pattern, pattern, pattern, pattern),
        out_specs=(data, data),
        check_vma=False,
    )
```

time: 60.1 us -> 45.9 us (0.76)
  waiting for transfers between devices: 35.1 us -> 24.5 us
  local copies, waits for them, and re-layouts: 3.86 us -> 0 us
  Pallas kernels: 4.78 us -> 6.84 us
  starting transfers between devices: 15.3 us -> 13.7 us
    ppermute x12, waiting for transfers between devices: 35.1 us -> 24.5 us  [shift(): lax.ppermute(block, axis, [(i, (i + by) % count) for i in range(count)])]
    unnamed x16 -> x0, local copies, waits for them, and re-layouts: 3.79 us -> none
    pallas_call x3 -> x7, Pallas kernels: 4.78 us -> 6.84 us  [the longest x1 1.68 us: shards(): pl.pallas_call(functools.partial(final_kernel, grid, slots), out_shape=[s...]
    ppermute x12, starting transfers between devices: 15.3 us -> 13.7 us  [shift(): lax.ppermute(block, axis, [(i, (i + by) % count) for i in range(count)])]
  transfers between devices with their start and end apart: 12 -> 12, of which waited for: 8 -> 10; matrix products, arithmetic and copies ran while one was open for 0% -> 0% of each run, Pallas kernels for 0% -> 3%
where the time goes in v2:
time: 45.9 us; the launch traced here: 45.7 us
  waiting for transfers between devices  24.5 us (53%)
  starting transfers between devices  13.7 us (30%)
  Pallas kernels  6.84 us (15%)
  between operations  0.67 us (1%)
    ppermute x12, waiting for transfers between devices, shift(): lax.ppermute(block, axis, [(i, (i + by) % count) for i in range(count)])  24.5 us
    ppermute x12, starting transfers between devices, shift(): lax.ppermute(block, axis, [(i, (i + by) % count) for i in range(count)])  13.7 us
    pallas_call x1, Pallas kernels, shards(): pl.pallas_call(functools.partial(final_kernel, grid, slots), out_shape=[s...  1.68 us
    pallas_call x1, Pallas kernels, shards(): pl.pallas_call(functools.partial(spread_kernel, grid, slots), out_shape=m...  1.48 us
    pallas_call x2, Pallas kernels, multiply(): pl.pallas_call(share_kernel, out_shape=[shape(2, 3, BLOCK, WIDE)] * 2 + [...  1.36 us
    pallas_call x2, Pallas kernels, multiply(): pl.pallas_call(own_kernel, out_shape=shape(2, 6, BLOCK, WIDE), in_specs=[...  1.22 us
    pallas_call x1, Pallas kernels, shards(): pl.pallas_call(functools.partial(next_kernel, grid, slots), out_shape=mes...  1.11 us
  transfers between devices with their start and end apart: 12, of which 10 were waited for; matrix products, arithmetic and copies ran while one was open for 0% of the time, Pallas kernels for 3%

profile of v2, /device:TPU:1, one launch (start us, length us, event | category | flops | bytes accessed | tf_op | source)
XLA Modules:
  0.0 45.7 jit_solution(9729272594157347476)
XLA Ops:
  0.6 1.5 %spread.1 = (f32[2,3,64,128]{3,2,1,0:T(8,128)S(1)}, f32[2,3,64,128]{3,2,1,0:T(8,128)S(1)}, f32[2,96,128]{2,1,0:T(8,128)S(1)}, f32[2,96,128]{2,1,0:T(8,128)S(1)}) custom-call(s32[1,8]{1,0:T(1,128)} %bitcast.12, s32[1,8]{1,0:T(1,128)} %bitcast.13, f32[8,4096]{1,0:T(8,128)} %bitcast.10, f32[8,4096]{1,0:T(8,128)} %bitcast.11), custom_call_target="tpu_custom_call" | custom-call | tf_op jit(solution)/shard_map/spread/pallas_call | solution.py:307
  2.1 4.2 %collective-permute-start.1 = (f32[2,3,64,128]{3,2,1,0:T(8,128)S(1)}, f32[2,3,64,128]{3,2,1,0:T(8,128)S(1)}, u32[]{:S(2)}, u32[]{:S(2)}) collective-permute-start(f32[2,3,64,128]{3,2,1,0:T(8,128)S(1)} %get-tuple-element.20.own_left), channel_id=1, source_target_pairs={{0,3},{1,0},{2,1},{3,2},{4,7},{5,4},{6,5},{7,6},{8,11},{9,8},{10,9... | collective-permute-start | bytes 589832 | tf_op jit(solution)/shard_map/ppermute | solution.py:243
  6.3 0.0 collective-permute-start
  6.3 2.0 %collective-permute-start.2 = (f32[2,96,128]{2,1,0:T(8,128)S(1)}, f32[2,96,128]{2,1,0:T(8,128)S(1)}, u32[]{:S(2)}, u32[]{:S(2)}) collective-permute-start(f32[2,96,128]{2,1,0:T(8,128)S(1)} %get-tuple-element.22), channel_id=1, source_target_pairs={{0,4},{4,8},{8,12},{12,0},{1,5},{5,9},{9,13},{13,1},{2,6},{6,10},{... | collective-permute-start | bytes 294920 | tf_op jit(solution)/shard_map/ppermute | solution.py:243
  8.4 0.0 collective-permute-start.3
  8.4 1.8 %collective-permute-done.2.from_last = f32[2,96,128]{2,1,0:T(8,128)S(1)} collective-permute-done((f32[2,96,128]{2,1,0:T(8,128)S(1)}, f32[2,96,128]{2,1,0:T(8,128)S(1)}, u32[]{:S(2)}, u32[]{:S(2)}) %collective-permute-start.2) | collective-permute-done | bytes 98336 | tf_op jit(solution)/shard_map/ppermute | solution.py:243
  10.2 2.2 %collective-permute-done.3.from_next = f32[2,96,128]{2,1,0:T(8,128)S(1)} collective-permute-done((f32[2,96,128]{2,1,0:T(8,128)S(1)}, f32[2,96,128]{2,1,0:T(8,128)S(1)}, u32[]{:S(2)}, u32[]{:S(2)}) %collective-permute-start.3) | collective-permute-done | bytes 98336 | tf_op jit(solution)/shard_map/ppermute | solution.py:243
  12.4 0.0 collective-permute-done.1.from_right
  12.4 2.7 %collective-permute-done.from_left = f32[2,3,64,128]{3,2,1,0:T(8,128)S(1)} collective-permute-done((f32[2,3,64,128]{3,2,1,0:T(8,128)S(1)}, f32[2,3,64,128]{3,2,1,0:T(8,128)S(1)}, u32[]{:S(2)}, u32[]{:S(2)}) %collective-permute-start) | collective-permute-done | bytes 196640 | tf_op jit(solution)/shard_map/ppermute | solution.py:243
  15.1 0.7 %share.2 = (f32[2,3,64,128]{3,2,1,0:T(8,128)S(1)}, f32[2,3,64,128]{3,2,1,0:T(8,128)S(1)}, bf16[2,192,768]{2,1,0:T(8,128)(2,1)S(1)}, bf16[2,192,768]{2,1,0:T(8,128)(2,1)S(1)}) custom-call(f32[2,3,64,128]{3,2,1,0:T(8,128)S(1)} %get-tuple-element.20.own_left, f32[2,3,64,128]{3,2,1,0:T(8,128)S(1)} %get-tuple-element.21.own_right, ...), custom_call_target="tpu_custom_call" | custom-call | tf_op jit(solution)/shard_map/share/pallas_call | solution.py:266
  15.8 2.6 %collective-permute-start.4 = (f32[2,3,64,128]{3,2,1,0:T(8,128)S(1)}, f32[2,3,64,128]{3,2,1,0:T(8,128)S(1)}, u32[]{:S(2)}, u32[]{:S(2)}) collective-permute-start(f32[2,3,64,128]{3,2,1,0:T(8,128)S(1)} %get-tuple-element.26), channel_id=1, source_target_pairs={{0,4},{4,8},{8,12},{12,0},{1,5},{5,9},{9,13},{13,1},{2,6},{6,10},{... | collective-permute-start | bytes 589832 | tf_op jit(solution)/shard_map/ppermute | solution.py:243
  18.4 0.0 collective-permute-start.5
  18.4 0.6 %own.2.refs_2_ = f32[2,6,64,128]{3,2,1,0:T(8,128)S(1)} custom-call(f32[2,3,64,128]{3,2,1,0:T(8,128)S(1)} %get-tuple-element.20.own_left, f32[2,3,64,128]{3,2,1,0:T(8,128)S(1)} %get-tuple-element.21.own_right, bf16[2,192,768]{2,1,0:T(8,128)(2,1)S(1)} %get-tuple-element.24.by_first, bf16[2,192,768]{2,1,0:T(8,128)(2,1)S(1)} %get-tuple-element.25.by_second), custom_call_target="tpu_custom_call" | custom-call | flops 1000000000 | bytes 3000000 | tf_op jit(solution)/shard_map/own/pallas_call | solution.py:275
  19.0 3.3 %collective-permute-done.4.refs_3_ = f32[2,3,64,128]{3,2,1,0:T(8,128)S(1)} collective-permute-done((f32[2,3,64,128]{3,2,1,0:T(8,128)S(1)}, f32[2,3,64,128]{3,2,1,0:T(8,128)S(1)}, u32[]{:S(2)}, u32[]{:S(2)}) %collective-permute-start.4) | collective-permute-done | bytes 196640 | tf_op jit(solution)/shard_map/ppermute | solution.py:243
  22.3 1.5 %collective-permute-done.5.refs_4_ = f32[2,3,64,128]{3,2,1,0:T(8,128)S(1)} collective-permute-done((f32[2,3,64,128]{3,2,1,0:T(8,128)S(1)}, f32[2,3,64,128]{3,2,1,0:T(8,128)S(1)}, u32[]{:S(2)}, u32[]{:S(2)}) %collective-permute-start.5) | collective-permute-done | bytes 196640 | tf_op jit(solution)/shard_map/ppermute | solution.py:243
  23.8 1.1 %next_step.1 = (f32[2,3,64,128]{3,2,1,0:T(8,128)S(1)}, f32[2,3,64,128]{3,2,1,0:T(8,128)S(1)}, f32[2,96,128]{2,1,0:T(8,128)S(1)}, f32[2,96,128]{2,1,0:T(8,128)S(1)}) custom-call(s32[1,8]{1,0:T(1,128)} %bitcast.14, s32[1,8]{1,0:T(1,128)} %bitcast.15, f32[2,6,64,128]{3,2,1,0:T(8,128)S(1)} %own.2.refs_2_, f32[2,3,64,128]{3,2,1,0:T(8,128)S(1)} %collective-permute-done.4.refs_3_, ...), custom_call_target="tpu_custom_call" | custom-call | tf_op jit(solution)/shard_map/next_step/pallas_call | solution.py:323
  24.9 1.5 %collective-permute-start.7 = (f32[2,3,64,128]{3,2,1,0:T(8,128)S(1)}, f32[2,3,64,128]{3,2,1,0:T(8,128)S(1)}, u32[]{:S(2)}, u32[]{:S(2)}) collective-permute-start(f32[2,3,64,128]{3,2,1,0:T(8,128)S(1)} %get-tuple-element.28.own_left.refs_2_), channel_id=1, source_target_pairs={{0,3},{1,0},{2,1},{3,2},{4,7},{5,4},{6,5},{7,6},{8,11},{9,8},{10,9... | collective-permute-start | bytes 589832 | tf_op jit(solution)/shard_map/ppermute | solution.py:243
  26.4 0.0 collective-permute-start.6
  26.4 1.5 %collective-permute-start.8 = (f32[2,96,128]{2,1,0:T(8,128)S(1)}, f32[2,96,128]{2,1,0:T(8,128)S(1)}, u32[]{:S(2)}, u32[]{:S(2)}) collective-permute-start(f32[2,96,128]{2,1,0:T(8,128)S(1)} %get-tuple-element.30), channel_id=1, source_target_pairs={{0,4},{4,8},{8,12},{12,0},{1,5},{5,9},{9,13},{13,1},{2,6},{6,10},{... | collective-permute-start | bytes 294920 | tf_op jit(solution)/shard_map/ppermute | solution.py:243
  28.0 0.0 collective-permute-start.9
  28.0 2.0 %collective-permute-done.8.from_last = f32[2,96,128]{2,1,0:T(8,128)S(1)} collective-permute-done((f32[2,96,128]{2,1,0:T(8,128)S(1)}, f32[2,96,128]{2,1,0:T(8,128)S(1)}, u32[]{:S(2)}, u32[]{:S(2)}) %collective-permute-start.8) | collective-permute-done | bytes 98336 | tf_op jit(solution)/shard_map/ppermute | solution.py:243
  30.0 2.3 %collective-permute-done.9.from_next = f32[2,96,128]{2,1,0:T(8,128)S(1)} collective-permute-done((f32[2,96,128]{2,1,0:T(8,128)S(1)}, f32[2,96,128]{2,1,0:T(8,128)S(1)}, u32[]{:S(2)}, u32[]{:S(2)}) %collective-permute-start.9) | collective-permute-done | bytes 98336 | tf_op jit(solution)/shard_map/ppermute | solution.py:243
  32.3 0.0 collective-permute-done.7.from_right
  32.3 3.8 %collective-permute-done.6.from_left = f32[2,3,64,128]{3,2,1,0:T(8,128)S(1)} collective-permute-done((f32[2,3,64,128]{3,2,1,0:T(8,128)S(1)}, f32[2,3,64,128]{3,2,1,0:T(8,128)S(1)}, u32[]{:S(2)}, u32[]{:S(2)}) %collective-permute-start.6) | collective-permute-done | bytes 196640 | tf_op jit(solution)/shard_map/ppermute | solution.py:243
  36.2 0.7 %share.3 = (f32[2,3,64,128]{3,2,1,0:T(8,128)S(1)}, f32[2,3,64,128]{3,2,1,0:T(8,128)S(1)}, bf16[2,192,768]{2,1,0:T(8,128)(2,1)S(1)}, bf16[2,192,768]{2,1,0:T(8,128)(2,1)S(1)}) custom-call(f32[2,3,64,128]{3,2,1,0:T(8,128)S(1)} %get-tuple-element.28.own_left.refs_2_, f32[2,3,64,128]{3,2,1,0:T(8,128)S(1)} %get-tuple-element.29.own_right.refs_3_, ...), custom_call_target="tpu_custom_call" | custom-call | tf_op jit(solution)/shard_map/share/pallas_call | solution.py:266
  36.9 1.8 %collective-permute-start.10 = (f32[2,3,64,128]{3,2,1,0:T(8,128)S(1)}, f32[2,3,64,128]{3,2,1,0:T(8,128)S(1)}, u32[]{:S(2)}, u32[]{:S(2)}) collective-permute-start(f32[2,3,64,128]{3,2,1,0:T(8,128)S(1)} %get-tuple-element.34), channel_id=1, source_target_pairs={{0,4},{4,8},{8,12},{12,0},{1,5},{5,9},{9,13},{13,1},{2,6},{6,10},{... | collective-permute-start | bytes 589832 | tf_op jit(solution)/shard_map/ppermute | solution.py:243
  38.6 0.0 collective-permute-start.11
  38.6 0.6 %own.3.refs_4_ = f32[2,6,64,128]{3,2,1,0:T(8,128)S(1)} custom-call(f32[2,3,64,128]{3,2,1,0:T(8,128)S(1)} %get-tuple-element.28.own_left.refs_2_, f32[2,3,64,128]{3,2,1,0:T(8,128)S(1)} %get-tuple-element.29.own_right.refs_3_, bf16[2,192,768]{2,1,0:T(8,128)(2,1)S(1)} %get-tuple-element.32.by_first, bf16[2,192,768]{2,1,0:T(8,128)(2,1)S(1)} %get-tuple-element.33.by_second), custom_call_target="tpu_custom_call" | custom-call | flops 1000000000 | bytes 3000000 | tf_op jit(solution)/shard_map/own/pallas_call | solution.py:275
  39.2 3.3 %collective-permute-done.10.refs_5_ = f32[2,3,64,128]{3,2,1,0:T(8,128)S(1)} collective-permute-done((f32[2,3,64,128]{3,2,1,0:T(8,128)S(1)}, f32[2,3,64,128]{3,2,1,0:T(8,128)S(1)}, u32[]{:S(2)}, u32[]{:S(2)}) %collective-permute-start.10) | collective-permute-done | bytes 196640 | tf_op jit(solution)/shard_map/ppermute | solution.py:243
  42.5 1.5 %collective-permute-done.11.refs_6_ = f32[2,3,64,128]{3,2,1,0:T(8,128)S(1)} collective-permute-done((f32[2,3,64,128]{3,2,1,0:T(8,128)S(1)}, f32[2,3,64,128]{3,2,1,0:T(8,128)S(1)}, u32[]{:S(2)}, u32[]{:S(2)}) %collective-permute-start.11) | collective-permute-done | bytes 196640 | tf_op jit(solution)/shard_map/ppermute | solution.py:243
  44.0 1.7 %final_step.1 = (f32[8,4096]{1,0:T(8,128)}, f32[8,4096]{1,0:T(8,128)}) custom-call(s32[1,8]{1,0:T(1,128)} %bitcast.16, s32[1,8]{1,0:T(1,128)} %bitcast.17, f32[2,3,64,128]{3,2,1,0:T(8,128)S(1)} %get-tuple-element.28.own_left.refs_2_, f32[2,3,64,128]{3,2,1,0:T(8,128)S(1)} %get-tuple-element.29.own_right.refs_3_, f32[2,6,64,128]{3,2,1,0:T(8,128)S(1)} %own.3.refs_4_, ...), custom_call_target="tpu_custom_call" | custom-call | tf_op jit(solution)/shard_map/final_step/pallas_call | solution.py:332
Async XLA Ops:
  2.1 10.3 %collective-permute-start.1 = (f32[2,3,64,128]{3,2,1,0:T(8,128)S(1)}, f32[2,3,64,128]{3,2,1,0:T(8,128)S(1)}, u32[]{:S(2)}, u32[]{:S(2)}) collective-permute-start(f32[2,3,64,128]{3,2,1,0:T(8,128)S(1)} %get-tuple-element.20.own_left), channel_id=1, source_target_pairs={{0,3},{1,0},{2,1},{3,2},{4,7},{5,4},{6,5},{7,6},{8,11},{9,8},{10,9... | collective-permute-start | bytes 589832 | tf_op jit(solution)/shard_map/ppermute | solution.py:243
  6.3 8.8 %collective-permute-start = (f32[2,3,64,128]{3,2,1,0:T(8,128)S(1)}, f32[2,3,64,128]{3,2,1,0:T(8,128)S(1)}, u32[]{:S(2)}, u32[]{:S(2)}) collective-permute-start(f32[2,3,64,128]{3,2,1,0:T(8,128)S(1)} %get-tuple-element.21.own_right), channel_id=1, source_target_pairs={{0,1},{1,2},{2,3},{3,0},{4,5},{5,6},{6,7},{7,4},{8,9},{9,10},{10,1... | collective-permute-start | bytes 589832 | tf_op jit(solution)/shard_map/ppermute | solution.py:243
  6.3 3.9 %collective-permute-start.2 = (f32[2,96,128]{2,1,0:T(8,128)S(1)}, f32[2,96,128]{2,1,0:T(8,128)S(1)}, u32[]{:S(2)}, u32[]{:S(2)}) collective-permute-start(f32[2,96,128]{2,1,0:T(8,128)S(1)} %get-tuple-element.22), channel_id=1, source_target_pairs={{0,4},{4,8},{8,12},{12,0},{1,5},{5,9},{9,13},{13,1},{2,6},{6,10},{... | collective-permute-start | bytes 294920 | tf_op jit(solution)/shard_map/ppermute | solution.py:243
  8.4 4.0 %collective-permute-start.3 = (f32[2,96,128]{2,1,0:T(8,128)S(1)}, f32[2,96,128]{2,1,0:T(8,128)S(1)}, u32[]{:S(2)}, u32[]{:S(2)}) collective-permute-start(f32[2,96,128]{2,1,0:T(8,128)S(1)} %get-tuple-element.23), channel_id=1, source_target_pairs={{0,12},{4,0},{8,4},{12,8},{1,13},{5,1},{9,5},{13,9},{2,14},{6,2},{... | collective-permute-start | bytes 294920 | tf_op jit(solution)/shard_map/ppermute | solution.py:243
  15.8 6.5 %collective-permute-start.4 = (f32[2,3,64,128]{3,2,1,0:T(8,128)S(1)}, f32[2,3,64,128]{3,2,1,0:T(8,128)S(1)}, u32[]{:S(2)}, u32[]{:S(2)}) collective-permute-start(f32[2,3,64,128]{3,2,1,0:T(8,128)S(1)} %get-tuple-element.26), channel_id=1, source_target_pairs={{0,4},{4,8},{8,12},{12,0},{1,5},{5,9},{9,13},{13,1},{2,6},{6,10},{... | collective-permute-start | bytes 589832 | tf_op jit(solution)/shard_map/ppermute | solution.py:243
  18.4 5.4 %collective-permute-start.5 = (f32[2,3,64,128]{3,2,1,0:T(8,128)S(1)}, f32[2,3,64,128]{3,2,1,0:T(8,128)S(1)}, u32[]{:S(2)}, u32[]{:S(2)}) collective-permute-start(f32[2,3,64,128]{3,2,1,0:T(8,128)S(1)} %get-tuple-element.27), channel_id=1, source_target_pairs={{0,12},{4,0},{8,4},{12,8},{1,13},{5,1},{9,5},{13,9},{2,14},{6,2},{... | collective-permute-start | bytes 589832 | tf_op jit(solution)/shard_map/ppermute | solution.py:243
  24.9 7.4 %collective-permute-start.7 = (f32[2,3,64,128]{3,2,1,0:T(8,128)S(1)}, f32[2,3,64,128]{3,2,1,0:T(8,128)S(1)}, u32[]{:S(2)}, u32[]{:S(2)}) collective-permute-start(f32[2,3,64,128]{3,2,1,0:T(8,128)S(1)} %get-tuple-element.28.own_left.refs_2_), channel_id=1, source_target_pairs={{0,3},{1,0},{2,1},{3,2},{4,7},{5,4},{6,5},{7,6},{8,11},{9,8},{10,9... | collective-permute-start | bytes 589832 | tf_op jit(solution)/shard_map/ppermute | solution.py:243
  26.4 9.7 %collective-permute-start.6 = (f32[2,3,64,128]{3,2,1,0:T(8,128)S(1)}, f32[2,3,64,128]{3,2,1,0:T(8,128)S(1)}, u32[]{:S(2)}, u32[]{:S(2)}) collective-permute-start(f32[2,3,64,128]{3,2,1,0:T(8,128)S(1)} %get-tuple-element.29.own_right.refs_3_), channel_id=1, source_target_pairs={{0,1},{1,2},{2,3},{3,0},{4,5},{5,6},{6,7},{7,4},{8,9},{9,10},{10,1... | collective-permute-start | bytes 589832 | tf_op jit(solution)/shard_map/ppermute | solution.py:243
  26.4 3.6 %collective-permute-start.8 = (f32[2,96,128]{2,1,0:T(8,128)S(1)}, f32[2,96,128]{2,1,0:T(8,128)S(1)}, u32[]{:S(2)}, u32[]{:S(2)}) collective-permute-start(f32[2,96,128]{2,1,0:T(8,128)S(1)} %get-tuple-element.30), channel_id=1, source_target_pairs={{0,4},{4,8},{8,12},{12,0},{1,5},{5,9},{9,13},{13,1},{2,6},{6,10},{... | collective-permute-start | bytes 294920 | tf_op jit(solution)/shard_map/ppermute | solution.py:243
  28.0 4.3 %collective-permute-start.9 = (f32[2,96,128]{2,1,0:T(8,128)S(1)}, f32[2,96,128]{2,1,0:T(8,128)S(1)}, u32[]{:S(2)}, u32[]{:S(2)}) collective-permute-start(f32[2,96,128]{2,1,0:T(8,128)S(1)} %get-tuple-element.31), channel_id=1, source_target_pairs={{0,12},{4,0},{8,4},{12,8},{1,13},{5,1},{9,5},{13,9},{2,14},{6,2},{... | collective-permute-start | bytes 294920 | tf_op jit(solution)/shard_map/ppermute | solution.py:243
  36.9 5.7 %collective-permute-start.10 = (f32[2,3,64,128]{3,2,1,0:T(8,128)S(1)}, f32[2,3,64,128]{3,2,1,0:T(8,128)S(1)}, u32[]{:S(2)}, u32[]{:S(2)}) collective-permute-start(f32[2,3,64,128]{3,2,1,0:T(8,128)S(1)} %get-tuple-element.34), channel_id=1, source_target_pairs={{0,4},{4,8},{8,12},{12,0},{1,5},{5,9},{9,13},{13,1},{2,6},{6,10},{... | collective-permute-start | bytes 589832 | tf_op jit(solution)/shard_map/ppermute | solution.py:243
  38.6 5.4 %collective-permute-start.11 = (f32[2,3,64,128]{3,2,1,0:T(8,128)S(1)}, f32[2,3,64,128]{3,2,1,0:T(8,128)S(1)}, u32[]{:S(2)}, u32[]{:S(2)}) collective-permute-start(f32[2,3,64,128]{3,2,1,0:T(8,128)S(1)} %get-tuple-element.35), channel_id=1, source_target_pairs={{0,12},{4,0},{8,4},{12,8},{1,13},{5,1},{9,5},{13,9},{2,14},{6,2},{... | collective-permute-start | bytes 589832 | tf_op jit(solution)/shard_map/ppermute | solution.py:243

commit v3 on v2

v3 whole, which is shorter than its diff:
```python
import functools

import jax
import jax.numpy as jnp
from jax import lax
from jax.experimental import pallas as pl
from jax.experimental.pallas import tpu as pltpu
from jax.sharding import PartitionSpec as P

BLOCK = 64
WIDE = 2 * BLOCK
HALF = BLOCK // 2
DEPTH = 3 * BLOCK
ASK_ROWS = BLOCK + HALF
KEEP_ROWS = 8
F32 = jnp.float32
BF16 = jnp.bfloat16
VMEM_LIMIT = 16 * 1024 * 1024


def on_left(rows):
    return lax.broadcasted_iota(jnp.int32, (rows, WIDE), 1) < BLOCK


def swap(tile):
    return pltpu.roll(tile, BLOCK, 1)


def place_of(ident, grid):
    rows, cols = grid
    source = jnp.maximum(ident, 0)
    owner_row = lax.div(source, jnp.int32(cols))
    owner_col = lax.rem(source, jnp.int32(cols))
    down = lax.rem(owner_row - lax.axis_index("row") + 1 + rows, jnp.int32(rows))
    across = lax.rem(owner_col - lax.axis_index("col") + 1 + cols, jnp.int32(cols))
    return jnp.where(ident < 0, 9, down * 3 + across)


def note_slots(pattern, table, grid, slots):
    for place in range(10):
        table[place] = slots
    for slot in range(slots):
        table[place_of(pattern[0, slot], grid)] = slot


def note_live(pattern, table, keep, which, grid, slots):
    for place in range(10):
        table[place] = 0
    for slot in range(slots):
        table[place_of(pattern[0, slot], grid)] = 1
    first = on_left(1)
    for side in range(2):
        for e in range(3):
            low = 3 * e + side
            keep[which, 3 * side + e : 3 * side + e + 1, :] = jnp.where(first, table[low], table[low + 1]).astype(F32)


def fetch(sources, targets, sems):
    copies = [pltpu.make_async_copy(s, t, sems.at[i]) for i, (s, t) in enumerate(zip(sources, targets))]
    for copy in copies:
        copy.start()
    return copies


def spread(slots, grid, pattern, data, to_left, to_right, rows, table, copies):
    first_half = on_left(HALF)
    even, odd = pl.ds(0, HALF, stride=2), pl.ds(1, HALF, stride=2)
    copies[0].wait()
    note_slots(pattern, table, grid, slots)
    rows[slots * HALF : (slots + 1) * HALF, :] = jnp.zeros((HALF, WIDE), F32)
    copies[1].wait()
    for step in range(HALF):
        rows[pl.ds(step, slots, stride=HALF), :] = data[:, step * WIDE : (step + 1) * WIDE]

    def block(place):
        own = rows[pl.ds(pl.multiple_of(table[place] * HALF, HALF), HALF), :]
        return own, swap(own)

    def tile(low, high):
        return (jnp.where(first_half, low[0], high[1]), jnp.where(first_half, low[1], high[0]))

    for e in range(3):
        a, b, c = block(3 * e), block(3 * e + 1), block(3 * e + 2)
        left, right = tile(a, b), tile(b, c)
        for part, stride in enumerate((even, odd)):
            to_left[e, stride, :] = left[part]
            to_right[e, stride, :] = right[part]


def spread_kernel(grid, slots, *refs):
    sources, (first_left, first_right, second_left, second_right, ask_next, ask_last, keep) = refs[:6], refs[6:13]
    patterns, next_patterns, datas, rows, table, sems = refs[13:15], refs[15:17], refs[17:19], *refs[19:]
    copies = fetch(sources, (*patterns, *datas, *next_patterns), sems)
    pairs = ((first_left, first_right), (second_left, second_right))
    for which, pair in enumerate(pairs):
        spread(slots, grid, patterns[which], datas[which], *pair, rows.at[which], table, copies[which :: 2])
    for which, next_pattern in enumerate(next_patterns):
        copies[4 + which].wait()
        note_live(next_pattern, table, keep, which, grid, slots)
    for which, (left, right) in enumerate(pairs):
        at = which * ASK_ROWS
        for ask, e in ((ask_last, 0), (ask_next, 2)):
            ask[at : at + BLOCK, :] = left[e]
            ask[at + BLOCK : at + ASK_ROWS, :] = fold(right[e])
            masks = 2 * ASK_ROWS + KEEP_ROWS * which
            wide = jnp.broadcast_to(keep[which, 3 + e : 4 + e, BLOCK:], (1, BLOCK))
            ask[masks : masks + 1, :] = keep[which, e : e + 1, :]
            ask[masks + 1 : masks + 2, :] = jnp.concatenate([wide, wide], axis=1)
            ask[masks + 2 : masks + KEEP_ROWS, :] = jnp.zeros((KEEP_ROWS - 2, WIDE), F32)


def fold(right):
    return jnp.where(on_left(HALF), swap(right[:HALF]), right[HALF:])


def split(tile):
    high = tile.astype(BF16)
    return high, (tile - high.astype(F32)).astype(BF16)


def fill_left_factor(left, folded, factor):
    for part in range(2):
        at = part * BLOCK
        factor[at : at + BLOCK, :WIDE] = split(left)[part]
        factor[at : at + HALF, WIDE:] = split(folded)[part][:, :BLOCK]
        factor[at + HALF : at + BLOCK, WIDE:] = split(swap(folded))[part][:, :BLOCK]


def fill_right_factor(own_left, own_right, from_left, from_right, factor):
    first = on_left(BLOCK)
    zero = jnp.zeros((BLOCK, WIDE), BF16)
    for e in range(3):
        column = e * 2 * WIDE
        tiles = (
            (from_left[e], None),
            (own_left[e], jnp.where(first, 0.0, own_right[e])),
            (None, from_right[e]),
        )
        for k, pair in enumerate(tiles):
            for side, tile in enumerate(pair):
                values = (zero, zero) if tile is None else split(tile)
                at = pl.ds(column + side * WIDE, WIDE)
                for part in range(2):
                    factor[part, k * BLOCK : (k + 1) * BLOCK, at] = values[part]


def dot(a, b):
    return lax.dot_general(a, b, (((1,), (0,)), ((), ())), preferred_element_type=F32)


def product(factor, by, low, count):
    at = slice(low * 2 * WIDE, (low + count) * 2 * WIDE)
    high = dot(factor[...], by[0, :, at])
    return high[:BLOCK] + (high[BLOCK:] + dot(factor[:BLOCK, :], by[1, :, at]))


def tiles_of(total, count):
    first = on_left(BLOCK)
    left, right = [], []
    for e in range(count):
        a = total[:, 2 * e * WIDE : (2 * e + 1) * WIDE]
        b = total[:, (2 * e + 1) * WIDE : (2 * e + 2) * WIDE]
        left.append(a + jnp.where(first, 0.0, swap(b)))
        right.append(b)
    return left, right


def put_share(total, share):
    left, right = tiles_of(total, 2)
    share[:BLOCK, :] = left[0]
    share[BLOCK:WIDE, :] = left[1]
    share[WIDE:DEPTH, :] = jnp.where(on_left(BLOCK), swap(right[0]), right[1])


def put_sums(total, sums):
    left, right = tiles_of(total, 3)
    for e in range(3):
        sums[e] = left[e]
        sums[3 + e] = right[e]


def put_outer(sums, to_last, to_next):
    for share, e in ((to_last, 0), (to_next, 2)):
        share[DEPTH : DEPTH + BLOCK, :] = sums[e]
        share[DEPTH + BLOCK :, :] = fold(sums[3 + e])


def fill_own(left, right, factor):
    fill_left_factor(left[1], fold(right[1]), factor)


def first_step_first_kernel(own_left, own_right, from_left, from_right, from_last, from_next, *refs):
    to_last, to_next, sums, by, factors = refs
    fill_right_factor(own_left, own_right, from_left, from_right, by)
    for at, (asked, share) in enumerate(((from_last, to_last), (from_next, to_next))):
        factor = factors.at[at]
        fill_left_factor(asked[:BLOCK], asked[BLOCK:ASK_ROWS], factor)
        put_share(product(factor, by, at, 2), share)
    fill_own(own_left, own_right, factors.at[2])
    put_sums(product(factors.at[2], by, 0, 3), sums)
    put_outer(sums, to_last, to_next)


def first_step_second_kernel(own_left, own_right, from_left, from_right, from_last, from_next, *refs):
    first_by, first_factors, to_last, to_next, sums, by, factor = refs
    fill_right_factor(own_left, own_right, from_left, from_right, by)
    for at, (asked, share) in enumerate(((from_last, to_last), (from_next, to_next))):
        fill_left_factor(asked[ASK_ROWS : ASK_ROWS + BLOCK], asked[ASK_ROWS + BLOCK : 2 * ASK_ROWS], factor)
        put_share(product(factor, first_by, at, 2) + product(first_factors.at[at], by, at, 2), share)
    fill_own(own_left, own_right, factor)
    put_sums(product(factor, first_by, 0, 3) + product(first_factors.at[2], by, 0, 3), sums)
    put_outer(sums, to_last, to_next)


def fill_asked(which, masks, received, sent, at, factor):
    pack = sent[WIDE:DEPTH]
    if at == 0:
        left, folded = sent[BLOCK:WIDE], fold(pack)
    else:
        left, folded = sent[:BLOCK], jnp.where(on_left(HALF), pack[:HALF], swap(pack[HALF:]))
    row = 2 * ASK_ROWS + KEEP_ROWS * which
    left = jnp.where(masks[row : row + 1, :] > 0, left + received[DEPTH : DEPTH + BLOCK], 0.0)
    folded = jnp.where(masks[row + 1 : row + 2, :] > 0, folded + received[DEPTH + BLOCK :], 0.0)
    fill_left_factor(left, folded, factor)


def second_step_first_kernel(own_left, own_right, from_left, from_right, *refs):
    asks, received, sent, (to_last, to_next, by, factors) = refs[:2], refs[2:4], refs[4:6], refs[6:]
    fill_right_factor(own_left, own_right, from_left, from_right, by)
    for at, share in enumerate((to_last, to_next)):
        fill_asked(0, asks[at], received[at], sent[at], at, factors.at[at])
        put_share(product(factors.at[at], by, at, 2), share)


def second_step_second_kernel(own_left, own_right, from_left, from_right, *refs):
    asks, received, sent, (first_by, first_factors, to_last, to_next, by, factor) = refs[:2], refs[2:4], refs[4:6], refs[6:]
    fill_right_factor(own_left, own_right, from_left, from_right, by)
    for at, share in enumerate((to_last, to_next)):
        fill_asked(1, asks[at], received[at], sent[at], at, factor)
        put_share(product(factor, first_by, at, 2) + product(first_factors.at[at], by, at, 2), share)


def first_own_kernel(own_left, own_right, by, sums, factor):
    fill_own(own_left, own_right, factor)
    put_sums(product(factor, by, 0, 3), sums)


def second_own_kernel(first_left, first_right, own_left, own_right, first_by, by, sums, factor):
    fill_own(first_left, first_right, factor)
    total = product(factor, by, 0, 3)
    fill_own(own_left, own_right, factor)
    put_sums(total + product(factor, first_by, 0, 3), sums)


def total(sums, from_last, from_next):
    left = [sums[e] for e in range(3)]
    right = [sums[3 + e] for e in range(3)]
    for share, low in ((from_last, 0), (from_next, 1)):
        pack = share[WIDE:DEPTH]
        left[low] += share[:BLOCK]
        left[low + 1] += share[BLOCK:WIDE]
        right[low] += swap(pack)
        right[low + 1] += pack
    return left, right


def next_kernel(which, keep, sums, from_last, from_next, to_left, to_right):
    first = on_left(BLOCK)
    left, right = total(sums, from_last, from_next)
    for e in range(3):
        to_left[e] = jnp.where(keep[which, e : e + 1, :] > 0, left[e], 0.0)
        to_right[e] = jnp.where(keep[which, 3 + e : 4 + e, :] > 0, jnp.where(first, swap(left[e]), right[e]), 0.0)


def final_kernel(grid, slots, pattern_hbm, own_left, own_right, sums, from_last, from_next, _, out, *refs):
    pattern, dense, packed, chosen, sems = refs
    (copy,) = fetch((pattern_hbm,), (pattern,), sems)
    first_half = on_left(HALF)
    even, odd = pl.ds(0, HALF, stride=2), pl.ds(1, HALF, stride=2)
    left, right = total(sums, from_last, from_next)
    for e in range(3):
        dense[e] = 2.0 * own_left[e] - left[e]
        dense[3 + e] = 2.0 * own_right[e] - right[e]
    for e in range(3):
        a, b = dense[e, even, :], dense[e, odd, :]
        packed[3 * e] = jnp.where(first_half, a, swap(b))
        packed[3 * e + 1] = jnp.where(first_half, swap(a), b)
        a, b = dense[3 + e, even, :], dense[3 + e, odd, :]
        packed[3 * e + 2] = jnp.where(first_half, swap(a), b)
    packed[9] = jnp.zeros((HALF, WIDE), F32)
    copy.wait()
    for slot in range(slots):
        chosen[slot * HALF : (slot + 1) * HALF, :] = packed[place_of(pattern[0, slot], grid)]
    for step in range(HALF):
        out[:, step * WIDE : (step + 1) * WIDE] = chosen[pl.ds(step, slots, stride=HALF), :]


def shift(block, axis, by):
    count = lax.axis_size(axis)
    return lax.ppermute(block, axis, [(i, (i + by) % count) for i in range(count)])


VM = pl.BlockSpec(memory_space=pltpu.VMEM)
HB = pl.BlockSpec(memory_space=pltpu.HBM)
PARAMS = pltpu.CompilerParams(vmem_limit_bytes=VMEM_LIMIT)


def stay(operand):
    return pltpu.with_memory_space_constraint(operand, pltpu.HBM)


def shape(*sizes):
    return jax.ShapeDtypeStruct(sizes, F32)


def call(kernel, out_shape, in_specs, out_specs, scratch, name, flops=0):
    return pl.pallas_call(
        kernel,
        out_shape=out_shape,
        in_specs=in_specs,
        out_specs=out_specs,
        scratch_shapes=scratch,
        compiler_params=PARAMS,
        cost_estimate=pl.CostEstimate(flops=flops, bytes_accessed=10**6, transcendentals=0),
        name=name,
    )


TILES = shape(3, BLOCK, WIDE)
ASKS = shape(2 * (ASK_ROWS + KEEP_ROWS), WIDE)
SHARE = shape(DEPTH, WIDE)
LONG_SHARE = shape(DEPTH + ASK_ROWS, WIDE)
SUMS = shape(6, BLOCK, WIDE)
BY = jax.ShapeDtypeStruct((2, DEPTH, 6 * WIDE), BF16)
FACTOR = pltpu.VMEM((WIDE, DEPTH), BF16)


def factors(count):
    return jax.ShapeDtypeStruct((count, WIDE, DEPTH), BF16)


def call_all(kernel, outputs, operands, scratch, name):
    return call(kernel, outputs, [VM] * len(operands), [VM] * len(outputs), scratch, name)(*operands)


def along_col(to_left, to_right):
    return to_left, to_right, shift(to_right, "col", 1), shift(to_left, "col", -1)


def along_row(to_last, to_next):
    return shift(to_next, "row", 1), shift(to_last, "row", -1)


def shards(
    density,
    density_pattern,
    response,
    response_pattern,
    density_next_pattern,
    response_next_pattern,
    density_out_pattern,
    response_out_pattern,
):
    slots = density.shape[3]
    grid = (lax.axis_size("row"), lax.axis_size("col"))
    pattern_scratch = pltpu.SMEM((1, slots), jnp.int32)
    table = pltpu.SMEM((16,), jnp.int32)

    def flat(pattern):
        return stay(pattern.reshape(1, slots))

    def flat_data(data):
        return stay(data.reshape(slots, BLOCK * BLOCK))

    def final_of(pattern, own, parts, earlier):
        scratch = [
            pattern_scratch,
            pltpu.VMEM((6, BLOCK, WIDE), F32),
            pltpu.VMEM((10, HALF, WIDE), F32),
            pltpu.VMEM((slots * HALF, WIDE), F32),
            pltpu.SemaphoreType.DMA((1,)),
        ]
        kernel = functools.partial(final_kernel, grid, slots)
        out = call(kernel, shape(slots, BLOCK * BLOCK), [HB] + [VM] * 5 + [HB], VM, scratch, "final_step")(
            flat(pattern), *own[:2], *parts, stay(earlier)
        )
        return out

    *tiles, ask_next, ask_last, keep = call(
        functools.partial(spread_kernel, grid, slots),
        [TILES] * 4 + [ASKS] * 2 + [shape(2, 8, WIDE)],
        [HB] * 6,
        [VM] * 7,
        [pattern_scratch] * 4
        + [pltpu.VMEM((slots, BLOCK * BLOCK), F32)] * 2
        + [pltpu.VMEM((2, (slots + 1) * HALF, WIDE), F32), table, pltpu.SemaphoreType.DMA((6,))],
        "spread",
    )(
        flat(density_pattern),
        flat(response_pattern),
        flat_data(density),
        flat_data(response),
        flat(density_next_pattern),
        flat(response_next_pattern),
    )

    first = along_col(*tiles[:2])
    asks = along_row(ask_last, ask_next)
    second = along_col(*tiles[2:])
    *first_sent, first_sums, first_by, first_factors = call_all(
        first_step_first_kernel, [LONG_SHARE] * 2 + [SUMS, BY, factors(3)], (*first, *asks), [], "first_share"
    )
    first_got = along_row(*first_sent)
    *second_sent, second_sums = call_all(
        first_step_second_kernel,
        [LONG_SHARE] * 2 + [SUMS],
        (*second, *asks, first_by, first_factors),
        [pltpu.VMEM((2, DEPTH, 6 * WIDE), BF16), FACTOR],
        "second_share",
    )
    second_got = along_row(*second_sent)

    first = along_col(
        *call_all(
            functools.partial(next_kernel, 0), [TILES] * 2, (keep, first_sums, *first_got), [], "first_next"
        )
    )
    second = along_col(
        *call_all(
            functools.partial(next_kernel, 1), [TILES] * 2, (keep, second_sums, *second_got), [], "second_next"
        )
    )
    *first_sent, first_by, first_factors = call_all(
        second_step_first_kernel,
        [SHARE] * 2 + [BY, factors(2)],
        (*first, *asks, *first_got, *first_sent),
        [],
        "first_share",
    )
    first_got = along_row(*first_sent)
    *second_sent, second_by = call_all(
        second_step_second_kernel,
        [SHARE] * 2 + [BY],
        (*second, *asks, *second_got, *second_sent, first_by, first_factors),
        [FACTOR],
        "second_share",
    )
    second_got = along_row(*second_sent)
    (first_sums,) = call_all(first_own_kernel, [SUMS], (*first[:2], first_by), [FACTOR], "first_own")
    (second_sums,) = call_all(
        second_own_kernel, [SUMS], (*first[:2], *second[:2], first_by, second_by), [FACTOR], "second_own"
    )
    first_parts, second_parts = (first_sums, *first_got), (second_sums, *second_got)
    first_out = final_of(density_out_pattern, first, first_parts, flat_data(density))
    second_out = final_of(response_out_pattern, second, second_parts, first_out)
    return first_out.reshape(density.shape), second_out.reshape(density.shape)


def solution(mesh):
    data = P(("groups", "row"), "col", None, None, None)
    pattern = P(("groups", "row"), "col", None, None)
    return jax.shard_map(
        shards,
        mesh=mesh,
        in_specs=(data, pattern, data, pattern, pattern, pattern, pattern, pattern),
        out_specs=(data, data),
        check_vma=False,
    )
```

time: 45.9 us -> 41.6 us (0.906)
  waiting for transfers between devices: 24.5 us -> 10.9 us
  starting transfers between devices: 13.7 us -> 21.6 us
  Pallas kernels: 6.84 us -> 8.18 us
    ppermute x12 -> x18, waiting for transfers between devices: 24.5 us -> 10.9 us  [shift(): lax.ppermute(block, axis, [(i, (i + by) % count) for i in range(count)])]
    ppermute x12 -> x18, starting transfers between devices: 13.7 us -> 21.6 us  [shift(): lax.ppermute(block, axis, [(i, (i + by) % count) for i in range(count)])]
    pallas_call x7 -> x11, Pallas kernels: 6.84 us -> 8.18 us  [the longest x8 3.51 us: call_all(): call(kernel, outputs, [VM] * len(operands), [VM] * len(outputs), scratch,...]
  transfers between devices with their start and end apart: 12 -> 18, of which waited for: 10 -> 7; matrix products, arithmetic and copies ran while one was open for 0% -> 0% of each run, Pallas kernels for 3% -> 12%
where the time goes in v3:
time: 41.6 us; the launch traced here: 41.4 us
  starting transfers between devices  21.6 us (52%)
  waiting for transfers between devices  10.9 us (26%)
  Pallas kernels  8.18 us (20%)
  between operations  0.74 us (2%)
    ppermute x18, starting transfers between devices, shift(): lax.ppermute(block, axis, [(i, (i + by) % count) for i in range(count)])  21.6 us
    ppermute x18, waiting for transfers between devices, shift(): lax.ppermute(block, axis, [(i, (i + by) % count) for i in range(count)])  10.9 us
    pallas_call x8, Pallas kernels, call_all(): call(kernel, outputs, [VM] * len(operands), [VM] * len(outputs), scratch,...  3.51 us
    pallas_call x2, Pallas kernels, final_of(): call(kernel, shape(slots, BLOCK * BLOCK), [HB] + [VM] * 5 + [HB], VM, scr...  3.05 us
    pallas_call x1, Pallas kernels, shards(): call(functools.partial(spread_kernel, grid, slots), [TILES] * 4 + [ASKS]...  1.61 us
  transfers between devices with their start and end apart: 18, of which 7 were waited for; matrix products, arithmetic and copies ran while one was open for 0% of the time, Pallas kernels for 12%

profile of v3, /device:TPU:1, one launch (start us, length us, event | category | flops | bytes accessed | tf_op | source)
XLA Modules:
  0.0 41.4 jit_solution(7676140179606902542)
XLA Ops:
  0.6 1.6 %spread.1 = (f32[3,64,128]{2,1,0:T(8,128)S(1)}, f32[3,64,128]{2,1,0:T(8,128)S(1)}, f32[3,64,128]{2,1,0:T(8,128)S(1)}, f32[3,64,128]{2,1,0:T(8,128)S(1)}, f32[208...) custom-call(s32[1,8]{1,0:T(1,128)} %bitcast.15, s32[1,8]{1,0:T(1,128)} %bitcast.16, ...), custom_call_target="tpu_custom_call" | custom-call | bytes 1000000 | tf_op jit(solution)/shard_map/spread/pallas_call | solution.py:389
  2.3 4.2 %collective-permute-start.1 = (f32[3,64,128]{2,1,0:T(8,128)S(1)}, f32[3,64,128]{2,1,0:T(8,128)S(1)}, u32[]{:S(2)}, u32[]{:S(2)}) collective-permute-start(f32[3,64,128]{2,1,0:T(8,128)S(1)} %get-tuple-element.29.own_left), channel_id=1, source_target_pairs={{0,3},{1,0},{2,1},{3,2},{4,7},{5,4},{6,5},{7,6},{8,11},{9,8},{10,9... | collective-permute-start | bytes 294920 | tf_op jit(solution)/shard_map/ppermute | solution.py:300
  6.5 2.1 %collective-permute-start.2 = (f32[208,128]{1,0:T(8,128)S(1)}, f32[208,128]{1,0:T(8,128)S(1)}, u32[]{:S(2)}, u32[]{:S(2)}) collective-permute-start(f32[208,128]{1,0:T(8,128)S(1)} %get-tuple-element.31), channel_id=1, source_target_pairs={{0,4},{4,8},{8,12},{12,0},{1,5},{5,9},{9,13},{13,1},{2,6},{6,10},{... | collective-permute-start | bytes 319496 | tf_op jit(solution)/shard_map/ppermute | solution.py:300
  8.5 0.0 collective-permute-start.3
  8.5 0.0 collective-permute-start
  8.5 3.3 %collective-permute-start.11 = (f32[3,64,128]{2,1,0:T(8,128)S(1)}, f32[3,64,128]{2,1,0:T(8,128)S(1)}, u32[]{:S(2)}, u32[]{:S(2)}) collective-permute-start(f32[3,64,128]{2,1,0:T(8,128)S(1)} %get-tuple-element.41.own_left), channel_id=1, source_target_pairs={{0,3},{1,0},{2,1},{3,2},{4,7},{5,4},{6,5},{7,6},{8,11},{9,8},{10,9... | collective-permute-start | bytes 294920 | tf_op jit(solution)/shard_map/ppermute | solution.py:300
  11.8 0.0 collective-permute-done.1.from_right
  11.8 0.0 collective-permute-start.10
  11.8 2.1 %collective-permute-done.from_left = f32[3,64,128]{2,1,0:T(8,128)S(1)} collective-permute-done((f32[3,64,128]{2,1,0:T(8,128)S(1)}, f32[3,64,128]{2,1,0:T(8,128)S(1)}, u32[]{:S(2)}, u32[]{:S(2)}) %collective-permute-start) | collective-permute-done | bytes 98336 | tf_op jit(solution)/shard_map/ppermute | solution.py:300
  13.9 0.0 collective-permute-done.2.from_last.refs_0_
  13.9 0.0 collective-permute-done.3.from_next.refs_1_
  13.9 0.5 %first_share.2 = (f32[288,128]{1,0:T(8,128)S(1)}, f32[288,128]{1,0:T(8,128)S(1)}, f32[6,64,128]{2,1,0:T(8,128)S(1)}, bf16[2,192,768]{2,1,0:T(8,128)(2,1)S(1)}, bf16[3,128,192]{2,1,0:T(8,128)(2,1)S(1)}) custom-call(f32[3,64,128]{2,1,0:T(8,128)S(1)} %get-tuple-element.29.own_left, f32[3,64,128]{2,1,0:T(8,128)S(1)} %get-tuple-element.30.own_right, ...), custom_call_target="tpu_custom_call" | custom-call | bytes 1000000 | tf_op jit(solution)/shard_map/first_share/pallas_call | solution.py:343
  14.4 3.0 %collective-permute-start.4 = (f32[288,128]{1,0:T(8,128)S(1)}, f32[288,128]{1,0:T(8,128)S(1)}, u32[]{:S(2)}, u32[]{:S(2)}) collective-permute-start(f32[288,128]{1,0:T(8,128)S(1)} %get-tuple-element.34.refs_5_), channel_id=1, source_target_pairs={{0,4},{4,8},{8,12},{12,0},{1,5},{5,9},{9,13},{13,1},{2,6},{6,10},{... | collective-permute-start | bytes 442376 | tf_op jit(solution)/shard_map/ppermute | solution.py:300
  17.4 0.0 collective-permute-start.5
  17.4 0.0 collective-permute-done.11.from_right
  17.4 1.1 %collective-permute-done.10.from_left = f32[3,64,128]{2,1,0:T(8,128)S(1)} collective-permute-done((f32[3,64,128]{2,1,0:T(8,128)S(1)}, f32[3,64,128]{2,1,0:T(8,128)S(1)}, u32[]{:S(2)}, u32[]{:S(2)}) %collective-permute-start.10) | collective-permute-done | bytes 98336 | tf_op jit(solution)/shard_map/ppermute | solution.py:300
  18.5 0.7 %second_share.2 = (f32[288,128]{1,0:T(8,128)S(1)}, f32[288,128]{1,0:T(8,128)S(1)}, f32[6,64,128]{2,1,0:T(8,128)S(1)}) custom-call(f32[3,64,128]{2,1,0:T(8,128)S(1)} %get-tuple-element.41.own_left, f32[3,64,128]{2,1,0:T(8,128)S(1)} %get-tuple-element.42.own_right, f32[3,64,128]{2,1,0:T(8,128)S(1)} %collective-permute-done.10.from_left, ...), custom_call_target="tpu_custom_call" | custom-call | bytes 1000000 | tf_op jit(solution)/shard_map/second_share/pallas_call | solution.py:343
  19.2 2.1 %collective-permute-start.12 = (f32[288,128]{1,0:T(8,128)S(1)}, f32[288,128]{1,0:T(8,128)S(1)}, u32[]{:S(2)}, u32[]{:S(2)}) collective-permute-start(f32[288,128]{1,0:T(8,128)S(1)} %get-tuple-element.46.refs_5_), channel_id=1, source_target_pairs={{0,4},{4,8},{8,12},{12,0},{1,5},{5,9},{9,13},{13,1},{2,6},{6,10},{... | collective-permute-start | bytes 442376 | tf_op jit(solution)/shard_map/ppermute | solution.py:300
  21.3 0.0 collective-permute-start.13
  21.3 0.0 collective-permute-done.4.from_last.refs_2_
  21.3 1.3 %collective-permute-done.5.from_next.refs_3_ = f32[288,128]{1,0:T(8,128)S(1)} collective-permute-done((f32[288,128]{1,0:T(8,128)S(1)}, f32[288,128]{1,0:T(8,128)S(1)}, u32[]{:S(2)}, u32[]{:S(2)}) %collective-permute-start.5) | collective-permute-done | bytes 147488 | tf_op jit(solution)/shard_map/ppermute | solution.py:300
  22.6 0.1 first_next.1
  22.7 0.2 collective-permute-start.7
  22.9 1.3 %collective-permute-start.6 = (f32[3,64,128]{2,1,0:T(8,128)S(1)}, f32[3,64,128]{2,1,0:T(8,128)S(1)}, u32[]{:S(2)}, u32[]{:S(2)}) collective-permute-start(f32[3,64,128]{2,1,0:T(8,128)S(1)} %get-tuple-element.37.own_right.first_right), channel_id=1, source_target_pairs={{0,1},{1,2},{2,3},{3,0},{4,5},{5,6},{6,7},{7,4},{8,9},{9,10},{10,1... | collective-permute-start | bytes 294920 | tf_op jit(solution)/shard_map/ppermute | solution.py:300
  24.2 0.0 collective-permute-done.12.from_last.refs_2_
  24.2 2.0 %collective-permute-done.13.from_next.refs_3_ = f32[288,128]{1,0:T(8,128)S(1)} collective-permute-done((f32[288,128]{1,0:T(8,128)S(1)}, f32[288,128]{1,0:T(8,128)S(1)}, u32[]{:S(2)}, u32[]{:S(2)}) %collective-permute-start.13) | collective-permute-done | bytes 147488 | tf_op jit(solution)/shard_map/ppermute | solution.py:300
  26.3 0.1 second_next.1
  26.4 0.8 %collective-permute-start.15 = (f32[3,64,128]{2,1,0:T(8,128)S(1)}, f32[3,64,128]{2,1,0:T(8,128)S(1)}, u32[]{:S(2)}, u32[]{:S(2)}) collective-permute-start(f32[3,64,128]{2,1,0:T(8,128)S(1)} %get-tuple-element.48.own_left), channel_id=1, source_target_pairs={{0,3},{1,0},{2,1},{3,2},{4,7},{5,4},{6,5},{7,6},{8,11},{9,8},{10,9... | collective-permute-start | bytes 294920 | tf_op jit(solution)/shard_map/ppermute | solution.py:300
  27.1 0.8 %collective-permute-start.14 = (f32[3,64,128]{2,1,0:T(8,128)S(1)}, f32[3,64,128]{2,1,0:T(8,128)S(1)}, u32[]{:S(2)}, u32[]{:S(2)}) collective-permute-start(f32[3,64,128]{2,1,0:T(8,128)S(1)} %get-tuple-element.49.own_right), channel_id=1, source_target_pairs={{0,1},{1,2},{2,3},{3,0},{4,5},{5,6},{6,7},{7,4},{8,9},{9,10},{10,1... | collective-permute-start | bytes 294920 | tf_op jit(solution)/shard_map/ppermute | solution.py:300
  27.9 0.0 collective-permute-done.7.from_right
  27.9 1.3 %collective-permute-done.6.from_left = f32[3,64,128]{2,1,0:T(8,128)S(1)} collective-permute-done((f32[3,64,128]{2,1,0:T(8,128)S(1)}, f32[3,64,128]{2,1,0:T(8,128)S(1)}, u32[]{:S(2)}, u32[]{:S(2)}) %collective-permute-start.6) | collective-permute-done | bytes 98336 | tf_op jit(solution)/shard_map/ppermute | solution.py:300
  29.2 0.5 %first_share.3 = (f32[192,128]{1,0:T(8,128)S(1)}, f32[192,128]{1,0:T(8,128)S(1)}, bf16[2,192,768]{2,1,0:T(8,128)(2,1)S(1)}, bf16[2,128,192]{2,1,0:T(8,128)(2,1)S(1)}) custom-call(f32[3,64,128]{2,1,0:T(8,128)S(1)} %get-tuple-element.36.own_left.first_left, f32[3,64,128]{2,1,0:T(8,128)S(1)} %get-tuple-element.37.own_right.first_right, ...), custom_call_target="tpu_custom_call" | custom-call | bytes 1000000 | tf_op jit(solution)/shard_map/first_share/pallas_call | solution.py:343
  29.7 2.6 %collective-permute-start.8 = (f32[192,128]{1,0:T(8,128)S(1)}, f32[192,128]{1,0:T(8,128)S(1)}, u32[]{:S(2)}, u32[]{:S(2)}) collective-permute-start(f32[192,128]{1,0:T(8,128)S(1)} %get-tuple-element.39), channel_id=1, source_target_pairs={{0,4},{4,8},{8,12},{12,0},{1,5},{5,9},{9,13},{13,1},{2,6},{6,10},{... | collective-permute-start | bytes 294920 | tf_op jit(solution)/shard_map/ppermute | solution.py:300
  32.3 0.0 collective-permute-start.9
  32.4 1.6 %collective-permute-done.15.from_right = f32[3,64,128]{2,1,0:T(8,128)S(1)} collective-permute-done((f32[3,64,128]{2,1,0:T(8,128)S(1)}, f32[3,64,128]{2,1,0:T(8,128)S(1)}, u32[]{:S(2)}, u32[]{:S(2)}) %collective-permute-start.15) | collective-permute-done | bytes 98336 | tf_op jit(solution)/shard_map/ppermute | solution.py:300
  33.9 0.0 collective-permute-done.14.from_left
  33.9 0.6 %second_share.3 = (f32[192,128]{1,0:T(8,128)S(1)}, f32[192,128]{1,0:T(8,128)S(1)}, bf16[2,192,768]{2,1,0:T(8,128)(2,1)S(1)}) custom-call(f32[3,64,128]{2,1,0:T(8,128)S(1)} %get-tuple-element.48.own_left, f32[3,64,128]{2,1,0:T(8,128)S(1)} %get-tuple-element.49.own_right, f32[3,64,128]{2,1,0:T(8,128)S(1)} %collective-permute-done.14.from_left, ...), custom_call_target="tpu_custom_call" | custom-call | bytes 1000000 | tf_op jit(solution)/shard_map/second_share/pallas_call | solution.py:343
  34.5 1.3 %collective-permute-start.16 = (f32[192,128]{1,0:T(8,128)S(1)}, f32[192,128]{1,0:T(8,128)S(1)}, u32[]{:S(2)}, u32[]{:S(2)}) collective-permute-start(f32[192,128]{1,0:T(8,128)S(1)} %get-tuple-element.52), channel_id=1, source_target_pairs={{0,4},{4,8},{8,12},{12,0},{1,5},{5,9},{9,13},{13,1},{2,6},{6,10},{... | collective-permute-start | bytes 294920 | tf_op jit(solution)/shard_map/ppermute | solution.py:300
  35.8 0.0 collective-permute-start.17
  35.8 0.4 %first_own.1.sums = f32[6,64,128]{2,1,0:T(8,128)S(1)} custom-call(f32[3,64,128]{2,1,0:T(8,128)S(1)} %get-tuple-element.36.own_left.first_left, f32[3,64,128]{2,1,0:T(8,128)S(1)} %get-tuple-element.37.own_right.first_right, bf16[2,192,768]{2,1,0:T(8,128)(2,1)S(1)} %get-tuple-element.38.by.refs_6_.first_by), custom_call_target="tpu_custom_call" | custom-call | bytes 1000000 | tf_op jit(solution)/shard_map/first_own/pallas_call | solution.py:343
  36.3 0.5 %second_own.1.sums = f32[6,64,128]{2,1,0:T(8,128)S(1)} custom-call(f32[3,64,128]{2,1,0:T(8,128)S(1)} %get-tuple-element.36.own_left.first_left, f32[3,64,128]{2,1,0:T(8,128)S(1)} %get-tuple-element.37.own_right.first_right, f32[3,64,128]{2,1,0:T(8,128)S(1)} %get-tuple-element.48.own_left, f32[3,64,128]{2,1,0:T(8,128)S(1)} %get-tuple-element.49.own_right, ...), custom_call_target="tpu_custom_call" | custom-call | bytes 1000000 | tf_op jit(solution)/shard_map/second_own/pallas_call | solution.py:343
  36.8 0.0 collective-permute-done.8.from_last
  36.8 0.0 collective-permute-done.9.from_next
  36.8 1.5 %final_step.2._ = f32[8,4096]{1,0:T(8,128)} custom-call(s32[1,8]{1,0:T(1,128)} %bitcast.19, f32[3,64,128]{2,1,0:T(8,128)S(1)} %get-tuple-element.36.own_left.first_left, f32[3,64,128]{2,1,0:T(8,128)S(1)} %get-tuple-element.37.own_right.first_right, f32[6,64,128]{2,1,0:T(8,128)S(1)} %first_own.1.sums, f32[192,128]{1,0:T(8,128)S(1)} %collective-permute-done.8.from_last, ...), custom_call_target="tpu_custom_call" | custom-call | bytes 1000000 | tf_op jit(solution)/shard_map/final_step/pallas_call | solution.py:384
  38.4 0.0 collective-permute-done.16.from_last
  38.4 1.5 %collective-permute-done.17.from_next = f32[192,128]{1,0:T(8,128)S(1)} collective-permute-done((f32[192,128]{1,0:T(8,128)S(1)}, f32[192,128]{1,0:T(8,128)S(1)}, u32[]{:S(2)}, u32[]{:S(2)}) %collective-permute-start.17) | collective-permute-done | bytes 98336 | tf_op jit(solution)/shard_map/ppermute | solution.py:300
  39.9 1.5 %final_step.3 = f32[8,4096]{1,0:T(8,128)} custom-call(s32[1,8]{1,0:T(1,128)} %bitcast.20, f32[3,64,128]{2,1,0:T(8,128)S(1)} %get-tuple-element.48.own_left, f32[3,64,128]{2,1,0:T(8,128)S(1)} %get-tuple-element.49.own_right, f32[6,64,128]{2,1,0:T(8,128)S(1)} %second_own.1.sums, f32[192,128]{1,0:T(8,128)S(1)} %collective-permute-done.16.from_last, ...), custom_call_target="tpu_custom_call" | custom-call | bytes 1000000 | tf_op jit(solution)/shard_map/final_step/pallas_call | solution.py:384
Async XLA Ops:
  2.3 9.5 %collective-permute-start.1 = (f32[3,64,128]{2,1,0:T(8,128)S(1)}, f32[3,64,128]{2,1,0:T(8,128)S(1)}, u32[]{:S(2)}, u32[]{:S(2)}) collective-permute-start(f32[3,64,128]{2,1,0:T(8,128)S(1)} %get-tuple-element.29.own_left), channel_id=1, source_target_pairs={{0,3},{1,0},{2,1},{3,2},{4,7},{5,4},{6,5},{7,6},{8,11},{9,8},{10,9... | collective-permute-start | bytes 294920 | tf_op jit(solution)/shard_map/ppermute | solution.py:300
  6.5 7.4 %collective-permute-start.2 = (f32[208,128]{1,0:T(8,128)S(1)}, f32[208,128]{1,0:T(8,128)S(1)}, u32[]{:S(2)}, u32[]{:S(2)}) collective-permute-start(f32[208,128]{1,0:T(8,128)S(1)} %get-tuple-element.31), channel_id=1, source_target_pairs={{0,4},{4,8},{8,12},{12,0},{1,5},{5,9},{9,13},{13,1},{2,6},{6,10},{... | collective-permute-start | bytes 319496 | tf_op jit(solution)/shard_map/ppermute | solution.py:300
  8.5 5.4 %collective-permute-start.3 = (f32[208,128]{1,0:T(8,128)S(1)}, f32[208,128]{1,0:T(8,128)S(1)}, u32[]{:S(2)}, u32[]{:S(2)}) collective-permute-start(f32[208,128]{1,0:T(8,128)S(1)} %get-tuple-element.32), channel_id=1, source_target_pairs={{0,12},{4,0},{8,4},{12,8},{1,13},{5,1},{9,5},{13,9},{2,14},{6,2},{... | collective-permute-start | bytes 319496 | tf_op jit(solution)/shard_map/ppermute | solution.py:300
  8.5 5.4 %collective-permute-start = (f32[3,64,128]{2,1,0:T(8,128)S(1)}, f32[3,64,128]{2,1,0:T(8,128)S(1)}, u32[]{:S(2)}, u32[]{:S(2)}) collective-permute-start(f32[3,64,128]{2,1,0:T(8,128)S(1)} %get-tuple-element.30.own_right), channel_id=1, source_target_pairs={{0,1},{1,2},{2,3},{3,0},{4,5},{5,6},{6,7},{7,4},{8,9},{9,10},{10,1... | collective-permute-start | bytes 294920 | tf_op jit(solution)/shard_map/ppermute | solution.py:300
  8.5 8.9 %collective-permute-start.11 = (f32[3,64,128]{2,1,0:T(8,128)S(1)}, f32[3,64,128]{2,1,0:T(8,128)S(1)}, u32[]{:S(2)}, u32[]{:S(2)}) collective-permute-start(f32[3,64,128]{2,1,0:T(8,128)S(1)} %get-tuple-element.41.own_left), channel_id=1, source_target_pairs={{0,3},{1,0},{2,1},{3,2},{4,7},{5,4},{6,5},{7,6},{8,11},{9,8},{10,9... | collective-permute-start | bytes 294920 | tf_op jit(solution)/shard_map/ppermute | solution.py:300
  11.8 6.7 %collective-permute-start.10 = (f32[3,64,128]{2,1,0:T(8,128)S(1)}, f32[3,64,128]{2,1,0:T(8,128)S(1)}, u32[]{:S(2)}, u32[]{:S(2)}) collective-permute-start(f32[3,64,128]{2,1,0:T(8,128)S(1)} %get-tuple-element.42.own_right), channel_id=1, source_target_pairs={{0,1},{1,2},{2,3},{3,0},{4,5},{5,6},{6,7},{7,4},{8,9},{9,10},{10,1... | collective-permute-start | bytes 294920 | tf_op jit(solution)/shard_map/ppermute | solution.py:300
  14.4 6.9 %collective-permute-start.4 = (f32[288,128]{1,0:T(8,128)S(1)}, f32[288,128]{1,0:T(8,128)S(1)}, u32[]{:S(2)}, u32[]{:S(2)}) collective-permute-start(f32[288,128]{1,0:T(8,128)S(1)} %get-tuple-element.34.refs_5_), channel_id=1, source_target_pairs={{0,4},{4,8},{8,12},{12,0},{1,5},{5,9},{9,13},{13,1},{2,6},{6,10},{... | collective-permute-start | bytes 442376 | tf_op jit(solution)/shard_map/ppermute | solution.py:300
  17.4 5.2 %collective-permute-start.5 = (f32[288,128]{1,0:T(8,128)S(1)}, f32[288,128]{1,0:T(8,128)S(1)}, u32[]{:S(2)}, u32[]{:S(2)}) collective-permute-start(f32[288,128]{1,0:T(8,128)S(1)} %get-tuple-element.35.refs_4_), channel_id=1, source_target_pairs={{0,12},{4,0},{8,4},{12,8},{1,13},{5,1},{9,5},{13,9},{2,14},{6,2},{... | collective-permute-start | bytes 442376 | tf_op jit(solution)/shard_map/ppermute | solution.py:300
  19.2 5.1 %collective-permute-start.12 = (f32[288,128]{1,0:T(8,128)S(1)}, f32[288,128]{1,0:T(8,128)S(1)}, u32[]{:S(2)}, u32[]{:S(2)}) collective-permute-start(f32[288,128]{1,0:T(8,128)S(1)} %get-tuple-element.46.refs_5_), channel_id=1, source_target_pairs={{0,4},{4,8},{8,12},{12,0},{1,5},{5,9},{9,13},{13,1},{2,6},{6,10},{... | collective-permute-start | bytes 442376 | tf_op jit(solution)/shard_map/ppermute | solution.py:300
  21.3 5.0 %collective-permute-start.13 = (f32[288,128]{1,0:T(8,128)S(1)}, f32[288,128]{1,0:T(8,128)S(1)}, u32[]{:S(2)}, u32[]{:S(2)}) collective-permute-start(f32[288,128]{1,0:T(8,128)S(1)} %get-tuple-element.47.refs_4_), channel_id=1, source_target_pairs={{0,12},{4,0},{8,4},{12,8},{1,13},{5,1},{9,5},{13,9},{2,14},{6,2},{... | collective-permute-start | bytes 442376 | tf_op jit(solution)/shard_map/ppermute | solution.py:300
  22.7 5.2 %collective-permute-start.7 = (f32[3,64,128]{2,1,0:T(8,128)S(1)}, f32[3,64,128]{2,1,0:T(8,128)S(1)}, u32[]{:S(2)}, u32[]{:S(2)}) collective-permute-start(f32[3,64,128]{2,1,0:T(8,128)S(1)} %get-tuple-element.36.own_left.first_left), channel_id=1, source_target_pairs={{0,3},{1,0},{2,1},{3,2},{4,7},{5,4},{6,5},{7,6},{8,11},{9,8},{10,9... | collective-permute-start | bytes 294920 | tf_op jit(solution)/shard_map/ppermute | solution.py:300
  22.9 6.3 %collective-permute-start.6 = (f32[3,64,128]{2,1,0:T(8,128)S(1)}, f32[3,64,128]{2,1,0:T(8,128)S(1)}, u32[]{:S(2)}, u32[]{:S(2)}) collective-permute-start(f32[3,64,128]{2,1,0:T(8,128)S(1)} %get-tuple-element.37.own_right.first_right), channel_id=1, source_target_pairs={{0,1},{1,2},{2,3},{3,0},{4,5},{5,6},{6,7},{7,4},{8,9},{9,10},{10,1... | collective-permute-start | bytes 294920 | tf_op jit(solution)/shard_map/ppermute | solution.py:300
  26.4 7.5 %collective-permute-start.15 = (f32[3,64,128]{2,1,0:T(8,128)S(1)}, f32[3,64,128]{2,1,0:T(8,128)S(1)}, u32[]{:S(2)}, u32[]{:S(2)}) collective-permute-start(f32[3,64,128]{2,1,0:T(8,128)S(1)} %get-tuple-element.48.own_left), channel_id=1, source_target_pairs={{0,3},{1,0},{2,1},{3,2},{4,7},{5,4},{6,5},{7,6},{8,11},{9,8},{10,9... | collective-permute-start | bytes 294920 | tf_op jit(solution)/shard_map/ppermute | solution.py:300
  27.1 6.8 %collective-permute-start.14 = (f32[3,64,128]{2,1,0:T(8,128)S(1)}, f32[3,64,128]{2,1,0:T(8,128)S(1)}, u32[]{:S(2)}, u32[]{:S(2)}) collective-permute-start(f32[3,64,128]{2,1,0:T(8,128)S(1)} %get-tuple-element.49.own_right), channel_id=1, source_target_pairs={{0,1},{1,2},{2,3},{3,0},{4,5},{5,6},{6,7},{7,4},{8,9},{9,10},{10,1... | collective-permute-start | bytes 294920 | tf_op jit(solution)/shard_map/ppermute | solution.py:300
  29.7 7.1 %collective-permute-start.8 = (f32[192,128]{1,0:T(8,128)S(1)}, f32[192,128]{1,0:T(8,128)S(1)}, u32[]{:S(2)}, u32[]{:S(2)}) collective-permute-start(f32[192,128]{1,0:T(8,128)S(1)} %get-tuple-element.39), channel_id=1, source_target_pairs={{0,4},{4,8},{8,12},{12,0},{1,5},{5,9},{9,13},{13,1},{2,6},{6,10},{... | collective-permute-start | bytes 294920 | tf_op jit(solution)/shard_map/ppermute | solution.py:300
  32.3 4.5 %collective-permute-start.9 = (f32[192,128]{1,0:T(8,128)S(1)}, f32[192,128]{1,0:T(8,128)S(1)}, u32[]{:S(2)}, u32[]{:S(2)}) collective-permute-start(f32[192,128]{1,0:T(8,128)S(1)} %get-tuple-element.40), channel_id=1, source_target_pairs={{0,12},{4,0},{8,4},{12,8},{1,13},{5,1},{9,5},{13,9},{2,14},{6,2},{... | collective-permute-start | bytes 294920 | tf_op jit(solution)/shard_map/ppermute | solution.py:300
  34.5 3.8 %collective-permute-start.16 = (f32[192,128]{1,0:T(8,128)S(1)}, f32[192,128]{1,0:T(8,128)S(1)}, u32[]{:S(2)}, u32[]{:S(2)}) collective-permute-start(f32[192,128]{1,0:T(8,128)S(1)} %get-tuple-element.52), channel_id=1, source_target_pairs={{0,4},{4,8},{8,12},{12,0},{1,5},{5,9},{9,13},{13,1},{2,6},{6,10},{... | collective-permute-start | bytes 294920 | tf_op jit(solution)/shard_map/ppermute | solution.py:300
  35.8 4.0 %collective-permute-start.17 = (f32[192,128]{1,0:T(8,128)S(1)}, f32[192,128]{1,0:T(8,128)S(1)}, u32[]{:S(2)}, u32[]{:S(2)}) collective-permute-start(f32[192,128]{1,0:T(8,128)S(1)} %get-tuple-element.53), channel_id=1, source_target_pairs={{0,12},{4,0},{8,4},{12,8},{1,13},{5,1},{9,5},{13,9},{2,14},{6,2},{... | collective-permute-start | bytes 294920 | tf_op jit(solution)/shard_map/ppermute | solution.py:300

commit v4 on v3

--- a/solution.py
+++ b/solution.py
@@ -13,6 +13,7 @@
 DEPTH = 3 * BLOCK
 ASK_ROWS = BLOCK + HALF
 KEEP_ROWS = 8
+PADS = (8, 0, 0, 0, 8, 16, 0, 8)
 F32 = jnp.float32
 BF16 = jnp.bfloat16
 VMEM_LIMIT = 16 * 1024 * 1024
@@ -55,6 +56,10 @@
             keep[which, 3 * side + e : 3 * side + e + 1, :] = jnp.where(first, table[low], table[low + 1]).astype(F32)
 
 
+def tile_at(e):
+    return slice(e * BLOCK, (e + 1) * BLOCK)
+
+
 def fetch(sources, targets, sems):
     copies = [pltpu.make_async_copy(s, t, sems.at[i]) for i, (s, t) in enumerate(zip(sources, targets))]
     for copy in copies:
@@ -62,9 +67,13 @@
     return copies
 
 
+def fill_rest(message):
+    if message.shape[0] > DEPTH:
+        message[DEPTH:, :] = jnp.zeros((message.shape[0] - DEPTH, WIDE), F32)
+
+
 def spread(slots, grid, pattern, data, to_left, to_right, rows, table, copies):
     first_half = on_left(HALF)
-    even, odd = pl.ds(0, HALF, stride=2), pl.ds(1, HALF, stride=2)
     copies[0].wait()
     note_slots(pattern, table, grid, slots)
     rows[slots * HALF : (slots + 1) * HALF, :] = jnp.zeros((HALF, WIDE), F32)
@@ -82,9 +91,11 @@
     for e in range(3):
         a, b, c = block(3 * e), block(3 * e + 1), block(3 * e + 2)
         left, right = tile(a, b), tile(b, c)
-        for part, stride in enumerate((even, odd)):
-            to_left[e, stride, :] = left[part]
-            to_right[e, stride, :] = right[part]
+        for part in range(2):
+            to_left[pl.ds(e * BLOCK + part, HALF, stride=2), :] = left[part]
+            to_right[pl.ds(e * BLOCK + part, HALF, stride=2), :] = right[part]
+    fill_rest(to_left)
+    fill_rest(to_right)
 
 
 def spread_kernel(grid, slots, *refs):
@@ -100,8 +111,8 @@
     for which, (left, right) in enumerate(pairs):
         at = which * ASK_ROWS
         for ask, e in ((ask_last, 0), (ask_next, 2)):
-            ask[at : at + BLOCK, :] = left[e]
-            ask[at + BLOCK : at + ASK_ROWS, :] = fold(right[e])
+            ask[at : at + BLOCK, :] = left[tile_at(e)]
+            ask[at + BLOCK : at + ASK_ROWS, :] = fold(right[tile_at(e)])
             masks = 2 * ASK_ROWS + KEEP_ROWS * which
             wide = jnp.broadcast_to(keep[which, 3 + e : 4 + e, BLOCK:], (1, BLOCK))
             ask[masks : masks + 1, :] = keep[which, e : e + 1, :]
@@ -132,9 +143,9 @@
     for e in range(3):
         column = e * 2 * WIDE
         tiles = (
-            (from_left[e], None),
-            (own_left[e], jnp.where(first, 0.0, own_right[e])),
-            (None, from_right[e]),
+            (from_left[tile_at(e)], None),
+            (own_left[tile_at(e)], jnp.where(first, 0.0, own_right[tile_at(e)])),
+            (None, from_right[tile_at(e)]),
         )
         for k, pair in enumerate(tiles):
             for side, tile in enumerate(pair):
@@ -186,7 +197,7 @@
 
 
 def fill_own(left, right, factor):
-    fill_left_factor(left[1], fold(right[1]), factor)
+    fill_left_factor(left[tile_at(1)], fold(right[tile_at(1)]), factor)
 
 
 def first_step_first_kernel(own_left, own_right, from_left, from_right, from_last, from_next, *refs):
@@ -268,8 +279,11 @@
     first = on_left(BLOCK)
     left, right = total(sums, from_last, from_next)
     for e in range(3):
-        to_left[e] = jnp.where(keep[which, e : e + 1, :] > 0, left[e], 0.0)
-        to_right[e] = jnp.where(keep[which, 3 + e : 4 + e, :] > 0, jnp.where(first, swap(left[e]), right[e]), 0.0)
+        to_left[tile_at(e), :] = jnp.where(keep[which, e : e + 1, :] > 0, left[e], 0.0)
+        right_tile = jnp.where(first, swap(left[e]), right[e])
+        to_right[tile_at(e), :] = jnp.where(keep[which, 3 + e : 4 + e, :] > 0, right_tile, 0.0)
+    fill_rest(to_left)
+    fill_rest(to_right)
 
 
 def final_kernel(grid, slots, pattern_hbm, own_left, own_right, sums, from_last, from_next, _, out, *refs):
@@ -279,8 +293,8 @@
     even, odd = pl.ds(0, HALF, stride=2), pl.ds(1, HALF, stride=2)
     left, right = total(sums, from_last, from_next)
     for e in range(3):
-        dense[e] = 2.0 * own_left[e] - left[e]
-        dense[3 + e] = 2.0 * own_right[e] - right[e]
+        dense[e] = 2.0 * own_left[tile_at(e)] - left[e]
+        dense[3 + e] = 2.0 * own_right[tile_at(e)] - right[e]
     for e in range(3):
         a, b = dense[e, even, :], dense[e, odd, :]
         packed[3 * e] = jnp.where(first_half, a, swap(b))
@@ -326,7 +340,10 @@
     )
 
 
-TILES = shape(3, BLOCK, WIDE)
+def tiles_shape(rest):
+    return shape(DEPTH + rest, WIDE)
+
+
 ASKS = shape(2 * (ASK_ROWS + KEEP_ROWS), WIDE)
 SHARE = shape(DEPTH, WIDE)
 LONG_SHARE = shape(DEPTH + ASK_ROWS, WIDE)
@@ -388,7 +405,7 @@
 
     *tiles, ask_next, ask_last, keep = call(
         functools.partial(spread_kernel, grid, slots),
-        [TILES] * 4 + [ASKS] * 2 + [shape(2, 8, WIDE)],
+        [tiles_shape(r) for r in PADS[:4]] + [ASKS] * 2 + [shape(2, 8, WIDE)],
         [HB] * 6,
         [VM] * 7,
         [pattern_scratch] * 4
@@ -422,12 +439,12 @@
 
     first = along_col(
         *call_all(
-            functools.partial(next_kernel, 0), [TILES] * 2, (keep, first_sums, *first_got), [], "first_next"
+            functools.partial(next_kernel, 0), [tiles_shape(r) for r in PADS[4:6]], (keep, first_sums, *first_got), [], "first_next"
         )
     )
     second = along_col(
         *call_all(
-            functools.partial(next_kernel, 1), [TILES] * 2, (keep, second_sums, *second_got), [], "second_next"
+            functools.partial(next_kernel, 1), [tiles_shape(r) for r in PADS[6:8]], (keep, second_sums, *second_got), [], "second_next"
         )
     )
     *first_sent, first_by, first_factors = call_all(

time: 41.6 us -> 39.9 us (0.959)
  waiting for transfers between devices: 10.9 us -> 8.33 us
  starting transfers between devices: 21.6 us -> 22.5 us
    ppermute x18, waiting for transfers between devices: 10.9 us -> 8.33 us  [shift(): lax.ppermute(block, axis, [(i, (i + by) % count) for i in range(count)])]
    ppermute x18, starting transfers between devices: 21.6 us -> 22.5 us  [shift(): lax.ppermute(block, axis, [(i, (i + by) % count) for i in range(count)])]
  transfers between devices with their start and end apart: 18 -> 18, of which waited for: 7 -> 5; matrix products, arithmetic and copies ran while one was open for 0% -> 0% of each run, Pallas kernels for 12% -> 13%
where the time goes in v4:
time: 39.9 us; the launch traced here: 39.8 us
  starting transfers between devices  22.5 us (56%)
  waiting for transfers between devices  8.33 us (21%)
  Pallas kernels  8.21 us (21%)
  between operations  0.75 us (2%)
    ppermute x18, starting transfers between devices, shift(): lax.ppermute(block, axis, [(i, (i + by) % count) for i in range(count)])  22.5 us
    ppermute x18, waiting for transfers between devices, shift(): lax.ppermute(block, axis, [(i, (i + by) % count) for i in range(count)])  8.33 us
    pallas_call x8, Pallas kernels, call_all(): call(kernel, outputs, [VM] * len(operands), [VM] * len(outputs), scratch,...  3.54 us
    pallas_call x2, Pallas kernels, final_of(): call(kernel, shape(slots, BLOCK * BLOCK), [HB] + [VM] * 5 + [HB], VM, scr...  3.06 us
    pallas_call x1, Pallas kernels, shards(): call(functools.partial(spread_kernel, grid, slots), [tiles_shape(r) for r...  1.61 us
  transfers between devices with their start and end apart: 18, of which 5 were waited for; matrix products, arithmetic and copies ran while one was open for 0% of the time, Pallas kernels for 13%

profile of v4, /device:TPU:1, one launch (start us, length us, event | category | flops | bytes accessed | tf_op | source)
XLA Modules:
  0.0 39.8 jit_solution(7562147482552658643)
XLA Ops:
  0.6 1.6 %spread.1 = (f32[200,128]{1,0:T(8,128)S(1)}, f32[192,128]{1,0:T(8,128)S(1)}, f32[192,128]{1,0:T(8,128)S(1)}, f32[192,128]{1,0:T(8,128)S(1)}, f32[208,128]{1,0:T(...) custom-call(s32[1,8]{1,0:T(1,128)} %bitcast.15, s32[1,8]{1,0:T(1,128)} %bitcast.16, f32[8,4096]{1,0:T(8,128)} %bitcast.10, ...), custom_call_target="tpu_custom_call" | custom-call | bytes 1000000 | tf_op jit(solution)/shard_map/spread/pallas_call | solution.py:406
  2.3 2.2 %collective-permute-start = (f32[192,128]{1,0:T(8,128)S(1)}, f32[192,128]{1,0:T(8,128)S(1)}, u32[]{:S(2)}, u32[]{:S(2)}) collective-permute-start(f32[192,128]{1,0:T(8,128)S(1)} %get-tuple-element.30.own_right), channel_id=1, source_target_pairs={{0,1},{1,2},{2,3},{3,0},{4,5},{5,6},{6,7},{7,4},{8,9},{9,10},{10,1... | collective-permute-start | bytes 294920 | tf_op jit(solution)/shard_map/ppermute | solution.py:314
  4.4 2.1 %collective-permute-start.2 = (f32[208,128]{1,0:T(8,128)S(1)}, f32[208,128]{1,0:T(8,128)S(1)}, u32[]{:S(2)}, u32[]{:S(2)}) collective-permute-start(f32[208,128]{1,0:T(8,128)S(1)} %get-tuple-element.31), channel_id=1, source_target_pairs={{0,4},{4,8},{8,12},{12,0},{1,5},{5,9},{9,13},{13,1},{2,6},{6,10},{... | collective-permute-start | bytes 319496 | tf_op jit(solution)/shard_map/ppermute | solution.py:314
  6.5 0.0 collective-permute-start.3
  6.5 2.0 %collective-permute-start.1 = (f32[200,128]{1,0:T(8,128)S(1)}, f32[200,128]{1,0:T(8,128)S(1)}, u32[]{:S(2)}, u32[]{:S(2)}) collective-permute-start(f32[200,128]{1,0:T(8,128)S(1)} %get-tuple-element.29.own_left), channel_id=1, source_target_pairs={{0,3},{1,0},{2,1},{3,2},{4,7},{5,4},{6,5},{7,6},{8,11},{9,8},{10,9... | collective-permute-start | bytes 307208 | tf_op jit(solution)/shard_map/ppermute | solution.py:314
  8.5 1.5 %collective-permute-start.11 = (f32[192,128]{1,0:T(8,128)S(1)}, f32[192,128]{1,0:T(8,128)S(1)}, u32[]{:S(2)}, u32[]{:S(2)}) collective-permute-start(f32[192,128]{1,0:T(8,128)S(1)} %get-tuple-element.41.own_left), channel_id=1, source_target_pairs={{0,3},{1,0},{2,1},{3,2},{4,7},{5,4},{6,5},{7,6},{8,11},{9,8},{10,9... | collective-permute-start | bytes 294920 | tf_op jit(solution)/shard_map/ppermute | solution.py:314
  10.0 0.0 collective-permute-done.from_left
  10.0 0.0 collective-permute-start.10
  10.0 1.5 %collective-permute-done.1.from_right = f32[200,128]{1,0:T(8,128)S(1)} collective-permute-done((f32[200,128]{1,0:T(8,128)S(1)}, f32[200,128]{1,0:T(8,128)S(1)}, u32[]{:S(2)}, u32[]{:S(2)}) %collective-permute-start.1) | collective-permute-done | bytes 102432 | tf_op jit(solution)/shard_map/ppermute | solution.py:314
  11.5 0.0 collective-permute-done.2.from_last.refs_0_
  11.5 0.0 collective-permute-done.3.from_next.refs_1_
  11.5 0.5 %first_share.2 = (f32[288,128]{1,0:T(8,128)S(1)}, f32[288,128]{1,0:T(8,128)S(1)}, f32[6,64,128]{2,1,0:T(8,128)S(1)}, bf16[2,192,768]{2,1,0:T(8,128)(2,1)S(1)}, bf16[3,128,192]{2,1,0:T(8,128)(2,1)S(1)}) custom-call(f32[200,128]{1,0:T(8,128)S(1)} %get-tuple-element.29.own_left, f32[192,128]{1,0:T(8,128)S(1)} %get-tuple-element.30.own_right, ...), custom_call_target="tpu_custom_call" | custom-call | bytes 1000000 | tf_op jit(solution)/shard_map/first_share/pallas_call | solution.py:360
  12.0 2.6 %collective-permute-start.4 = (f32[288,128]{1,0:T(8,128)S(1)}, f32[288,128]{1,0:T(8,128)S(1)}, u32[]{:S(2)}, u32[]{:S(2)}) collective-permute-start(f32[288,128]{1,0:T(8,128)S(1)} %get-tuple-element.34.refs_5_), channel_id=1, source_target_pairs={{0,4},{4,8},{8,12},{12,0},{1,5},{5,9},{9,13},{13,1},{2,6},{6,10},{... | collective-permute-start | bytes 442376 | tf_op jit(solution)/shard_map/ppermute | solution.py:314
  14.6 0.0 collective-permute-start.5
  14.6 0.0 collective-permute-done.11.from_right
  14.6 2.0 %collective-permute-done.10.from_left = f32[192,128]{1,0:T(8,128)S(1)} collective-permute-done((f32[192,128]{1,0:T(8,128)S(1)}, f32[192,128]{1,0:T(8,128)S(1)}, u32[]{:S(2)}, u32[]{:S(2)}) %collective-permute-start.10) | collective-permute-done | bytes 98336 | tf_op jit(solution)/shard_map/ppermute | solution.py:314
  16.7 0.7 %second_share.2 = (f32[288,128]{1,0:T(8,128)S(1)}, f32[288,128]{1,0:T(8,128)S(1)}, f32[6,64,128]{2,1,0:T(8,128)S(1)}) custom-call(f32[192,128]{1,0:T(8,128)S(1)} %get-tuple-element.41.own_left, f32[192,128]{1,0:T(8,128)S(1)} %get-tuple-element.42.own_right, f32[192,128]{1,0:T(8,128)S(1)} %collective-permute-done.10.from_left, ...), custom_call_target="tpu_custom_call" | custom-call | bytes 1000000 | tf_op jit(solution)/shard_map/second_share/pallas_call | solution.py:360
  17.4 2.1 %collective-permute-start.12 = (f32[288,128]{1,0:T(8,128)S(1)}, f32[288,128]{1,0:T(8,128)S(1)}, u32[]{:S(2)}, u32[]{:S(2)}) collective-permute-start(f32[288,128]{1,0:T(8,128)S(1)} %get-tuple-element.46.refs_5_), channel_id=1, source_target_pairs={{0,4},{4,8},{8,12},{12,0},{1,5},{5,9},{9,13},{13,1},{2,6},{6,10},{... | collective-permute-start | bytes 442376 | tf_op jit(solution)/shard_map/ppermute | solution.py:314
  19.5 0.0 collective-permute-start.13
  19.5 0.0 collective-permute-done.4.from_last.refs_2_
  19.5 0.0 collective-permute-done.5.from_next.refs_3_
  19.5 0.1 first_next.1
  19.6 0.7 %collective-permute-start.6 = (f32[208,128]{1,0:T(8,128)S(1)}, f32[208,128]{1,0:T(8,128)S(1)}, u32[]{:S(2)}, u32[]{:S(2)}) collective-permute-start(f32[208,128]{1,0:T(8,128)S(1)} %get-tuple-element.37.own_right.first_right), channel_id=1, source_target_pairs={{0,1},{1,2},{2,3},{3,0},{4,5},{5,6},{6,7},{7,4},{8,9},{9,10},{10,1... | collective-permute-start | bytes 319496 | tf_op jit(solution)/shard_map/ppermute | solution.py:314
  20.3 2.8 %collective-permute-start.7 = (f32[200,128]{1,0:T(8,128)S(1)}, f32[200,128]{1,0:T(8,128)S(1)}, u32[]{:S(2)}, u32[]{:S(2)}) collective-permute-start(f32[200,128]{1,0:T(8,128)S(1)} %get-tuple-element.36.own_left.first_left), channel_id=1, source_target_pairs={{0,3},{1,0},{2,1},{3,2},{4,7},{5,4},{6,5},{7,6},{8,11},{9,8},{10,9... | collective-permute-start | bytes 307208 | tf_op jit(solution)/shard_map/ppermute | solution.py:314
  23.1 0.0 collective-permute-done.12.from_last.refs_2_
  23.1 1.4 %collective-permute-done.13.from_next.refs_3_ = f32[288,128]{1,0:T(8,128)S(1)} collective-permute-done((f32[288,128]{1,0:T(8,128)S(1)}, f32[288,128]{1,0:T(8,128)S(1)}, u32[]{:S(2)}, u32[]{:S(2)}) %collective-permute-start.13) | collective-permute-done | bytes 147488 | tf_op jit(solution)/shard_map/ppermute | solution.py:314
  24.6 0.1 second_next.1
  24.7 0.1 collective-permute-start.14
  24.7 3.3 %collective-permute-start.15 = (f32[192,128]{1,0:T(8,128)S(1)}, f32[192,128]{1,0:T(8,128)S(1)}, u32[]{:S(2)}, u32[]{:S(2)}) collective-permute-start(f32[192,128]{1,0:T(8,128)S(1)} %get-tuple-element.48.own_left), channel_id=1, source_target_pairs={{0,3},{1,0},{2,1},{3,2},{4,7},{5,4},{6,5},{7,6},{8,11},{9,8},{10,9... | collective-permute-start | bytes 294920 | tf_op jit(solution)/shard_map/ppermute | solution.py:314
  28.0 0.0 collective-permute-done.7.from_right
  28.0 0.0 collective-permute-done.6.from_left
  28.0 0.5 %first_share.3 = (f32[192,128]{1,0:T(8,128)S(1)}, f32[192,128]{1,0:T(8,128)S(1)}, bf16[2,192,768]{2,1,0:T(8,128)(2,1)S(1)}, bf16[2,128,192]{2,1,0:T(8,128)(2,1)S(1)}) custom-call(f32[200,128]{1,0:T(8,128)S(1)} %get-tuple-element.36.own_left.first_left, f32[208,128]{1,0:T(8,128)S(1)} %get-tuple-element.37.own_right.first_right, ...), custom_call_target="tpu_custom_call" | custom-call | bytes 1000000 | tf_op jit(solution)/shard_map/first_share/pallas_call | solution.py:360
  28.5 1.3 %collective-permute-start.8 = (f32[192,128]{1,0:T(8,128)S(1)}, f32[192,128]{1,0:T(8,128)S(1)}, u32[]{:S(2)}, u32[]{:S(2)}) collective-permute-start(f32[192,128]{1,0:T(8,128)S(1)} %get-tuple-element.39), channel_id=1, source_target_pairs={{0,4},{4,8},{8,12},{12,0},{1,5},{5,9},{9,13},{13,1},{2,6},{6,10},{... | collective-permute-start | bytes 294920 | tf_op jit(solution)/shard_map/ppermute | solution.py:314
  29.8 0.0 collective-permute-start.9
  29.8 1.8 %collective-permute-done.15.from_right = f32[192,128]{1,0:T(8,128)S(1)} collective-permute-done((f32[192,128]{1,0:T(8,128)S(1)}, f32[192,128]{1,0:T(8,128)S(1)}, u32[]{:S(2)}, u32[]{:S(2)}) %collective-permute-start.15) | collective-permute-done | bytes 98336 | tf_op jit(solution)/shard_map/ppermute | solution.py:314
  31.6 0.0 collective-permute-done.14.from_left
  31.6 0.6 %second_share.3 = (f32[192,128]{1,0:T(8,128)S(1)}, f32[192,128]{1,0:T(8,128)S(1)}, bf16[2,192,768]{2,1,0:T(8,128)(2,1)S(1)}) custom-call(f32[192,128]{1,0:T(8,128)S(1)} %get-tuple-element.48.own_left, f32[200,128]{1,0:T(8,128)S(1)} %get-tuple-element.49.own_right, f32[200,128]{1,0:T(8,128)S(1)} %collective-permute-done.14.from_left, ...), custom_call_target="tpu_custom_call" | custom-call | bytes 1000000 | tf_op jit(solution)/shard_map/second_share/pallas_call | solution.py:360
  32.3 1.9 %collective-permute-start.16 = (f32[192,128]{1,0:T(8,128)S(1)}, f32[192,128]{1,0:T(8,128)S(1)}, u32[]{:S(2)}, u32[]{:S(2)}) collective-permute-start(f32[192,128]{1,0:T(8,128)S(1)} %get-tuple-element.52), channel_id=1, source_target_pairs={{0,4},{4,8},{8,12},{12,0},{1,5},{5,9},{9,13},{13,1},{2,6},{6,10},{... | collective-permute-start | bytes 294920 | tf_op jit(solution)/shard_map/ppermute | solution.py:314
  34.2 0.0 collective-permute-start.17
  34.2 0.4 %first_own.1.sums = f32[6,64,128]{2,1,0:T(8,128)S(1)} custom-call(f32[200,128]{1,0:T(8,128)S(1)} %get-tuple-element.36.own_left.first_left, f32[208,128]{1,0:T(8,128)S(1)} %get-tuple-element.37.own_right.first_right, bf16[2,192,768]{2,1,0:T(8,128)(2,1)S(1)} %get-tuple-element.38.by.refs_6_.first_by), custom_call_target="tpu_custom_call" | custom-call | bytes 1000000 | tf_op jit(solution)/shard_map/first_own/pallas_call | solution.py:360
  34.6 0.5 %second_own.1.sums = f32[6,64,128]{2,1,0:T(8,128)S(1)} custom-call(f32[200,128]{1,0:T(8,128)S(1)} %get-tuple-element.36.own_left.first_left, f32[208,128]{1,0:T(8,128)S(1)} %get-tuple-element.37.own_right.first_right, f32[192,128]{1,0:T(8,128)S(1)} %get-tuple-element.48.own_left, f32[200,128]{1,0:T(8,128)S(1)} %get-tuple-element.49.own_right, ...), custom_call_target="tpu_custom_call" | custom-call | bytes 1000000 | tf_op jit(solution)/shard_map/second_own/pallas_call | solution.py:360
  35.2 0.0 collective-permute-done.8.from_last
  35.2 0.0 collective-permute-done.9.from_next
  35.2 1.5 %final_step.2._ = f32[8,4096]{1,0:T(8,128)} custom-call(s32[1,8]{1,0:T(1,128)} %bitcast.19, f32[200,128]{1,0:T(8,128)S(1)} %get-tuple-element.36.own_left.first_left, f32[208,128]{1,0:T(8,128)S(1)} %get-tuple-element.37.own_right.first_right, f32[6,64,128]{2,1,0:T(8,128)S(1)} %first_own.1.sums, f32[192,128]{1,0:T(8,128)S(1)} %collective-permute-done.8.from_last, ...), custom_call_target="tpu_custom_call" | custom-call | bytes 1000000 | tf_op jit(solution)/shard_map/final_step/pallas_call | solution.py:401
  36.7 0.0 collective-permute-done.16.from_last
  36.7 1.5 %collective-permute-done.17.from_next = f32[192,128]{1,0:T(8,128)S(1)} collective-permute-done((f32[192,128]{1,0:T(8,128)S(1)}, f32[192,128]{1,0:T(8,128)S(1)}, u32[]{:S(2)}, u32[]{:S(2)}) %collective-permute-start.17) | collective-permute-done | bytes 98336 | tf_op jit(solution)/shard_map/ppermute | solution.py:314
  38.2 1.5 %final_step.3 = f32[8,4096]{1,0:T(8,128)} custom-call(s32[1,8]{1,0:T(1,128)} %bitcast.20, f32[192,128]{1,0:T(8,128)S(1)} %get-tuple-element.48.own_left, f32[200,128]{1,0:T(8,128)S(1)} %get-tuple-element.49.own_right, f32[6,64,128]{2,1,0:T(8,128)S(1)} %second_own.1.sums, f32[192,128]{1,0:T(8,128)S(1)} %collective-permute-done.16.from_last, ...), custom_call_target="tpu_custom_call" | custom-call | bytes 1000000 | tf_op jit(solution)/shard_map/final_step/pallas_call | solution.py:401
Async XLA Ops:
  2.3 7.7 %collective-permute-start = (f32[192,128]{1,0:T(8,128)S(1)}, f32[192,128]{1,0:T(8,128)S(1)}, u32[]{:S(2)}, u32[]{:S(2)}) collective-permute-start(f32[192,128]{1,0:T(8,128)S(1)} %get-tuple-element.30.own_right), channel_id=1, source_target_pairs={{0,1},{1,2},{2,3},{3,0},{4,5},{5,6},{6,7},{7,4},{8,9},{9,10},{10,1... | collective-permute-start | bytes 294920 | tf_op jit(solution)/shard_map/ppermute | solution.py:314
  4.4 7.1 %collective-permute-start.2 = (f32[208,128]{1,0:T(8,128)S(1)}, f32[208,128]{1,0:T(8,128)S(1)}, u32[]{:S(2)}, u32[]{:S(2)}) collective-permute-start(f32[208,128]{1,0:T(8,128)S(1)} %get-tuple-element.31), channel_id=1, source_target_pairs={{0,4},{4,8},{8,12},{12,0},{1,5},{5,9},{9,13},{13,1},{2,6},{6,10},{... | collective-permute-start | bytes 319496 | tf_op jit(solution)/shard_map/ppermute | solution.py:314
  6.5 5.0 %collective-permute-start.3 = (f32[208,128]{1,0:T(8,128)S(1)}, f32[208,128]{1,0:T(8,128)S(1)}, u32[]{:S(2)}, u32[]{:S(2)}) collective-permute-start(f32[208,128]{1,0:T(8,128)S(1)} %get-tuple-element.32), channel_id=1, source_target_pairs={{0,12},{4,0},{8,4},{12,8},{1,13},{5,1},{9,5},{13,9},{2,14},{6,2},{... | collective-permute-start | bytes 319496 | tf_op jit(solution)/shard_map/ppermute | solution.py:314
  6.5 5.0 %collective-permute-start.1 = (f32[200,128]{1,0:T(8,128)S(1)}, f32[200,128]{1,0:T(8,128)S(1)}, u32[]{:S(2)}, u32[]{:S(2)}) collective-permute-start(f32[200,128]{1,0:T(8,128)S(1)} %get-tuple-element.29.own_left), channel_id=1, source_target_pairs={{0,3},{1,0},{2,1},{3,2},{4,7},{5,4},{6,5},{7,6},{8,11},{9,8},{10,9... | collective-permute-start | bytes 307208 | tf_op jit(solution)/shard_map/ppermute | solution.py:314
  8.5 6.2 %collective-permute-start.11 = (f32[192,128]{1,0:T(8,128)S(1)}, f32[192,128]{1,0:T(8,128)S(1)}, u32[]{:S(2)}, u32[]{:S(2)}) collective-permute-start(f32[192,128]{1,0:T(8,128)S(1)} %get-tuple-element.41.own_left), channel_id=1, source_target_pairs={{0,3},{1,0},{2,1},{3,2},{4,7},{5,4},{6,5},{7,6},{8,11},{9,8},{10,9... | collective-permute-start | bytes 294920 | tf_op jit(solution)/shard_map/ppermute | solution.py:314
  10.0 6.7 %collective-permute-start.10 = (f32[192,128]{1,0:T(8,128)S(1)}, f32[192,128]{1,0:T(8,128)S(1)}, u32[]{:S(2)}, u32[]{:S(2)}) collective-permute-start(f32[192,128]{1,0:T(8,128)S(1)} %get-tuple-element.42.own_right), channel_id=1, source_target_pairs={{0,1},{1,2},{2,3},{3,0},{4,5},{5,6},{6,7},{7,4},{8,9},{9,10},{10,1... | collective-permute-start | bytes 294920 | tf_op jit(solution)/shard_map/ppermute | solution.py:314
  12.0 7.5 %collective-permute-start.4 = (f32[288,128]{1,0:T(8,128)S(1)}, f32[288,128]{1,0:T(8,128)S(1)}, u32[]{:S(2)}, u32[]{:S(2)}) collective-permute-start(f32[288,128]{1,0:T(8,128)S(1)} %get-tuple-element.34.refs_5_), channel_id=1, source_target_pairs={{0,4},{4,8},{8,12},{12,0},{1,5},{5,9},{9,13},{13,1},{2,6},{6,10},{... | collective-permute-start | bytes 442376 | tf_op jit(solution)/shard_map/ppermute | solution.py:314
  14.6 4.9 %collective-permute-start.5 = (f32[288,128]{1,0:T(8,128)S(1)}, f32[288,128]{1,0:T(8,128)S(1)}, u32[]{:S(2)}, u32[]{:S(2)}) collective-permute-start(f32[288,128]{1,0:T(8,128)S(1)} %get-tuple-element.35.refs_4_), channel_id=1, source_target_pairs={{0,12},{4,0},{8,4},{12,8},{1,13},{5,1},{9,5},{13,9},{2,14},{6,2},{... | collective-permute-start | bytes 442376 | tf_op jit(solution)/shard_map/ppermute | solution.py:314
  17.4 5.7 %collective-permute-start.12 = (f32[288,128]{1,0:T(8,128)S(1)}, f32[288,128]{1,0:T(8,128)S(1)}, u32[]{:S(2)}, u32[]{:S(2)}) collective-permute-start(f32[288,128]{1,0:T(8,128)S(1)} %get-tuple-element.46.refs_5_), channel_id=1, source_target_pairs={{0,4},{4,8},{8,12},{12,0},{1,5},{5,9},{9,13},{13,1},{2,6},{6,10},{... | collective-permute-start | bytes 442376 | tf_op jit(solution)/shard_map/ppermute | solution.py:314
  19.5 5.1 %collective-permute-start.13 = (f32[288,128]{1,0:T(8,128)S(1)}, f32[288,128]{1,0:T(8,128)S(1)}, u32[]{:S(2)}, u32[]{:S(2)}) collective-permute-start(f32[288,128]{1,0:T(8,128)S(1)} %get-tuple-element.47.refs_4_), channel_id=1, source_target_pairs={{0,12},{4,0},{8,4},{12,8},{1,13},{5,1},{9,5},{13,9},{2,14},{6,2},{... | collective-permute-start | bytes 442376 | tf_op jit(solution)/shard_map/ppermute | solution.py:314
  19.6 8.4 %collective-permute-start.6 = (f32[208,128]{1,0:T(8,128)S(1)}, f32[208,128]{1,0:T(8,128)S(1)}, u32[]{:S(2)}, u32[]{:S(2)}) collective-permute-start(f32[208,128]{1,0:T(8,128)S(1)} %get-tuple-element.37.own_right.first_right), channel_id=1, source_target_pairs={{0,1},{1,2},{2,3},{3,0},{4,5},{5,6},{6,7},{7,4},{8,9},{9,10},{10,1... | collective-permute-start | bytes 319496 | tf_op jit(solution)/shard_map/ppermute | solution.py:314
  20.3 7.6 %collective-permute-start.7 = (f32[200,128]{1,0:T(8,128)S(1)}, f32[200,128]{1,0:T(8,128)S(1)}, u32[]{:S(2)}, u32[]{:S(2)}) collective-permute-start(f32[200,128]{1,0:T(8,128)S(1)} %get-tuple-element.36.own_left.first_left), channel_id=1, source_target_pairs={{0,3},{1,0},{2,1},{3,2},{4,7},{5,4},{6,5},{7,6},{8,11},{9,8},{10,9... | collective-permute-start | bytes 307208 | tf_op jit(solution)/shard_map/ppermute | solution.py:314
  24.7 7.0 %collective-permute-start.14 = (f32[200,128]{1,0:T(8,128)S(1)}, f32[200,128]{1,0:T(8,128)S(1)}, u32[]{:S(2)}, u32[]{:S(2)}) collective-permute-start(f32[200,128]{1,0:T(8,128)S(1)} %get-tuple-element.49.own_right), channel_id=1, source_target_pairs={{0,1},{1,2},{2,3},{3,0},{4,5},{5,6},{6,7},{7,4},{8,9},{9,10},{10,1... | collective-permute-start | bytes 307208 | tf_op jit(solution)/shard_map/ppermute | solution.py:314
  24.7 6.9 %collective-permute-start.15 = (f32[192,128]{1,0:T(8,128)S(1)}, f32[192,128]{1,0:T(8,128)S(1)}, u32[]{:S(2)}, u32[]{:S(2)}) collective-permute-start(f32[192,128]{1,0:T(8,128)S(1)} %get-tuple-element.48.own_left), channel_id=1, source_target_pairs={{0,3},{1,0},{2,1},{3,2},{4,7},{5,4},{6,5},{7,6},{8,11},{9,8},{10,9... | collective-permute-start | bytes 294920 | tf_op jit(solution)/shard_map/ppermute | solution.py:314
  28.5 6.7 %collective-permute-start.8 = (f32[192,128]{1,0:T(8,128)S(1)}, f32[192,128]{1,0:T(8,128)S(1)}, u32[]{:S(2)}, u32[]{:S(2)}) collective-permute-start(f32[192,128]{1,0:T(8,128)S(1)} %get-tuple-element.39), channel_id=1, source_target_pairs={{0,4},{4,8},{8,12},{12,0},{1,5},{5,9},{9,13},{13,1},{2,6},{6,10},{... | collective-permute-start | bytes 294920 | tf_op jit(solution)/shard_map/ppermute | solution.py:314
  29.8 5.4 %collective-permute-start.9 = (f32[192,128]{1,0:T(8,128)S(1)}, f32[192,128]{1,0:T(8,128)S(1)}, u32[]{:S(2)}, u32[]{:S(2)}) collective-permute-start(f32[192,128]{1,0:T(8,128)S(1)} %get-tuple-element.40), channel_id=1, source_target_pairs={{0,12},{4,0},{8,4},{12,8},{1,13},{5,1},{9,5},{13,9},{2,14},{6,2},{... | collective-permute-start | bytes 294920 | tf_op jit(solution)/shard_map/ppermute | solution.py:314
  32.3 4.5 %collective-permute-start.16 = (f32[192,128]{1,0:T(8,128)S(1)}, f32[192,128]{1,0:T(8,128)S(1)}, u32[]{:S(2)}, u32[]{:S(2)}) collective-permute-start(f32[192,128]{1,0:T(8,128)S(1)} %get-tuple-element.52), channel_id=1, source_target_pairs={{0,4},{4,8},{8,12},{12,0},{1,5},{5,9},{9,13},{13,1},{2,6},{6,10},{... | collective-permute-start | bytes 294920 | tf_op jit(solution)/shard_map/ppermute | solution.py:314
  34.2 4.0 %collective-permute-start.17 = (f32[192,128]{1,0:T(8,128)S(1)}, f32[192,128]{1,0:T(8,128)S(1)}, u32[]{:S(2)}, u32[]{:S(2)}) collective-permute-start(f32[192,128]{1,0:T(8,128)S(1)} %get-tuple-element.53), channel_id=1, source_target_pairs={{0,12},{4,0},{8,4},{12,8},{1,13},{5,1},{9,5},{13,9},{2,14},{6,2},{... | collective-permute-start | bytes 294920 | tf_op jit(solution)/shard_map/ppermute | solution.py:314

commit v5 on v4

v5 whole, which is shorter than its diff:
```python
import functools

import jax
import jax.numpy as jnp
from jax import lax
from jax.experimental import pallas as pl
from jax.experimental.pallas import tpu as pltpu
from jax.sharding import PartitionSpec as P

BLOCK = 64
WIDE = 2 * BLOCK
HALF = BLOCK // 2
DEPTH = 3 * BLOCK
ASK_ROWS = BLOCK + HALF
PADS = (16, 8, 0, 0, 8, 16, 0, 8)
F32 = jnp.float32
BF16 = jnp.bfloat16
VMEM_LIMIT = 16 * 1024 * 1024


def on_left(rows):
    return lax.broadcasted_iota(jnp.int32, (rows, WIDE), 1) < BLOCK


def swap(tile):
    return pltpu.roll(tile, BLOCK, 1)


def place_of(ident, grid):
    rows, cols = grid
    source = jnp.maximum(ident, 0)
    owner_row = lax.div(source, jnp.int32(cols))
    owner_col = lax.rem(source, jnp.int32(cols))
    down = lax.rem(owner_row - lax.axis_index("row") + 1 + rows, jnp.int32(rows))
    across = lax.rem(owner_col - lax.axis_index("col") + 1 + cols, jnp.int32(cols))
    return jnp.where(ident < 0, 9, down * 3 + across)


def note_slots(pattern, table, grid, slots):
    for place in range(10):
        table[place] = slots
    for slot in range(slots):
        table[place_of(pattern[0, slot], grid)] = slot


def ident_at(place, grid):
    rows, cols = grid
    row = lax.rem(lax.axis_index("row") + place // 3 - 1 + rows, jnp.int32(rows))
    col = lax.rem(lax.axis_index("col") + place % 3 - 1 + cols, jnp.int32(cols))
    return (row * cols + col).astype(F32)


def pair_at(low, high, grid):
    return jnp.where(on_left(1), ident_at(low, grid), ident_at(high, grid))


def is_live(idents, wanted):
    return jnp.max(jnp.where(idents == wanted, 1.0, 0.0), axis=0, keepdims=True) > 0


def tile_at(e):
    return slice(e * BLOCK, (e + 1) * BLOCK)


def fetch(sources, targets, sems):
    copies = [pltpu.make_async_copy(s, t, sems.at[i]) for i, (s, t) in enumerate(zip(sources, targets))]
    for copy in copies:
        copy.start()
    return copies


def fill_rest(message):
    if message.shape[0] > DEPTH:
        message[DEPTH:, :] = jnp.zeros((message.shape[0] - DEPTH, WIDE), F32)


def spread(slots, grid, pattern, data, to_left, to_right, rows, table, copies):
    first_half = on_left(HALF)
    copies[0].wait()
    note_slots(pattern, table, grid, slots)
    rows[slots * HALF : (slots + 1) * HALF, :] = jnp.zeros((HALF, WIDE), F32)
    copies[1].wait()
    for step in range(HALF):
        rows[pl.ds(step, slots, stride=HALF), :] = data[:, step * WIDE : (step + 1) * WIDE]

    def block(place):
        own = rows[pl.ds(pl.multiple_of(table[place] * HALF, HALF), HALF), :]
        return own, swap(own)

    def tile(low, high):
        return (jnp.where(first_half, low[0], high[1]), jnp.where(first_half, low[1], high[0]))

    for e in range(3):
        a, b, c = block(3 * e), block(3 * e + 1), block(3 * e + 2)
        left, right = tile(a, b), tile(b, c)
        for part in range(2):
            to_left[pl.ds(e * BLOCK + part, HALF, stride=2), :] = left[part]
            to_right[pl.ds(e * BLOCK + part, HALF, stride=2), :] = right[part]
    fill_rest(to_left)
    fill_rest(to_right)


def spread_kernel(grid, slots, *refs):
    sources, (first_left, first_right, second_left, second_right, idents) = refs[:8], refs[8:13]
    patterns, datas, later, (rows, table, sems) = refs[13:15], refs[15:17], refs[17:21], refs[21:]
    copies = fetch(sources, (*patterns, *datas, *later), sems)
    pairs = ((first_left, first_right), (second_left, second_right))
    for which, pair in enumerate(pairs):
        spread(slots, grid, patterns[which], datas[which], *pair, rows.at[which], table, copies[which :: 2])
    for which, pattern in enumerate(later):
        copies[4 + which].wait()
        for slot in range(slots):
            idents[which, slot : slot + 1, :] = jnp.full((1, WIDE), pattern[0, slot].astype(F32), F32)


def ask_kernel(slots, first_left, first_right, second_left, second_right, idents, ask_last, ask_next):
    for which, (left, right) in enumerate(((first_left, first_right), (second_left, second_right))):
        at = which * ASK_ROWS
        for ask, e in ((ask_last, 0), (ask_next, 2)):
            ask[at : at + BLOCK, :] = left[tile_at(e)]
            ask[at + BLOCK : at + ASK_ROWS, :] = fold(right[tile_at(e)])
            masks = 2 * ASK_ROWS + slots * which
            ask[masks : masks + slots, :] = idents[which]


def fold(right):
    return jnp.where(on_left(HALF), swap(right[:HALF]), right[HALF:])


def split(tile):
    high = tile.astype(BF16)
    return high, (tile - high.astype(F32)).astype(BF16)


def put_depth(factor, rows, tile):
    high, low = split(tile)
    for part, value in enumerate((high, low, high)):
        factor[rows, part * WIDE : (part + 1) * WIDE] = value


def fill_left_factor(at, left, right, factor):
    rows = tile_at(at)
    put_depth(factor.at[0], rows, left)
    put_depth(factor.at[1], rows, right)


def unfold(left, folded):
    first = on_left(HALF)
    other = jnp.concatenate([jnp.where(first, folded, swap(folded)), jnp.where(first, swap(folded), folded)], axis=0)
    return jnp.where(on_left(BLOCK), swap(left), other)


def fill_right_factor(own_left, own_right, from_left, from_right, factor):
    first = on_left(BLOCK)
    for e in range(3):
        at = pl.ds(e * WIDE, WIDE)
        near = jnp.where(first, 0.0, own_right[tile_at(e)])
        for side, pair in enumerate(((from_left[tile_at(e)], own_left[tile_at(e)]), (near, from_right[tile_at(e)]))):
            for k, tile in enumerate(pair):
                high, low = split(tile)
                for part, value in enumerate((high, high, low)):
                    factor[side, tile_at(2 * part + k), at] = value


def product(factor, by):
    return [
        lax.dot_general(factor[side], by[side], (((1,), (0,)), ((), ())), preferred_element_type=F32)
        for side in range(2)
    ]


def tiles_of(total, at, low, count):
    first = on_left(BLOCK)
    left, right = [], []
    for e in range(low, low + count):
        a, b = (side[tile_at(at), e * WIDE : (e + 1) * WIDE] for side in total)
        left.append(a + jnp.where(first, 0.0, swap(b)))
        right.append(b)
    return left, right


def put_all(total, to_last, to_next, sums):
    for at, low, share in ((0, 0, to_last), (1, 1, to_next)):
        left, right = tiles_of(total, at, low, 2)
        share[:BLOCK, :] = left[0]
        share[BLOCK:WIDE, :] = left[1]
        share[WIDE:DEPTH, :] = jnp.where(on_left(BLOCK), swap(right[0]), right[1])
    left, right = tiles_of(total, 2, 0, 3)
    for e in range(3):
        sums[e] = left[e]
        sums[3 + e] = right[e]
    for share, e in ((to_last, 0), (to_next, 2)):
        if share.shape[0] > DEPTH:
            share[DEPTH : DEPTH + BLOCK, :] = left[e]
            share[DEPTH + BLOCK :, :] = fold(right[e])


def fill_own(left, right, factor):
    fill_left_factor(2, left[tile_at(1)], right[tile_at(1)], factor)


def fill_asked(which, grid, slots, asks, got, sent, factor):
    for at in range(2):
        if got is None:
            row = which * ASK_ROWS
            left, folded = asks[at][row : row + BLOCK], asks[at][row + BLOCK : row + ASK_ROWS]
        else:
            pack = sent[at][WIDE:DEPTH]
            if at == 0:
                left, folded = sent[at][BLOCK:WIDE], fold(pack)
            else:
                left, folded = sent[at][:BLOCK], jnp.where(on_left(HALF), pack[:HALF], swap(pack[HALF:]))
            row = 2 * ASK_ROWS + slots * which
            idents = asks[at][row : row + slots]
            left = jnp.where(is_live(idents, pair_at(3, 4, grid)), left + got[at][DEPTH : DEPTH + BLOCK], 0.0)
            folded = jnp.where(is_live(idents, ident_at(5, grid)), folded + got[at][DEPTH + BLOCK :], 0.0)
        fill_left_factor(at, left, unfold(left, folded), factor)


def first_share_kernel(grid, slots, earlier, *refs):
    tiles, asks, refs = refs[:4], refs[4:6], refs[6:]
    got, sent = (refs[:2], refs[2:4]) if earlier else (None, None)
    to_last, to_next, sums, by, factor = refs[4 if earlier else 0 :]
    fill_right_factor(*tiles, by)
    fill_asked(0, grid, slots, asks, got, sent, factor)
    fill_own(tiles[0], tiles[1], factor)
    put_all(product(factor, by), to_last, to_next, sums)


def second_share_kernel(grid, slots, earlier, *refs):
    tiles, asks, refs = refs[:4], refs[4:6], refs[6:]
    got, sent = (refs[:2], refs[2:4]) if earlier else (None, None)
    first_by, first_factor, to_last, to_next, sums, by, factor = refs[4 if earlier else 0 :]
    fill_right_factor(*tiles, by)
    fill_asked(1, grid, slots, asks, got, sent, factor)
    fill_own(tiles[0], tiles[1], factor)
    both = [a + b for a, b in zip(product(factor, first_by), product(first_factor, by))]
    put_all(both, to_last, to_next, sums)


def total(sums, from_last, from_next):
    left = [sums[e] for e in range(3)]
    right = [sums[3 + e] for e in range(3)]
    for share, low in ((from_last, 0), (from_next, 1)):
        pack = share[WIDE:DEPTH]
        left[low] += share[:BLOCK]
        left[low + 1] += share[BLOCK:WIDE]
        right[low] += swap(pack)
        right[low + 1] += pack
    return left, right


def next_kernel(which, grid, idents, sums, from_last, from_next, to_left, to_right):
    first = on_left(BLOCK)
    left, right = total(sums, from_last, from_next)
    for e in range(3):
        keep_left = is_live(idents[which], pair_at(3 * e, 3 * e + 1, grid))
        keep_right = is_live(idents[which], pair_at(3 * e + 1, 3 * e + 2, grid))
        to_left[tile_at(e), :] = jnp.where(keep_left, left[e], 0.0)
        to_right[tile_at(e), :] = jnp.where(keep_right, jnp.where(first, swap(left[e]), right[e]), 0.0)
    fill_rest(to_left)
    fill_rest(to_right)


def final_kernel(which, grid, slots, idents, own_left, own_right, sums, from_last, from_next, _, out, dense, packed):
    first_half = on_left(HALF)
    even, odd = pl.ds(0, HALF, stride=2), pl.ds(1, HALF, stride=2)
    left, right = total(sums, from_last, from_next)
    for e in range(3):
        dense[e] = 2.0 * own_left[tile_at(e)] - left[e]
        dense[3 + e] = 2.0 * own_right[tile_at(e)] - right[e]
    for e in range(3):
        a, b = dense[e, even, :], dense[e, odd, :]
        packed[3 * e] = jnp.where(first_half, a, swap(b))
        packed[3 * e + 1] = jnp.where(first_half, swap(a), b)
        a, b = dense[3 + e, even, :], dense[3 + e, odd, :]
        packed[3 * e + 2] = jnp.where(first_half, swap(a), b)
    slot_holds = [idents[2 + which] == ident_at(place, grid) for place in range(9)]
    for step in range(HALF):
        line = jnp.zeros((slots, WIDE), F32)
        for place in range(9):
            line = jnp.where(slot_holds[place], packed[place, step : step + 1, :], line)
        out[:, step * WIDE : (step + 1) * WIDE] = line


def shift(block, axis, by):
    count = lax.axis_size(axis)
    return lax.ppermute(block, axis, [(i, (i + by) % count) for i in range(count)])


VM = pl.BlockSpec(memory_space=pltpu.VMEM)
HB = pl.BlockSpec(memory_space=pltpu.HBM)
PARAMS = pltpu.CompilerParams(vmem_limit_bytes=VMEM_LIMIT)


def stay(operand):
    return pltpu.with_memory_space_constraint(operand, pltpu.HBM)


def shape(*sizes):
    return jax.ShapeDtypeStruct(sizes, F32)


def call(kernel, out_shape, in_specs, out_specs, scratch, name, flops=0):
    return pl.pallas_call(
        kernel,
        out_shape=out_shape,
        in_specs=in_specs,
        out_specs=out_specs,
        scratch_shapes=scratch,
        compiler_params=PARAMS,
        cost_estimate=pl.CostEstimate(flops=flops, bytes_accessed=10**6, transcendentals=0),
        name=name,
    )


def tiles_shape(rest):
    return shape(DEPTH + rest, WIDE)


SHARE = shape(DEPTH, WIDE)
LONG_SHARE = shape(DEPTH + ASK_ROWS, WIDE)
SUMS = shape(6, BLOCK, WIDE)
BY_SHAPE = (2, 3 * WIDE, 3 * WIDE)
FACTOR_SHAPE = (2, 3 * BLOCK, 3 * WIDE)


def call_all(kernel, outputs, operands, scratch, name):
    return call(kernel, outputs, [VM] * len(operands), [VM] * len(outputs), scratch, name)(*operands)


def along_col(to_left, to_right):
    return to_left, to_right, shift(to_right, "col", 1), shift(to_left, "col", -1)


def along_row(to_last, to_next):
    return shift(to_next, "row", 1), shift(to_last, "row", -1)


def shards(
    density,
    density_pattern,
    response,
    response_pattern,
    density_next_pattern,
    response_next_pattern,
    density_out_pattern,
    response_out_pattern,
):
    slots = density.shape[3]
    grid = (lax.axis_size("row"), lax.axis_size("col"))
    pattern_scratch = pltpu.SMEM((1, slots), jnp.int32)
    table = pltpu.SMEM((16,), jnp.int32)

    def flat(pattern):
        return stay(pattern.reshape(1, slots))

    def flat_data(data):
        return stay(data.reshape(slots, BLOCK * BLOCK))

    *tiles, idents = call(
        functools.partial(spread_kernel, grid, slots),
        [tiles_shape(r) for r in PADS[:4]] + [shape(4, slots, WIDE)],
        [HB] * 8,
        [VM] * 5,
        [pattern_scratch] * 2
        + [pltpu.VMEM((slots, BLOCK * BLOCK), F32)] * 2
        + [pattern_scratch] * 4
        + [pltpu.VMEM((2, (slots + 1) * HALF, WIDE), F32), table, pltpu.SemaphoreType.DMA((8,))],
        "spread",
    )(
        flat(density_pattern),
        flat(response_pattern),
        flat_data(density),
        flat_data(response),
        flat(density_next_pattern),
        flat(response_next_pattern),
        flat(density_out_pattern),
        flat(response_out_pattern),
    )

    def share(first, second, asks, shape_of_share, earlier):
        outputs = [shape_of_share] * 2 + [SUMS]
        factors = [jax.ShapeDtypeStruct(BY_SHAPE, BF16), jax.ShapeDtypeStruct(FACTOR_SHAPE, BF16)]
        scratch = [pltpu.VMEM(BY_SHAPE, BF16), pltpu.VMEM(FACTOR_SHAPE, BF16)]
        *first_sent, first_sums, first_by, first_factor = call_all(
            functools.partial(first_share_kernel, grid, slots, bool(earlier)),
            outputs + factors,
            (*first, *asks, *(earlier[0] if earlier else ())),
            [],
            "first_share",
        )
        first_got = along_row(*first_sent)
        *second_sent, second_sums = call_all(
            functools.partial(second_share_kernel, grid, slots, bool(earlier)),
            outputs,
            (*second, *asks, *(earlier[1] if earlier else ()), first_by, first_factor),
            scratch,
            "second_share",
        )
        second_got = along_row(*second_sent)
        return (first_sums, *first_got), (second_sums, *second_got), first_sent, second_sent

    first = along_col(*tiles[:2])
    asks = along_row(
        *call_all(
            functools.partial(ask_kernel, slots),
            [shape(2 * (ASK_ROWS + slots), WIDE)] * 2,
            (*tiles, idents),
            [],
            "ask",
        )
    )
    second = along_col(*tiles[2:])
    first_parts, second_parts, first_sent, second_sent = share(first, second, asks, LONG_SHARE, ())
    earlier = ((*first_parts[1:], *first_sent), (*second_parts[1:], *second_sent))
    next_tiles = [
        call_all(
            functools.partial(next_kernel, which, grid),
            [tiles_shape(r) for r in PADS[4 + 2 * which : 6 + 2 * which]],
            (idents, *parts),
            [],
            name,
        )
        for which, parts, name in ((0, first_parts, "first_next"), (1, second_parts, "second_next"))
    ]
    first, second = along_col(*next_tiles[0]), along_col(*next_tiles[1])
    first_parts, second_parts, _, _ = share(first, second, asks, SHARE, earlier)

    def final_of(which, own, parts, earlier, name):
        scratch = [pltpu.VMEM((6, BLOCK, WIDE), F32), pltpu.VMEM((9, HALF, WIDE), F32)]
        kernel = functools.partial(final_kernel, which, grid, slots)
        return call(kernel, shape(slots, BLOCK * BLOCK), [VM] * 6 + [HB], VM, scratch, name)(
            idents, *own[:2], *parts, stay(earlier)
        )

    first_out = final_of(0, first, first_parts, flat_data(density), "first_final")
    second_out = final_of(1, second, second_parts, first_out, "second_final")
    return first_out.reshape(density.shape), second_out.reshape(density.shape)


def solution(mesh):
    data = P(("groups", "row"), "col", None, None, None)
    pattern = P(("groups", "row"), "col", None, None)
    return jax.shard_map(
        shards,
        mesh=mesh,
        in_specs=(data, pattern, data, pattern, pattern, pattern, pattern, pattern),
        out_specs=(data, data),
        check_vma=False,
    )
```

time: 39.9 us -> 38.6 us (0.967)
  Pallas kernels: 8.21 us -> 5.76 us
  waiting for transfers between devices: 8.33 us -> 10.6 us
  starting transfers between devices: 22.5 us -> 21.4 us
    ppermute x18, waiting for transfers between devices: 8.33 us -> 10.6 us  [shift(): lax.ppermute(block, axis, [(i, (i + by) % count) for i in range(count)])]
    pallas_call x2, Pallas kernels: 3.06 us -> 1.74 us  [final_of(): call(kernel, shape(slots, BLOCK * BLOCK), [VM] * 6 + [HB], VM, scratch, n...]
    ppermute x18, starting transfers between devices: 22.5 us -> 21.4 us  [shift(): lax.ppermute(block, axis, [(i, (i + by) % count) for i in range(count)])]
    pallas_call x8 -> x7, Pallas kernels: 3.54 us -> 2.55 us  [call_all(): call(kernel, outputs, [VM] * len(operands), [VM] * len(outputs), scratch,...]
  transfers between devices with their start and end apart: 18 -> 18, of which waited for: 5 -> 9; matrix products, arithmetic and copies ran while one was open for 0% -> 0% of each run, Pallas kernels for 13% -> 9%
where the time goes in v5:
time: 38.6 us; the launch traced here: 38.5 us
  starting transfers between devices  21.4 us (55%)
  waiting for transfers between devices  10.6 us (27%)
  Pallas kernels  5.76 us (15%)
  between operations  0.72 us (2%)
    ppermute x18, starting transfers between devices, shift(): lax.ppermute(block, axis, [(i, (i + by) % count) for i in range(count)])  21.4 us
    ppermute x18, waiting for transfers between devices, shift(): lax.ppermute(block, axis, [(i, (i + by) % count) for i in range(count)])  10.6 us
    pallas_call x7, Pallas kernels, call_all(): call(kernel, outputs, [VM] * len(operands), [VM] * len(outputs), scratch,...  2.55 us
    pallas_call x2, Pallas kernels, final_of(): call(kernel, shape(slots, BLOCK * BLOCK), [VM] * 6 + [HB], VM, scratch, n...  1.74 us
    pallas_call x1, Pallas kernels, shards(): call(functools.partial(spread_kernel, grid, slots), [tiles_shape(r) for r...  1.48 us
  transfers between devices with their start and end apart: 18, of which 9 were waited for; matrix products, arithmetic and copies ran while one was open for 0% of the time, Pallas kernels for 9%

profile of v5, /device:TPU:1, one launch (start us, length us, event | category | flops | bytes accessed | tf_op | source)
XLA Modules:
  0.0 38.5 jit_solution(9464299920676579050)
XLA Ops:
  0.6 1.5 %spread.1 = (f32[208,128]{1,0:T(8,128)S(1)}, f32[200,128]{1,0:T(8,128)S(1)}, f32[192,128]{1,0:T(8,128)S(1)}, f32[192,128]{1,0:T(8,128)S(1)}, f32[4,8,128]{2,1,0:T(8,128)S(1)}) custom-call(s32[1,8]{1,0:T(1,128)} %bitcast.15, s32[1,8]{1,0:T(1,128)} %bitcast.16, f32[8,4096]{1,0:T(8,128)} %bitcast.10, f32[8,4096]{1,0:T(8,128)} %bitcast.13, s32[1,8]{1,0:T(1,128)} %bitcast.17, ...), custom_call_target="tpu_custom_call" | custom-call | bytes 1000000 | tf_op jit(solution)/shard_map/spread/pallas_call | solution.py:361
  2.1 2.2 %collective-permute-start = (f32[200,128]{1,0:T(8,128)S(1)}, f32[200,128]{1,0:T(8,128)S(1)}, u32[]{:S(2)}, u32[]{:S(2)}) collective-permute-start(f32[200,128]{1,0:T(8,128)S(1)} %get-tuple-element.31.first_right.refs_1_), channel_id=1, source_target_pairs={{0,1},{1,2},{2,3},{3,0},{4,5},{5,6},{6,7},{7,4},{8,9},{9,10},{10,1... | collective-permute-start | bytes 307208 | tf_op jit(solution)/shard_map/ppermute | solution.py:288
  4.3 2.1 %collective-permute-start.1 = (f32[208,128]{1,0:T(8,128)S(1)}, f32[208,128]{1,0:T(8,128)S(1)}, u32[]{:S(2)}, u32[]{:S(2)}) collective-permute-start(f32[208,128]{1,0:T(8,128)S(1)} %get-tuple-element.30.first_left.refs_0_), channel_id=1, source_target_pairs={{0,3},{1,0},{2,1},{3,2},{4,7},{5,4},{6,5},{7,6},{8,11},{9,8},{10,9... | collective-permute-start | bytes 319496 | tf_op jit(solution)/shard_map/ppermute | solution.py:288
  6.4 0.1 ask.1
  6.5 2.3 %collective-permute-start.2 = (f32[208,128]{1,0:T(8,128)S(1)}, f32[208,128]{1,0:T(8,128)S(1)}, u32[]{:S(2)}, u32[]{:S(2)}) collective-permute-start(f32[208,128]{1,0:T(8,128)S(1)} %get-tuple-element.34), channel_id=1, source_target_pairs={{0,4},{4,8},{8,12},{12,0},{1,5},{5,9},{9,13},{13,1},{2,6},{6,10},{... | collective-permute-start | bytes 319496 | tf_op jit(solution)/shard_map/ppermute | solution.py:288
  8.7 0.0 collective-permute-start.3
  8.7 1.5 %collective-permute-start.11 = (f32[192,128]{1,0:T(8,128)S(1)}, f32[192,128]{1,0:T(8,128)S(1)}, u32[]{:S(2)}, u32[]{:S(2)}) collective-permute-start(f32[192,128]{1,0:T(8,128)S(1)} %get-tuple-element.32.second_left.refs_0_), channel_id=1, source_target_pairs={{0,3},{1,0},{2,1},{3,2},{4,7},{5,4},{6,5},{7,6},{8,11},{9,8},{10,9... | collective-permute-start | bytes 294920 | tf_op jit(solution)/shard_map/ppermute | solution.py:288
  10.3 0.0 collective-permute-done.refs_2_
  10.3 0.0 collective-permute-start.10
  10.3 0.5 %collective-permute-done.1.refs_3_ = f32[208,128]{1,0:T(8,128)S(1)} collective-permute-done((f32[208,128]{1,0:T(8,128)S(1)}, f32[208,128]{1,0:T(8,128)S(1)}, u32[]{:S(2)}, u32[]{:S(2)}) %collective-permute-start.1) | collective-permute-done | bytes 106528 | tf_op jit(solution)/shard_map/ppermute | solution.py:288
  10.8 0.1 collective-permute-done.2.refs_4_
  10.9 2.3 %collective-permute-done.3.refs_5_ = f32[208,128]{1,0:T(8,128)S(1)} collective-permute-done((f32[208,128]{1,0:T(8,128)S(1)}, f32[208,128]{1,0:T(8,128)S(1)}, u32[]{:S(2)}, u32[]{:S(2)}) %collective-permute-start.3) | collective-permute-done | bytes 106528 | tf_op jit(solution)/shard_map/ppermute | solution.py:288
  13.2 0.5 %first_share.2 = (f32[288,128]{1,0:T(8,128)S(1)}, f32[288,128]{1,0:T(8,128)S(1)}, f32[6,64,128]{2,1,0:T(8,128)S(1)}, bf16[2,384,384]{2,1,0:T(8,128)(2,1)S(1)}, bf16[2,192,384]{2,1,0:T(8,128)(2,1)S(1)}) custom-call(f32[208,128]{1,0:T(8,128)S(1)} %get-tuple-element.30.first_left.refs_0_, f32[200,128]{1,0:T(8,128)S(1)} %get-tuple-element.31.first_right.refs_1_, ...), custom_call_target="tpu_custom_call" | custom-call | bytes 1000000 | tf_op jit(solution)/shard_map/first_share/pallas_call | solution.py:329
  13.6 0.6 %collective-permute-start.4 = (f32[288,128]{1,0:T(8,128)S(1)}, f32[288,128]{1,0:T(8,128)S(1)}, u32[]{:S(2)}, u32[]{:S(2)}) collective-permute-start(f32[288,128]{1,0:T(8,128)S(1)} %get-tuple-element.37.refs_9_), channel_id=1, source_target_pairs={{0,4},{4,8},{8,12},{12,0},{1,5},{5,9},{9,13},{13,1},{2,6},{6,10},{... | collective-permute-start | bytes 442376 | tf_op jit(solution)/shard_map/ppermute | solution.py:288
  14.2 0.0 collective-permute-start.5
  14.2 0.0 collective-permute-done.11.refs_3_
  14.2 1.3 %collective-permute-done.10.refs_2_ = f32[192,128]{1,0:T(8,128)S(1)} collective-permute-done((f32[192,128]{1,0:T(8,128)S(1)}, f32[192,128]{1,0:T(8,128)S(1)}, u32[]{:S(2)}, u32[]{:S(2)}) %collective-permute-start.10) | collective-permute-done | bytes 98336 | tf_op jit(solution)/shard_map/ppermute | solution.py:288
  15.5 0.6 %second_share.2 = (f32[288,128]{1,0:T(8,128)S(1)}, f32[288,128]{1,0:T(8,128)S(1)}, f32[6,64,128]{2,1,0:T(8,128)S(1)}) custom-call(f32[192,128]{1,0:T(8,128)S(1)} %get-tuple-element.32.second_left.refs_0_, f32[192,128]{1,0:T(8,128)S(1)} %get-tuple-element.33.second_right.refs_1_, f32[192,128]{1,0:T(8,128)S(1)} %collective-permute-done.10.refs_2_, ...), custom_call_target="tpu_custom_call" | custom-call | bytes 1000000 | tf_op jit(solution)/shard_map/second_share/pallas_call | solution.py:329
  16.2 3.2 %collective-permute-start.12 = (f32[288,128]{1,0:T(8,128)S(1)}, f32[288,128]{1,0:T(8,128)S(1)}, u32[]{:S(2)}, u32[]{:S(2)}) collective-permute-start(f32[288,128]{1,0:T(8,128)S(1)} %get-tuple-element.47.refs_9_), channel_id=1, source_target_pairs={{0,4},{4,8},{8,12},{12,0},{1,5},{5,9},{9,13},{13,1},{2,6},{6,10},{... | collective-permute-start | bytes 442376 | tf_op jit(solution)/shard_map/ppermute | solution.py:288
  19.4 0.0 collective-permute-start.13
  19.4 0.0 collective-permute-done.4.from_last.refs_6_
  19.4 0.0 collective-permute-done.5.from_next.refs_7_
  19.4 0.1 first_next.1
  19.5 0.3 collective-permute-start.6
  19.9 3.0 %collective-permute-start.7 = (f32[200,128]{1,0:T(8,128)S(1)}, f32[200,128]{1,0:T(8,128)S(1)}, u32[]{:S(2)}, u32[]{:S(2)}) collective-permute-start(f32[200,128]{1,0:T(8,128)S(1)} %get-tuple-element.39.refs_0_.own_left), channel_id=1, source_target_pairs={{0,3},{1,0},{2,1},{3,2},{4,7},{5,4},{6,5},{7,6},{8,11},{9,8},{10,9... | collective-permute-start | bytes 307208 | tf_op jit(solution)/shard_map/ppermute | solution.py:288
  22.8 0.0 collective-permute-done.12.from_last.refs_6_
  22.8 1.4 %collective-permute-done.13.from_next.refs_7_ = f32[288,128]{1,0:T(8,128)S(1)} collective-permute-done((f32[288,128]{1,0:T(8,128)S(1)}, f32[288,128]{1,0:T(8,128)S(1)}, u32[]{:S(2)}, u32[]{:S(2)}) %collective-permute-start.13) | collective-permute-done | bytes 147488 | tf_op jit(solution)/shard_map/ppermute | solution.py:288
  24.3 0.1 second_next.1
  24.4 0.1 collective-permute-start.14
  24.4 3.3 %collective-permute-start.15 = (f32[192,128]{1,0:T(8,128)S(1)}, f32[192,128]{1,0:T(8,128)S(1)}, u32[]{:S(2)}, u32[]{:S(2)}) collective-permute-start(f32[192,128]{1,0:T(8,128)S(1)} %get-tuple-element.49.refs_0_.own_left), channel_id=1, source_target_pairs={{0,3},{1,0},{2,1},{3,2},{4,7},{5,4},{6,5},{7,6},{8,11},{9,8},{10,9... | collective-permute-start | bytes 294920 | tf_op jit(solution)/shard_map/ppermute | solution.py:288
  27.7 0.0 collective-permute-done.7.refs_3_
  27.7 0.0 collective-permute-done.6.refs_2_
  27.7 0.5 %first_share.3 = (f32[192,128]{1,0:T(8,128)S(1)}, f32[192,128]{1,0:T(8,128)S(1)}, f32[6,64,128]{2,1,0:T(8,128)S(1)}, bf16[2,384,384]{2,1,0:T(8,128)(2,1)S(1)}, bf16[2,192,384]{2,1,0:T(8,128)(2,1)S(1)}) custom-call(f32[200,128]{1,0:T(8,128)S(1)} %get-tuple-element.39.refs_0_.own_left, f32[208,128]{1,0:T(8,128)S(1)} %get-tuple-element.40.refs_1_.own_right, ...), custom_call_target="tpu_custom_call" | custom-call | bytes 1000000 | tf_op jit(solution)/shard_map/first_share/pallas_call | solution.py:329
  28.2 1.5 %collective-permute-start.8 = (f32[192,128]{1,0:T(8,128)S(1)}, f32[192,128]{1,0:T(8,128)S(1)}, u32[]{:S(2)}, u32[]{:S(2)}) collective-permute-start(f32[192,128]{1,0:T(8,128)S(1)} %get-tuple-element.42), channel_id=1, source_target_pairs={{0,4},{4,8},{8,12},{12,0},{1,5},{5,9},{9,13},{13,1},{2,6},{6,10},{... | collective-permute-start | bytes 294920 | tf_op jit(solution)/shard_map/ppermute | solution.py:288
  29.7 0.0 collective-permute-start.9
  29.7 1.8 %collective-permute-done.15.refs_3_ = f32[192,128]{1,0:T(8,128)S(1)} collective-permute-done((f32[192,128]{1,0:T(8,128)S(1)}, f32[192,128]{1,0:T(8,128)S(1)}, u32[]{:S(2)}, u32[]{:S(2)}) %collective-permute-start.15) | collective-permute-done | bytes 98336 | tf_op jit(solution)/shard_map/ppermute | solution.py:288
  31.5 0.0 collective-permute-done.14.refs_2_
  31.5 0.6 %second_share.3 = (f32[192,128]{1,0:T(8,128)S(1)}, f32[192,128]{1,0:T(8,128)S(1)}, f32[6,64,128]{2,1,0:T(8,128)S(1)}) custom-call(f32[192,128]{1,0:T(8,128)S(1)} %get-tuple-element.49.refs_0_.own_left, f32[200,128]{1,0:T(8,128)S(1)} %get-tuple-element.50.refs_1_.own_right, f32[200,128]{1,0:T(8,128)S(1)} %collective-permute-done.14.refs_2_, ...), custom_call_target="tpu_custom_call" | custom-call | bytes 1000000 | tf_op jit(solution)/shard_map/second_share/pallas_call | solution.py:329
  32.2 1.4 %collective-permute-start.16 = (f32[192,128]{1,0:T(8,128)S(1)}, f32[192,128]{1,0:T(8,128)S(1)}, u32[]{:S(2)}, u32[]{:S(2)}) collective-permute-start(f32[192,128]{1,0:T(8,128)S(1)} %get-tuple-element.54), channel_id=1, source_target_pairs={{0,4},{4,8},{8,12},{12,0},{1,5},{5,9},{9,13},{13,1},{2,6},{6,10},{... | collective-permute-start | bytes 294920 | tf_op jit(solution)/shard_map/ppermute | solution.py:288
  33.6 0.0 collective-permute-start.17
  33.6 0.0 collective-permute-done.8.from_last
  33.6 0.2 collective-permute-done.9.from_next
  33.8 0.9 %first_final.1._ = f32[8,4096]{1,0:T(8,128)} custom-call(f32[4,8,128]{2,1,0:T(8,128)S(1)} %get-tuple-element.29.idents, f32[200,128]{1,0:T(8,128)S(1)} %get-tuple-element.39.refs_0_.own_left, f32[208,128]{1,0:T(8,128)S(1)} %get-tuple-element.40.refs_1_.own_right, f32[6,64,128]{2,1,0:T(8,128)S(1)} %get-tuple-element.41.sums, ...), custom_call_target="tpu_custom_call" | custom-call | bytes 1000000 | tf_op jit(solution)/shard_map/first_final/pallas_call | solution.py:433
  34.6 0.6 %collective-permute-done.16.from_last = f32[192,128]{1,0:T(8,128)S(1)} collective-permute-done((f32[192,128]{1,0:T(8,128)S(1)}, f32[192,128]{1,0:T(8,128)S(1)}, u32[]{:S(2)}, u32[]{:S(2)}) %collective-permute-start.16) | collective-permute-done | bytes 98336 | tf_op jit(solution)/shard_map/ppermute | solution.py:288
  35.2 2.4 %collective-permute-done.17.from_next = f32[192,128]{1,0:T(8,128)S(1)} collective-permute-done((f32[192,128]{1,0:T(8,128)S(1)}, f32[192,128]{1,0:T(8,128)S(1)}, u32[]{:S(2)}, u32[]{:S(2)}) %collective-permute-start.17) | collective-permute-done | bytes 98336 | tf_op jit(solution)/shard_map/ppermute | solution.py:288
  37.6 0.9 %second_final.1 = f32[8,4096]{1,0:T(8,128)} custom-call(f32[4,8,128]{2,1,0:T(8,128)S(1)} %get-tuple-element.29.idents, f32[192,128]{1,0:T(8,128)S(1)} %get-tuple-element.49.refs_0_.own_left, f32[200,128]{1,0:T(8,128)S(1)} %get-tuple-element.50.refs_1_.own_right, f32[6,64,128]{2,1,0:T(8,128)S(1)} %get-tuple-element.53.sums, ...), custom_call_target="tpu_custom_call" | custom-call | bytes 1000000 | tf_op jit(solution)/shard_map/second_final/pallas_call | solution.py:433
Async XLA Ops:
  2.1 8.1 %collective-permute-start = (f32[200,128]{1,0:T(8,128)S(1)}, f32[200,128]{1,0:T(8,128)S(1)}, u32[]{:S(2)}, u32[]{:S(2)}) collective-permute-start(f32[200,128]{1,0:T(8,128)S(1)} %get-tuple-element.31.first_right.refs_1_), channel_id=1, source_target_pairs={{0,1},{1,2},{2,3},{3,0},{4,5},{5,6},{6,7},{7,4},{8,9},{9,10},{10,1... | collective-permute-start | bytes 307208 | tf_op jit(solution)/shard_map/ppermute | solution.py:288
  4.3 6.5 %collective-permute-start.1 = (f32[208,128]{1,0:T(8,128)S(1)}, f32[208,128]{1,0:T(8,128)S(1)}, u32[]{:S(2)}, u32[]{:S(2)}) collective-permute-start(f32[208,128]{1,0:T(8,128)S(1)} %get-tuple-element.30.first_left.refs_0_), channel_id=1, source_target_pairs={{0,3},{1,0},{2,1},{3,2},{4,7},{5,4},{6,5},{7,6},{8,11},{9,8},{10,9... | collective-permute-start | bytes 319496 | tf_op jit(solution)/shard_map/ppermute | solution.py:288
  6.5 4.4 %collective-permute-start.2 = (f32[208,128]{1,0:T(8,128)S(1)}, f32[208,128]{1,0:T(8,128)S(1)}, u32[]{:S(2)}, u32[]{:S(2)}) collective-permute-start(f32[208,128]{1,0:T(8,128)S(1)} %get-tuple-element.34), channel_id=1, source_target_pairs={{0,4},{4,8},{8,12},{12,0},{1,5},{5,9},{9,13},{13,1},{2,6},{6,10},{... | collective-permute-start | bytes 319496 | tf_op jit(solution)/shard_map/ppermute | solution.py:288
  8.7 4.4 %collective-permute-start.3 = (f32[208,128]{1,0:T(8,128)S(1)}, f32[208,128]{1,0:T(8,128)S(1)}, u32[]{:S(2)}, u32[]{:S(2)}) collective-permute-start(f32[208,128]{1,0:T(8,128)S(1)} %get-tuple-element.35), channel_id=1, source_target_pairs={{0,12},{4,0},{8,4},{12,8},{1,13},{5,1},{9,5},{13,9},{2,14},{6,2},{... | collective-permute-start | bytes 319496 | tf_op jit(solution)/shard_map/ppermute | solution.py:288
  8.7 5.5 %collective-permute-start.11 = (f32[192,128]{1,0:T(8,128)S(1)}, f32[192,128]{1,0:T(8,128)S(1)}, u32[]{:S(2)}, u32[]{:S(2)}) collective-permute-start(f32[192,128]{1,0:T(8,128)S(1)} %get-tuple-element.32.second_left.refs_0_), channel_id=1, source_target_pairs={{0,3},{1,0},{2,1},{3,2},{4,7},{5,4},{6,5},{7,6},{8,11},{9,8},{10,9... | collective-permute-start | bytes 294920 | tf_op jit(solution)/shard_map/ppermute | solution.py:288
  10.3 5.3 %collective-permute-start.10 = (f32[192,128]{1,0:T(8,128)S(1)}, f32[192,128]{1,0:T(8,128)S(1)}, u32[]{:S(2)}, u32[]{:S(2)}) collective-permute-start(f32[192,128]{1,0:T(8,128)S(1)} %get-tuple-element.33.second_right.refs_1_), channel_id=1, source_target_pairs={{0,1},{1,2},{2,3},{3,0},{4,5},{5,6},{6,7},{7,4},{8,9},{9,10},{10,1... | collective-permute-start | bytes 294920 | tf_op jit(solution)/shard_map/ppermute | solution.py:288
  13.6 5.8 %collective-permute-start.4 = (f32[288,128]{1,0:T(8,128)S(1)}, f32[288,128]{1,0:T(8,128)S(1)}, u32[]{:S(2)}, u32[]{:S(2)}) collective-permute-start(f32[288,128]{1,0:T(8,128)S(1)} %get-tuple-element.37.refs_9_), channel_id=1, source_target_pairs={{0,4},{4,8},{8,12},{12,0},{1,5},{5,9},{9,13},{13,1},{2,6},{6,10},{... | collective-permute-start | bytes 442376 | tf_op jit(solution)/shard_map/ppermute | solution.py:288
  14.2 5.2 %collective-permute-start.5 = (f32[288,128]{1,0:T(8,128)S(1)}, f32[288,128]{1,0:T(8,128)S(1)}, u32[]{:S(2)}, u32[]{:S(2)}) collective-permute-start(f32[288,128]{1,0:T(8,128)S(1)} %get-tuple-element.38.refs_8_), channel_id=1, source_target_pairs={{0,12},{4,0},{8,4},{12,8},{1,13},{5,1},{9,5},{13,9},{2,14},{6,2},{... | collective-permute-start | bytes 442376 | tf_op jit(solution)/shard_map/ppermute | solution.py:288
  16.2 6.7 %collective-permute-start.12 = (f32[288,128]{1,0:T(8,128)S(1)}, f32[288,128]{1,0:T(8,128)S(1)}, u32[]{:S(2)}, u32[]{:S(2)}) collective-permute-start(f32[288,128]{1,0:T(8,128)S(1)} %get-tuple-element.47.refs_9_), channel_id=1, source_target_pairs={{0,4},{4,8},{8,12},{12,0},{1,5},{5,9},{9,13},{13,1},{2,6},{6,10},{... | collective-permute-start | bytes 442376 | tf_op jit(solution)/shard_map/ppermute | solution.py:288
  19.4 4.9 %collective-permute-start.13 = (f32[288,128]{1,0:T(8,128)S(1)}, f32[288,128]{1,0:T(8,128)S(1)}, u32[]{:S(2)}, u32[]{:S(2)}) collective-permute-start(f32[288,128]{1,0:T(8,128)S(1)} %get-tuple-element.48.refs_8_), channel_id=1, source_target_pairs={{0,12},{4,0},{8,4},{12,8},{1,13},{5,1},{9,5},{13,9},{2,14},{6,2},{... | collective-permute-start | bytes 442376 | tf_op jit(solution)/shard_map/ppermute | solution.py:288
  19.5 8.2 %collective-permute-start.6 = (f32[208,128]{1,0:T(8,128)S(1)}, f32[208,128]{1,0:T(8,128)S(1)}, u32[]{:S(2)}, u32[]{:S(2)}) collective-permute-start(f32[208,128]{1,0:T(8,128)S(1)} %get-tuple-element.40.refs_1_.own_right), channel_id=1, source_target_pairs={{0,1},{1,2},{2,3},{3,0},{4,5},{5,6},{6,7},{7,4},{8,9},{9,10},{10,1... | collective-permute-start | bytes 319496 | tf_op jit(solution)/shard_map/ppermute | solution.py:288
  19.9 7.8 %collective-permute-start.7 = (f32[200,128]{1,0:T(8,128)S(1)}, f32[200,128]{1,0:T(8,128)S(1)}, u32[]{:S(2)}, u32[]{:S(2)}) collective-permute-start(f32[200,128]{1,0:T(8,128)S(1)} %get-tuple-element.39.refs_0_.own_left), channel_id=1, source_target_pairs={{0,3},{1,0},{2,1},{3,2},{4,7},{5,4},{6,5},{7,6},{8,11},{9,8},{10,9... | collective-permute-start | bytes 307208 | tf_op jit(solution)/shard_map/ppermute | solution.py:288
  24.4 7.1 %collective-permute-start.14 = (f32[200,128]{1,0:T(8,128)S(1)}, f32[200,128]{1,0:T(8,128)S(1)}, u32[]{:S(2)}, u32[]{:S(2)}) collective-permute-start(f32[200,128]{1,0:T(8,128)S(1)} %get-tuple-element.50.refs_1_.own_right), channel_id=1, source_target_pairs={{0,1},{1,2},{2,3},{3,0},{4,5},{5,6},{6,7},{7,4},{8,9},{9,10},{10,1... | collective-permute-start | bytes 307208 | tf_op jit(solution)/shard_map/ppermute | solution.py:288
  24.4 7.1 %collective-permute-start.15 = (f32[192,128]{1,0:T(8,128)S(1)}, f32[192,128]{1,0:T(8,128)S(1)}, u32[]{:S(2)}, u32[]{:S(2)}) collective-permute-start(f32[192,128]{1,0:T(8,128)S(1)} %get-tuple-element.49.refs_0_.own_left), channel_id=1, source_target_pairs={{0,3},{1,0},{2,1},{3,2},{4,7},{5,4},{6,5},{7,6},{8,11},{9,8},{10,9... | collective-permute-start | bytes 294920 | tf_op jit(solution)/shard_map/ppermute | solution.py:288
  28.2 5.4 %collective-permute-start.8 = (f32[192,128]{1,0:T(8,128)S(1)}, f32[192,128]{1,0:T(8,128)S(1)}, u32[]{:S(2)}, u32[]{:S(2)}) collective-permute-start(f32[192,128]{1,0:T(8,128)S(1)} %get-tuple-element.42), channel_id=1, source_target_pairs={{0,4},{4,8},{8,12},{12,0},{1,5},{5,9},{9,13},{13,1},{2,6},{6,10},{... | collective-permute-start | bytes 294920 | tf_op jit(solution)/shard_map/ppermute | solution.py:288
  29.7 4.0 %collective-permute-start.9 = (f32[192,128]{1,0:T(8,128)S(1)}, f32[192,128]{1,0:T(8,128)S(1)}, u32[]{:S(2)}, u32[]{:S(2)}) collective-permute-start(f32[192,128]{1,0:T(8,128)S(1)} %get-tuple-element.43), channel_id=1, source_target_pairs={{0,12},{4,0},{8,4},{12,8},{1,13},{5,1},{9,5},{13,9},{2,14},{6,2},{... | collective-permute-start | bytes 294920 | tf_op jit(solution)/shard_map/ppermute | solution.py:288
  32.2 3.1 %collective-permute-start.16 = (f32[192,128]{1,0:T(8,128)S(1)}, f32[192,128]{1,0:T(8,128)S(1)}, u32[]{:S(2)}, u32[]{:S(2)}) collective-permute-start(f32[192,128]{1,0:T(8,128)S(1)} %get-tuple-element.54), channel_id=1, source_target_pairs={{0,4},{4,8},{8,12},{12,0},{1,5},{5,9},{9,13},{13,1},{2,6},{6,10},{... | collective-permute-start | bytes 294920 | tf_op jit(solution)/shard_map/ppermute | solution.py:288
  33.6 4.0 %collective-permute-start.17 = (f32[192,128]{1,0:T(8,128)S(1)}, f32[192,128]{1,0:T(8,128)S(1)}, u32[]{:S(2)}, u32[]{:S(2)}) collective-permute-start(f32[192,128]{1,0:T(8,128)S(1)} %get-tuple-element.55), channel_id=1, source_target_pairs={{0,12},{4,0},{8,4},{12,8},{1,13},{5,1},{9,5},{13,9},{2,14},{6,2},{... | collective-permute-start | bytes 294920 | tf_op jit(solution)/shard_map/ppermute | solution.py:288

commit v6 on v5

--- a/solution.py
+++ b/solution.py
@@ -12,7 +12,7 @@
 HALF = BLOCK // 2
 DEPTH = 3 * BLOCK
 ASK_ROWS = BLOCK + HALF
-PADS = (16, 8, 0, 0, 8, 16, 0, 8)
+PADS = (16, 0, 0, 8, 8, 16, 0, 8)
 F32 = jnp.float32
 BF16 = jnp.bfloat16
 VMEM_LIMIT = 16 * 1024 * 1024
@@ -36,11 +36,11 @@
     return jnp.where(ident < 0, 9, down * 3 + across)
 
 
-def note_slots(pattern, table, grid, slots):
+def note_slots(which, pattern, table, grid, slots):
     for place in range(10):
-        table[place] = slots
+        table[which, place] = slots
     for slot in range(slots):
-        table[place_of(pattern[0, slot], grid)] = slot
+        table[which, place_of(pattern[0, slot], grid)] = slot
 
 
 def ident_at(place, grid):
@@ -74,17 +74,14 @@
         message[DEPTH:, :] = jnp.zeros((message.shape[0] - DEPTH, WIDE), F32)
 
 
-def spread(slots, grid, pattern, data, to_left, to_right, rows, table, copies):
+def spread(which, slots, data, to_left, to_right, rows, table):
     first_half = on_left(HALF)
-    copies[0].wait()
-    note_slots(pattern, table, grid, slots)
     rows[slots * HALF : (slots + 1) * HALF, :] = jnp.zeros((HALF, WIDE), F32)
-    copies[1].wait()
     for step in range(HALF):
         rows[pl.ds(step, slots, stride=HALF), :] = data[:, step * WIDE : (step + 1) * WIDE]
 
     def block(place):
-        own = rows[pl.ds(pl.multiple_of(table[place] * HALF, HALF), HALF), :]
+        own = rows[pl.ds(pl.multiple_of(table[which, place] * HALF, HALF), HALF), :]
         return own, swap(own)
 
     def tile(low, high):
@@ -104,13 +101,16 @@
     sources, (first_left, first_right, second_left, second_right, idents) = refs[:8], refs[8:13]
     patterns, datas, later, (rows, table, sems) = refs[13:15], refs[15:17], refs[17:21], refs[21:]
     copies = fetch(sources, (*patterns, *datas, *later), sems)
-    pairs = ((first_left, first_right), (second_left, second_right))
-    for which, pair in enumerate(pairs):
-        spread(slots, grid, patterns[which], datas[which], *pair, rows.at[which], table, copies[which :: 2])
+    for which, pattern in enumerate(patterns):
+        copies[which].wait()
+        note_slots(which, pattern, table, grid, slots)
     for which, pattern in enumerate(later):
         copies[4 + which].wait()
         for slot in range(slots):
             idents[which, slot : slot + 1, :] = jnp.full((1, WIDE), pattern[0, slot].astype(F32), F32)
+    for which, pair in enumerate(((first_left, first_right), (second_left, second_right))):
+        copies[2 + which].wait()
+        spread(which, slots, datas[which], *pair, rows.at[which], table)
 
 
 def ask_kernel(slots, first_left, first_right, second_left, second_right, idents, ask_last, ask_next):
@@ -350,7 +350,7 @@
     slots = density.shape[3]
     grid = (lax.axis_size("row"), lax.axis_size("col"))
     pattern_scratch = pltpu.SMEM((1, slots), jnp.int32)
-    table = pltpu.SMEM((16,), jnp.int32)
+    table = pltpu.SMEM((2, 16), jnp.int32)
 
     def flat(pattern):
         return stay(pattern.reshape(1, slots))

time: 38.6 us -> 38.3 us (level)
  waiting for transfers between devices: 10.6 us -> 9.99 us
  starting transfers between devices: 21.4 us -> 21.8 us
    ppermute x18, waiting for transfers between devices: 10.6 us -> 9.99 us  [shift(): lax.ppermute(block, axis, [(i, (i + by) % count) for i in range(count)])]
  transfers between devices with their start and end apart: 18 -> 18, of which waited for: 9 -> 7; matrix products, arithmetic and copies ran while one was open for 0% -> 0% of each run, Pallas kernels for 9% -> 9%
where the time goes in v6:
time: 38.3 us; the launch traced here: 38.2 us
  starting transfers between devices  21.8 us (57%)
  waiting for transfers between devices  9.99 us (26%)
  Pallas kernels  5.66 us (15%)
  between operations  0.72 us (2%)
    ppermute x18, starting transfers between devices, shift(): lax.ppermute(block, axis, [(i, (i + by) % count) for i in range(count)])  21.8 us
    ppermute x18, waiting for transfers between devices, shift(): lax.ppermute(block, axis, [(i, (i + by) % count) for i in range(count)])  9.99 us
    pallas_call x7, Pallas kernels, call_all(): call(kernel, outputs, [VM] * len(operands), [VM] * len(outputs), scratch,...  2.57 us
    pallas_call x2, Pallas kernels, final_of(): call(kernel, shape(slots, BLOCK * BLOCK), [VM] * 6 + [HB], VM, scratch, n...  1.74 us
    pallas_call x1, Pallas kernels, shards(): call(functools.partial(spread_kernel, grid, slots), [tiles_shape(r) for r...  1.35 us
  transfers between devices with their start and end apart: 18, of which 7 were waited for; matrix products, arithmetic and copies ran while one was open for 0% of the time, Pallas kernels for 9%

profile of v6, /device:TPU:1, one launch (start us, length us, event | category | flops | bytes accessed | tf_op | source)
XLA Modules:
  0.0 38.2 jit_solution(9697997755462361131)
XLA Ops:
  0.6 1.4 %spread.1 = (f32[208,128]{1,0:T(8,128)S(1)}, f32[192,128]{1,0:T(8,128)S(1)}, f32[192,128]{1,0:T(8,128)S(1)}, f32[200,128]{1,0:T(8,128)S(1)}, f32[4,8,128]{2,1,0:T(8,128)S(1)}) custom-call(s32[1,8]{1,0:T(1,128)} %bitcast.15, s32[1,8]{1,0:T(1,128)} %bitcast.16, f32[8,4096]{1,0:T(8,128)} %bitcast.10, f32[8,4096]{1,0:T(8,128)} %bitcast.13, s32[1,8]{1,0:T(1,128)} %bitcast.17, ...), custom_call_target="tpu_custom_call" | custom-call | bytes 1000000 | tf_op jit(solution)/shard_map/spread/pallas_call | solution.py:361
  2.0 2.2 %collective-permute-start = (f32[192,128]{1,0:T(8,128)S(1)}, f32[192,128]{1,0:T(8,128)S(1)}, u32[]{:S(2)}, u32[]{:S(2)}) collective-permute-start(f32[192,128]{1,0:T(8,128)S(1)} %get-tuple-element.31.first_right.refs_1_), channel_id=1, source_target_pairs={{0,1},{1,2},{2,3},{3,0},{4,5},{5,6},{6,7},{7,4},{8,9},{9,10},{10,1... | collective-permute-start | bytes 294920 | tf_op jit(solution)/shard_map/ppermute | solution.py:288
  4.2 2.1 %collective-permute-start.1 = (f32[208,128]{1,0:T(8,128)S(1)}, f32[208,128]{1,0:T(8,128)S(1)}, u32[]{:S(2)}, u32[]{:S(2)}) collective-permute-start(f32[208,128]{1,0:T(8,128)S(1)} %get-tuple-element.30.first_left.refs_0_), channel_id=1, source_target_pairs={{0,3},{1,0},{2,1},{3,2},{4,7},{5,4},{6,5},{7,6},{8,11},{9,8},{10,9... | collective-permute-start | bytes 319496 | tf_op jit(solution)/shard_map/ppermute | solution.py:288
  6.3 0.1 ask.1
  6.4 2.3 %collective-permute-start.2 = (f32[208,128]{1,0:T(8,128)S(1)}, f32[208,128]{1,0:T(8,128)S(1)}, u32[]{:S(2)}, u32[]{:S(2)}) collective-permute-start(f32[208,128]{1,0:T(8,128)S(1)} %get-tuple-element.34), channel_id=1, source_target_pairs={{0,4},{4,8},{8,12},{12,0},{1,5},{5,9},{9,13},{13,1},{2,6},{6,10},{... | collective-permute-start | bytes 319496 | tf_op jit(solution)/shard_map/ppermute | solution.py:288
  8.6 0.0 collective-permute-start.3
  8.6 0.0 collective-permute-start.10
  8.6 0.1 collective-permute-done.refs_2_
  8.7 3.2 %collective-permute-start.11 = (f32[192,128]{1,0:T(8,128)S(1)}, f32[192,128]{1,0:T(8,128)S(1)}, u32[]{:S(2)}, u32[]{:S(2)}) collective-permute-start(f32[192,128]{1,0:T(8,128)S(1)} %get-tuple-element.32.second_left.refs_0_), channel_id=1, source_target_pairs={{0,3},{1,0},{2,1},{3,2},{4,7},{5,4},{6,5},{7,6},{8,11},{9,8},{10,9... | collective-permute-start | bytes 294920 | tf_op jit(solution)/shard_map/ppermute | solution.py:288
  11.9 0.0 collective-permute-done.1.refs_3_
  11.9 0.0 collective-permute-done.2.refs_4_
  11.9 0.9 %collective-permute-done.3.refs_5_ = f32[208,128]{1,0:T(8,128)S(1)} collective-permute-done((f32[208,128]{1,0:T(8,128)S(1)}, f32[208,128]{1,0:T(8,128)S(1)}, u32[]{:S(2)}, u32[]{:S(2)}) %collective-permute-start.3) | collective-permute-done | bytes 106528 | tf_op jit(solution)/shard_map/ppermute | solution.py:288
  12.7 0.5 %first_share.2 = (f32[288,128]{1,0:T(8,128)S(1)}, f32[288,128]{1,0:T(8,128)S(1)}, f32[6,64,128]{2,1,0:T(8,128)S(1)}, bf16[2,384,384]{2,1,0:T(8,128)(2,1)S(1)}, bf16[2,192,384]{2,1,0:T(8,128)(2,1)S(1)}) custom-call(f32[208,128]{1,0:T(8,128)S(1)} %get-tuple-element.30.first_left.refs_0_, f32[192,128]{1,0:T(8,128)S(1)} %get-tuple-element.31.first_right.refs_1_, ...), custom_call_target="tpu_custom_call" | custom-call | bytes 1000000 | tf_op jit(solution)/shard_map/first_share/pallas_call | solution.py:329
  13.2 1.6 %collective-permute-start.4 = (f32[288,128]{1,0:T(8,128)S(1)}, f32[288,128]{1,0:T(8,128)S(1)}, u32[]{:S(2)}, u32[]{:S(2)}) collective-permute-start(f32[288,128]{1,0:T(8,128)S(1)} %get-tuple-element.37.refs_9_), channel_id=1, source_target_pairs={{0,4},{4,8},{8,12},{12,0},{1,5},{5,9},{9,13},{13,1},{2,6},{6,10},{... | collective-permute-start | bytes 442376 | tf_op jit(solution)/shard_map/ppermute | solution.py:288
  14.8 0.0 collective-permute-start.5
  14.8 0.0 collective-permute-done.11.refs_3_
  14.8 0.0 collective-permute-done.10.refs_2_
  14.8 0.6 %second_share.2 = (f32[288,128]{1,0:T(8,128)S(1)}, f32[288,128]{1,0:T(8,128)S(1)}, f32[6,64,128]{2,1,0:T(8,128)S(1)}) custom-call(f32[192,128]{1,0:T(8,128)S(1)} %get-tuple-element.32.second_left.refs_0_, f32[200,128]{1,0:T(8,128)S(1)} %get-tuple-element.33.second_right.refs_1_, f32[200,128]{1,0:T(8,128)S(1)} %collective-permute-done.10.refs_2_, ...), custom_call_target="tpu_custom_call" | custom-call | bytes 1000000 | tf_op jit(solution)/shard_map/second_share/pallas_call | solution.py:329
  15.5 2.7 %collective-permute-start.12 = (f32[288,128]{1,0:T(8,128)S(1)}, f32[288,128]{1,0:T(8,128)S(1)}, u32[]{:S(2)}, u32[]{:S(2)}) collective-permute-start(f32[288,128]{1,0:T(8,128)S(1)} %get-tuple-element.47.refs_9_), channel_id=1, source_target_pairs={{0,4},{4,8},{8,12},{12,0},{1,5},{5,9},{9,13},{13,1},{2,6},{6,10},{... | collective-permute-start | bytes 442376 | tf_op jit(solution)/shard_map/ppermute | solution.py:288
  18.2 0.0 collective-permute-start.13
  18.2 0.0 collective-permute-done.4.from_last.refs_6_
  18.2 2.4 %collective-permute-done.5.from_next.refs_7_ = f32[288,128]{1,0:T(8,128)S(1)} collective-permute-done((f32[288,128]{1,0:T(8,128)S(1)}, f32[288,128]{1,0:T(8,128)S(1)}, u32[]{:S(2)}, u32[]{:S(2)}) %collective-permute-start.5) | collective-permute-done | bytes 147488 | tf_op jit(solution)/shard_map/ppermute | solution.py:288
  20.6 0.1 first_next.1
  20.8 0.1 collective-permute-start.6
  20.8 3.3 %collective-permute-start.7 = (f32[200,128]{1,0:T(8,128)S(1)}, f32[200,128]{1,0:T(8,128)S(1)}, u32[]{:S(2)}, u32[]{:S(2)}) collective-permute-start(f32[200,128]{1,0:T(8,128)S(1)} %get-tuple-element.39.refs_0_.own_left), channel_id=1, source_target_pairs={{0,3},{1,0},{2,1},{3,2},{4,7},{5,4},{6,5},{7,6},{8,11},{9,8},{10,9... | collective-permute-start | bytes 307208 | tf_op jit(solution)/shard_map/ppermute | solution.py:288
  24.1 0.0 collective-permute-done.12.from_last.refs_6_
  24.1 0.0 collective-permute-done.13.from_next.refs_7_
  24.1 0.1 second_next.1
  24.2 0.1 collective-permute-start.14
  24.3 3.3 %collective-permute-start.15 = (f32[192,128]{1,0:T(8,128)S(1)}, f32[192,128]{1,0:T(8,128)S(1)}, u32[]{:S(2)}, u32[]{:S(2)}) collective-permute-start(f32[192,128]{1,0:T(8,128)S(1)} %get-tuple-element.49.refs_0_.own_left), channel_id=1, source_target_pairs={{0,3},{1,0},{2,1},{3,2},{4,7},{5,4},{6,5},{7,6},{8,11},{9,8},{10,9... | collective-permute-start | bytes 294920 | tf_op jit(solution)/shard_map/ppermute | solution.py:288
  27.5 0.5 %collective-permute-done.7.refs_3_ = f32[200,128]{1,0:T(8,128)S(1)} collective-permute-done((f32[200,128]{1,0:T(8,128)S(1)}, f32[200,128]{1,0:T(8,128)S(1)}, u32[]{:S(2)}, u32[]{:S(2)}) %collective-permute-start.7) | collective-permute-done | bytes 102432 | tf_op jit(solution)/shard_map/ppermute | solution.py:288
  28.1 0.0 collective-permute-done.6.refs_2_
  28.1 0.5 %first_share.3 = (f32[192,128]{1,0:T(8,128)S(1)}, f32[192,128]{1,0:T(8,128)S(1)}, f32[6,64,128]{2,1,0:T(8,128)S(1)}, bf16[2,384,384]{2,1,0:T(8,128)(2,1)S(1)}, bf16[2,192,384]{2,1,0:T(8,128)(2,1)S(1)}) custom-call(f32[200,128]{1,0:T(8,128)S(1)} %get-tuple-element.39.refs_0_.own_left, f32[208,128]{1,0:T(8,128)S(1)} %get-tuple-element.40.refs_1_.own_right, ...), custom_call_target="tpu_custom_call" | custom-call | bytes 1000000 | tf_op jit(solution)/shard_map/first_share/pallas_call | solution.py:329
  28.6 0.5 %collective-permute-start.8 = (f32[192,128]{1,0:T(8,128)S(1)}, f32[192,128]{1,0:T(8,128)S(1)}, u32[]{:S(2)}, u32[]{:S(2)}) collective-permute-start(f32[192,128]{1,0:T(8,128)S(1)} %get-tuple-element.42), channel_id=1, source_target_pairs={{0,4},{4,8},{8,12},{12,0},{1,5},{5,9},{9,13},{13,1},{2,6},{6,10},{... | collective-permute-start | bytes 294920 | tf_op jit(solution)/shard_map/ppermute | solution.py:288
  29.1 0.1 collective-permute-start.9
  29.2 2.9 %collective-permute-done.15.refs_3_ = f32[192,128]{1,0:T(8,128)S(1)} collective-permute-done((f32[192,128]{1,0:T(8,128)S(1)}, f32[192,128]{1,0:T(8,128)S(1)}, u32[]{:S(2)}, u32[]{:S(2)}) %collective-permute-start.15) | collective-permute-done | bytes 98336 | tf_op jit(solution)/shard_map/ppermute | solution.py:288
  32.1 0.0 collective-permute-done.14.refs_2_
  32.1 0.6 %second_share.3 = (f32[192,128]{1,0:T(8,128)S(1)}, f32[192,128]{1,0:T(8,128)S(1)}, f32[6,64,128]{2,1,0:T(8,128)S(1)}) custom-call(f32[192,128]{1,0:T(8,128)S(1)} %get-tuple-element.49.refs_0_.own_left, f32[200,128]{1,0:T(8,128)S(1)} %get-tuple-element.50.refs_1_.own_right, f32[200,128]{1,0:T(8,128)S(1)} %collective-permute-done.14.refs_2_, ...), custom_call_target="tpu_custom_call" | custom-call | bytes 1000000 | tf_op jit(solution)/shard_map/second_share/pallas_call | solution.py:329
  32.7 0.5 %collective-permute-start.16 = (f32[192,128]{1,0:T(8,128)S(1)}, f32[192,128]{1,0:T(8,128)S(1)}, u32[]{:S(2)}, u32[]{:S(2)}) collective-permute-start(f32[192,128]{1,0:T(8,128)S(1)} %get-tuple-element.54), channel_id=1, source_target_pairs={{0,4},{4,8},{8,12},{12,0},{1,5},{5,9},{9,13},{13,1},{2,6},{6,10},{... | collective-permute-start | bytes 294920 | tf_op jit(solution)/shard_map/ppermute | solution.py:288
  33.3 0.0 collective-permute-start.17
  33.3 0.0 collective-permute-done.8.from_last
  33.3 0.0 collective-permute-done.9.from_next
  33.3 0.9 %first_final.1._ = f32[8,4096]{1,0:T(8,128)} custom-call(f32[4,8,128]{2,1,0:T(8,128)S(1)} %get-tuple-element.29.idents, f32[200,128]{1,0:T(8,128)S(1)} %get-tuple-element.39.refs_0_.own_left, f32[208,128]{1,0:T(8,128)S(1)} %get-tuple-element.40.refs_1_.own_right, f32[6,64,128]{2,1,0:T(8,128)S(1)} %get-tuple-element.41.sums, ...), custom_call_target="tpu_custom_call" | custom-call | bytes 1000000 | tf_op jit(solution)/shard_map/first_final/pallas_call | solution.py:433
  34.2 0.7 %collective-permute-done.16.from_last = f32[192,128]{1,0:T(8,128)S(1)} collective-permute-done((f32[192,128]{1,0:T(8,128)S(1)}, f32[192,128]{1,0:T(8,128)S(1)}, u32[]{:S(2)}, u32[]{:S(2)}) %collective-permute-start.16) | collective-permute-done | bytes 98336 | tf_op jit(solution)/shard_map/ppermute | solution.py:288
  34.9 2.4 %collective-permute-done.17.from_next = f32[192,128]{1,0:T(8,128)S(1)} collective-permute-done((f32[192,128]{1,0:T(8,128)S(1)}, f32[192,128]{1,0:T(8,128)S(1)}, u32[]{:S(2)}, u32[]{:S(2)}) %collective-permute-start.17) | collective-permute-done | bytes 98336 | tf_op jit(solution)/shard_map/ppermute | solution.py:288
  37.3 0.9 %second_final.1 = f32[8,4096]{1,0:T(8,128)} custom-call(f32[4,8,128]{2,1,0:T(8,128)S(1)} %get-tuple-element.29.idents, f32[192,128]{1,0:T(8,128)S(1)} %get-tuple-element.49.refs_0_.own_left, f32[200,128]{1,0:T(8,128)S(1)} %get-tuple-element.50.refs_1_.own_right, f32[6,64,128]{2,1,0:T(8,128)S(1)} %get-tuple-element.53.sums, ...), custom_call_target="tpu_custom_call" | custom-call | bytes 1000000 | tf_op jit(solution)/shard_map/second_final/pallas_call | solution.py:433
Async XLA Ops:
  2.0 6.7 %collective-permute-start = (f32[192,128]{1,0:T(8,128)S(1)}, f32[192,128]{1,0:T(8,128)S(1)}, u32[]{:S(2)}, u32[]{:S(2)}) collective-permute-start(f32[192,128]{1,0:T(8,128)S(1)} %get-tuple-element.31.first_right.refs_1_), channel_id=1, source_target_pairs={{0,1},{1,2},{2,3},{3,0},{4,5},{5,6},{6,7},{7,4},{8,9},{9,10},{10,1... | collective-permute-start | bytes 294920 | tf_op jit(solution)/shard_map/ppermute | solution.py:288
  4.2 7.7 %collective-permute-start.1 = (f32[208,128]{1,0:T(8,128)S(1)}, f32[208,128]{1,0:T(8,128)S(1)}, u32[]{:S(2)}, u32[]{:S(2)}) collective-permute-start(f32[208,128]{1,0:T(8,128)S(1)} %get-tuple-element.30.first_left.refs_0_), channel_id=1, source_target_pairs={{0,3},{1,0},{2,1},{3,2},{4,7},{5,4},{6,5},{7,6},{8,11},{9,8},{10,9... | collective-permute-start | bytes 319496 | tf_op jit(solution)/shard_map/ppermute | solution.py:288
  6.4 5.5 %collective-permute-start.2 = (f32[208,128]{1,0:T(8,128)S(1)}, f32[208,128]{1,0:T(8,128)S(1)}, u32[]{:S(2)}, u32[]{:S(2)}) collective-permute-start(f32[208,128]{1,0:T(8,128)S(1)} %get-tuple-element.34), channel_id=1, source_target_pairs={{0,4},{4,8},{8,12},{12,0},{1,5},{5,9},{9,13},{13,1},{2,6},{6,10},{... | collective-permute-start | bytes 319496 | tf_op jit(solution)/shard_map/ppermute | solution.py:288
  8.6 4.1 %collective-permute-start.3 = (f32[208,128]{1,0:T(8,128)S(1)}, f32[208,128]{1,0:T(8,128)S(1)}, u32[]{:S(2)}, u32[]{:S(2)}) collective-permute-start(f32[208,128]{1,0:T(8,128)S(1)} %get-tuple-element.35), channel_id=1, source_target_pairs={{0,12},{4,0},{8,4},{12,8},{1,13},{5,1},{9,5},{13,9},{2,14},{6,2},{... | collective-permute-start | bytes 319496 | tf_op jit(solution)/shard_map/ppermute | solution.py:288
  8.6 6.2 %collective-permute-start.10 = (f32[200,128]{1,0:T(8,128)S(1)}, f32[200,128]{1,0:T(8,128)S(1)}, u32[]{:S(2)}, u32[]{:S(2)}) collective-permute-start(f32[200,128]{1,0:T(8,128)S(1)} %get-tuple-element.33.second_right.refs_1_), channel_id=1, source_target_pairs={{0,1},{1,2},{2,3},{3,0},{4,5},{5,6},{6,7},{7,4},{8,9},{9,10},{10,1... | collective-permute-start | bytes 307208 | tf_op jit(solution)/shard_map/ppermute | solution.py:288
  8.7 6.1 %collective-permute-start.11 = (f32[192,128]{1,0:T(8,128)S(1)}, f32[192,128]{1,0:T(8,128)S(1)}, u32[]{:S(2)}, u32[]{:S(2)}) collective-permute-start(f32[192,128]{1,0:T(8,128)S(1)} %get-tuple-element.32.second_left.refs_0_), channel_id=1, source_target_pairs={{0,3},{1,0},{2,1},{3,2},{4,7},{5,4},{6,5},{7,6},{8,11},{9,8},{10,9... | collective-permute-start | bytes 294920 | tf_op jit(solution)/shard_map/ppermute | solution.py:288
  13.2 5.0 %collective-permute-start.4 = (f32[288,128]{1,0:T(8,128)S(1)}, f32[288,128]{1,0:T(8,128)S(1)}, u32[]{:S(2)}, u32[]{:S(2)}) collective-permute-start(f32[288,128]{1,0:T(8,128)S(1)} %get-tuple-element.37.refs_9_), channel_id=1, source_target_pairs={{0,4},{4,8},{8,12},{12,0},{1,5},{5,9},{9,13},{13,1},{2,6},{6,10},{... | collective-permute-start | bytes 442376 | tf_op jit(solution)/shard_map/ppermute | solution.py:288
  14.8 5.8 %collective-permute-start.5 = (f32[288,128]{1,0:T(8,128)S(1)}, f32[288,128]{1,0:T(8,128)S(1)}, u32[]{:S(2)}, u32[]{:S(2)}) collective-permute-start(f32[288,128]{1,0:T(8,128)S(1)} %get-tuple-element.38.refs_8_), channel_id=1, source_target_pairs={{0,12},{4,0},{8,4},{12,8},{1,13},{5,1},{9,5},{13,9},{2,14},{6,2},{... | collective-permute-start | bytes 442376 | tf_op jit(solution)/shard_map/ppermute | solution.py:288
  15.5 8.6 %collective-permute-start.12 = (f32[288,128]{1,0:T(8,128)S(1)}, f32[288,128]{1,0:T(8,128)S(1)}, u32[]{:S(2)}, u32[]{:S(2)}) collective-permute-start(f32[288,128]{1,0:T(8,128)S(1)} %get-tuple-element.47.refs_9_), channel_id=1, source_target_pairs={{0,4},{4,8},{8,12},{12,0},{1,5},{5,9},{9,13},{13,1},{2,6},{6,10},{... | collective-permute-start | bytes 442376 | tf_op jit(solution)/shard_map/ppermute | solution.py:288
  18.2 5.9 %collective-permute-start.13 = (f32[288,128]{1,0:T(8,128)S(1)}, f32[288,128]{1,0:T(8,128)S(1)}, u32[]{:S(2)}, u32[]{:S(2)}) collective-permute-start(f32[288,128]{1,0:T(8,128)S(1)} %get-tuple-element.48.refs_8_), channel_id=1, source_target_pairs={{0,12},{4,0},{8,4},{12,8},{1,13},{5,1},{9,5},{13,9},{2,14},{6,2},{... | collective-permute-start | bytes 442376 | tf_op jit(solution)/shard_map/ppermute | solution.py:288
  20.8 7.3 %collective-permute-start.6 = (f32[208,128]{1,0:T(8,128)S(1)}, f32[208,128]{1,0:T(8,128)S(1)}, u32[]{:S(2)}, u32[]{:S(2)}) collective-permute-start(f32[208,128]{1,0:T(8,128)S(1)} %get-tuple-element.40.refs_1_.own_right), channel_id=1, source_target_pairs={{0,1},{1,2},{2,3},{3,0},{4,5},{5,6},{6,7},{7,4},{8,9},{9,10},{10,1... | collective-permute-start | bytes 319496 | tf_op jit(solution)/shard_map/ppermute | solution.py:288
  20.8 7.2 %collective-permute-start.7 = (f32[200,128]{1,0:T(8,128)S(1)}, f32[200,128]{1,0:T(8,128)S(1)}, u32[]{:S(2)}, u32[]{:S(2)}) collective-permute-start(f32[200,128]{1,0:T(8,128)S(1)} %get-tuple-element.39.refs_0_.own_left), channel_id=1, source_target_pairs={{0,3},{1,0},{2,1},{3,2},{4,7},{5,4},{6,5},{7,6},{8,11},{9,8},{10,9... | collective-permute-start | bytes 307208 | tf_op jit(solution)/shard_map/ppermute | solution.py:288
  24.2 7.9 %collective-permute-start.14 = (f32[200,128]{1,0:T(8,128)S(1)}, f32[200,128]{1,0:T(8,128)S(1)}, u32[]{:S(2)}, u32[]{:S(2)}) collective-permute-start(f32[200,128]{1,0:T(8,128)S(1)} %get-tuple-element.50.refs_1_.own_right), channel_id=1, source_target_pairs={{0,1},{1,2},{2,3},{3,0},{4,5},{5,6},{6,7},{7,4},{8,9},{9,10},{10,1... | collective-permute-start | bytes 307208 | tf_op jit(solution)/shard_map/ppermute | solution.py:288
  24.3 7.8 %collective-permute-start.15 = (f32[192,128]{1,0:T(8,128)S(1)}, f32[192,128]{1,0:T(8,128)S(1)}, u32[]{:S(2)}, u32[]{:S(2)}) collective-permute-start(f32[192,128]{1,0:T(8,128)S(1)} %get-tuple-element.49.refs_0_.own_left), channel_id=1, source_target_pairs={{0,3},{1,0},{2,1},{3,2},{4,7},{5,4},{6,5},{7,6},{8,11},{9,8},{10,9... | collective-permute-start | bytes 294920 | tf_op jit(solution)/shard_map/ppermute | solution.py:288
  28.6 4.7 %collective-permute-start.8 = (f32[192,128]{1,0:T(8,128)S(1)}, f32[192,128]{1,0:T(8,128)S(1)}, u32[]{:S(2)}, u32[]{:S(2)}) collective-permute-start(f32[192,128]{1,0:T(8,128)S(1)} %get-tuple-element.42), channel_id=1, source_target_pairs={{0,4},{4,8},{8,12},{12,0},{1,5},{5,9},{9,13},{13,1},{2,6},{6,10},{... | collective-permute-start | bytes 294920 | tf_op jit(solution)/shard_map/ppermute | solution.py:288
  29.1 4.2 %collective-permute-start.9 = (f32[192,128]{1,0:T(8,128)S(1)}, f32[192,128]{1,0:T(8,128)S(1)}, u32[]{:S(2)}, u32[]{:S(2)}) collective-permute-start(f32[192,128]{1,0:T(8,128)S(1)} %get-tuple-element.43), channel_id=1, source_target_pairs={{0,12},{4,0},{8,4},{12,8},{1,13},{5,1},{9,5},{13,9},{2,14},{6,2},{... | collective-permute-start | bytes 294920 | tf_op jit(solution)/shard_map/ppermute | solution.py:288
  32.7 2.2 %collective-permute-start.16 = (f32[192,128]{1,0:T(8,128)S(1)}, f32[192,128]{1,0:T(8,128)S(1)}, u32[]{:S(2)}, u32[]{:S(2)}) collective-permute-start(f32[192,128]{1,0:T(8,128)S(1)} %get-tuple-element.54), channel_id=1, source_target_pairs={{0,4},{4,8},{8,12},{12,0},{1,5},{5,9},{9,13},{13,1},{2,6},{6,10},{... | collective-permute-start | bytes 294920 | tf_op jit(solution)/shard_map/ppermute | solution.py:288
  33.3 4.0 %collective-permute-start.17 = (f32[192,128]{1,0:T(8,128)S(1)}, f32[192,128]{1,0:T(8,128)S(1)}, u32[]{:S(2)}, u32[]{:S(2)}) collective-permute-start(f32[192,128]{1,0:T(8,128)S(1)} %get-tuple-element.55), channel_id=1, source_target_pairs={{0,12},{4,0},{8,4},{12,8},{1,13},{5,1},{9,5},{13,9},{2,14},{6,2},{... | collective-permute-start | bytes 294920 | tf_op jit(solution)/shard_map/ppermute | solution.py:288

commit v7 on v6

--- a/solution.py
+++ b/solution.py
@@ -13,6 +13,7 @@
 DEPTH = 3 * BLOCK
 ASK_ROWS = BLOCK + HALF
 PADS = (16, 0, 0, 8, 8, 16, 0, 8)
+NEAR_PAD = 8
 F32 = jnp.float32
 BF16 = jnp.bfloat16
 VMEM_LIMIT = 16 * 1024 * 1024
@@ -113,14 +114,26 @@
         spread(which, slots, datas[which], *pair, rows.at[which], table)
 
 
-def ask_kernel(slots, first_left, first_right, second_left, second_right, idents, ask_last, ask_next):
+def is_even():
+    return lax.rem(lax.axis_index("row"), 2) == 0
+
+
+def ask_kernel(slots, first_left, first_right, second_left, second_right, idents, far, near):
+    even = is_even()
     for which, (left, right) in enumerate(((first_left, first_right), (second_left, second_right))):
         at = which * ASK_ROWS
-        for ask, e in ((ask_last, 0), (ask_next, 2)):
-            ask[at : at + BLOCK, :] = left[tile_at(e)]
-            ask[at + BLOCK : at + ASK_ROWS, :] = fold(right[tile_at(e)])
-            masks = 2 * ASK_ROWS + slots * which
-            ask[masks : masks + slots, :] = idents[which]
+        last, following = left[tile_at(0)], left[tile_at(2)]
+        near[at : at + BLOCK, :] = jnp.where(even, following, last)
+        far[at : at + BLOCK, :] = jnp.where(even, last, following)
+        last, following = fold(right[tile_at(0)]), fold(right[tile_at(2)])
+        near[at + BLOCK : at + ASK_ROWS, :] = jnp.where(even, following, last)
+        far[at + BLOCK : at + ASK_ROWS, :] = jnp.where(even, last, following)
+        masks = 2 * ASK_ROWS + slots * which
+        near[masks : masks + slots, :] = idents[which]
+        far[masks : masks + slots, :] = idents[which]
+    rest = 2 * (ASK_ROWS + slots)
+    if near.shape[0] > rest:
+        near[rest:, :] = jnp.zeros((near.shape[0] - rest, WIDE), F32)
 
 
 def fold(right):
@@ -200,18 +213,24 @@
 
 
 def fill_asked(which, grid, slots, asks, got, sent, factor):
+    far, near = asks
+    even = is_even()
     for at in range(2):
+        from_far = even if at == 0 else jnp.logical_not(even)
+
+        def asked(start, count):
+            return jnp.where(from_far, far[start : start + count], near[start : start + count])
+
         if got is None:
             row = which * ASK_ROWS
-            left, folded = asks[at][row : row + BLOCK], asks[at][row + BLOCK : row + ASK_ROWS]
+            left, folded = asked(row, BLOCK), asked(row + BLOCK, HALF)
         else:
             pack = sent[at][WIDE:DEPTH]
             if at == 0:
                 left, folded = sent[at][BLOCK:WIDE], fold(pack)
             else:
                 left, folded = sent[at][:BLOCK], jnp.where(on_left(HALF), pack[:HALF], swap(pack[HALF:]))
-            row = 2 * ASK_ROWS + slots * which
-            idents = asks[at][row : row + slots]
+            idents = asked(2 * ASK_ROWS + slots * which, slots)
             left = jnp.where(is_live(idents, pair_at(3, 4, grid)), left + got[at][DEPTH : DEPTH + BLOCK], 0.0)
             folded = jnp.where(is_live(idents, ident_at(5, grid)), folded + got[at][DEPTH + BLOCK :], 0.0)
         fill_left_factor(at, left, unfold(left, folded), factor)
@@ -335,6 +354,12 @@
 
 def along_row(to_last, to_next):
     return shift(to_next, "row", 1), shift(to_last, "row", -1)
+
+
+def in_pairs(far, near):
+    rows = lax.axis_size("row")
+    far = lax.ppermute(far, "row", [(i, (((i + 1) ^ 1) - 1) % rows) for i in range(rows)])
+    return far, lax.ppermute(near, "row", [(i, i ^ 1) for i in range(rows)])
 
 
 def shards(
@@ -402,10 +427,10 @@
         return (first_sums, *first_got), (second_sums, *second_got), first_sent, second_sent
 
     first = along_col(*tiles[:2])
-    asks = along_row(
+    asks = in_pairs(
         *call_all(
             functools.partial(ask_kernel, slots),
-            [shape(2 * (ASK_ROWS + slots), WIDE)] * 2,
+            [shape(2 * (ASK_ROWS + slots) + rest, WIDE) for rest in (0, NEAR_PAD)],
             (*tiles, idents),
             [],
             "ask",

time: 38.3 us -> 37.8 us (0.987)
  waiting for transfers between devices: 9.99 us -> 7.52 us
  starting transfers between devices: 21.8 us -> 23.8 us
    ppermute x0 -> x2, starting transfers between devices: none -> 2.67 us  [the longest x1 1.65 us: in_pairs(): lax.ppermute(far, 'row', [(i, ((i + 1 ^ 1) - 1) % rows) for i in range(ro...]
    ppermute x18 -> x16, waiting for transfers between devices: 9.99 us -> 7.51 us  [shift(): lax.ppermute(block, axis, [(i, (i + by) % count) for i in range(count)])]
    ppermute x18 -> x16, starting transfers between devices: 21.8 us -> 21.2 us  [shift(): lax.ppermute(block, axis, [(i, (i + by) % count) for i in range(count)])]
  transfers between devices with their start and end apart: 18 -> 18, of which waited for: 7 -> 6; matrix products, arithmetic and copies ran while one was open for 0% -> 0% of each run, Pallas kernels for 9% -> 9%
where the time goes in v7:
time: 37.8 us; the launch traced here: 37.7 us
  starting transfers between devices  23.8 us (63%)
  waiting for transfers between devices  7.52 us (20%)
  Pallas kernels  5.64 us (15%)
  between operations  0.71 us (2%)
    ppermute x16, starting transfers between devices, shift(): lax.ppermute(block, axis, [(i, (i + by) % count) for i in range(count)])  21.2 us
    ppermute x16, waiting for transfers between devices, shift(): lax.ppermute(block, axis, [(i, (i + by) % count) for i in range(count)])  7.51 us
    pallas_call x7, Pallas kernels, call_all(): call(kernel, outputs, [VM] * len(operands), [VM] * len(outputs), scratch,...  2.55 us
    pallas_call x2, Pallas kernels, final_of(): call(kernel, shape(slots, BLOCK * BLOCK), [VM] * 6 + [HB], VM, scratch, n...  1.74 us
    ppermute x1, starting transfers between devices, in_pairs(): lax.ppermute(far, 'row', [(i, ((i + 1 ^ 1) - 1) % rows) for i in range(ro...  1.65 us
    pallas_call x1, Pallas kernels, shards(): call(functools.partial(spread_kernel, grid, slots), [tiles_shape(r) for r...  1.35 us
    ppermute x1, starting transfers between devices, in_pairs(): return (far, lax.ppermute(near, 'row', [(i, i ^ 1) for i in range(rows)]))  1.02 us
  transfers between devices with their start and end apart: 18, of which 6 were waited for; matrix products, arithmetic and copies ran while one was open for 0% of the time, Pallas kernels for 9%

profile of v7, /device:TPU:1, one launch (start us, length us, event | category | flops | bytes accessed | tf_op | source)
XLA Modules:
  0.0 37.7 jit_solution(12297774691022543871)
XLA Ops:
  0.6 1.4 %spread.1 = (f32[208,128]{1,0:T(8,128)S(1)}, f32[192,128]{1,0:T(8,128)S(1)}, f32[192,128]{1,0:T(8,128)S(1)}, f32[200,128]{1,0:T(8,128)S(1)}, f32[4,8,128]{2,1,0:T(8,128)S(1)}) custom-call(s32[1,8]{1,0:T(1,128)} %bitcast.15, s32[1,8]{1,0:T(1,128)} %bitcast.16, f32[8,4096]{1,0:T(8,128)} %bitcast.10, f32[8,4096]{1,0:T(8,128)} %bitcast.13, s32[1,8]{1,0:T(1,128)} %bitcast.17, ...), custom_call_target="tpu_custom_call" | custom-call | bytes 1000000 | tf_op jit(solution)/shard_map/spread/pallas_call | solution.py:386
  2.0 2.2 %collective-permute-start = (f32[192,128]{1,0:T(8,128)S(1)}, f32[192,128]{1,0:T(8,128)S(1)}, u32[]{:S(2)}, u32[]{:S(2)}) collective-permute-start(f32[192,128]{1,0:T(8,128)S(1)} %get-tuple-element.31.first_right.refs_1_), channel_id=1, source_target_pairs={{0,1},{1,2},{2,3},{3,0},{4,5},{5,6},{6,7},{7,4},{8,9},{9,10},{10,1... | collective-permute-start | bytes 294920 | tf_op jit(solution)/shard_map/ppermute | solution.py:307
  4.2 0.1 ask.1
  4.3 1.0 %collective-permute-start.3 = (f32[216,128]{1,0:T(8,128)S(1)}, f32[216,128]{1,0:T(8,128)S(1)}, u32[]{:S(2)}, u32[]{:S(2)}) collective-permute-start(f32[216,128]{1,0:T(8,128)S(1)} %get-tuple-element.35), channel_id=1, source_target_pairs={{0,4},{4,0},{8,12},{12,8},{1,5},{5,1},{9,13},{13,9},{2,6},{6,2},{1... | collective-permute-start | bytes 331784 | tf_op jit(solution)/shard_map/ppermute | solution.py:362
  5.3 1.8 %collective-permute-start.1 = (f32[208,128]{1,0:T(8,128)S(1)}, f32[208,128]{1,0:T(8,128)S(1)}, u32[]{:S(2)}, u32[]{:S(2)}) collective-permute-start(f32[208,128]{1,0:T(8,128)S(1)} %get-tuple-element.30.first_left.refs_0_), channel_id=1, source_target_pairs={{0,3},{1,0},{2,1},{3,2},{4,7},{5,4},{6,5},{7,6},{8,11},{9,8},{10,9... | collective-permute-start | bytes 319496 | tf_op jit(solution)/shard_map/ppermute | solution.py:307
  7.0 1.7 %collective-permute-start.2 = (f32[208,128]{1,0:T(8,128)S(1)}, f32[208,128]{1,0:T(8,128)S(1)}, u32[]{:S(2)}, u32[]{:S(2)}) collective-permute-start(f32[208,128]{1,0:T(8,128)S(1)} %get-tuple-element.34), channel_id=1, source_target_pairs={{0,12},{4,8},{8,4},{12,0},{1,13},{5,9},{9,5},{13,1},{2,14},{6,10},... | collective-permute-start | bytes 319496 | tf_op jit(solution)/shard_map/ppermute | solution.py:361
  8.7 0.0 collective-permute-start.10
  8.7 0.0 collective-permute-done.refs_2_
  8.7 3.2 %collective-permute-start.11 = (f32[192,128]{1,0:T(8,128)S(1)}, f32[192,128]{1,0:T(8,128)S(1)}, u32[]{:S(2)}, u32[]{:S(2)}) collective-permute-start(f32[192,128]{1,0:T(8,128)S(1)} %get-tuple-element.32.second_left.refs_0_), channel_id=1, source_target_pairs={{0,3},{1,0},{2,1},{3,2},{4,7},{5,4},{6,5},{7,6},{8,11},{9,8},{10,9... | collective-permute-start | bytes 294920 | tf_op jit(solution)/shard_map/ppermute | solution.py:307
  12.0 0.0 collective-permute-done.1.refs_3_
  12.0 0.0 collective-permute-done.2.refs_4_
  12.0 0.0 collective-permute-done.3.refs_5_
  12.0 0.5 %first_share.2 = (f32[288,128]{1,0:T(8,128)S(1)}, f32[288,128]{1,0:T(8,128)S(1)}, f32[6,64,128]{2,1,0:T(8,128)S(1)}, bf16[2,384,384]{2,1,0:T(8,128)(2,1)S(1)}, bf16[2,192,384]{2,1,0:T(8,128)(2,1)S(1)}) custom-call(f32[208,128]{1,0:T(8,128)S(1)} %get-tuple-element.30.first_left.refs_0_, f32[192,128]{1,0:T(8,128)S(1)} %get-tuple-element.31.first_right.refs_1_, ...), custom_call_target="tpu_custom_call" | custom-call | bytes 1000000 | tf_op jit(solution)/shard_map/first_share/pallas_call | solution.py:348
  12.4 1.7 %collective-permute-start.4 = (f32[288,128]{1,0:T(8,128)S(1)}, f32[288,128]{1,0:T(8,128)S(1)}, u32[]{:S(2)}, u32[]{:S(2)}) collective-permute-start(f32[288,128]{1,0:T(8,128)S(1)} %get-tuple-element.37.refs_9_), channel_id=1, source_target_pairs={{0,4},{4,8},{8,12},{12,0},{1,5},{5,9},{9,13},{13,1},{2,6},{6,10},{... | collective-permute-start | bytes 442376 | tf_op jit(solution)/shard_map/ppermute | solution.py:307
  14.1 0.0 collective-permute-start.5
  14.1 0.0 collective-permute-done.11.refs_3_
  14.2 0.7 %collective-permute-done.10.refs_2_ = f32[200,128]{1,0:T(8,128)S(1)} collective-permute-done((f32[200,128]{1,0:T(8,128)S(1)}, f32[200,128]{1,0:T(8,128)S(1)}, u32[]{:S(2)}, u32[]{:S(2)}) %collective-permute-start.10) | collective-permute-done | bytes 102432 | tf_op jit(solution)/shard_map/ppermute | solution.py:307
  14.9 0.6 %second_share.2 = (f32[288,128]{1,0:T(8,128)S(1)}, f32[288,128]{1,0:T(8,128)S(1)}, f32[6,64,128]{2,1,0:T(8,128)S(1)}) custom-call(f32[192,128]{1,0:T(8,128)S(1)} %get-tuple-element.32.second_left.refs_0_, f32[200,128]{1,0:T(8,128)S(1)} %get-tuple-element.33.second_right.refs_1_, f32[200,128]{1,0:T(8,128)S(1)} %collective-permute-done.10.refs_2_, ...), custom_call_target="tpu_custom_call" | custom-call | bytes 1000000 | tf_op jit(solution)/shard_map/second_share/pallas_call | solution.py:348
  15.5 2.8 %collective-permute-start.12 = (f32[288,128]{1,0:T(8,128)S(1)}, f32[288,128]{1,0:T(8,128)S(1)}, u32[]{:S(2)}, u32[]{:S(2)}) collective-permute-start(f32[288,128]{1,0:T(8,128)S(1)} %get-tuple-element.47.refs_9_), channel_id=1, source_target_pairs={{0,4},{4,8},{8,12},{12,0},{1,5},{5,9},{9,13},{13,1},{2,6},{6,10},{... | collective-permute-start | bytes 442376 | tf_op jit(solution)/shard_map/ppermute | solution.py:307
  18.3 0.0 collective-permute-start.13
  18.3 0.0 collective-permute-done.4.from_last.refs_6_
  18.3 0.4 %collective-permute-done.5.from_next.refs_7_ = f32[288,128]{1,0:T(8,128)S(1)} collective-permute-done((f32[288,128]{1,0:T(8,128)S(1)}, f32[288,128]{1,0:T(8,128)S(1)}, u32[]{:S(2)}, u32[]{:S(2)}) %collective-permute-start.5) | collective-permute-done | bytes 147488 | tf_op jit(solution)/shard_map/ppermute | solution.py:307
  18.7 0.1 first_next.1
  18.8 0.1 collective-permute-start.6
  18.9 3.2 %collective-permute-start.7 = (f32[200,128]{1,0:T(8,128)S(1)}, f32[200,128]{1,0:T(8,128)S(1)}, u32[]{:S(2)}, u32[]{:S(2)}) collective-permute-start(f32[200,128]{1,0:T(8,128)S(1)} %get-tuple-element.39.refs_0_.own_left), channel_id=1, source_target_pairs={{0,3},{1,0},{2,1},{3,2},{4,7},{5,4},{6,5},{7,6},{8,11},{9,8},{10,9... | collective-permute-start | bytes 307208 | tf_op jit(solution)/shard_map/ppermute | solution.py:307
  22.1 0.0 collective-permute-done.12.from_last.refs_6_
  22.1 1.2 %collective-permute-done.13.from_next.refs_7_ = f32[288,128]{1,0:T(8,128)S(1)} collective-permute-done((f32[288,128]{1,0:T(8,128)S(1)}, f32[288,128]{1,0:T(8,128)S(1)}, u32[]{:S(2)}, u32[]{:S(2)}) %collective-permute-start.13) | collective-permute-done | bytes 147488 | tf_op jit(solution)/shard_map/ppermute | solution.py:307
  23.3 0.1 second_next.1
  23.4 0.2 collective-permute-start.14
  23.7 3.1 %collective-permute-start.15 = (f32[192,128]{1,0:T(8,128)S(1)}, f32[192,128]{1,0:T(8,128)S(1)}, u32[]{:S(2)}, u32[]{:S(2)}) collective-permute-start(f32[192,128]{1,0:T(8,128)S(1)} %get-tuple-element.49.refs_0_.own_left), channel_id=1, source_target_pairs={{0,3},{1,0},{2,1},{3,2},{4,7},{5,4},{6,5},{7,6},{8,11},{9,8},{10,9... | collective-permute-start | bytes 294920 | tf_op jit(solution)/shard_map/ppermute | solution.py:307
  26.7 0.0 collective-permute-done.7.refs_3_
  26.8 0.0 collective-permute-done.6.refs_2_
  26.8 0.5 %first_share.3 = (f32[192,128]{1,0:T(8,128)S(1)}, f32[192,128]{1,0:T(8,128)S(1)}, f32[6,64,128]{2,1,0:T(8,128)S(1)}, bf16[2,384,384]{2,1,0:T(8,128)(2,1)S(1)}, bf16[2,192,384]{2,1,0:T(8,128)(2,1)S(1)}) custom-call(f32[200,128]{1,0:T(8,128)S(1)} %get-tuple-element.39.refs_0_.own_left, f32[208,128]{1,0:T(8,128)S(1)} %get-tuple-element.40.refs_1_.own_right, ...), custom_call_target="tpu_custom_call" | custom-call | bytes 1000000 | tf_op jit(solution)/shard_map/first_share/pallas_call | solution.py:348
  27.3 1.4 %collective-permute-start.8 = (f32[192,128]{1,0:T(8,128)S(1)}, f32[192,128]{1,0:T(8,128)S(1)}, u32[]{:S(2)}, u32[]{:S(2)}) collective-permute-start(f32[192,128]{1,0:T(8,128)S(1)} %get-tuple-element.42), channel_id=1, source_target_pairs={{0,4},{4,8},{8,12},{12,0},{1,5},{5,9},{9,13},{13,1},{2,6},{6,10},{... | collective-permute-start | bytes 294920 | tf_op jit(solution)/shard_map/ppermute | solution.py:307
  28.6 0.0 collective-permute-start.9
  28.6 2.0 %collective-permute-done.15.refs_3_ = f32[192,128]{1,0:T(8,128)S(1)} collective-permute-done((f32[192,128]{1,0:T(8,128)S(1)}, f32[192,128]{1,0:T(8,128)S(1)}, u32[]{:S(2)}, u32[]{:S(2)}) %collective-permute-start.15) | collective-permute-done | bytes 98336 | tf_op jit(solution)/shard_map/ppermute | solution.py:307
  30.7 0.0 collective-permute-done.14.refs_2_
  30.7 0.6 %second_share.3 = (f32[192,128]{1,0:T(8,128)S(1)}, f32[192,128]{1,0:T(8,128)S(1)}, f32[6,64,128]{2,1,0:T(8,128)S(1)}) custom-call(f32[192,128]{1,0:T(8,128)S(1)} %get-tuple-element.49.refs_0_.own_left, f32[200,128]{1,0:T(8,128)S(1)} %get-tuple-element.50.refs_1_.own_right, f32[200,128]{1,0:T(8,128)S(1)} %collective-permute-done.14.refs_2_, ...), custom_call_target="tpu_custom_call" | custom-call | bytes 1000000 | tf_op jit(solution)/shard_map/second_share/pallas_call | solution.py:348
  31.3 1.5 %collective-permute-start.16 = (f32[192,128]{1,0:T(8,128)S(1)}, f32[192,128]{1,0:T(8,128)S(1)}, u32[]{:S(2)}, u32[]{:S(2)}) collective-permute-start(f32[192,128]{1,0:T(8,128)S(1)} %get-tuple-element.54), channel_id=1, source_target_pairs={{0,4},{4,8},{8,12},{12,0},{1,5},{5,9},{9,13},{13,1},{2,6},{6,10},{... | collective-permute-start | bytes 294920 | tf_op jit(solution)/shard_map/ppermute | solution.py:307
  32.8 0.0 collective-permute-start.17
  32.8 0.0 collective-permute-done.8.from_last
  32.8 0.0 collective-permute-done.9.from_next
  32.8 0.9 %first_final.1._ = f32[8,4096]{1,0:T(8,128)} custom-call(f32[4,8,128]{2,1,0:T(8,128)S(1)} %get-tuple-element.29.idents, f32[200,128]{1,0:T(8,128)S(1)} %get-tuple-element.39.refs_0_.own_left, f32[208,128]{1,0:T(8,128)S(1)} %get-tuple-element.40.refs_1_.own_right, f32[6,64,128]{2,1,0:T(8,128)S(1)} %get-tuple-element.41.sums, ...), custom_call_target="tpu_custom_call" | custom-call | bytes 1000000 | tf_op jit(solution)/shard_map/first_final/pallas_call | solution.py:458
  33.7 0.8 %collective-permute-done.16.from_last = f32[192,128]{1,0:T(8,128)S(1)} collective-permute-done((f32[192,128]{1,0:T(8,128)S(1)}, f32[192,128]{1,0:T(8,128)S(1)}, u32[]{:S(2)}, u32[]{:S(2)}) %collective-permute-start.16) | collective-permute-done | bytes 98336 | tf_op jit(solution)/shard_map/ppermute | solution.py:307
  34.4 2.4 %collective-permute-done.17.from_next = f32[192,128]{1,0:T(8,128)S(1)} collective-permute-done((f32[192,128]{1,0:T(8,128)S(1)}, f32[192,128]{1,0:T(8,128)S(1)}, u32[]{:S(2)}, u32[]{:S(2)}) %collective-permute-start.17) | collective-permute-done | bytes 98336 | tf_op jit(solution)/shard_map/ppermute | solution.py:307
  36.8 0.9 %second_final.1 = f32[8,4096]{1,0:T(8,128)} custom-call(f32[4,8,128]{2,1,0:T(8,128)S(1)} %get-tuple-element.29.idents, f32[192,128]{1,0:T(8,128)S(1)} %get-tuple-element.49.refs_0_.own_left, f32[200,128]{1,0:T(8,128)S(1)} %get-tuple-element.50.refs_1_.own_right, f32[6,64,128]{2,1,0:T(8,128)S(1)} %get-tuple-element.53.sums, ...), custom_call_target="tpu_custom_call" | custom-call | bytes 1000000 | tf_op jit(solution)/shard_map/second_final/pallas_call | solution.py:458
Async XLA Ops:
  2.0 6.7 %collective-permute-start = (f32[192,128]{1,0:T(8,128)S(1)}, f32[192,128]{1,0:T(8,128)S(1)}, u32[]{:S(2)}, u32[]{:S(2)}) collective-permute-start(f32[192,128]{1,0:T(8,128)S(1)} %get-tuple-element.31.first_right.refs_1_), channel_id=1, source_target_pairs={{0,1},{1,2},{2,3},{3,0},{4,5},{5,6},{6,7},{7,4},{8,9},{9,10},{10,1... | collective-permute-start | bytes 294920 | tf_op jit(solution)/shard_map/ppermute | solution.py:307
  4.3 7.7 %collective-permute-start.3 = (f32[216,128]{1,0:T(8,128)S(1)}, f32[216,128]{1,0:T(8,128)S(1)}, u32[]{:S(2)}, u32[]{:S(2)}) collective-permute-start(f32[216,128]{1,0:T(8,128)S(1)} %get-tuple-element.35), channel_id=1, source_target_pairs={{0,4},{4,0},{8,12},{12,8},{1,5},{5,1},{9,13},{13,9},{2,6},{6,2},{1... | collective-permute-start | bytes 331784 | tf_op jit(solution)/shard_map/ppermute | solution.py:362
  5.3 6.7 %collective-permute-start.1 = (f32[208,128]{1,0:T(8,128)S(1)}, f32[208,128]{1,0:T(8,128)S(1)}, u32[]{:S(2)}, u32[]{:S(2)}) collective-permute-start(f32[208,128]{1,0:T(8,128)S(1)} %get-tuple-element.30.first_left.refs_0_), channel_id=1, source_target_pairs={{0,3},{1,0},{2,1},{3,2},{4,7},{5,4},{6,5},{7,6},{8,11},{9,8},{10,9... | collective-permute-start | bytes 319496 | tf_op jit(solution)/shard_map/ppermute | solution.py:307
  7.0 4.9 %collective-permute-start.2 = (f32[208,128]{1,0:T(8,128)S(1)}, f32[208,128]{1,0:T(8,128)S(1)}, u32[]{:S(2)}, u32[]{:S(2)}) collective-permute-start(f32[208,128]{1,0:T(8,128)S(1)} %get-tuple-element.34), channel_id=1, source_target_pairs={{0,12},{4,8},{8,4},{12,0},{1,13},{5,9},{9,5},{13,1},{2,14},{6,10},... | collective-permute-start | bytes 319496 | tf_op jit(solution)/shard_map/ppermute | solution.py:361
  8.7 6.2 %collective-permute-start.10 = (f32[200,128]{1,0:T(8,128)S(1)}, f32[200,128]{1,0:T(8,128)S(1)}, u32[]{:S(2)}, u32[]{:S(2)}) collective-permute-start(f32[200,128]{1,0:T(8,128)S(1)} %get-tuple-element.33.second_right.refs_1_), channel_id=1, source_target_pairs={{0,1},{1,2},{2,3},{3,0},{4,5},{5,6},{6,7},{7,4},{8,9},{9,10},{10,1... | collective-permute-start | bytes 307208 | tf_op jit(solution)/shard_map/ppermute | solution.py:307
  8.7 5.4 %collective-permute-start.11 = (f32[192,128]{1,0:T(8,128)S(1)}, f32[192,128]{1,0:T(8,128)S(1)}, u32[]{:S(2)}, u32[]{:S(2)}) collective-permute-start(f32[192,128]{1,0:T(8,128)S(1)} %get-tuple-element.32.second_left.refs_0_), channel_id=1, source_target_pairs={{0,3},{1,0},{2,1},{3,2},{4,7},{5,4},{6,5},{7,6},{8,11},{9,8},{10,9... | collective-permute-start | bytes 294920 | tf_op jit(solution)/shard_map/ppermute | solution.py:307
  12.4 5.9 %collective-permute-start.4 = (f32[288,128]{1,0:T(8,128)S(1)}, f32[288,128]{1,0:T(8,128)S(1)}, u32[]{:S(2)}, u32[]{:S(2)}) collective-permute-start(f32[288,128]{1,0:T(8,128)S(1)} %get-tuple-element.37.refs_9_), channel_id=1, source_target_pairs={{0,4},{4,8},{8,12},{12,0},{1,5},{5,9},{9,13},{13,1},{2,6},{6,10},{... | collective-permute-start | bytes 442376 | tf_op jit(solution)/shard_map/ppermute | solution.py:307
  14.1 4.6 %collective-permute-start.5 = (f32[288,128]{1,0:T(8,128)S(1)}, f32[288,128]{1,0:T(8,128)S(1)}, u32[]{:S(2)}, u32[]{:S(2)}) collective-permute-start(f32[288,128]{1,0:T(8,128)S(1)} %get-tuple-element.38.refs_8_), channel_id=1, source_target_pairs={{0,12},{4,0},{8,4},{12,8},{1,13},{5,1},{9,5},{13,9},{2,14},{6,2},{... | collective-permute-start | bytes 442376 | tf_op jit(solution)/shard_map/ppermute | solution.py:307
  15.5 6.6 %collective-permute-start.12 = (f32[288,128]{1,0:T(8,128)S(1)}, f32[288,128]{1,0:T(8,128)S(1)}, u32[]{:S(2)}, u32[]{:S(2)}) collective-permute-start(f32[288,128]{1,0:T(8,128)S(1)} %get-tuple-element.47.refs_9_), channel_id=1, source_target_pairs={{0,4},{4,8},{8,12},{12,0},{1,5},{5,9},{9,13},{13,1},{2,6},{6,10},{... | collective-permute-start | bytes 442376 | tf_op jit(solution)/shard_map/ppermute | solution.py:307
  18.3 5.0 %collective-permute-start.13 = (f32[288,128]{1,0:T(8,128)S(1)}, f32[288,128]{1,0:T(8,128)S(1)}, u32[]{:S(2)}, u32[]{:S(2)}) collective-permute-start(f32[288,128]{1,0:T(8,128)S(1)} %get-tuple-element.48.refs_8_), channel_id=1, source_target_pairs={{0,12},{4,0},{8,4},{12,8},{1,13},{5,1},{9,5},{13,9},{2,14},{6,2},{... | collective-permute-start | bytes 442376 | tf_op jit(solution)/shard_map/ppermute | solution.py:307
  18.8 7.9 %collective-permute-start.6 = (f32[208,128]{1,0:T(8,128)S(1)}, f32[208,128]{1,0:T(8,128)S(1)}, u32[]{:S(2)}, u32[]{:S(2)}) collective-permute-start(f32[208,128]{1,0:T(8,128)S(1)} %get-tuple-element.40.refs_1_.own_right), channel_id=1, source_target_pairs={{0,1},{1,2},{2,3},{3,0},{4,5},{5,6},{6,7},{7,4},{8,9},{9,10},{10,1... | collective-permute-start | bytes 319496 | tf_op jit(solution)/shard_map/ppermute | solution.py:307
  18.9 7.8 %collective-permute-start.7 = (f32[200,128]{1,0:T(8,128)S(1)}, f32[200,128]{1,0:T(8,128)S(1)}, u32[]{:S(2)}, u32[]{:S(2)}) collective-permute-start(f32[200,128]{1,0:T(8,128)S(1)} %get-tuple-element.39.refs_0_.own_left), channel_id=1, source_target_pairs={{0,3},{1,0},{2,1},{3,2},{4,7},{5,4},{6,5},{7,6},{8,11},{9,8},{10,9... | collective-permute-start | bytes 307208 | tf_op jit(solution)/shard_map/ppermute | solution.py:307
  23.4 7.3 %collective-permute-start.14 = (f32[200,128]{1,0:T(8,128)S(1)}, f32[200,128]{1,0:T(8,128)S(1)}, u32[]{:S(2)}, u32[]{:S(2)}) collective-permute-start(f32[200,128]{1,0:T(8,128)S(1)} %get-tuple-element.50.refs_1_.own_right), channel_id=1, source_target_pairs={{0,1},{1,2},{2,3},{3,0},{4,5},{5,6},{6,7},{7,4},{8,9},{9,10},{10,1... | collective-permute-start | bytes 307208 | tf_op jit(solution)/shard_map/ppermute | solution.py:307
  23.7 7.0 %collective-permute-start.15 = (f32[192,128]{1,0:T(8,128)S(1)}, f32[192,128]{1,0:T(8,128)S(1)}, u32[]{:S(2)}, u32[]{:S(2)}) collective-permute-start(f32[192,128]{1,0:T(8,128)S(1)} %get-tuple-element.49.refs_0_.own_left), channel_id=1, source_target_pairs={{0,3},{1,0},{2,1},{3,2},{4,7},{5,4},{6,5},{7,6},{8,11},{9,8},{10,9... | collective-permute-start | bytes 294920 | tf_op jit(solution)/shard_map/ppermute | solution.py:307
  27.3 5.5 %collective-permute-start.8 = (f32[192,128]{1,0:T(8,128)S(1)}, f32[192,128]{1,0:T(8,128)S(1)}, u32[]{:S(2)}, u32[]{:S(2)}) collective-permute-start(f32[192,128]{1,0:T(8,128)S(1)} %get-tuple-element.42), channel_id=1, source_target_pairs={{0,4},{4,8},{8,12},{12,0},{1,5},{5,9},{9,13},{13,1},{2,6},{6,10},{... | collective-permute-start | bytes 294920 | tf_op jit(solution)/shard_map/ppermute | solution.py:307
  28.6 4.1 %collective-permute-start.9 = (f32[192,128]{1,0:T(8,128)S(1)}, f32[192,128]{1,0:T(8,128)S(1)}, u32[]{:S(2)}, u32[]{:S(2)}) collective-permute-start(f32[192,128]{1,0:T(8,128)S(1)} %get-tuple-element.43), channel_id=1, source_target_pairs={{0,12},{4,0},{8,4},{12,8},{1,13},{5,1},{9,5},{13,9},{2,14},{6,2},{... | collective-permute-start | bytes 294920 | tf_op jit(solution)/shard_map/ppermute | solution.py:307
  31.3 3.1 %collective-permute-start.16 = (f32[192,128]{1,0:T(8,128)S(1)}, f32[192,128]{1,0:T(8,128)S(1)}, u32[]{:S(2)}, u32[]{:S(2)}) collective-permute-start(f32[192,128]{1,0:T(8,128)S(1)} %get-tuple-element.54), channel_id=1, source_target_pairs={{0,4},{4,8},{8,12},{12,0},{1,5},{5,9},{9,13},{13,1},{2,6},{6,10},{... | collective-permute-start | bytes 294920 | tf_op jit(solution)/shard_map/ppermute | solution.py:307
  32.8 4.0 %collective-permute-start.17 = (f32[192,128]{1,0:T(8,128)S(1)}, f32[192,128]{1,0:T(8,128)S(1)}, u32[]{:S(2)}, u32[]{:S(2)}) collective-permute-start(f32[192,128]{1,0:T(8,128)S(1)} %get-tuple-element.55), channel_id=1, source_target_pairs={{0,12},{4,0},{8,4},{12,8},{1,13},{5,1},{9,5},{13,9},{2,14},{6,2},{... | collective-permute-start | bytes 294920 | tf_op jit(solution)/shard_map/ppermute | solution.py:307

commit v8 on v7

--- a/solution.py
+++ b/solution.py
@@ -14,6 +14,7 @@
 ASK_ROWS = BLOCK + HALF
 PADS = (16, 0, 0, 8, 8, 16, 0, 8)
 NEAR_PAD = 8
+SHARE_PADS = (8, 8), (0, 8)
 F32 = jnp.float32
 BF16 = jnp.bfloat16
 VMEM_LIMIT = 16 * 1024 * 1024
@@ -192,20 +193,28 @@
     return left, right
 
 
-def put_all(total, to_last, to_next, sums):
-    for at, low, share in ((0, 0, to_last), (1, 1, to_next)):
+def put_all(total, first_out, second_out, sums, paired):
+    shares = []
+    for at, low in ((0, 0), (1, 1)):
         left, right = tiles_of(total, at, low, 2)
-        share[:BLOCK, :] = left[0]
-        share[BLOCK:WIDE, :] = left[1]
-        share[WIDE:DEPTH, :] = jnp.where(on_left(BLOCK), swap(right[0]), right[1])
+        shares.append((left[0], left[1], jnp.where(on_left(BLOCK), swap(right[0]), right[1])))
+    even = is_even()
+    for part, (last, following) in enumerate(zip(*shares)):
+        if paired:
+            last, following = jnp.where(even, last, following), jnp.where(even, following, last)
+        first_out[tile_at(part), :] = last
+        second_out[tile_at(part), :] = following
     left, right = tiles_of(total, 2, 0, 3)
     for e in range(3):
         sums[e] = left[e]
         sums[3 + e] = right[e]
-    for share, e in ((to_last, 0), (to_next, 2)):
-        if share.shape[0] > DEPTH:
-            share[DEPTH : DEPTH + BLOCK, :] = left[e]
-            share[DEPTH + BLOCK :, :] = fold(right[e])
+    if paired:
+        fill_rest(first_out)
+        fill_rest(second_out)
+        return
+    for share, e in ((first_out, 0), (second_out, 2)):
+        share[DEPTH : DEPTH + BLOCK, :] = left[e]
+        share[DEPTH + BLOCK :, :] = fold(right[e])
 
 
 def fill_own(left, right, factor):
@@ -243,7 +252,7 @@
     fill_right_factor(*tiles, by)
     fill_asked(0, grid, slots, asks, got, sent, factor)
     fill_own(tiles[0], tiles[1], factor)
-    put_all(product(factor, by), to_last, to_next, sums)
+    put_all(product(factor, by), to_last, to_next, sums, earlier)
 
 
 def second_share_kernel(grid, slots, earlier, *refs):
@@ -254,7 +263,7 @@
     fill_asked(1, grid, slots, asks, got, sent, factor)
     fill_own(tiles[0], tiles[1], factor)
     both = [a + b for a, b in zip(product(factor, first_by), product(first_factor, by))]
-    put_all(both, to_last, to_next, sums)
+    put_all(both, to_last, to_next, sums, earlier)
 
 
 def total(sums, from_last, from_next):
@@ -281,9 +290,12 @@
     fill_rest(to_right)
 
 
-def final_kernel(which, grid, slots, idents, own_left, own_right, sums, from_last, from_next, _, out, dense, packed):
+def final_kernel(which, grid, slots, idents, own_left, own_right, sums, far, near, _, out, dense, packed):
     first_half = on_left(HALF)
     even, odd = pl.ds(0, HALF, stride=2), pl.ds(1, HALF, stride=2)
+    on_even = is_even()
+    from_last = jnp.where(on_even, far[:DEPTH], near[:DEPTH])
+    from_next = jnp.where(on_even, near[:DEPTH], far[:DEPTH])
     left, right = total(sums, from_last, from_next)
     for e in range(3):
         dense[e] = 2.0 * own_left[tile_at(e)] - left[e]
@@ -337,7 +349,7 @@
     return shape(DEPTH + rest, WIDE)
 
 
-SHARE = shape(DEPTH, WIDE)
+SHARES = tuple(tuple(shape(DEPTH + rest, WIDE) for rest in pair) for pair in SHARE_PADS)
 LONG_SHARE = shape(DEPTH + ASK_ROWS, WIDE)
 SUMS = shape(6, BLOCK, WIDE)
 BY_SHAPE = (2, 3 * WIDE, 3 * WIDE)
@@ -404,26 +416,27 @@
         flat(response_out_pattern),
     )
 
-    def share(first, second, asks, shape_of_share, earlier):
-        outputs = [shape_of_share] * 2 + [SUMS]
+    def share(first, second, asks, shapes_of_share, earlier):
+        first_outputs, second_outputs = ([*shapes, SUMS] for shapes in shapes_of_share)
+        send = in_pairs if earlier else along_row
         factors = [jax.ShapeDtypeStruct(BY_SHAPE, BF16), jax.ShapeDtypeStruct(FACTOR_SHAPE, BF16)]
         scratch = [pltpu.VMEM(BY_SHAPE, BF16), pltpu.VMEM(FACTOR_SHAPE, BF16)]
         *first_sent, first_sums, first_by, first_factor = call_all(
             functools.partial(first_share_kernel, grid, slots, bool(earlier)),
-            outputs + factors,
+            first_outputs + factors,
             (*first, *asks, *(earlier[0] if earlier else ())),
             [],
             "first_share",
         )
-        first_got = along_row(*first_sent)
+        first_got = send(*first_sent)
         *second_sent, second_sums = call_all(
             functools.partial(second_share_kernel, grid, slots, bool(earlier)),
-            outputs,
+            second_outputs,
             (*second, *asks, *(earlier[1] if earlier else ()), first_by, first_factor),
             scratch,
             "second_share",
         )
-        second_got = along_row(*second_sent)
+        second_got = send(*second_sent)
         return (first_sums, *first_got), (second_sums, *second_got), first_sent, second_sent
 
     first = along_col(*tiles[:2])
@@ -437,7 +450,7 @@
         )
     )
     second = along_col(*tiles[2:])
-    first_parts, second_parts, first_sent, second_sent = share(first, second, asks, LONG_SHARE, ())
+    first_parts, second_parts, first_sent, second_sent = share(first, second, asks, ([LONG_SHARE] * 2,) * 2, ())
     earlier = ((*first_parts[1:], *first_sent), (*second_parts[1:], *second_sent))
     next_tiles = [
         call_all(
@@ -450,7 +463,7 @@
         for which, parts, name in ((0, first_parts, "first_next"), (1, second_parts, "second_next"))
     ]
     first, second = along_col(*next_tiles[0]), along_col(*next_tiles[1])
-    first_parts, second_parts, _, _ = share(first, second, asks, SHARE, earlier)
+    first_parts, second_parts, _, _ = share(first, second, asks, SHARES, earlier)
 
     def final_of(which, own, parts, earlier, name):
         scratch = [pltpu.VMEM((6, BLOCK, WIDE), F32), pltpu.VMEM((9, HALF, WIDE), F32)]

time: 37.8 us -> 37.6 us (level)
  waiting for transfers between devices: 7.52 us -> 6.97 us
    ppermute x16 -> x12, waiting for transfers between devices: 7.51 us -> 4.28 us  [shift(): lax.ppermute(block, axis, [(i, (i + by) % count) for i in range(count)])]
    ppermute x16 -> x12, starting transfers between devices: 21.2 us -> 18.3 us  [shift(): lax.ppermute(block, axis, [(i, (i + by) % count) for i in range(count)])]
    ppermute x1 -> x3, waiting for transfers between devices: 0.01 us -> 2.68 us  [in_pairs(): lax.ppermute(far, 'row', [(i, ((i + 1 ^ 1) - 1) % rows) for i in range(ro...]
    ppermute x1 -> x3, starting transfers between devices: 1.65 us -> 3.97 us  [in_pairs(): lax.ppermute(far, 'row', [(i, ((i + 1 ^ 1) - 1) % rows) for i in range(ro...]
    ppermute x1 -> x3, starting transfers between devices: 1.02 us -> 1.66 us  [in_pairs(): return (far, lax.ppermute(near, 'row', [(i, i ^ 1) for i in range(rows)]))]
  transfers between devices with their start and end apart: 18 -> 18, of which waited for: 6 -> 5; matrix products, arithmetic and copies ran while one was open for 0% -> 0% of each run, Pallas kernels for 9% -> 9%
where the time goes in v8:
time: 37.6 us; the launch traced here: 37.3 us
  starting transfers between devices  24 us (64%)
  waiting for transfers between devices  6.97 us (19%)
  Pallas kernels  5.7 us (15%)
  between operations  0.71 us (2%)
    ppermute x12, starting transfers between devices, shift(): lax.ppermute(block, axis, [(i, (i + by) % count) for i in range(count)])  18.3 us
    ppermute x12, waiting for transfers between devices, shift(): lax.ppermute(block, axis, [(i, (i + by) % count) for i in range(count)])  4.28 us
    ppermute x3, starting transfers between devices, in_pairs(): lax.ppermute(far, 'row', [(i, ((i + 1 ^ 1) - 1) % rows) for i in range(ro...  3.97 us
    ppermute x3, waiting for transfers between devices, in_pairs(): lax.ppermute(far, 'row', [(i, ((i + 1 ^ 1) - 1) % rows) for i in range(ro...  2.68 us
    pallas_call x7, Pallas kernels, call_all(): call(kernel, outputs, [VM] * len(operands), [VM] * len(outputs), scratch,...  2.59 us
    pallas_call x2, Pallas kernels, final_of(): call(kernel, shape(slots, BLOCK * BLOCK), [VM] * 6 + [HB], VM, scratch, n...  1.77 us
    ppermute x3, starting transfers between devices, in_pairs(): return (far, lax.ppermute(near, 'row', [(i, i ^ 1) for i in range(rows)]))  1.66 us
    pallas_call x1, Pallas kernels, shards(): call(functools.partial(spread_kernel, grid, slots), [tiles_shape(r) for r...  1.35 us
  transfers between devices with their start and end apart: 18, of which 5 were waited for; matrix products, arithmetic and copies ran while one was open for 0% of the time, Pallas kernels for 9%

profile of v8, /device:TPU:1, one launch (start us, length us, event | category | flops | bytes accessed | tf_op | source)
XLA Modules:
  0.0 37.3 jit_solution(16843833232236878396)
XLA Ops:
  0.6 1.4 %spread.1 = (f32[208,128]{1,0:T(8,128)S(1)}, f32[192,128]{1,0:T(8,128)S(1)}, f32[192,128]{1,0:T(8,128)S(1)}, f32[200,128]{1,0:T(8,128)S(1)}, f32[4,8,128]{2,1,0:T(8,128)S(1)}) custom-call(s32[1,8]{1,0:T(1,128)} %bitcast.15, s32[1,8]{1,0:T(1,128)} %bitcast.16, f32[8,4096]{1,0:T(8,128)} %bitcast.10, f32[8,4096]{1,0:T(8,128)} %bitcast.13, s32[1,8]{1,0:T(1,128)} %bitcast.17, ...), custom_call_target="tpu_custom_call" | custom-call | bytes 1000000 | tf_op jit(solution)/shard_map/spread/pallas_call | solution.py:398
  2.0 2.2 %collective-permute-start = (f32[192,128]{1,0:T(8,128)S(1)}, f32[192,128]{1,0:T(8,128)S(1)}, u32[]{:S(2)}, u32[]{:S(2)}) collective-permute-start(f32[192,128]{1,0:T(8,128)S(1)} %get-tuple-element.31.first_right.refs_1_), channel_id=1, source_target_pairs={{0,1},{1,2},{2,3},{3,0},{4,5},{5,6},{6,7},{7,4},{8,9},{9,10},{10,1... | collective-permute-start | bytes 294920 | tf_op jit(solution)/shard_map/ppermute | solution.py:319
  4.2 0.1 ask.1
  4.3 1.0 %collective-permute-start.3 = (f32[216,128]{1,0:T(8,128)S(1)}, f32[216,128]{1,0:T(8,128)S(1)}, u32[]{:S(2)}, u32[]{:S(2)}) collective-permute-start(f32[216,128]{1,0:T(8,128)S(1)} %get-tuple-element.35), channel_id=1, source_target_pairs={{0,4},{4,0},{8,12},{12,8},{1,5},{5,1},{9,13},{13,9},{2,6},{6,2},{1... | collective-permute-start | bytes 331784 | tf_op jit(solution)/shard_map/ppermute | solution.py:374
  5.3 1.8 %collective-permute-start.1 = (f32[208,128]{1,0:T(8,128)S(1)}, f32[208,128]{1,0:T(8,128)S(1)}, u32[]{:S(2)}, u32[]{:S(2)}) collective-permute-start(f32[208,128]{1,0:T(8,128)S(1)} %get-tuple-element.30.first_left.refs_0_), channel_id=1, source_target_pairs={{0,3},{1,0},{2,1},{3,2},{4,7},{5,4},{6,5},{7,6},{8,11},{9,8},{10,9... | collective-permute-start | bytes 319496 | tf_op jit(solution)/shard_map/ppermute | solution.py:319
  7.0 1.6 %collective-permute-start.2 = (f32[208,128]{1,0:T(8,128)S(1)}, f32[208,128]{1,0:T(8,128)S(1)}, u32[]{:S(2)}, u32[]{:S(2)}) collective-permute-start(f32[208,128]{1,0:T(8,128)S(1)} %get-tuple-element.34), channel_id=1, source_target_pairs={{0,12},{4,8},{8,4},{12,0},{1,13},{5,9},{9,5},{13,1},{2,14},{6,10},... | collective-permute-start | bytes 319496 | tf_op jit(solution)/shard_map/ppermute | solution.py:373
  8.7 0.0 collective-permute-start.10
  8.7 0.0 collective-permute-done.refs_2_
  8.7 3.2 %collective-permute-start.11 = (f32[192,128]{1,0:T(8,128)S(1)}, f32[192,128]{1,0:T(8,128)S(1)}, u32[]{:S(2)}, u32[]{:S(2)}) collective-permute-start(f32[192,128]{1,0:T(8,128)S(1)} %get-tuple-element.32.second_left.refs_0_), channel_id=1, source_target_pairs={{0,3},{1,0},{2,1},{3,2},{4,7},{5,4},{6,5},{7,6},{8,11},{9,8},{10,9... | collective-permute-start | bytes 294920 | tf_op jit(solution)/shard_map/ppermute | solution.py:319
  12.0 0.0 collective-permute-done.1.refs_3_
  12.0 0.0 collective-permute-done.2.refs_4_
  12.0 0.0 collective-permute-done.3.refs_5_
  12.0 0.5 %first_share.2 = (f32[288,128]{1,0:T(8,128)S(1)}, f32[288,128]{1,0:T(8,128)S(1)}, f32[6,64,128]{2,1,0:T(8,128)S(1)}, bf16[2,384,384]{2,1,0:T(8,128)(2,1)S(1)}, bf16[2,192,384]{2,1,0:T(8,128)(2,1)S(1)}) custom-call(f32[208,128]{1,0:T(8,128)S(1)} %get-tuple-element.30.first_left.refs_0_, f32[192,128]{1,0:T(8,128)S(1)} %get-tuple-element.31.first_right.refs_1_, ...), custom_call_target="tpu_custom_call" | custom-call | bytes 1000000 | tf_op jit(solution)/shard_map/first_share/pallas_call | solution.py:360
  12.4 1.7 %collective-permute-start.4 = (f32[288,128]{1,0:T(8,128)S(1)}, f32[288,128]{1,0:T(8,128)S(1)}, u32[]{:S(2)}, u32[]{:S(2)}) collective-permute-start(f32[288,128]{1,0:T(8,128)S(1)} %get-tuple-element.37.refs_9_), channel_id=1, source_target_pairs={{0,4},{4,8},{8,12},{12,0},{1,5},{5,9},{9,13},{13,1},{2,6},{6,10},{... | collective-permute-start | bytes 442376 | tf_op jit(solution)/shard_map/ppermute | solution.py:319
  14.1 0.0 collective-permute-start.5
  14.1 0.0 collective-permute-done.11.refs_3_
  14.1 0.7 %collective-permute-done.10.refs_2_ = f32[200,128]{1,0:T(8,128)S(1)} collective-permute-done((f32[200,128]{1,0:T(8,128)S(1)}, f32[200,128]{1,0:T(8,128)S(1)}, u32[]{:S(2)}, u32[]{:S(2)}) %collective-permute-start.10) | collective-permute-done | bytes 102432 | tf_op jit(solution)/shard_map/ppermute | solution.py:319
  14.9 0.6 %second_share.2 = (f32[288,128]{1,0:T(8,128)S(1)}, f32[288,128]{1,0:T(8,128)S(1)}, f32[6,64,128]{2,1,0:T(8,128)S(1)}) custom-call(f32[192,128]{1,0:T(8,128)S(1)} %get-tuple-element.32.second_left.refs_0_, f32[200,128]{1,0:T(8,128)S(1)} %get-tuple-element.33.second_right.refs_1_, f32[200,128]{1,0:T(8,128)S(1)} %collective-permute-done.10.refs_2_, ...), custom_call_target="tpu_custom_call" | custom-call | bytes 1000000 | tf_op jit(solution)/shard_map/second_share/pallas_call | solution.py:360
  15.5 2.8 %collective-permute-start.12 = (f32[288,128]{1,0:T(8,128)S(1)}, f32[288,128]{1,0:T(8,128)S(1)}, u32[]{:S(2)}, u32[]{:S(2)}) collective-permute-start(f32[288,128]{1,0:T(8,128)S(1)} %get-tuple-element.47.refs_9_), channel_id=1, source_target_pairs={{0,4},{4,8},{8,12},{12,0},{1,5},{5,9},{9,13},{13,1},{2,6},{6,10},{... | collective-permute-start | bytes 442376 | tf_op jit(solution)/shard_map/ppermute | solution.py:319
  18.3 0.0 collective-permute-start.13
  18.3 0.0 collective-permute-done.4.from_last.refs_6_
  18.3 0.4 collective-permute-done.5.from_next.refs_7_
  18.7 0.1 first_next.1
  18.8 0.1 collective-permute-start.6
  18.9 3.2 %collective-permute-start.7 = (f32[200,128]{1,0:T(8,128)S(1)}, f32[200,128]{1,0:T(8,128)S(1)}, u32[]{:S(2)}, u32[]{:S(2)}) collective-permute-start(f32[200,128]{1,0:T(8,128)S(1)} %get-tuple-element.39.refs_0_.own_left), channel_id=1, source_target_pairs={{0,3},{1,0},{2,1},{3,2},{4,7},{5,4},{6,5},{7,6},{8,11},{9,8},{10,9... | collective-permute-start | bytes 307208 | tf_op jit(solution)/shard_map/ppermute | solution.py:319
  22.1 0.0 collective-permute-done.12.from_last.refs_6_
  22.1 1.2 %collective-permute-done.13.from_next.refs_7_ = f32[288,128]{1,0:T(8,128)S(1)} collective-permute-done((f32[288,128]{1,0:T(8,128)S(1)}, f32[288,128]{1,0:T(8,128)S(1)}, u32[]{:S(2)}, u32[]{:S(2)}) %collective-permute-start.13) | collective-permute-done | bytes 147488 | tf_op jit(solution)/shard_map/ppermute | solution.py:319
  23.3 0.1 second_next.1
  23.4 0.2 collective-permute-start.14
  23.7 3.1 %collective-permute-start.15 = (f32[192,128]{1,0:T(8,128)S(1)}, f32[192,128]{1,0:T(8,128)S(1)}, u32[]{:S(2)}, u32[]{:S(2)}) collective-permute-start(f32[192,128]{1,0:T(8,128)S(1)} %get-tuple-element.49.refs_0_.own_left), channel_id=1, source_target_pairs={{0,3},{1,0},{2,1},{3,2},{4,7},{5,4},{6,5},{7,6},{8,11},{9,8},{10,9... | collective-permute-start | bytes 294920 | tf_op jit(solution)/shard_map/ppermute | solution.py:319
  26.7 0.0 collective-permute-done.7.refs_3_
  26.7 0.0 collective-permute-done.6.refs_2_
  26.8 0.5 %first_share.3 = (f32[200,128]{1,0:T(8,128)S(1)}, f32[200,128]{1,0:T(8,128)S(1)}, f32[6,64,128]{2,1,0:T(8,128)S(1)}, bf16[2,384,384]{2,1,0:T(8,128)(2,1)S(1)}, bf16[2,192,384]{2,1,0:T(8,128)(2,1)S(1)}) custom-call(f32[200,128]{1,0:T(8,128)S(1)} %get-tuple-element.39.refs_0_.own_left, f32[208,128]{1,0:T(8,128)S(1)} %get-tuple-element.40.refs_1_.own_right, ...), custom_call_target="tpu_custom_call" | custom-call | bytes 1000000 | tf_op jit(solution)/shard_map/first_share/pallas_call | solution.py:360
  27.3 1.4 %collective-permute-start.8 = (f32[200,128]{1,0:T(8,128)S(1)}, f32[200,128]{1,0:T(8,128)S(1)}, u32[]{:S(2)}, u32[]{:S(2)}) collective-permute-start(f32[200,128]{1,0:T(8,128)S(1)} %get-tuple-element.42), channel_id=1, source_target_pairs={{0,12},{4,8},{8,4},{12,0},{1,13},{5,9},{9,5},{13,1},{2,14},{6,10},... | collective-permute-start | bytes 307208 | tf_op jit(solution)/shard_map/ppermute | solution.py:373
  28.7 0.0 collective-permute-start.9
  28.7 2.0 %collective-permute-done.15.refs_3_ = f32[192,128]{1,0:T(8,128)S(1)} collective-permute-done((f32[192,128]{1,0:T(8,128)S(1)}, f32[192,128]{1,0:T(8,128)S(1)}, u32[]{:S(2)}, u32[]{:S(2)}) %collective-permute-start.15) | collective-permute-done | bytes 98336 | tf_op jit(solution)/shard_map/ppermute | solution.py:319
  30.7 0.0 collective-permute-done.14.refs_2_
  30.7 0.7 %second_share.3 = (f32[192,128]{1,0:T(8,128)S(1)}, f32[200,128]{1,0:T(8,128)S(1)}, f32[6,64,128]{2,1,0:T(8,128)S(1)}) custom-call(f32[192,128]{1,0:T(8,128)S(1)} %get-tuple-element.49.refs_0_.own_left, f32[200,128]{1,0:T(8,128)S(1)} %get-tuple-element.50.refs_1_.own_right, f32[200,128]{1,0:T(8,128)S(1)} %collective-permute-done.14.refs_2_, ...), custom_call_target="tpu_custom_call" | custom-call | bytes 1000000 | tf_op jit(solution)/shard_map/second_share/pallas_call | solution.py:360
  31.3 0.6 %collective-permute-start.17 = (f32[200,128]{1,0:T(8,128)S(1)}, f32[200,128]{1,0:T(8,128)S(1)}, u32[]{:S(2)}, u32[]{:S(2)}) collective-permute-start(f32[200,128]{1,0:T(8,128)S(1)} %get-tuple-element.55), channel_id=1, source_target_pairs={{0,4},{4,0},{8,12},{12,8},{1,5},{5,1},{9,13},{13,9},{2,6},{6,2},{1... | collective-permute-start | bytes 307208 | tf_op jit(solution)/shard_map/ppermute | solution.py:374
  32.0 0.9 %collective-permute-start.16 = (f32[192,128]{1,0:T(8,128)S(1)}, f32[192,128]{1,0:T(8,128)S(1)}, u32[]{:S(2)}, u32[]{:S(2)}) collective-permute-start(f32[192,128]{1,0:T(8,128)S(1)} %get-tuple-element.54), channel_id=1, source_target_pairs={{0,12},{4,8},{8,4},{12,0},{1,13},{5,9},{9,5},{13,1},{2,14},{6,10},... | collective-permute-start | bytes 294920 | tf_op jit(solution)/shard_map/ppermute | solution.py:373
  32.9 0.0 collective-permute-done.8.far
  32.9 0.0 collective-permute-done.9.near
  32.9 0.9 %first_final.1._ = f32[8,4096]{1,0:T(8,128)} custom-call(f32[4,8,128]{2,1,0:T(8,128)S(1)} %get-tuple-element.29.idents, f32[200,128]{1,0:T(8,128)S(1)} %get-tuple-element.39.refs_0_.own_left, f32[208,128]{1,0:T(8,128)S(1)} %get-tuple-element.40.refs_1_.own_right, f32[6,64,128]{2,1,0:T(8,128)S(1)} %get-tuple-element.41.sums, ...), custom_call_target="tpu_custom_call" | custom-call | bytes 1000000 | tf_op jit(solution)/shard_map/first_final/pallas_call | solution.py:471
  33.8 2.7 %collective-permute-done.16.far = f32[192,128]{1,0:T(8,128)S(1)} collective-permute-done((f32[192,128]{1,0:T(8,128)S(1)}, f32[192,128]{1,0:T(8,128)S(1)}, u32[]{:S(2)}, u32[]{:S(2)}) %collective-permute-start.16) | collective-permute-done | bytes 98336 | tf_op jit(solution)/shard_map/ppermute | solution.py:373
  36.5 0.0 collective-permute-done.17.near
  36.5 0.9 %second_final.1 = f32[8,4096]{1,0:T(8,128)} custom-call(f32[4,8,128]{2,1,0:T(8,128)S(1)} %get-tuple-element.29.idents, f32[192,128]{1,0:T(8,128)S(1)} %get-tuple-element.49.refs_0_.own_left, f32[200,128]{1,0:T(8,128)S(1)} %get-tuple-element.50.refs_1_.own_right, f32[6,64,128]{2,1,0:T(8,128)S(1)} %get-tuple-element.53.sums, ...), custom_call_target="tpu_custom_call" | custom-call | bytes 1000000 | tf_op jit(solution)/shard_map/second_final/pallas_call | solution.py:471
Async XLA Ops:
  2.0 6.7 %collective-permute-start = (f32[192,128]{1,0:T(8,128)S(1)}, f32[192,128]{1,0:T(8,128)S(1)}, u32[]{:S(2)}, u32[]{:S(2)}) collective-permute-start(f32[192,128]{1,0:T(8,128)S(1)} %get-tuple-element.31.first_right.refs_1_), channel_id=1, source_target_pairs={{0,1},{1,2},{2,3},{3,0},{4,5},{5,6},{6,7},{7,4},{8,9},{9,10},{10,1... | collective-permute-start | bytes 294920 | tf_op jit(solution)/shard_map/ppermute | solution.py:319
  4.3 7.7 %collective-permute-start.3 = (f32[216,128]{1,0:T(8,128)S(1)}, f32[216,128]{1,0:T(8,128)S(1)}, u32[]{:S(2)}, u32[]{:S(2)}) collective-permute-start(f32[216,128]{1,0:T(8,128)S(1)} %get-tuple-element.35), channel_id=1, source_target_pairs={{0,4},{4,0},{8,12},{12,8},{1,5},{5,1},{9,13},{13,9},{2,6},{6,2},{1... | collective-permute-start | bytes 331784 | tf_op jit(solution)/shard_map/ppermute | solution.py:374
  5.3 6.7 %collective-permute-start.1 = (f32[208,128]{1,0:T(8,128)S(1)}, f32[208,128]{1,0:T(8,128)S(1)}, u32[]{:S(2)}, u32[]{:S(2)}) collective-permute-start(f32[208,128]{1,0:T(8,128)S(1)} %get-tuple-element.30.first_left.refs_0_), channel_id=1, source_target_pairs={{0,3},{1,0},{2,1},{3,2},{4,7},{5,4},{6,5},{7,6},{8,11},{9,8},{10,9... | collective-permute-start | bytes 319496 | tf_op jit(solution)/shard_map/ppermute | solution.py:319
  7.0 4.9 %collective-permute-start.2 = (f32[208,128]{1,0:T(8,128)S(1)}, f32[208,128]{1,0:T(8,128)S(1)}, u32[]{:S(2)}, u32[]{:S(2)}) collective-permute-start(f32[208,128]{1,0:T(8,128)S(1)} %get-tuple-element.34), channel_id=1, source_target_pairs={{0,12},{4,8},{8,4},{12,0},{1,13},{5,9},{9,5},{13,1},{2,14},{6,10},... | collective-permute-start | bytes 319496 | tf_op jit(solution)/shard_map/ppermute | solution.py:373
  8.7 6.2 %collective-permute-start.10 = (f32[200,128]{1,0:T(8,128)S(1)}, f32[200,128]{1,0:T(8,128)S(1)}, u32[]{:S(2)}, u32[]{:S(2)}) collective-permute-start(f32[200,128]{1,0:T(8,128)S(1)} %get-tuple-element.33.second_right.refs_1_), channel_id=1, source_target_pairs={{0,1},{1,2},{2,3},{3,0},{4,5},{5,6},{6,7},{7,4},{8,9},{9,10},{10,1... | collective-permute-start | bytes 307208 | tf_op jit(solution)/shard_map/ppermute | solution.py:319
  8.7 5.4 %collective-permute-start.11 = (f32[192,128]{1,0:T(8,128)S(1)}, f32[192,128]{1,0:T(8,128)S(1)}, u32[]{:S(2)}, u32[]{:S(2)}) collective-permute-start(f32[192,128]{1,0:T(8,128)S(1)} %get-tuple-element.32.second_left.refs_0_), channel_id=1, source_target_pairs={{0,3},{1,0},{2,1},{3,2},{4,7},{5,4},{6,5},{7,6},{8,11},{9,8},{10,9... | collective-permute-start | bytes 294920 | tf_op jit(solution)/shard_map/ppermute | solution.py:319
  12.4 5.9 %collective-permute-start.4 = (f32[288,128]{1,0:T(8,128)S(1)}, f32[288,128]{1,0:T(8,128)S(1)}, u32[]{:S(2)}, u32[]{:S(2)}) collective-permute-start(f32[288,128]{1,0:T(8,128)S(1)} %get-tuple-element.37.refs_9_), channel_id=1, source_target_pairs={{0,4},{4,8},{8,12},{12,0},{1,5},{5,9},{9,13},{13,1},{2,6},{6,10},{... | collective-permute-start | bytes 442376 | tf_op jit(solution)/shard_map/ppermute | solution.py:319
  14.1 4.6 %collective-permute-start.5 = (f32[288,128]{1,0:T(8,128)S(1)}, f32[288,128]{1,0:T(8,128)S(1)}, u32[]{:S(2)}, u32[]{:S(2)}) collective-permute-start(f32[288,128]{1,0:T(8,128)S(1)} %get-tuple-element.38.refs_8_), channel_id=1, source_target_pairs={{0,12},{4,0},{8,4},{12,8},{1,13},{5,1},{9,5},{13,9},{2,14},{6,2},{... | collective-permute-start | bytes 442376 | tf_op jit(solution)/shard_map/ppermute | solution.py:319
  15.5 6.6 %collective-permute-start.12 = (f32[288,128]{1,0:T(8,128)S(1)}, f32[288,128]{1,0:T(8,128)S(1)}, u32[]{:S(2)}, u32[]{:S(2)}) collective-permute-start(f32[288,128]{1,0:T(8,128)S(1)} %get-tuple-element.47.refs_9_), channel_id=1, source_target_pairs={{0,4},{4,8},{8,12},{12,0},{1,5},{5,9},{9,13},{13,1},{2,6},{6,10},{... | collective-permute-start | bytes 442376 | tf_op jit(solution)/shard_map/ppermute | solution.py:319
  18.3 5.0 %collective-permute-start.13 = (f32[288,128]{1,0:T(8,128)S(1)}, f32[288,128]{1,0:T(8,128)S(1)}, u32[]{:S(2)}, u32[]{:S(2)}) collective-permute-start(f32[288,128]{1,0:T(8,128)S(1)} %get-tuple-element.48.refs_8_), channel_id=1, source_target_pairs={{0,12},{4,0},{8,4},{12,8},{1,13},{5,1},{9,5},{13,9},{2,14},{6,2},{... | collective-permute-start | bytes 442376 | tf_op jit(solution)/shard_map/ppermute | solution.py:319
  18.8 7.9 %collective-permute-start.6 = (f32[208,128]{1,0:T(8,128)S(1)}, f32[208,128]{1,0:T(8,128)S(1)}, u32[]{:S(2)}, u32[]{:S(2)}) collective-permute-start(f32[208,128]{1,0:T(8,128)S(1)} %get-tuple-element.40.refs_1_.own_right), channel_id=1, source_target_pairs={{0,1},{1,2},{2,3},{3,0},{4,5},{5,6},{6,7},{7,4},{8,9},{9,10},{10,1... | collective-permute-start | bytes 319496 | tf_op jit(solution)/shard_map/ppermute | solution.py:319
  18.9 7.8 %collective-permute-start.7 = (f32[200,128]{1,0:T(8,128)S(1)}, f32[200,128]{1,0:T(8,128)S(1)}, u32[]{:S(2)}, u32[]{:S(2)}) collective-permute-start(f32[200,128]{1,0:T(8,128)S(1)} %get-tuple-element.39.refs_0_.own_left), channel_id=1, source_target_pairs={{0,3},{1,0},{2,1},{3,2},{4,7},{5,4},{6,5},{7,6},{8,11},{9,8},{10,9... | collective-permute-start | bytes 307208 | tf_op jit(solution)/shard_map/ppermute | solution.py:319
  23.4 7.3 %collective-permute-start.14 = (f32[200,128]{1,0:T(8,128)S(1)}, f32[200,128]{1,0:T(8,128)S(1)}, u32[]{:S(2)}, u32[]{:S(2)}) collective-permute-start(f32[200,128]{1,0:T(8,128)S(1)} %get-tuple-element.50.refs_1_.own_right), channel_id=1, source_target_pairs={{0,1},{1,2},{2,3},{3,0},{4,5},{5,6},{6,7},{7,4},{8,9},{9,10},{10,1... | collective-permute-start | bytes 307208 | tf_op jit(solution)/shard_map/ppermute | solution.py:319
  23.7 7.0 %collective-permute-start.15 = (f32[192,128]{1,0:T(8,128)S(1)}, f32[192,128]{1,0:T(8,128)S(1)}, u32[]{:S(2)}, u32[]{:S(2)}) collective-permute-start(f32[192,128]{1,0:T(8,128)S(1)} %get-tuple-element.49.refs_0_.own_left), channel_id=1, source_target_pairs={{0,3},{1,0},{2,1},{3,2},{4,7},{5,4},{6,5},{7,6},{8,11},{9,8},{10,9... | collective-permute-start | bytes 294920 | tf_op jit(solution)/shard_map/ppermute | solution.py:319
  27.3 5.6 %collective-permute-start.8 = (f32[200,128]{1,0:T(8,128)S(1)}, f32[200,128]{1,0:T(8,128)S(1)}, u32[]{:S(2)}, u32[]{:S(2)}) collective-permute-start(f32[200,128]{1,0:T(8,128)S(1)} %get-tuple-element.42), channel_id=1, source_target_pairs={{0,12},{4,8},{8,4},{12,0},{1,13},{5,9},{9,5},{13,1},{2,14},{6,10},... | collective-permute-start | bytes 307208 | tf_op jit(solution)/shard_map/ppermute | solution.py:373
  28.7 4.2 %collective-permute-start.9 = (f32[200,128]{1,0:T(8,128)S(1)}, f32[200,128]{1,0:T(8,128)S(1)}, u32[]{:S(2)}, u32[]{:S(2)}) collective-permute-start(f32[200,128]{1,0:T(8,128)S(1)} %get-tuple-element.43), channel_id=1, source_target_pairs={{0,4},{4,0},{8,12},{12,8},{1,5},{5,1},{9,13},{13,9},{2,6},{6,2},{1... | collective-permute-start | bytes 307208 | tf_op jit(solution)/shard_map/ppermute | solution.py:374
  31.3 5.1 %collective-permute-start.17 = (f32[200,128]{1,0:T(8,128)S(1)}, f32[200,128]{1,0:T(8,128)S(1)}, u32[]{:S(2)}, u32[]{:S(2)}) collective-permute-start(f32[200,128]{1,0:T(8,128)S(1)} %get-tuple-element.55), channel_id=1, source_target_pairs={{0,4},{4,0},{8,12},{12,8},{1,5},{5,1},{9,13},{13,9},{2,6},{6,2},{1... | collective-permute-start | bytes 307208 | tf_op jit(solution)/shard_map/ppermute | solution.py:374
  32.0 4.5 %collective-permute-start.16 = (f32[192,128]{1,0:T(8,128)S(1)}, f32[192,128]{1,0:T(8,128)S(1)}, u32[]{:S(2)}, u32[]{:S(2)}) collective-permute-start(f32[192,128]{1,0:T(8,128)S(1)} %get-tuple-element.54), channel_id=1, source_target_pairs={{0,12},{4,8},{8,4},{12,0},{1,13},{5,9},{9,5},{13,1},{2,14},{6,10},... | collective-permute-start | bytes 294920 | tf_op jit(solution)/shard_map/ppermute | solution.py:373

commit v9 on v8

--- a/solution.py
+++ b/solution.py
@@ -15,6 +15,7 @@
 PADS = (16, 0, 0, 8, 8, 16, 0, 8)
 NEAR_PAD = 8
 SHARE_PADS = (8, 8), (0, 8)
+LONG_PADS = (0, 8), (0, 8)
 F32 = jnp.float32
 BF16 = jnp.bfloat16
 VMEM_LIMIT = 16 * 1024 * 1024
@@ -193,28 +194,36 @@
     return left, right
 
 
-def put_all(total, first_out, second_out, sums, paired):
+def put_all(total, far, near, sums):
+    even = is_even()
+
+    def put(rows, last, following):
+        far[rows, :] = jnp.where(even, last, following)
+        near[rows, :] = jnp.where(even, following, last)
+
     shares = []
     for at, low in ((0, 0), (1, 1)):
         left, right = tiles_of(total, at, low, 2)
         shares.append((left[0], left[1], jnp.where(on_left(BLOCK), swap(right[0]), right[1])))
-    even = is_even()
-    for part, (last, following) in enumerate(zip(*shares)):
-        if paired:
-            last, following = jnp.where(even, last, following), jnp.where(even, following, last)
-        first_out[tile_at(part), :] = last
-        second_out[tile_at(part), :] = following
+    for part, pair in enumerate(zip(*shares)):
+        put(tile_at(part), *pair)
     left, right = tiles_of(total, 2, 0, 3)
     for e in range(3):
         sums[e] = left[e]
         sums[3 + e] = right[e]
-    if paired:
-        fill_rest(first_out)
-        fill_rest(second_out)
-        return
-    for share, e in ((first_out, 0), (second_out, 2)):
-        share[DEPTH : DEPTH + BLOCK, :] = left[e]
-        share[DEPTH + BLOCK :, :] = fold(right[e])
+    if far.shape[0] >= DEPTH + ASK_ROWS:
+        put(slice(DEPTH, DEPTH + BLOCK), left[0], left[2])
+        put(slice(DEPTH + BLOCK, DEPTH + ASK_ROWS), fold(right[0]), fold(right[2]))
+    for message in (far, near):
+        for length in (DEPTH, DEPTH + ASK_ROWS):
+            if length < message.shape[0] < length + BLOCK:
+                message[length:, :] = jnp.zeros((message.shape[0] - length, WIDE), F32)
+
+
+def pick(pair, at, rows):
+    far, near = pair
+    even = is_even()
+    return jnp.where(even if at == 0 else jnp.logical_not(even), far[rows], near[rows])
 
 
 def fill_own(left, right, factor):
@@ -234,14 +243,15 @@
             row = which * ASK_ROWS
             left, folded = asked(row, BLOCK), asked(row + BLOCK, HALF)
         else:
-            pack = sent[at][WIDE:DEPTH]
+            pack = pick(sent, at, slice(WIDE, DEPTH))
+            outer, outer_fold = slice(DEPTH, DEPTH + BLOCK), slice(DEPTH + BLOCK, DEPTH + ASK_ROWS)
             if at == 0:
-                left, folded = sent[at][BLOCK:WIDE], fold(pack)
+                left, folded = pick(sent, 0, slice(BLOCK, WIDE)), fold(pack)
             else:
-                left, folded = sent[at][:BLOCK], jnp.where(on_left(HALF), pack[:HALF], swap(pack[HALF:]))
+                left, folded = pick(sent, 1, slice(0, BLOCK)), jnp.where(on_left(HALF), pack[:HALF], swap(pack[HALF:]))
             idents = asked(2 * ASK_ROWS + slots * which, slots)
-            left = jnp.where(is_live(idents, pair_at(3, 4, grid)), left + got[at][DEPTH : DEPTH + BLOCK], 0.0)
-            folded = jnp.where(is_live(idents, ident_at(5, grid)), folded + got[at][DEPTH + BLOCK :], 0.0)
+            left = jnp.where(is_live(idents, pair_at(3, 4, grid)), left + pick(got, at, outer), 0.0)
+            folded = jnp.where(is_live(idents, ident_at(5, grid)), folded + pick(got, at, outer_fold), 0.0)
         fill_left_factor(at, left, unfold(left, folded), factor)
 
 
@@ -252,7 +262,7 @@
     fill_right_factor(*tiles, by)
     fill_asked(0, grid, slots, asks, got, sent, factor)
     fill_own(tiles[0], tiles[1], factor)
-    put_all(product(factor, by), to_last, to_next, sums, earlier)
+    put_all(product(factor, by), to_last, to_next, sums)
 
 
 def second_share_kernel(grid, slots, earlier, *refs):
@@ -263,13 +273,14 @@
     fill_asked(1, grid, slots, asks, got, sent, factor)
     fill_own(tiles[0], tiles[1], factor)
     both = [a + b for a, b in zip(product(factor, first_by), product(first_factor, by))]
-    put_all(both, to_last, to_next, sums, earlier)
-
-
-def total(sums, from_last, from_next):
+    put_all(both, to_last, to_next, sums)
+
+
+def total(sums, far, near):
     left = [sums[e] for e in range(3)]
     right = [sums[3 + e] for e in range(3)]
-    for share, low in ((from_last, 0), (from_next, 1)):
+    for low in range(2):
+        share = pick((far, near), low, slice(0, DEPTH))
         pack = share[WIDE:DEPTH]
         left[low] += share[:BLOCK]
         left[low + 1] += share[BLOCK:WIDE]
@@ -278,9 +289,9 @@
     return left, right
 
 
-def next_kernel(which, grid, idents, sums, from_last, from_next, to_left, to_right):
+def next_kernel(which, grid, idents, sums, far, near, to_left, to_right):
     first = on_left(BLOCK)
-    left, right = total(sums, from_last, from_next)
+    left, right = total(sums, far, near)
     for e in range(3):
         keep_left = is_live(idents[which], pair_at(3 * e, 3 * e + 1, grid))
         keep_right = is_live(idents[which], pair_at(3 * e + 1, 3 * e + 2, grid))
@@ -293,10 +304,7 @@
 def final_kernel(which, grid, slots, idents, own_left, own_right, sums, far, near, _, out, dense, packed):
     first_half = on_left(HALF)
     even, odd = pl.ds(0, HALF, stride=2), pl.ds(1, HALF, stride=2)
-    on_even = is_even()
-    from_last = jnp.where(on_even, far[:DEPTH], near[:DEPTH])
-    from_next = jnp.where(on_even, near[:DEPTH], far[:DEPTH])
-    left, right = total(sums, from_last, from_next)
+    left, right = total(sums, far, near)
     for e in range(3):
         dense[e] = 2.0 * own_left[tile_at(e)] - left[e]
         dense[3 + e] = 2.0 * own_right[tile_at(e)] - right[e]
@@ -350,7 +358,7 @@
 
 
 SHARES = tuple(tuple(shape(DEPTH + rest, WIDE) for rest in pair) for pair in SHARE_PADS)
-LONG_SHARE = shape(DEPTH + ASK_ROWS, WIDE)
+LONG_SHARES = tuple(tuple(shape(DEPTH + ASK_ROWS + rest, WIDE) for rest in pair) for pair in LONG_PADS)
 SUMS = shape(6, BLOCK, WIDE)
 BY_SHAPE = (2, 3 * WIDE, 3 * WIDE)
 FACTOR_SHAPE = (2, 3 * BLOCK, 3 * WIDE)
@@ -362,10 +370,6 @@
 
 def along_col(to_left, to_right):
     return to_left, to_right, shift(to_right, "col", 1), shift(to_left, "col", -1)
-
-
-def along_row(to_last, to_next):
-    return shift(to_next, "row", 1), shift(to_last, "row", -1)
 
 
 def in_pairs(far, near):
@@ -418,7 +422,6 @@
 
     def share(first, second, asks, shapes_of_share, earlier):
         first_outputs, second_outputs = ([*shapes, SUMS] for shapes in shapes_of_share)
-        send = in_pairs if earlier else along_row
         factors = [jax.ShapeDtypeStruct(BY_SHAPE, BF16), jax.ShapeDtypeStruct(FACTOR_SHAPE, BF16)]
         scratch = [pltpu.VMEM(BY_SHAPE, BF16), pltpu.VMEM(FACTOR_SHAPE, BF16)]
         *first_sent, first_sums, first_by, first_factor = call_all(
@@ -428,7 +431,7 @@
             [],
             "first_share",
         )
-        first_got = send(*first_sent)
+        first_got = in_pairs(*first_sent)
         *second_sent, second_sums = call_all(
             functools.partial(second_share_kernel, grid, slots, bool(earlier)),
             second_outputs,
@@ -436,7 +439,7 @@
             scratch,
             "second_share",
         )
-        second_got = send(*second_sent)
+        second_got = in_pairs(*second_sent)
         return (first_sums, *first_got), (second_sums, *second_got), first_sent, second_sent
 
     first = along_col(*tiles[:2])
@@ -450,7 +453,7 @@
         )
     )
     second = along_col(*tiles[2:])
-    first_parts, second_parts, first_sent, second_sent = share(first, second, asks, ([LONG_SHARE] * 2,) * 2, ())
+    first_parts, second_parts, first_sent, second_sent = share(first, second, asks, LONG_SHARES, ())
     earlier = ((*first_parts[1:], *first_sent), (*second_parts[1:], *second_sent))
     next_tiles = [
         call_all(

time: 37.6 us -> 37.4 us (level)
  waiting for transfers between devices: 6.97 us -> 5.95 us
  starting transfers between devices: 24 us -> 24.8 us
    ppermute x12 -> x8, starting transfers between devices: 18.3 us -> 13.8 us  [shift(): lax.ppermute(block, axis, [(i, (i + by) % count) for i in range(count)])]
    ppermute x3 -> x5, starting transfers between devices: 1.66 us -> 5.08 us  [in_pairs(): return (far, lax.ppermute(near, 'row', [(i, i ^ 1) for i in range(rows)]))]
    ppermute x12 -> x8, waiting for transfers between devices: 4.28 us -> 1.88 us  [shift(): lax.ppermute(block, axis, [(i, (i + by) % count) for i in range(count)])]
    ppermute x3 -> x5, starting transfers between devices: 3.97 us -> 5.9 us  [in_pairs(): lax.ppermute(far, 'row', [(i, ((i + 1 ^ 1) - 1) % rows) for i in range(ro...]
    ppermute x3 -> x5, waiting for transfers between devices: 2.68 us -> 4.06 us  [in_pairs(): lax.ppermute(far, 'row', [(i, ((i + 1 ^ 1) - 1) % rows) for i in range(ro...]
  transfers between devices with their start and end apart: 18 -> 18, of which waited for: 5 -> 6; matrix products, arithmetic and copies ran while one was open for 0% -> 0% of each run, Pallas kernels for 9% -> 9%
where the time goes in v9:
time: 37.4 us; the launch traced here: 37.2 us
  starting transfers between devices  24.8 us (66%)
  waiting for transfers between devices  5.95 us (16%)
  Pallas kernels  5.74 us (15%)
  between operations  0.72 us (2%)
    ppermute x8, starting transfers between devices, shift(): lax.ppermute(block, axis, [(i, (i + by) % count) for i in range(count)])  13.8 us
    ppermute x5, starting transfers between devices, in_pairs(): lax.ppermute(far, 'row', [(i, ((i + 1 ^ 1) - 1) % rows) for i in range(ro...  5.9 us
    ppermute x5, starting transfers between devices, in_pairs(): return (far, lax.ppermute(near, 'row', [(i, i ^ 1) for i in range(rows)]))  5.08 us
    ppermute x5, waiting for transfers between devices, in_pairs(): lax.ppermute(far, 'row', [(i, ((i + 1 ^ 1) - 1) % rows) for i in range(ro...  4.06 us
    pallas_call x7, Pallas kernels, call_all(): call(kernel, outputs, [VM] * len(operands), [VM] * len(outputs), scratch,...  2.62 us
    ppermute x8, waiting for transfers between devices, shift(): lax.ppermute(block, axis, [(i, (i + by) % count) for i in range(count)])  1.88 us
    pallas_call x2, Pallas kernels, final_of(): call(kernel, shape(slots, BLOCK * BLOCK), [VM] * 6 + [HB], VM, scratch, n...  1.77 us
    pallas_call x1, Pallas kernels, shards(): call(functools.partial(spread_kernel, grid, slots), [tiles_shape(r) for r...  1.35 us
  transfers between devices with their start and end apart: 18, of which 6 were waited for; matrix products, arithmetic and copies ran while one was open for 0% of the time, Pallas kernels for 9%

profile of v9, /device:TPU:1, one launch (start us, length us, event | category | flops | bytes accessed | tf_op | source)
XLA Modules:
  0.0 37.2 jit_solution(16983064727623959260)
XLA Ops:
  0.6 1.3 %spread.1 = (f32[208,128]{1,0:T(8,128)S(1)}, f32[192,128]{1,0:T(8,128)S(1)}, f32[192,128]{1,0:T(8,128)S(1)}, f32[200,128]{1,0:T(8,128)S(1)}, f32[4,8,128]{2,1,0:T(8,128)S(1)}) custom-call(s32[1,8]{1,0:T(1,128)} %bitcast.15, s32[1,8]{1,0:T(1,128)} %bitcast.16, f32[8,4096]{1,0:T(8,128)} %bitcast.10, f32[8,4096]{1,0:T(8,128)} %bitcast.13, s32[1,8]{1,0:T(1,128)} %bitcast.17, ...), custom_call_target="tpu_custom_call" | custom-call | bytes 1000000 | tf_op jit(solution)/shard_map/spread/pallas_call | solution.py:402
  2.0 2.2 %collective-permute-start = (f32[192,128]{1,0:T(8,128)S(1)}, f32[192,128]{1,0:T(8,128)S(1)}, u32[]{:S(2)}, u32[]{:S(2)}) collective-permute-start(f32[192,128]{1,0:T(8,128)S(1)} %get-tuple-element.31.first_right.refs_1_), channel_id=1, source_target_pairs={{0,1},{1,2},{2,3},{3,0},{4,5},{5,6},{6,7},{7,4},{8,9},{9,10},{10,1... | collective-permute-start | bytes 294920 | tf_op jit(solution)/shard_map/ppermute | solution.py:327
  4.2 0.1 ask.1
  4.3 1.0 %collective-permute-start.3 = (f32[216,128]{1,0:T(8,128)S(1)}, f32[216,128]{1,0:T(8,128)S(1)}, u32[]{:S(2)}, u32[]{:S(2)}) collective-permute-start(f32[216,128]{1,0:T(8,128)S(1)} %get-tuple-element.35), channel_id=1, source_target_pairs={{0,4},{4,0},{8,12},{12,8},{1,5},{5,1},{9,13},{13,9},{2,6},{6,2},{1... | collective-permute-start | bytes 331784 | tf_op jit(solution)/shard_map/ppermute | solution.py:378
  5.3 1.8 %collective-permute-start.1 = (f32[208,128]{1,0:T(8,128)S(1)}, f32[208,128]{1,0:T(8,128)S(1)}, u32[]{:S(2)}, u32[]{:S(2)}) collective-permute-start(f32[208,128]{1,0:T(8,128)S(1)} %get-tuple-element.30.first_left.refs_0_), channel_id=1, source_target_pairs={{0,3},{1,0},{2,1},{3,2},{4,7},{5,4},{6,5},{7,6},{8,11},{9,8},{10,9... | collective-permute-start | bytes 319496 | tf_op jit(solution)/shard_map/ppermute | solution.py:327
  7.0 1.6 %collective-permute-start.2 = (f32[208,128]{1,0:T(8,128)S(1)}, f32[208,128]{1,0:T(8,128)S(1)}, u32[]{:S(2)}, u32[]{:S(2)}) collective-permute-start(f32[208,128]{1,0:T(8,128)S(1)} %get-tuple-element.34), channel_id=1, source_target_pairs={{0,12},{4,8},{8,4},{12,0},{1,13},{5,9},{9,5},{13,1},{2,14},{6,10},... | collective-permute-start | bytes 319496 | tf_op jit(solution)/shard_map/ppermute | solution.py:377
  8.7 0.0 collective-permute-start.10
  8.7 0.0 collective-permute-done.refs_2_
  8.7 3.2 %collective-permute-start.11 = (f32[192,128]{1,0:T(8,128)S(1)}, f32[192,128]{1,0:T(8,128)S(1)}, u32[]{:S(2)}, u32[]{:S(2)}) collective-permute-start(f32[192,128]{1,0:T(8,128)S(1)} %get-tuple-element.32.second_left.refs_0_), channel_id=1, source_target_pairs={{0,3},{1,0},{2,1},{3,2},{4,7},{5,4},{6,5},{7,6},{8,11},{9,8},{10,9... | collective-permute-start | bytes 294920 | tf_op jit(solution)/shard_map/ppermute | solution.py:327
  12.0 0.0 collective-permute-done.1.refs_3_
  12.0 0.0 collective-permute-done.2.refs_4_
  12.0 0.0 collective-permute-done.3.refs_5_
  12.0 0.5 %first_share.2 = (f32[288,128]{1,0:T(8,128)S(1)}, f32[296,128]{1,0:T(8,128)S(1)}, f32[6,64,128]{2,1,0:T(8,128)S(1)}, bf16[2,384,384]{2,1,0:T(8,128)(2,1)S(1)}, bf16[2,192,384]{2,1,0:T(8,128)(2,1)S(1)}) custom-call(f32[208,128]{1,0:T(8,128)S(1)} %get-tuple-element.30.first_left.refs_0_, f32[192,128]{1,0:T(8,128)S(1)} %get-tuple-element.31.first_right.refs_1_, ...), custom_call_target="tpu_custom_call" | custom-call | bytes 1000000 | tf_op jit(solution)/shard_map/first_share/pallas_call | solution.py:368
  12.4 0.8 %collective-permute-start.5 = (f32[296,128]{1,0:T(8,128)S(1)}, f32[296,128]{1,0:T(8,128)S(1)}, u32[]{:S(2)}, u32[]{:S(2)}) collective-permute-start(f32[296,128]{1,0:T(8,128)S(1)} %get-tuple-element.38.refs_9_), channel_id=1, source_target_pairs={{0,4},{4,0},{8,12},{12,8},{1,5},{5,1},{9,13},{13,9},{2,6},{6,2},{1... | collective-permute-start | bytes 454664 | tf_op jit(solution)/shard_map/ppermute | solution.py:378
  13.2 1.1 %collective-permute-start.4 = (f32[288,128]{1,0:T(8,128)S(1)}, f32[288,128]{1,0:T(8,128)S(1)}, u32[]{:S(2)}, u32[]{:S(2)}) collective-permute-start(f32[288,128]{1,0:T(8,128)S(1)} %get-tuple-element.37.refs_8_), channel_id=1, source_target_pairs={{0,12},{4,8},{8,4},{12,0},{1,13},{5,9},{9,5},{13,1},{2,14},{6,10},... | collective-permute-start | bytes 442376 | tf_op jit(solution)/shard_map/ppermute | solution.py:377
  14.3 0.0 collective-permute-done.11.refs_3_
  14.3 0.5 %collective-permute-done.10.refs_2_ = f32[200,128]{1,0:T(8,128)S(1)} collective-permute-done((f32[200,128]{1,0:T(8,128)S(1)}, f32[200,128]{1,0:T(8,128)S(1)}, u32[]{:S(2)}, u32[]{:S(2)}) %collective-permute-start.10) | collective-permute-done | bytes 102432 | tf_op jit(solution)/shard_map/ppermute | solution.py:327
  14.9 0.6 %second_share.2 = (f32[288,128]{1,0:T(8,128)S(1)}, f32[296,128]{1,0:T(8,128)S(1)}, f32[6,64,128]{2,1,0:T(8,128)S(1)}) custom-call(f32[192,128]{1,0:T(8,128)S(1)} %get-tuple-element.32.second_left.refs_0_, f32[200,128]{1,0:T(8,128)S(1)} %get-tuple-element.33.second_right.refs_1_, f32[200,128]{1,0:T(8,128)S(1)} %collective-permute-done.10.refs_2_, ...), custom_call_target="tpu_custom_call" | custom-call | bytes 1000000 | tf_op jit(solution)/shard_map/second_share/pallas_call | solution.py:368
  15.5 2.1 %collective-permute-start.13 = (f32[296,128]{1,0:T(8,128)S(1)}, f32[296,128]{1,0:T(8,128)S(1)}, u32[]{:S(2)}, u32[]{:S(2)}) collective-permute-start(f32[296,128]{1,0:T(8,128)S(1)} %get-tuple-element.48.refs_9_), channel_id=1, source_target_pairs={{0,4},{4,0},{8,12},{12,8},{1,5},{5,1},{9,13},{13,9},{2,6},{6,2},{1... | collective-permute-start | bytes 454664 | tf_op jit(solution)/shard_map/ppermute | solution.py:378
  17.6 0.8 %collective-permute-start.12 = (f32[288,128]{1,0:T(8,128)S(1)}, f32[288,128]{1,0:T(8,128)S(1)}, u32[]{:S(2)}, u32[]{:S(2)}) collective-permute-start(f32[288,128]{1,0:T(8,128)S(1)} %get-tuple-element.47.refs_8_), channel_id=1, source_target_pairs={{0,12},{4,8},{8,4},{12,0},{1,13},{5,9},{9,5},{13,1},{2,14},{6,10},... | collective-permute-start | bytes 442376 | tf_op jit(solution)/shard_map/ppermute | solution.py:377
  18.4 0.4 collective-permute-done.4.far.refs_6_
  18.8 0.0 collective-permute-done.5.near.refs_7_
  18.8 0.1 first_next.1
  18.9 0.1 collective-permute-start.6
  19.0 3.3 %collective-permute-start.7 = (f32[200,128]{1,0:T(8,128)S(1)}, f32[200,128]{1,0:T(8,128)S(1)}, u32[]{:S(2)}, u32[]{:S(2)}) collective-permute-start(f32[200,128]{1,0:T(8,128)S(1)} %get-tuple-element.39.refs_0_.own_left), channel_id=1, source_target_pairs={{0,3},{1,0},{2,1},{3,2},{4,7},{5,4},{6,5},{7,6},{8,11},{9,8},{10,9... | collective-permute-start | bytes 307208 | tf_op jit(solution)/shard_map/ppermute | solution.py:327
  22.2 1.2 %collective-permute-done.12.far.refs_6_ = f32[288,128]{1,0:T(8,128)S(1)} collective-permute-done((f32[288,128]{1,0:T(8,128)S(1)}, f32[288,128]{1,0:T(8,128)S(1)}, u32[]{:S(2)}, u32[]{:S(2)}) %collective-permute-start.12) | collective-permute-done | bytes 147488 | tf_op jit(solution)/shard_map/ppermute | solution.py:377
  23.4 0.0 collective-permute-done.13.near.refs_7_
  23.4 0.1 second_next.1
  23.5 0.1 collective-permute-start.14
  23.6 3.3 %collective-permute-start.15 = (f32[192,128]{1,0:T(8,128)S(1)}, f32[192,128]{1,0:T(8,128)S(1)}, u32[]{:S(2)}, u32[]{:S(2)}) collective-permute-start(f32[192,128]{1,0:T(8,128)S(1)} %get-tuple-element.49.refs_0_.own_left), channel_id=1, source_target_pairs={{0,3},{1,0},{2,1},{3,2},{4,7},{5,4},{6,5},{7,6},{8,11},{9,8},{10,9... | collective-permute-start | bytes 294920 | tf_op jit(solution)/shard_map/ppermute | solution.py:327
  26.9 0.0 collective-permute-done.7.refs_3_
  26.9 0.0 collective-permute-done.6.refs_2_
  26.9 0.5 %first_share.3 = (f32[200,128]{1,0:T(8,128)S(1)}, f32[200,128]{1,0:T(8,128)S(1)}, f32[6,64,128]{2,1,0:T(8,128)S(1)}, bf16[2,384,384]{2,1,0:T(8,128)(2,1)S(1)}, bf16[2,192,384]{2,1,0:T(8,128)(2,1)S(1)}) custom-call(f32[200,128]{1,0:T(8,128)S(1)} %get-tuple-element.39.refs_0_.own_left, f32[208,128]{1,0:T(8,128)S(1)} %get-tuple-element.40.refs_1_.own_right, ...), custom_call_target="tpu_custom_call" | custom-call | bytes 1000000 | tf_op jit(solution)/shard_map/first_share/pallas_call | solution.py:368
  27.4 1.2 %collective-permute-start.8 = (f32[200,128]{1,0:T(8,128)S(1)}, f32[200,128]{1,0:T(8,128)S(1)}, u32[]{:S(2)}, u32[]{:S(2)}) collective-permute-start(f32[200,128]{1,0:T(8,128)S(1)} %get-tuple-element.42), channel_id=1, source_target_pairs={{0,12},{4,8},{8,4},{12,0},{1,13},{5,9},{9,5},{13,1},{2,14},{6,10},... | collective-permute-start | bytes 307208 | tf_op jit(solution)/shard_map/ppermute | solution.py:377
  28.7 0.1 collective-permute-start.9
  28.7 0.3 collective-permute-done.15.refs_3_
  29.0 1.0 %collective-permute-done.14.refs_2_ = f32[200,128]{1,0:T(8,128)S(1)} collective-permute-done((f32[200,128]{1,0:T(8,128)S(1)}, f32[200,128]{1,0:T(8,128)S(1)}, u32[]{:S(2)}, u32[]{:S(2)}) %collective-permute-start.14) | collective-permute-done | bytes 102432 | tf_op jit(solution)/shard_map/ppermute | solution.py:327
  30.1 0.7 %second_share.3 = (f32[192,128]{1,0:T(8,128)S(1)}, f32[200,128]{1,0:T(8,128)S(1)}, f32[6,64,128]{2,1,0:T(8,128)S(1)}) custom-call(f32[192,128]{1,0:T(8,128)S(1)} %get-tuple-element.49.refs_0_.own_left, f32[200,128]{1,0:T(8,128)S(1)} %get-tuple-element.50.refs_1_.own_right, f32[200,128]{1,0:T(8,128)S(1)} %collective-permute-done.14.refs_2_, ...), custom_call_target="tpu_custom_call" | custom-call | bytes 1000000 | tf_op jit(solution)/shard_map/second_share/pallas_call | solution.py:368
  30.7 1.1 %collective-permute-start.17 = (f32[200,128]{1,0:T(8,128)S(1)}, f32[200,128]{1,0:T(8,128)S(1)}, u32[]{:S(2)}, u32[]{:S(2)}) collective-permute-start(f32[200,128]{1,0:T(8,128)S(1)} %get-tuple-element.55), channel_id=1, source_target_pairs={{0,4},{4,0},{8,12},{12,8},{1,5},{5,1},{9,13},{13,9},{2,6},{6,2},{1... | collective-permute-start | bytes 307208 | tf_op jit(solution)/shard_map/ppermute | solution.py:378
  31.8 1.1 %collective-permute-start.16 = (f32[192,128]{1,0:T(8,128)S(1)}, f32[192,128]{1,0:T(8,128)S(1)}, u32[]{:S(2)}, u32[]{:S(2)}) collective-permute-start(f32[192,128]{1,0:T(8,128)S(1)} %get-tuple-element.54), channel_id=1, source_target_pairs={{0,12},{4,8},{8,4},{12,0},{1,13},{5,9},{9,5},{13,1},{2,14},{6,10},... | collective-permute-start | bytes 294920 | tf_op jit(solution)/shard_map/ppermute | solution.py:377
  32.9 0.0 collective-permute-done.8.far
  32.9 0.0 collective-permute-done.9.near
  32.9 0.9 %first_final.1._ = f32[8,4096]{1,0:T(8,128)} custom-call(f32[4,8,128]{2,1,0:T(8,128)S(1)} %get-tuple-element.29.idents, f32[200,128]{1,0:T(8,128)S(1)} %get-tuple-element.39.refs_0_.own_left, f32[208,128]{1,0:T(8,128)S(1)} %get-tuple-element.40.refs_1_.own_right, f32[6,64,128]{2,1,0:T(8,128)S(1)} %get-tuple-element.41.sums, ...), custom_call_target="tpu_custom_call" | custom-call | bytes 1000000 | tf_op jit(solution)/shard_map/first_final/pallas_call | solution.py:474
  33.8 2.5 %collective-permute-done.16.far = f32[192,128]{1,0:T(8,128)S(1)} collective-permute-done((f32[192,128]{1,0:T(8,128)S(1)}, f32[192,128]{1,0:T(8,128)S(1)}, u32[]{:S(2)}, u32[]{:S(2)}) %collective-permute-start.16) | collective-permute-done | bytes 98336 | tf_op jit(solution)/shard_map/ppermute | solution.py:377
  36.3 0.0 collective-permute-done.17.near
  36.3 0.9 %second_final.1 = f32[8,4096]{1,0:T(8,128)} custom-call(f32[4,8,128]{2,1,0:T(8,128)S(1)} %get-tuple-element.29.idents, f32[192,128]{1,0:T(8,128)S(1)} %get-tuple-element.49.refs_0_.own_left, f32[200,128]{1,0:T(8,128)S(1)} %get-tuple-element.50.refs_1_.own_right, f32[6,64,128]{2,1,0:T(8,128)S(1)} %get-tuple-element.53.sums, ...), custom_call_target="tpu_custom_call" | custom-call | bytes 1000000 | tf_op jit(solution)/shard_map/second_final/pallas_call | solution.py:474
Async XLA Ops:
  2.0 6.7 %collective-permute-start = (f32[192,128]{1,0:T(8,128)S(1)}, f32[192,128]{1,0:T(8,128)S(1)}, u32[]{:S(2)}, u32[]{:S(2)}) collective-permute-start(f32[192,128]{1,0:T(8,128)S(1)} %get-tuple-element.31.first_right.refs_1_), channel_id=1, source_target_pairs={{0,1},{1,2},{2,3},{3,0},{4,5},{5,6},{6,7},{7,4},{8,9},{9,10},{10,1... | collective-permute-start | bytes 294920 | tf_op jit(solution)/shard_map/ppermute | solution.py:327
  4.3 7.7 %collective-permute-start.3 = (f32[216,128]{1,0:T(8,128)S(1)}, f32[216,128]{1,0:T(8,128)S(1)}, u32[]{:S(2)}, u32[]{:S(2)}) collective-permute-start(f32[216,128]{1,0:T(8,128)S(1)} %get-tuple-element.35), channel_id=1, source_target_pairs={{0,4},{4,0},{8,12},{12,8},{1,5},{5,1},{9,13},{13,9},{2,6},{6,2},{1... | collective-permute-start | bytes 331784 | tf_op jit(solution)/shard_map/ppermute | solution.py:378
  5.3 6.7 %collective-permute-start.1 = (f32[208,128]{1,0:T(8,128)S(1)}, f32[208,128]{1,0:T(8,128)S(1)}, u32[]{:S(2)}, u32[]{:S(2)}) collective-permute-start(f32[208,128]{1,0:T(8,128)S(1)} %get-tuple-element.30.first_left.refs_0_), channel_id=1, source_target_pairs={{0,3},{1,0},{2,1},{3,2},{4,7},{5,4},{6,5},{7,6},{8,11},{9,8},{10,9... | collective-permute-start | bytes 319496 | tf_op jit(solution)/shard_map/ppermute | solution.py:327
  7.0 4.9 %collective-permute-start.2 = (f32[208,128]{1,0:T(8,128)S(1)}, f32[208,128]{1,0:T(8,128)S(1)}, u32[]{:S(2)}, u32[]{:S(2)}) collective-permute-start(f32[208,128]{1,0:T(8,128)S(1)} %get-tuple-element.34), channel_id=1, source_target_pairs={{0,12},{4,8},{8,4},{12,0},{1,13},{5,9},{9,5},{13,1},{2,14},{6,10},... | collective-permute-start | bytes 319496 | tf_op jit(solution)/shard_map/ppermute | solution.py:377
  8.7 6.2 %collective-permute-start.10 = (f32[200,128]{1,0:T(8,128)S(1)}, f32[200,128]{1,0:T(8,128)S(1)}, u32[]{:S(2)}, u32[]{:S(2)}) collective-permute-start(f32[200,128]{1,0:T(8,128)S(1)} %get-tuple-element.33.second_right.refs_1_), channel_id=1, source_target_pairs={{0,1},{1,2},{2,3},{3,0},{4,5},{5,6},{6,7},{7,4},{8,9},{9,10},{10,1... | collective-permute-start | bytes 307208 | tf_op jit(solution)/shard_map/ppermute | solution.py:327
  8.7 5.6 %collective-permute-start.11 = (f32[192,128]{1,0:T(8,128)S(1)}, f32[192,128]{1,0:T(8,128)S(1)}, u32[]{:S(2)}, u32[]{:S(2)}) collective-permute-start(f32[192,128]{1,0:T(8,128)S(1)} %get-tuple-element.32.second_left.refs_0_), channel_id=1, source_target_pairs={{0,3},{1,0},{2,1},{3,2},{4,7},{5,4},{6,5},{7,6},{8,11},{9,8},{10,9... | collective-permute-start | bytes 294920 | tf_op jit(solution)/shard_map/ppermute | solution.py:327
  12.4 6.3 %collective-permute-start.5 = (f32[296,128]{1,0:T(8,128)S(1)}, f32[296,128]{1,0:T(8,128)S(1)}, u32[]{:S(2)}, u32[]{:S(2)}) collective-permute-start(f32[296,128]{1,0:T(8,128)S(1)} %get-tuple-element.38.refs_9_), channel_id=1, source_target_pairs={{0,4},{4,0},{8,12},{12,8},{1,5},{5,1},{9,13},{13,9},{2,6},{6,2},{1... | collective-permute-start | bytes 454664 | tf_op jit(solution)/shard_map/ppermute | solution.py:378
  13.2 5.5 %collective-permute-start.4 = (f32[288,128]{1,0:T(8,128)S(1)}, f32[288,128]{1,0:T(8,128)S(1)}, u32[]{:S(2)}, u32[]{:S(2)}) collective-permute-start(f32[288,128]{1,0:T(8,128)S(1)} %get-tuple-element.37.refs_8_), channel_id=1, source_target_pairs={{0,12},{4,8},{8,4},{12,0},{1,13},{5,9},{9,5},{13,1},{2,14},{6,10},... | collective-permute-start | bytes 442376 | tf_op jit(solution)/shard_map/ppermute | solution.py:377
  15.5 7.9 %collective-permute-start.13 = (f32[296,128]{1,0:T(8,128)S(1)}, f32[296,128]{1,0:T(8,128)S(1)}, u32[]{:S(2)}, u32[]{:S(2)}) collective-permute-start(f32[296,128]{1,0:T(8,128)S(1)} %get-tuple-element.48.refs_9_), channel_id=1, source_target_pairs={{0,4},{4,0},{8,12},{12,8},{1,5},{5,1},{9,13},{13,9},{2,6},{6,2},{1... | collective-permute-start | bytes 454664 | tf_op jit(solution)/shard_map/ppermute | solution.py:378
  17.6 5.8 %collective-permute-start.12 = (f32[288,128]{1,0:T(8,128)S(1)}, f32[288,128]{1,0:T(8,128)S(1)}, u32[]{:S(2)}, u32[]{:S(2)}) collective-permute-start(f32[288,128]{1,0:T(8,128)S(1)} %get-tuple-element.47.refs_8_), channel_id=1, source_target_pairs={{0,12},{4,8},{8,4},{12,0},{1,13},{5,9},{9,5},{13,1},{2,14},{6,10},... | collective-permute-start | bytes 442376 | tf_op jit(solution)/shard_map/ppermute | solution.py:377
  18.9 8.0 %collective-permute-start.6 = (f32[208,128]{1,0:T(8,128)S(1)}, f32[208,128]{1,0:T(8,128)S(1)}, u32[]{:S(2)}, u32[]{:S(2)}) collective-permute-start(f32[208,128]{1,0:T(8,128)S(1)} %get-tuple-element.40.refs_1_.own_right), channel_id=1, source_target_pairs={{0,1},{1,2},{2,3},{3,0},{4,5},{5,6},{6,7},{7,4},{8,9},{9,10},{10,1... | collective-permute-start | bytes 319496 | tf_op jit(solution)/shard_map/ppermute | solution.py:327
  19.0 7.9 %collective-permute-start.7 = (f32[200,128]{1,0:T(8,128)S(1)}, f32[200,128]{1,0:T(8,128)S(1)}, u32[]{:S(2)}, u32[]{:S(2)}) collective-permute-start(f32[200,128]{1,0:T(8,128)S(1)} %get-tuple-element.39.refs_0_.own_left), channel_id=1, source_target_pairs={{0,3},{1,0},{2,1},{3,2},{4,7},{5,4},{6,5},{7,6},{8,11},{9,8},{10,9... | collective-permute-start | bytes 307208 | tf_op jit(solution)/shard_map/ppermute | solution.py:327
  23.5 6.5 %collective-permute-start.14 = (f32[200,128]{1,0:T(8,128)S(1)}, f32[200,128]{1,0:T(8,128)S(1)}, u32[]{:S(2)}, u32[]{:S(2)}) collective-permute-start(f32[200,128]{1,0:T(8,128)S(1)} %get-tuple-element.50.refs_1_.own_right), channel_id=1, source_target_pairs={{0,1},{1,2},{2,3},{3,0},{4,5},{5,6},{6,7},{7,4},{8,9},{9,10},{10,1... | collective-permute-start | bytes 307208 | tf_op jit(solution)/shard_map/ppermute | solution.py:327
  23.6 5.4 %collective-permute-start.15 = (f32[192,128]{1,0:T(8,128)S(1)}, f32[192,128]{1,0:T(8,128)S(1)}, u32[]{:S(2)}, u32[]{:S(2)}) collective-permute-start(f32[192,128]{1,0:T(8,128)S(1)} %get-tuple-element.49.refs_0_.own_left), channel_id=1, source_target_pairs={{0,3},{1,0},{2,1},{3,2},{4,7},{5,4},{6,5},{7,6},{8,11},{9,8},{10,9... | collective-permute-start | bytes 294920 | tf_op jit(solution)/shard_map/ppermute | solution.py:327
  27.4 5.5 %collective-permute-start.8 = (f32[200,128]{1,0:T(8,128)S(1)}, f32[200,128]{1,0:T(8,128)S(1)}, u32[]{:S(2)}, u32[]{:S(2)}) collective-permute-start(f32[200,128]{1,0:T(8,128)S(1)} %get-tuple-element.42), channel_id=1, source_target_pairs={{0,12},{4,8},{8,4},{12,0},{1,13},{5,9},{9,5},{13,1},{2,14},{6,10},... | collective-permute-start | bytes 307208 | tf_op jit(solution)/shard_map/ppermute | solution.py:377
  28.7 4.3 %collective-permute-start.9 = (f32[200,128]{1,0:T(8,128)S(1)}, f32[200,128]{1,0:T(8,128)S(1)}, u32[]{:S(2)}, u32[]{:S(2)}) collective-permute-start(f32[200,128]{1,0:T(8,128)S(1)} %get-tuple-element.43), channel_id=1, source_target_pairs={{0,4},{4,0},{8,12},{12,8},{1,5},{5,1},{9,13},{13,9},{2,6},{6,2},{1... | collective-permute-start | bytes 307208 | tf_op jit(solution)/shard_map/ppermute | solution.py:378
  30.7 5.6 %collective-permute-start.17 = (f32[200,128]{1,0:T(8,128)S(1)}, f32[200,128]{1,0:T(8,128)S(1)}, u32[]{:S(2)}, u32[]{:S(2)}) collective-permute-start(f32[200,128]{1,0:T(8,128)S(1)} %get-tuple-element.55), channel_id=1, source_target_pairs={{0,4},{4,0},{8,12},{12,8},{1,5},{5,1},{9,13},{13,9},{2,6},{6,2},{1... | collective-permute-start | bytes 307208 | tf_op jit(solution)/shard_map/ppermute | solution.py:378
  31.8 4.5 %collective-permute-start.16 = (f32[192,128]{1,0:T(8,128)S(1)}, f32[192,128]{1,0:T(8,128)S(1)}, u32[]{:S(2)}, u32[]{:S(2)}) collective-permute-start(f32[192,128]{1,0:T(8,128)S(1)} %get-tuple-element.54), channel_id=1, source_target_pairs={{0,12},{4,8},{8,4},{12,0},{1,13},{5,9},{9,5},{13,1},{2,14},{6,10},... | collective-permute-start | bytes 294920 | tf_op jit(solution)/shard_map/ppermute | solution.py:377

commit v10 on v9

--- a/solution.py
+++ b/solution.py
@@ -67,7 +67,7 @@
 
 def fetch(sources, targets, sems):
     copies = [pltpu.make_async_copy(s, t, sems.at[i]) for i, (s, t) in enumerate(zip(sources, targets))]
-    for copy in copies:
+    for copy in copies[2:4] + copies[:2] + copies[4:]:
         copy.start()
     return copies
 

time: 37.4 us -> 37.5 us (level)
  no operation moved by 1% of the time
where the time goes in v10:
time: 37.5 us; the launch traced here: 37.3 us
  starting transfers between devices  24.8 us (66%)
  waiting for transfers between devices  5.94 us (16%)
  Pallas kernels  5.83 us (16%)
  between operations  0.72 us (2%)
    ppermute x8, starting transfers between devices, shift(): lax.ppermute(block, axis, [(i, (i + by) % count) for i in range(count)])  13.8 us
    ppermute x5, starting transfers between devices, in_pairs(): lax.ppermute(far, 'row', [(i, ((i + 1 ^ 1) - 1) % rows) for i in range(ro...  5.9 us
    ppermute x5, starting transfers between devices, in_pairs(): return (far, lax.ppermute(near, 'row', [(i, i ^ 1) for i in range(rows)]))  5.08 us
    ppermute x5, waiting for transfers between devices, in_pairs(): lax.ppermute(far, 'row', [(i, ((i + 1 ^ 1) - 1) % rows) for i in range(ro...  4.06 us
    pallas_call x7, Pallas kernels, call_all(): call(kernel, outputs, [VM] * len(operands), [VM] * len(outputs), scratch,...  2.62 us
    ppermute x8, waiting for transfers between devices, shift(): lax.ppermute(block, axis, [(i, (i + by) % count) for i in range(count)])  1.87 us
    pallas_call x2, Pallas kernels, final_of(): call(kernel, shape(slots, BLOCK * BLOCK), [VM] * 6 + [HB], VM, scratch, n...  1.77 us
    pallas_call x1, Pallas kernels, shards(): call(functools.partial(spread_kernel, grid, slots), [tiles_shape(r) for r...  1.44 us
  transfers between devices with their start and end apart: 18, of which 6 were waited for; matrix products, arithmetic and copies ran while one was open for 0% of the time, Pallas kernels for 9%

profile of v10, /device:TPU:1, one launch (start us, length us, event | category | flops | bytes accessed | tf_op | source)
XLA Modules:
  0.0 37.3 jit_solution(17632295701719284417)
XLA Ops:
  0.6 1.4 %spread.1 = (f32[208,128]{1,0:T(8,128)S(1)}, f32[192,128]{1,0:T(8,128)S(1)}, f32[192,128]{1,0:T(8,128)S(1)}, f32[200,128]{1,0:T(8,128)S(1)}, f32[4,8,128]{2,1,0:T(8,128)S(1)}) custom-call(s32[1,8]{1,0:T(1,128)} %bitcast.15, s32[1,8]{1,0:T(1,128)} %bitcast.16, f32[8,4096]{1,0:T(8,128)} %bitcast.10, f32[8,4096]{1,0:T(8,128)} %bitcast.13, s32[1,8]{1,0:T(1,128)} %bitcast.17, ...), custom_call_target="tpu_custom_call" | custom-call | bytes 1000000 | tf_op jit(solution)/shard_map/spread/pallas_call | solution.py:402
  2.1 2.2 %collective-permute-start = (f32[192,128]{1,0:T(8,128)S(1)}, f32[192,128]{1,0:T(8,128)S(1)}, u32[]{:S(2)}, u32[]{:S(2)}) collective-permute-start(f32[192,128]{1,0:T(8,128)S(1)} %get-tuple-element.31.first_right.refs_1_), channel_id=1, source_target_pairs={{0,1},{1,2},{2,3},{3,0},{4,5},{5,6},{6,7},{7,4},{8,9},{9,10},{10,1... | collective-permute-start | bytes 294920 | tf_op jit(solution)/shard_map/ppermute | solution.py:327
  4.3 0.1 ask.1
  4.3 1.0 %collective-permute-start.3 = (f32[216,128]{1,0:T(8,128)S(1)}, f32[216,128]{1,0:T(8,128)S(1)}, u32[]{:S(2)}, u32[]{:S(2)}) collective-permute-start(f32[216,128]{1,0:T(8,128)S(1)} %get-tuple-element.35), channel_id=1, source_target_pairs={{0,4},{4,0},{8,12},{12,8},{1,5},{5,1},{9,13},{13,9},{2,6},{6,2},{1... | collective-permute-start | bytes 331784 | tf_op jit(solution)/shard_map/ppermute | solution.py:378
  5.4 1.8 %collective-permute-start.1 = (f32[208,128]{1,0:T(8,128)S(1)}, f32[208,128]{1,0:T(8,128)S(1)}, u32[]{:S(2)}, u32[]{:S(2)}) collective-permute-start(f32[208,128]{1,0:T(8,128)S(1)} %get-tuple-element.30.first_left.refs_0_), channel_id=1, source_target_pairs={{0,3},{1,0},{2,1},{3,2},{4,7},{5,4},{6,5},{7,6},{8,11},{9,8},{10,9... | collective-permute-start | bytes 319496 | tf_op jit(solution)/shard_map/ppermute | solution.py:327
  7.1 1.6 %collective-permute-start.2 = (f32[208,128]{1,0:T(8,128)S(1)}, f32[208,128]{1,0:T(8,128)S(1)}, u32[]{:S(2)}, u32[]{:S(2)}) collective-permute-start(f32[208,128]{1,0:T(8,128)S(1)} %get-tuple-element.34), channel_id=1, source_target_pairs={{0,12},{4,8},{8,4},{12,0},{1,13},{5,9},{9,5},{13,1},{2,14},{6,10},... | collective-permute-start | bytes 319496 | tf_op jit(solution)/shard_map/ppermute | solution.py:377
  8.8 0.0 collective-permute-start.10
  8.8 0.0 collective-permute-done.refs_2_
  8.8 3.2 %collective-permute-start.11 = (f32[192,128]{1,0:T(8,128)S(1)}, f32[192,128]{1,0:T(8,128)S(1)}, u32[]{:S(2)}, u32[]{:S(2)}) collective-permute-start(f32[192,128]{1,0:T(8,128)S(1)} %get-tuple-element.32.second_left.refs_0_), channel_id=1, source_target_pairs={{0,3},{1,0},{2,1},{3,2},{4,7},{5,4},{6,5},{7,6},{8,11},{9,8},{10,9... | collective-permute-start | bytes 294920 | tf_op jit(solution)/shard_map/ppermute | solution.py:327
  12.0 0.0 collective-permute-done.1.refs_3_
  12.0 0.0 collective-permute-done.2.refs_4_
  12.1 0.0 collective-permute-done.3.refs_5_
  12.1 0.5 %first_share.2 = (f32[288,128]{1,0:T(8,128)S(1)}, f32[296,128]{1,0:T(8,128)S(1)}, f32[6,64,128]{2,1,0:T(8,128)S(1)}, bf16[2,384,384]{2,1,0:T(8,128)(2,1)S(1)}, bf16[2,192,384]{2,1,0:T(8,128)(2,1)S(1)}) custom-call(f32[208,128]{1,0:T(8,128)S(1)} %get-tuple-element.30.first_left.refs_0_, f32[192,128]{1,0:T(8,128)S(1)} %get-tuple-element.31.first_right.refs_1_, ...), custom_call_target="tpu_custom_call" | custom-call | bytes 1000000 | tf_op jit(solution)/shard_map/first_share/pallas_call | solution.py:368
  12.5 0.8 %collective-permute-start.5 = (f32[296,128]{1,0:T(8,128)S(1)}, f32[296,128]{1,0:T(8,128)S(1)}, u32[]{:S(2)}, u32[]{:S(2)}) collective-permute-start(f32[296,128]{1,0:T(8,128)S(1)} %get-tuple-element.38.refs_9_), channel_id=1, source_target_pairs={{0,4},{4,0},{8,12},{12,8},{1,5},{5,1},{9,13},{13,9},{2,6},{6,2},{1... | collective-permute-start | bytes 454664 | tf_op jit(solution)/shard_map/ppermute | solution.py:378
  13.3 1.1 %collective-permute-start.4 = (f32[288,128]{1,0:T(8,128)S(1)}, f32[288,128]{1,0:T(8,128)S(1)}, u32[]{:S(2)}, u32[]{:S(2)}) collective-permute-start(f32[288,128]{1,0:T(8,128)S(1)} %get-tuple-element.37.refs_8_), channel_id=1, source_target_pairs={{0,12},{4,8},{8,4},{12,0},{1,13},{5,9},{9,5},{13,1},{2,14},{6,10},... | collective-permute-start | bytes 442376 | tf_op jit(solution)/shard_map/ppermute | solution.py:377
  14.4 0.0 collective-permute-done.11.refs_3_
  14.4 0.5 %collective-permute-done.10.refs_2_ = f32[200,128]{1,0:T(8,128)S(1)} collective-permute-done((f32[200,128]{1,0:T(8,128)S(1)}, f32[200,128]{1,0:T(8,128)S(1)}, u32[]{:S(2)}, u32[]{:S(2)}) %collective-permute-start.10) | collective-permute-done | bytes 102432 | tf_op jit(solution)/shard_map/ppermute | solution.py:327
  14.9 0.6 %second_share.2 = (f32[288,128]{1,0:T(8,128)S(1)}, f32[296,128]{1,0:T(8,128)S(1)}, f32[6,64,128]{2,1,0:T(8,128)S(1)}) custom-call(f32[192,128]{1,0:T(8,128)S(1)} %get-tuple-element.32.second_left.refs_0_, f32[200,128]{1,0:T(8,128)S(1)} %get-tuple-element.33.second_right.refs_1_, f32[200,128]{1,0:T(8,128)S(1)} %collective-permute-done.10.refs_2_, ...), custom_call_target="tpu_custom_call" | custom-call | bytes 1000000 | tf_op jit(solution)/shard_map/second_share/pallas_call | solution.py:368
  15.6 2.1 %collective-permute-start.13 = (f32[296,128]{1,0:T(8,128)S(1)}, f32[296,128]{1,0:T(8,128)S(1)}, u32[]{:S(2)}, u32[]{:S(2)}) collective-permute-start(f32[296,128]{1,0:T(8,128)S(1)} %get-tuple-element.48.refs_9_), channel_id=1, source_target_pairs={{0,4},{4,0},{8,12},{12,8},{1,5},{5,1},{9,13},{13,9},{2,6},{6,2},{1... | collective-permute-start | bytes 454664 | tf_op jit(solution)/shard_map/ppermute | solution.py:378
  17.7 0.8 %collective-permute-start.12 = (f32[288,128]{1,0:T(8,128)S(1)}, f32[288,128]{1,0:T(8,128)S(1)}, u32[]{:S(2)}, u32[]{:S(2)}) collective-permute-start(f32[288,128]{1,0:T(8,128)S(1)} %get-tuple-element.47.refs_8_), channel_id=1, source_target_pairs={{0,12},{4,8},{8,4},{12,0},{1,13},{5,9},{9,5},{13,1},{2,14},{6,10},... | collective-permute-start | bytes 442376 | tf_op jit(solution)/shard_map/ppermute | solution.py:377
  18.5 0.4 collective-permute-done.4.far.refs_6_
  18.9 0.0 collective-permute-done.5.near.refs_7_
  18.9 0.1 first_next.1
  19.0 0.1 collective-permute-start.6
  19.1 3.3 %collective-permute-start.7 = (f32[200,128]{1,0:T(8,128)S(1)}, f32[200,128]{1,0:T(8,128)S(1)}, u32[]{:S(2)}, u32[]{:S(2)}) collective-permute-start(f32[200,128]{1,0:T(8,128)S(1)} %get-tuple-element.39.refs_0_.own_left), channel_id=1, source_target_pairs={{0,3},{1,0},{2,1},{3,2},{4,7},{5,4},{6,5},{7,6},{8,11},{9,8},{10,9... | collective-permute-start | bytes 307208 | tf_op jit(solution)/shard_map/ppermute | solution.py:327
  22.3 1.2 %collective-permute-done.12.far.refs_6_ = f32[288,128]{1,0:T(8,128)S(1)} collective-permute-done((f32[288,128]{1,0:T(8,128)S(1)}, f32[288,128]{1,0:T(8,128)S(1)}, u32[]{:S(2)}, u32[]{:S(2)}) %collective-permute-start.12) | collective-permute-done | bytes 147488 | tf_op jit(solution)/shard_map/ppermute | solution.py:377
  23.5 0.0 collective-permute-done.13.near.refs_7_
  23.5 0.1 second_next.1
  23.6 0.1 collective-permute-start.14
  23.7 3.3 %collective-permute-start.15 = (f32[192,128]{1,0:T(8,128)S(1)}, f32[192,128]{1,0:T(8,128)S(1)}, u32[]{:S(2)}, u32[]{:S(2)}) collective-permute-start(f32[192,128]{1,0:T(8,128)S(1)} %get-tuple-element.49.refs_0_.own_left), channel_id=1, source_target_pairs={{0,3},{1,0},{2,1},{3,2},{4,7},{5,4},{6,5},{7,6},{8,11},{9,8},{10,9... | collective-permute-start | bytes 294920 | tf_op jit(solution)/shard_map/ppermute | solution.py:327
  27.0 0.0 collective-permute-done.7.refs_3_
  27.0 0.0 collective-permute-done.6.refs_2_
  27.0 0.5 %first_share.3 = (f32[200,128]{1,0:T(8,128)S(1)}, f32[200,128]{1,0:T(8,128)S(1)}, f32[6,64,128]{2,1,0:T(8,128)S(1)}, bf16[2,384,384]{2,1,0:T(8,128)(2,1)S(1)}, bf16[2,192,384]{2,1,0:T(8,128)(2,1)S(1)}) custom-call(f32[200,128]{1,0:T(8,128)S(1)} %get-tuple-element.39.refs_0_.own_left, f32[208,128]{1,0:T(8,128)S(1)} %get-tuple-element.40.refs_1_.own_right, ...), custom_call_target="tpu_custom_call" | custom-call | bytes 1000000 | tf_op jit(solution)/shard_map/first_share/pallas_call | solution.py:368
  27.5 1.2 %collective-permute-start.8 = (f32[200,128]{1,0:T(8,128)S(1)}, f32[200,128]{1,0:T(8,128)S(1)}, u32[]{:S(2)}, u32[]{:S(2)}) collective-permute-start(f32[200,128]{1,0:T(8,128)S(1)} %get-tuple-element.42), channel_id=1, source_target_pairs={{0,12},{4,8},{8,4},{12,0},{1,13},{5,9},{9,5},{13,1},{2,14},{6,10},... | collective-permute-start | bytes 307208 | tf_op jit(solution)/shard_map/ppermute | solution.py:377
  28.8 0.1 collective-permute-start.9
  28.8 0.3 collective-permute-done.15.refs_3_
  29.1 1.0 %collective-permute-done.14.refs_2_ = f32[200,128]{1,0:T(8,128)S(1)} collective-permute-done((f32[200,128]{1,0:T(8,128)S(1)}, f32[200,128]{1,0:T(8,128)S(1)}, u32[]{:S(2)}, u32[]{:S(2)}) %collective-permute-start.14) | collective-permute-done | bytes 102432 | tf_op jit(solution)/shard_map/ppermute | solution.py:327
  30.1 0.7 %second_share.3 = (f32[192,128]{1,0:T(8,128)S(1)}, f32[200,128]{1,0:T(8,128)S(1)}, f32[6,64,128]{2,1,0:T(8,128)S(1)}) custom-call(f32[192,128]{1,0:T(8,128)S(1)} %get-tuple-element.49.refs_0_.own_left, f32[200,128]{1,0:T(8,128)S(1)} %get-tuple-element.50.refs_1_.own_right, f32[200,128]{1,0:T(8,128)S(1)} %collective-permute-done.14.refs_2_, ...), custom_call_target="tpu_custom_call" | custom-call | bytes 1000000 | tf_op jit(solution)/shard_map/second_share/pallas_call | solution.py:368
  30.8 1.1 %collective-permute-start.17 = (f32[200,128]{1,0:T(8,128)S(1)}, f32[200,128]{1,0:T(8,128)S(1)}, u32[]{:S(2)}, u32[]{:S(2)}) collective-permute-start(f32[200,128]{1,0:T(8,128)S(1)} %get-tuple-element.55), channel_id=1, source_target_pairs={{0,4},{4,0},{8,12},{12,8},{1,5},{5,1},{9,13},{13,9},{2,6},{6,2},{1... | collective-permute-start | bytes 307208 | tf_op jit(solution)/shard_map/ppermute | solution.py:378
  31.9 1.1 %collective-permute-start.16 = (f32[192,128]{1,0:T(8,128)S(1)}, f32[192,128]{1,0:T(8,128)S(1)}, u32[]{:S(2)}, u32[]{:S(2)}) collective-permute-start(f32[192,128]{1,0:T(8,128)S(1)} %get-tuple-element.54), channel_id=1, source_target_pairs={{0,12},{4,8},{8,4},{12,0},{1,13},{5,9},{9,5},{13,1},{2,14},{6,10},... | collective-permute-start | bytes 294920 | tf_op jit(solution)/shard_map/ppermute | solution.py:377
  33.0 0.0 collective-permute-done.8.far
  33.0 0.0 collective-permute-done.9.near
  33.0 0.9 %first_final.1._ = f32[8,4096]{1,0:T(8,128)} custom-call(f32[4,8,128]{2,1,0:T(8,128)S(1)} %get-tuple-element.29.idents, f32[200,128]{1,0:T(8,128)S(1)} %get-tuple-element.39.refs_0_.own_left, f32[208,128]{1,0:T(8,128)S(1)} %get-tuple-element.40.refs_1_.own_right, f32[6,64,128]{2,1,0:T(8,128)S(1)} %get-tuple-element.41.sums, ...), custom_call_target="tpu_custom_call" | custom-call | bytes 1000000 | tf_op jit(solution)/shard_map/first_final/pallas_call | solution.py:474
  33.9 2.5 %collective-permute-done.16.far = f32[192,128]{1,0:T(8,128)S(1)} collective-permute-done((f32[192,128]{1,0:T(8,128)S(1)}, f32[192,128]{1,0:T(8,128)S(1)}, u32[]{:S(2)}, u32[]{:S(2)}) %collective-permute-start.16) | collective-permute-done | bytes 98336 | tf_op jit(solution)/shard_map/ppermute | solution.py:377
  36.4 0.0 collective-permute-done.17.near
  36.4 0.9 %second_final.1 = f32[8,4096]{1,0:T(8,128)} custom-call(f32[4,8,128]{2,1,0:T(8,128)S(1)} %get-tuple-element.29.idents, f32[192,128]{1,0:T(8,128)S(1)} %get-tuple-element.49.refs_0_.own_left, f32[200,128]{1,0:T(8,128)S(1)} %get-tuple-element.50.refs_1_.own_right, f32[6,64,128]{2,1,0:T(8,128)S(1)} %get-tuple-element.53.sums, ...), custom_call_target="tpu_custom_call" | custom-call | bytes 1000000 | tf_op jit(solution)/shard_map/second_final/pallas_call | solution.py:474
Async XLA Ops:
  2.1 6.7 %collective-permute-start = (f32[192,128]{1,0:T(8,128)S(1)}, f32[192,128]{1,0:T(8,128)S(1)}, u32[]{:S(2)}, u32[]{:S(2)}) collective-permute-start(f32[192,128]{1,0:T(8,128)S(1)} %get-tuple-element.31.first_right.refs_1_), channel_id=1, source_target_pairs={{0,1},{1,2},{2,3},{3,0},{4,5},{5,6},{6,7},{7,4},{8,9},{9,10},{10,1... | collective-permute-start | bytes 294920 | tf_op jit(solution)/shard_map/ppermute | solution.py:327
  4.3 7.7 %collective-permute-start.3 = (f32[216,128]{1,0:T(8,128)S(1)}, f32[216,128]{1,0:T(8,128)S(1)}, u32[]{:S(2)}, u32[]{:S(2)}) collective-permute-start(f32[216,128]{1,0:T(8,128)S(1)} %get-tuple-element.35), channel_id=1, source_target_pairs={{0,4},{4,0},{8,12},{12,8},{1,5},{5,1},{9,13},{13,9},{2,6},{6,2},{1... | collective-permute-start | bytes 331784 | tf_op jit(solution)/shard_map/ppermute | solution.py:378
  5.4 6.7 %collective-permute-start.1 = (f32[208,128]{1,0:T(8,128)S(1)}, f32[208,128]{1,0:T(8,128)S(1)}, u32[]{:S(2)}, u32[]{:S(2)}) collective-permute-start(f32[208,128]{1,0:T(8,128)S(1)} %get-tuple-element.30.first_left.refs_0_), channel_id=1, source_target_pairs={{0,3},{1,0},{2,1},{3,2},{4,7},{5,4},{6,5},{7,6},{8,11},{9,8},{10,9... | collective-permute-start | bytes 319496 | tf_op jit(solution)/shard_map/ppermute | solution.py:327
  7.1 4.9 %collective-permute-start.2 = (f32[208,128]{1,0:T(8,128)S(1)}, f32[208,128]{1,0:T(8,128)S(1)}, u32[]{:S(2)}, u32[]{:S(2)}) collective-permute-start(f32[208,128]{1,0:T(8,128)S(1)} %get-tuple-element.34), channel_id=1, source_target_pairs={{0,12},{4,8},{8,4},{12,0},{1,13},{5,9},{9,5},{13,1},{2,14},{6,10},... | collective-permute-start | bytes 319496 | tf_op jit(solution)/shard_map/ppermute | solution.py:377
  8.8 6.2 %collective-permute-start.10 = (f32[200,128]{1,0:T(8,128)S(1)}, f32[200,128]{1,0:T(8,128)S(1)}, u32[]{:S(2)}, u32[]{:S(2)}) collective-permute-start(f32[200,128]{1,0:T(8,128)S(1)} %get-tuple-element.33.second_right.refs_1_), channel_id=1, source_target_pairs={{0,1},{1,2},{2,3},{3,0},{4,5},{5,6},{6,7},{7,4},{8,9},{9,10},{10,1... | collective-permute-start | bytes 307208 | tf_op jit(solution)/shard_map/ppermute | solution.py:327
  8.8 5.6 %collective-permute-start.11 = (f32[192,128]{1,0:T(8,128)S(1)}, f32[192,128]{1,0:T(8,128)S(1)}, u32[]{:S(2)}, u32[]{:S(2)}) collective-permute-start(f32[192,128]{1,0:T(8,128)S(1)} %get-tuple-element.32.second_left.refs_0_), channel_id=1, source_target_pairs={{0,3},{1,0},{2,1},{3,2},{4,7},{5,4},{6,5},{7,6},{8,11},{9,8},{10,9... | collective-permute-start | bytes 294920 | tf_op jit(solution)/shard_map/ppermute | solution.py:327
  12.5 6.3 %collective-permute-start.5 = (f32[296,128]{1,0:T(8,128)S(1)}, f32[296,128]{1,0:T(8,128)S(1)}, u32[]{:S(2)}, u32[]{:S(2)}) collective-permute-start(f32[296,128]{1,0:T(8,128)S(1)} %get-tuple-element.38.refs_9_), channel_id=1, source_target_pairs={{0,4},{4,0},{8,12},{12,8},{1,5},{5,1},{9,13},{13,9},{2,6},{6,2},{1... | collective-permute-start | bytes 454664 | tf_op jit(solution)/shard_map/ppermute | solution.py:378
  13.3 5.5 %collective-permute-start.4 = (f32[288,128]{1,0:T(8,128)S(1)}, f32[288,128]{1,0:T(8,128)S(1)}, u32[]{:S(2)}, u32[]{:S(2)}) collective-permute-start(f32[288,128]{1,0:T(8,128)S(1)} %get-tuple-element.37.refs_8_), channel_id=1, source_target_pairs={{0,12},{4,8},{8,4},{12,0},{1,13},{5,9},{9,5},{13,1},{2,14},{6,10},... | collective-permute-start | bytes 442376 | tf_op jit(solution)/shard_map/ppermute | solution.py:377
  15.6 7.9 %collective-permute-start.13 = (f32[296,128]{1,0:T(8,128)S(1)}, f32[296,128]{1,0:T(8,128)S(1)}, u32[]{:S(2)}, u32[]{:S(2)}) collective-permute-start(f32[296,128]{1,0:T(8,128)S(1)} %get-tuple-element.48.refs_9_), channel_id=1, source_target_pairs={{0,4},{4,0},{8,12},{12,8},{1,5},{5,1},{9,13},{13,9},{2,6},{6,2},{1... | collective-permute-start | bytes 454664 | tf_op jit(solution)/shard_map/ppermute | solution.py:378
  17.7 5.8 %collective-permute-start.12 = (f32[288,128]{1,0:T(8,128)S(1)}, f32[288,128]{1,0:T(8,128)S(1)}, u32[]{:S(2)}, u32[]{:S(2)}) collective-permute-start(f32[288,128]{1,0:T(8,128)S(1)} %get-tuple-element.47.refs_8_), channel_id=1, source_target_pairs={{0,12},{4,8},{8,4},{12,0},{1,13},{5,9},{9,5},{13,1},{2,14},{6,10},... | collective-permute-start | bytes 442376 | tf_op jit(solution)/shard_map/ppermute | solution.py:377
  19.0 8.0 %collective-permute-start.6 = (f32[208,128]{1,0:T(8,128)S(1)}, f32[208,128]{1,0:T(8,128)S(1)}, u32[]{:S(2)}, u32[]{:S(2)}) collective-permute-start(f32[208,128]{1,0:T(8,128)S(1)} %get-tuple-element.40.refs_1_.own_right), channel_id=1, source_target_pairs={{0,1},{1,2},{2,3},{3,0},{4,5},{5,6},{6,7},{7,4},{8,9},{9,10},{10,1... | collective-permute-start | bytes 319496 | tf_op jit(solution)/shard_map/ppermute | solution.py:327
  19.1 7.9 %collective-permute-start.7 = (f32[200,128]{1,0:T(8,128)S(1)}, f32[200,128]{1,0:T(8,128)S(1)}, u32[]{:S(2)}, u32[]{:S(2)}) collective-permute-start(f32[200,128]{1,0:T(8,128)S(1)} %get-tuple-element.39.refs_0_.own_left), channel_id=1, source_target_pairs={{0,3},{1,0},{2,1},{3,2},{4,7},{5,4},{6,5},{7,6},{8,11},{9,8},{10,9... | collective-permute-start | bytes 307208 | tf_op jit(solution)/shard_map/ppermute | solution.py:327
  23.6 6.5 %collective-permute-start.14 = (f32[200,128]{1,0:T(8,128)S(1)}, f32[200,128]{1,0:T(8,128)S(1)}, u32[]{:S(2)}, u32[]{:S(2)}) collective-permute-start(f32[200,128]{1,0:T(8,128)S(1)} %get-tuple-element.50.refs_1_.own_right), channel_id=1, source_target_pairs={{0,1},{1,2},{2,3},{3,0},{4,5},{5,6},{6,7},{7,4},{8,9},{9,10},{10,1... | collective-permute-start | bytes 307208 | tf_op jit(solution)/shard_map/ppermute | solution.py:327
  23.7 5.4 %collective-permute-start.15 = (f32[192,128]{1,0:T(8,128)S(1)}, f32[192,128]{1,0:T(8,128)S(1)}, u32[]{:S(2)}, u32[]{:S(2)}) collective-permute-start(f32[192,128]{1,0:T(8,128)S(1)} %get-tuple-element.49.refs_0_.own_left), channel_id=1, source_target_pairs={{0,3},{1,0},{2,1},{3,2},{4,7},{5,4},{6,5},{7,6},{8,11},{9,8},{10,9... | collective-permute-start | bytes 294920 | tf_op jit(solution)/shard_map/ppermute | solution.py:327
  27.5 5.5 %collective-permute-start.8 = (f32[200,128]{1,0:T(8,128)S(1)}, f32[200,128]{1,0:T(8,128)S(1)}, u32[]{:S(2)}, u32[]{:S(2)}) collective-permute-start(f32[200,128]{1,0:T(8,128)S(1)} %get-tuple-element.42), channel_id=1, source_target_pairs={{0,12},{4,8},{8,4},{12,0},{1,13},{5,9},{9,5},{13,1},{2,14},{6,10},... | collective-permute-start | bytes 307208 | tf_op jit(solution)/shard_map/ppermute | solution.py:377
  28.8 4.3 %collective-permute-start.9 = (f32[200,128]{1,0:T(8,128)S(1)}, f32[200,128]{1,0:T(8,128)S(1)}, u32[]{:S(2)}, u32[]{:S(2)}) collective-permute-start(f32[200,128]{1,0:T(8,128)S(1)} %get-tuple-element.43), channel_id=1, source_target_pairs={{0,4},{4,0},{8,12},{12,8},{1,5},{5,1},{9,13},{13,9},{2,6},{6,2},{1... | collective-permute-start | bytes 307208 | tf_op jit(solution)/shard_map/ppermute | solution.py:378
  30.8 5.6 %collective-permute-start.17 = (f32[200,128]{1,0:T(8,128)S(1)}, f32[200,128]{1,0:T(8,128)S(1)}, u32[]{:S(2)}, u32[]{:S(2)}) collective-permute-start(f32[200,128]{1,0:T(8,128)S(1)} %get-tuple-element.55), channel_id=1, source_target_pairs={{0,4},{4,0},{8,12},{12,8},{1,5},{5,1},{9,13},{13,9},{2,6},{6,2},{1... | collective-permute-start | bytes 307208 | tf_op jit(solution)/shard_map/ppermute | solution.py:378
  31.9 4.5 %collective-permute-start.16 = (f32[192,128]{1,0:T(8,128)S(1)}, f32[192,128]{1,0:T(8,128)S(1)}, u32[]{:S(2)}, u32[]{:S(2)}) collective-permute-start(f32[192,128]{1,0:T(8,128)S(1)} %get-tuple-element.54), channel_id=1, source_target_pairs={{0,12},{4,8},{8,4},{12,0},{1,13},{5,9},{9,5},{13,1},{2,14},{6,10},... | collective-permute-start | bytes 294920 | tf_op jit(solution)/shard_map/ppermute | solution.py:377
